TPU v7x, 256 devices: a whole 4x4x8 slice. The times are simulated.
256 devices in a mesh: rows: 32 (over x, z), tp: 8 (over y, core).
Axes of the slice: x: 4, y: 4, z: 8, core: 2. Of those that a mesh axis runs over, the one named last changes fastest.
Arguments:
- text_embed: bfloat16 [24576, 8192], P('rows', 'tp'), may hold values from -24 to 24
- image_embed: bfloat16 [12288, 8192], P('rows', 'tp'), may hold values from -24 to 24
- image_start: int32 [512], replicated, may hold values from 0 to 24552, as said below
- norm_gain: float32 [8192], P('tp'), may hold values from 0.25 to 1.75
- key_weight: bfloat16 [8192, 1024], P('tp'), may hold values from -0.0625 to 0.0625
- value_weight: bfloat16 [8192, 1024], P('tp'), may hold values from -0.0625 to 0.0625
- key_target: bfloat16 [24576, 1024], P('rows', 'tp'), may hold values from -6 to 6
- value_target: bfloat16 [24576, 1024], P('rows', 'tp'), may hold values from -6 to 6
Outputs:
- keys: bfloat16 [24576, 1024], P('rows', 'tp')
- values: bfloat16 [24576, 1024], P('rows', 'tp')
- text_grad: bfloat16 [24576, 8192], P('rows', 'tp')
- image_grad: bfloat16 [12288, 8192], P('rows', 'tp')
Inputs may be any that keep to these rules, and one draw needn't show every extreme that they name: `image_start`: every image lies inside one block of 768 positions (block b holds positions b * 768 .. (b + 1) * 768 - 1); images never intersect; the 16 images of one index of rows (images r * 16 .. r * 16 + 15) lie in 16 different blocks; a block holds at most 32 images, and some block holds exactly that many (it holds no text) while another holds none.
All inputs are finite; a program needn't handle non-finite values.
Results may differ from a plain program's by a relative error of at most 0.014.
Values may be sent and summed in bfloat16 or wider, within the bound.
No kernel may reach another device: no remote copies, remote signals or barrier semaphores. Data moves between devices by JAX's collectives and lax.ppermute only.
A program may use at most 64 MiB of HBM per device.

v0:
```python
import jax
import jax.numpy as jnp
from jax import lax
from jax.sharding import PartitionSpec as P

WIDTH = 8192


epsilon = 1e-06


def on_device(
    text_embed,
    image_embed,
    image_start,
    norm_gain,
    key_weight,
    value_weight,
    key_target,
    value_target,
):
    shards = lax.axis_size("rows")
    myself = lax.axis_index("rows")
    images_here = shards // 2
    seq_rows = text_embed.shape[0]
    columns = text_embed.shape[1]
    image_len = image_embed.shape[0] // images_here
    starts = image_start.reshape(shards, images_here)
    shard_of = starts // seq_rows
    offset = starts % seq_rows
    own_dest = lax.dynamic_index_in_dim(shard_of, myself, 0, keepdims=False)
    pieces = image_embed.reshape(images_here, image_len, columns)
    outgoing = jnp.zeros((shards, image_len, columns), jnp.bfloat16).at[own_dest].set(pieces)
    incoming = lax.all_to_all(outgoing, "rows", split_axis=0, concat_axis=0, tiled=True)
    matched = shard_of == myself
    present = jnp.any(matched, axis=1)
    first_row = jnp.sum(jnp.where(matched, offset, 0), axis=1)
    within = jnp.arange(image_len, dtype=jnp.int32)
    landing = jnp.where(present[:, None], first_row[:, None] + within[None, :], seq_rows).reshape(
        -1
    )
    assembled = text_embed.at[landing].set(incoming.reshape(-1, columns), mode="drop")
    stream = assembled.astype(jnp.float32)
    partial_sq = jnp.sum(stream * stream, axis=1)
    scaled = (norm_gain[None, :] * stream).astype(jnp.bfloat16)
    key_part = jnp.dot(scaled, key_weight, preferred_element_type=jnp.float32)
    value_part = jnp.dot(scaled, value_weight, preferred_element_type=jnp.float32)
    squares = lax.psum(partial_sq, "tp")
    key_raw, value_raw = (
        lax.psum_scatter(key_part, "tp", scatter_dimension=1, tiled=True),
        lax.psum_scatter(value_part, "tp", scatter_dimension=1, tiled=True),
    )
    inverse = lax.rsqrt(squares / WIDTH + epsilon)
    keys = (inverse[:, None] * key_raw).astype(jnp.bfloat16)
    values = (inverse[:, None] * value_raw).astype(jnp.bfloat16)
    key_resid = (keys.astype(jnp.float32) - key_target.astype(jnp.float32)).astype(jnp.bfloat16)
    value_resid = (values.astype(jnp.float32) - value_target.astype(jnp.float32)).astype(
        jnp.bfloat16
    )
    key_all, value_all, keys_all, values_all = (
        lax.all_gather(key_resid, "tp", axis=1, tiled=True),
        lax.all_gather(value_resid, "tp", axis=1, tiled=True),
        lax.all_gather(keys, "tp", axis=1, tiled=True),
        lax.all_gather(values, "tp", axis=1, tiled=True),
    )
    radial = (
        jnp.sum(
            key_all.astype(jnp.float32) * keys_all.astype(jnp.float32)
            + value_all.astype(jnp.float32) * values_all.astype(jnp.float32),
            axis=1,
        )
        / inverse
    )
    contract = (((1,), (1,)), ((), ()))
    back = lax.dot_general(key_all, key_weight, contract, preferred_element_type=jnp.float32)
    back = back + lax.dot_general(
        value_all, value_weight, contract, preferred_element_type=jnp.float32
    )
    grad = (
        norm_gain[None, :] * inverse[:, None] * back
        - (inverse**3 * radial / WIDTH)[:, None] * stream
    )
    grad_round = grad.astype(jnp.bfloat16)
    marked = jnp.zeros((seq_rows,), jnp.bool_).at[landing].set(True, mode="drop")
    text_grad = jnp.where(marked[:, None], jnp.zeros_like(grad_round), grad_round)
    sendback = jnp.take(grad_round, landing, axis=0, mode="fill", fill_value=0).reshape(
        shards, image_len, columns
    )
    returned = lax.all_to_all(sendback, "rows", split_axis=0, concat_axis=0, tiled=True)
    image_grad = returned[own_dest].reshape(-1, columns)
    return (keys, values, text_grad, image_grad)


def solution(mesh):
    in_specs = (
        P("rows", "tp"),
        P("rows", "tp"),
        P(),
        P("tp"),
        P("tp", None),
        P("tp", None),
        P("rows", "tp"),
        P("rows", "tp"),
    )
    out_specs = (P("rows", "tp"), P("rows", "tp"), P("rows", "tp"), P("rows", "tp"))
    return jax.shard_map(
        on_device, mesh=mesh, in_specs=in_specs, out_specs=out_specs, check_vma=False
    )
```

profile of v0, /device:TPU:1, one launch (start us, length us, event | category | flops | bytes accessed | tf_op | source)
XLA Modules:
  0.0 352.1 jit_solution(11674426282750954378)
XLA Ops:
  7.2 0.0 copy-start
  7.2 0.0 copy-start.7
  7.2 2.8 copy.15
  10.0 0.0 copy-start.4
  10.0 0.0 copy-done.7
  10.0 0.1 div.19
  10.1 0.1 ne.27
  10.2 0.1 rem.19
  10.3 0.1 fusion.16
  10.4 1.4 broadcast_in_dim.61
  11.8 0.0 copy-done.4
  11.8 2.8 scatter_fusion
  14.6 12.0 %all-to-all-start = ((bf16[32,24,1024]{2,1,0:T(8,128)(2,1)}), bf16[32,24,1024]{2,1,0:T(8,128)(2,1)}, u32[]{:S(2)}, u32[]{:S(2)}) async-start(bf16[32,24,1024]{2,1,0:T(8,128)(2,1)} %scatter_fusion), calls=%async_computation | async-start | bytes 3145728 | tf_op jit(solution)/shard_map/all_to_all | solution.py:34
  26.6 0.0 reduce-scatter.5.cloned.1.call-start
  26.6 0.1 fusion.9
  26.7 0.1 add_select_fusion.2
  26.8 0.1 select_n.81
  26.9 36.4 %all-to-all-done = bf16[32,24,1024]{2,1,0:T(8,128)(2,1)} async-done(((bf16[32,24,1024]{2,1,0:T(8,128)(2,1)}), bf16[32,24,1024]{2,1,0:T(8,128)(2,1)}, u32[]{:S(2)}, u32[]{:S(2)}) %all-to-all-start) | async-done | bytes 1572896 | tf_op jit(solution)/shard_map/all_to_all | solution.py:34
  63.4 0.0 copy-start.9
  63.4 9.1 %scatter_fusion.1 = bf16[768,1024]{1,0:T(8,128)(2,1)} fusion(bf16[768,1024]{1,0:T(8,128)(2,1)} %copy.15, s32[768]{0:T(1024)S(1)} %fusion.12, bf16[768,1024]{1,0:T(8,128)(2,1)} %bitcast.3), kind=kCustom, calls=%fused_computation.3 | custom fusion | bytes 4721664 | tf_op jit(solution)/shard_map/scatter | solution.py:42
  72.5 0.0 copy-done
  72.5 0.0 copy-done.9
  72.5 4.8 %fusion.4 = f32[768,1024]{1,0:T(8,128)} fusion(bf16[1024,1024]{1,0:T(8,128)(2,1)S(1)} %copy-done, bf16[768,1024]{1,0:T(8,128)(2,1)} %scatter_fusion.1, f32[1024]{0:T(1024)S(1)} %copy-done.9), kind=kOutput, calls=%fused_computation.15 | convolution fusion | flops 1612972032 | bytes 6819840 | tf_op jit(solution)/shard_map/dot_general | solution.py:47
  77.4 0.0 reduce-scatter.5.cloned.1.call-update
  77.4 0.0 reduce-scatter.3.cloned.1.call-start
  77.4 5.5 %fusion.6 = f32[768,1024]{1,0:T(8,128)} fusion(bf16[1024,1024]{1,0:T(8,128)(2,1)} %param.12, bf16[768,1024]{1,0:T(8,128)(2,1)} %scatter_fusion.1, f32[1024]{0:T(1024)S(1)} %copy-done.9), kind=kOutput, calls=%fused_computation.16 | convolution fusion | flops 1612972032 | bytes 6819840 | tf_op jit(solution)/shard_map/dot_general | solution.py:46
  83.0 0.0 reduce-scatter.3.cloned.1.call-update
  83.0 0.0 copy-start.5
  83.0 0.0 copy-start.6
  83.0 0.0 all-gather.11.cloned.1.call-start
  83.1 1.9 fusion
  84.9 15.5 %psum.7 = f32[768]{0:T(1024)S(1)} all-reduce(f32[768]{0:T(1024)S(1)} %fusion), channel_id=1, replica_groups=mesh['rows'=32,'tp'=8] {'tp'}, use_global_device_ids=true, to_apply=%region_5.6 | all-reduce | flops 768 | bytes 6144 | tf_op jit(solution)/shard_map/psum | solution.py:48
  100.4 12.8 %reduce-scatter.5.cloned.1.call-done = f32[768,128]{1,0:T(8,128)} async-done(((f32[768,1024]{1,0:T(8,128)}), f32[768,128]{1,0:T(8,128)}) %reduce-scatter.5.cloned.1.call-update) | async-done | bytes 393232 | tf_op jit(solution)/shard_map/reduce_scatter | solution.py:51
  113.2 39.8 %reduce-scatter.3.cloned.1.call-done = f32[768,128]{1,0:T(8,128)} async-done(((f32[768,1024]{1,0:T(8,128)}), f32[768,128]{1,0:T(8,128)}) %reduce-scatter.3.cloned.1.call-update) | async-done | bytes 393232 | tf_op jit(solution)/shard_map/reduce_scatter | solution.py:50
  153.0 0.0 copy-done.5
  153.0 0.0 copy-done.6
  153.0 2.2 subtract_convert_fusion
  155.2 0.0 all-gather.11.cloned.1.call-update
  155.2 0.0 all-gather.7.cloned.1.call-start
  155.3 0.5 all-gather.7.cloned.1.call-update
  155.8 0.0 all-gather.9.cloned.1.call-start
  155.9 0.5 all-gather.9.cloned.1.call-update
  156.4 0.0 all-gather.5.cloned.1.call-start
  156.4 0.5 all-gather.5.cloned.1.call-update
  157.0 3.6 %scatter_custom_fusion.2 = pred[768]{0:T(1024)(128)(4,1)S(1)} fusion(s32[768]{0:T(1024)S(1)} %fusion.12, pred[768]{0:T(1024)(128)(4,1)S(1)} %broadcast.97, pred[]{:T(512)} %constant.35.clone.1), kind=kCustom, calls=%fused_computation.40 | custom fusion | bytes 769 | tf_op jit(solution)/shard_map/scatter | solution.py:84
  160.6 0.1 compare_and_fusion
  160.7 24.5 %all-gather.11.cloned.1.call-done = bf16[768,1024]{1,0:T(8,128)(2,1)} async-done(((bf16[768,128]{1,0:T(8,128)(2,1)}), bf16[768,1024]{1,0:T(8,128)(2,1)}) %all-gather.11.cloned.1.call-update) | async-done | bytes 1572880 | tf_op jit(solution)/shard_map/all_gather | solution.py:64
  185.2 31.0 %all-gather.7.cloned.1.call-done = bf16[768,1024]{1,0:T(8,128)(2,1)} async-done(((bf16[768,128]{1,0:T(8,128)(2,1)}), bf16[768,1024]{1,0:T(8,128)(2,1)}) %all-gather.7.cloned.1.call-update) | async-done | bytes 1572880 | tf_op jit(solution)/shard_map/all_gather | solution.py:62
  216.2 31.0 %all-gather.9.cloned.1.call-done = bf16[768,1024]{1,0:T(8,128)(2,1)} async-done(((bf16[768,128]{1,0:T(8,128)(2,1)}), bf16[768,1024]{1,0:T(8,128)(2,1)}) %all-gather.9.cloned.1.call-update) | async-done | bytes 1572880 | tf_op jit(solution)/shard_map/all_gather | solution.py:63
  247.2 30.4 %all-gather.5.cloned.1.call-done = bf16[768,1024]{1,0:T(8,128)(2,1)} async-done(((bf16[768,128]{1,0:T(8,128)(2,1)}), bf16[768,1024]{1,0:T(8,128)(2,1)}) %all-gather.5.cloned.1.call-update) | async-done | bytes 1572880 | tf_op jit(solution)/shard_map/all_gather | solution.py:61
  277.6 0.0 copy-start.3
  277.6 3.9 %add_reduce_fusion = f32[768]{0:T(1024)S(1)} fusion(bf16[768,1024]{1,0:T(8,128)(2,1)} %all-gather.11.cloned.1.call-done, bf16[768,1024]{1,0:T(8,128)(2,1)} %all-gather.7.cloned.1.call-done, bf16[768,1024]{1,0:T(8,128)(2,1)} %all-gather.9.cloned.1.call-done, bf16[768,1024]{1,0:T(8,128)(2,1)} %all-gather.5.cloned.1.call-done), kind=kLoop, calls=%fused_computation.12 | loop fusion | flops 6290688 | bytes 6294528 | tf_op jit(solution)/shard_map/reduce_sum | solution.py:67
  281.5 0.0 copy-done.3
  281.5 0.1 copy-done.8
  281.6 0.0 copy-start.2
  281.6 1.9 fusion.17
  283.4 0.0 copy-done.1
  283.4 0.0 copy-done.2
  283.5 3.9 %broadcast_select_fusion = (bf16[768,1024]{1,0:T(8,128)(2,1)}, bf16[768,1024]{1,0:T(8,128)(2,1)}) fusion(pred[768]{0:T(1024)(128)(4,1)S(1)} %scatter_custom_fusion.2, bf16[768,1024]{1,0:T(8,128)(2,1)S(1)} %copy-done.1, f32[768]{0:T(1024)S(1)} %fusion.11, f32[768,1024]{1,0:T(8,128)S(1)} %fusion.17, bf16[768,1024]{1,0:T(8,128)(2,1)S(1)} %copy-done.2, ...), kind=kOutput, calls=%fused_computation.13 | convolution fusion | flops 1616904192 | bytes 11545344 | tf_op jit(solution)/shard_map/dot_general | solution.py:76
  287.3 6.2 %gather_fusion = bf16[768,1024]{1,0:T(8,128)(2,1)} fusion(bf16[768,1024]{1,0:T(8,128)(2,1)} %get-tuple-element.16, s32[1024]{0:T(1024)S(1)} %pad_clamp_fusion.1), kind=kCustom, calls=%fused_computation | custom fusion | bytes 3148800 | tf_op jit(solution)/shard_map/jit(_take)/gather | solution.py:86
  293.5 2.8 broadcast_select_fusion.1
  296.2 9.6 %all-to-all-start.1 = ((bf16[32,24,1024]{2,1,0:T(8,128)(2,1)}), bf16[32,24,1024]{2,1,0:T(8,128)(2,1)}, u32[]{:S(2)}, u32[]{:S(2)}) async-start(bf16[32,24,1024]{2,1,0:T(8,128)(2,1)} %broadcast_select_fusion.1), calls=%async_computation.3 | async-start | bytes 3145728 | tf_op jit(solution)/shard_map/all_to_all | solution.py:89
  305.9 36.5 %all-to-all-done.1 = bf16[32,24,1024]{2,1,0:T(8,128)(2,1)} async-done(((bf16[32,24,1024]{2,1,0:T(8,128)(2,1)}), bf16[32,24,1024]{2,1,0:T(8,128)(2,1)}, u32[]{:S(2)}, u32[]{:S(2)}) %all-to-all-start.1) | async-done | bytes 1572896 | tf_op jit(solution)/shard_map/all_to_all | solution.py:89
  342.4 2.9 gather_fusion.1
  (11 shorter events, 0.1 us)
Async XLA Ops:
  7.2 65.3 %copy-start = (bf16[1024,1024]{1,0:T(8,128)(2,1)S(1)}, bf16[1024,1024]{1,0:T(8,128)(2,1)}, u32[]{:S(2)}) copy-start(bf16[1024,1024]{1,0:T(8,128)(2,1)} %param.13) | copy-start | bytes 6291460
  7.2 2.8 copy-start.7
  10.0 1.8 copy-start.4
  14.6 48.8 %all-to-all-start = ((bf16[32,24,1024]{2,1,0:T(8,128)(2,1)}), bf16[32,24,1024]{2,1,0:T(8,128)(2,1)}, u32[]{:S(2)}, u32[]{:S(2)}) async-start(bf16[32,24,1024]{2,1,0:T(8,128)(2,1)} %scatter_fusion), calls=%async_computation | async-start | bytes 3145728 | tf_op jit(solution)/shard_map/all_to_all | solution.py:34
  26.6 86.6 %reduce-scatter.5.cloned.1.call-start = ((), (), s32[]{:S(2)}) async-start(), calls=%async_computation.5 | async-start | bytes 3538944 | tf_op jit(solution)/shard_map/reduce_scatter | solution.py:51
  63.4 9.2 %copy-start.9 = (f32[1024]{0:T(1024)S(1)}, f32[1024]{0:T(1024)}, u32[]{:S(2)}) copy-start(f32[1024]{0:T(1024)} %param.11) | copy-start | bytes 12292
  77.4 75.6 %reduce-scatter.3.cloned.1.call-start = ((), (), s32[]{:S(2)}) async-start(), calls=%async_computation.4 | async-start | bytes 3538944 | tf_op jit(solution)/shard_map/reduce_scatter | solution.py:50
  83.0 70.0 %copy-start.5 = (bf16[768,128]{1,0:T(8,128)(2,1)S(1)}, bf16[768,128]{1,0:T(8,128)(2,1)}, u32[]{:S(2)}) copy-start(bf16[768,128]{1,0:T(8,128)(2,1)} %param.15) | copy-start | bytes 589828
  83.0 70.0 %copy-start.6 = (bf16[768,128]{1,0:T(8,128)(2,1)S(1)}, bf16[768,128]{1,0:T(8,128)(2,1)}, u32[]{:S(2)}) copy-start(bf16[768,128]{1,0:T(8,128)(2,1)} %param.14) | copy-start | bytes 589828
  83.0 102.2 %all-gather.11.cloned.1.call-start = ((), (), s32[]{:S(2)}) async-start(), calls=%async_computation.9 | async-start | bytes 1769472 | tf_op jit(solution)/shard_map/all_gather | solution.py:64
  155.2 60.9 %all-gather.7.cloned.1.call-start = ((), (), s32[]{:S(2)}) async-start(), calls=%async_computation.7 | async-start | bytes 1769472 | tf_op jit(solution)/shard_map/all_gather | solution.py:62
  155.8 91.4 %all-gather.9.cloned.1.call-start = ((), (), s32[]{:S(2)}) async-start(), calls=%async_computation.8 | async-start | bytes 1769472 | tf_op jit(solution)/shard_map/all_gather | solution.py:63
  156.4 121.2 %all-gather.5.cloned.1.call-start = ((), (), s32[]{:S(2)}) async-start(), calls=%async_computation.6 | async-start | bytes 1769472 | tf_op jit(solution)/shard_map/all_gather | solution.py:61
  277.6 3.9 %copy-start.3 = (bf16[768,1024]{1,0:T(8,128)(2,1)S(1)}, bf16[768,1024]{1,0:T(8,128)(2,1)}, u32[]{:S(2)}) copy-start(bf16[768,1024]{1,0:T(8,128)(2,1)} %all-gather.5.cloned.1.call-done) | copy-start | bytes 4718596
  277.6 3.9 %copy-start.8 = (bf16[1024,1024]{1,0:T(8,128)(2,1)S(1)}, bf16[1024,1024]{1,0:T(8,128)(2,1)}, u32[]{:S(2)}) copy-start(bf16[1024,1024]{1,0:T(8,128)(2,1)} %param.12) | copy-start | bytes 6291460
  281.6 1.9 copy-start.1
  281.6 1.9 copy-start.2
  296.2 46.1 %all-to-all-start.1 = ((bf16[32,24,1024]{2,1,0:T(8,128)(2,1)}), bf16[32,24,1024]{2,1,0:T(8,128)(2,1)}, u32[]{:S(2)}, u32[]{:S(2)}) async-start(bf16[32,24,1024]{2,1,0:T(8,128)(2,1)} %broadcast_select_fusion.1), calls=%async_computation.3 | async-start | bytes 3145728 | tf_op jit(solution)/shard_map/all_to_all | solution.py:89
Sparse Core Ops, SparseCore 0:
  77.5 35.6 reduce-scatter.4
  115.7 37.2 reduce-scatter.2
  155.4 29.7 all-gather.10
  187.4 28.7 all-gather.6
  218.4 28.7 all-gather.8
  248.9 28.7 all-gather.4
where the time goes:
time: 354 us; the launch traced here: 352 us
  waiting for transfers between devices  244 us (69%)
  local copies, waits for them, and re-layouts  29.2 us (8%)
  starting transfers between devices  21.8 us (6%)
  matrix products  16.1 us (5%)
  blocking collectives  15.5 us (4%)
  between operations  14.3 us (4%)
  other arithmetic  11.2 us (3%)
    reduce_scatter x1, waiting for transfers between devices, on_device(): lax.psum_scatter(key_part, 'tp', scatter_dimension=1, tiled=True)  39.8 us
    all_to_all x1, waiting for transfers between devices, on_device(): lax.all_to_all(sendback, 'rows', split_axis=0, concat_axis=0, tiled=True)  36.5 us
    all_to_all x1, waiting for transfers between devices, on_device(): lax.all_to_all(outgoing, 'rows', split_axis=0, concat_axis=0, tiled=True)  36.4 us
    all_gather x1, waiting for transfers between devices, on_device(): lax.all_gather(value_resid, 'tp', axis=1, tiled=True)  31 us
    all_gather x1, waiting for transfers between devices, on_device(): lax.all_gather(keys, 'tp', axis=1, tiled=True)  31 us
    all_gather x1, waiting for transfers between devices, on_device(): lax.all_gather(key_resid, 'tp', axis=1, tiled=True)  30.4 us
    all_gather x1, waiting for transfers between devices, on_device(): lax.all_gather(values, 'tp', axis=1, tiled=True)  24.5 us
    psum x1, blocking collectives, on_device(): squares = lax.psum(partial_sq, 'tp')  15.5 us
  transfers between devices with their start and end apart: 8, of which 8 were waited for; matrix products, arithmetic and copies ran while one was open for 3% of the time, Pallas kernels for 0%

commit v1 on v0

v1 whole, which is shorter than its diff:
```python
import functools

import jax
import jax.numpy as jnp
from jax import lax
from jax.experimental import pallas as pl
from jax.experimental.pallas import tpu as pltpu
from jax.sharding import PartitionSpec as P

WIDTH = 8192
EPSILON = 1e-06
IMAGE_LEN = 24
GROUP = 384
EXTRA = 16
HEAD = 128
PAIR = 2 * HEAD
RINGS = 4

F32 = jnp.float32
BF16 = jnp.bfloat16
PARAMS = pltpu.CompilerParams(vmem_limit_bytes=40 * 2**20)


def identity_mask():
    shape = (HEAD, HEAD)
    return lax.broadcasted_iota(jnp.int32, shape, 0) == lax.broadcasted_iota(jnp.int32, shape, 1)


def column_to_lanes(column):
    eye = identity_mask()
    row = lax.broadcasted_iota(jnp.int32, (8, HEAD), 0)
    out = jnp.zeros((8, HEAD), F32)
    for p in range(GROUP // HEAD):
        piece = column[p * HEAD : (p + 1) * HEAD, :]
        lanes = jnp.sum(jnp.where(eye, piece, 0.0), axis=0, keepdims=True)
        out = jnp.where(row == p, lanes, out)
    return out


def lanes_to_column(lanes):
    eye = identity_mask()
    pieces = [
        jnp.sum(jnp.where(eye, lanes[p : p + 1, :], 0.0), axis=1, keepdims=True)
        for p in range(GROUP // HEAD)
    ]
    return jnp.concatenate(pieces, axis=0)


def split_extra(lanes):
    high = lanes.astype(BF16).astype(F32)
    both = jnp.concatenate([high, lanes - high], axis=0)
    return jnp.concatenate([both, jnp.zeros((EXTRA, HEAD), F32)], axis=1).astype(BF16)


def join_extra(block):
    block = block.astype(F32)
    return block[0:8, 0:HEAD] + block[8:16, 0:HEAD]


def prepare(x_ref, gain_ref, scaled, lanes):
    x = x_ref[...].astype(F32)
    scaled[...] = (gain_ref[...] * x).astype(BF16)
    lanes[...] = column_to_lanes(jnp.sum(x * x, axis=1, keepdims=True))


def product(scaled, wk_ref, wv_ref):
    weight = jnp.concatenate([wk_ref[...], wv_ref[...]], axis=1)
    return jnp.dot(scaled[...], weight, preferred_element_type=F32)


def forward_other_kernel(place, x_ref, gain_ref, wk_ref, wv_ref, out_ref, scaled, lanes):
    @pl.when(pl.program_id(0) == 0)
    def _():
        prepare(x_ref, gain_ref, scaled, lanes)

    out_ref[0, 0:GROUP, :] = product(scaled, wk_ref, wv_ref).astype(BF16)
    out_ref[0, GROUP:, :] = split_extra(lanes[...])


def forward_own_kernel(
    place, x_ref, gain_ref, wk_ref, wv_ref, in_ref, out0, out1, out2, out3, scaled, lanes
):
    step = pl.program_id(0)

    @pl.when(step == 0)
    def _():
        prepare(x_ref, gain_ref, scaled, lanes)

    total = (product(scaled, wk_ref, wv_ref) + in_ref[0, 0:GROUP, :].astype(F32)).astype(BF16)
    extra = split_extra(lanes[...] + join_extra(in_ref[0, GROUP:, :]))
    for d, out_ref in enumerate((out0, out1, out2, out3)):

        @pl.when(step == d)
        def _(out_ref=out_ref):
            out_ref[0:GROUP, :] = total
            out_ref[GROUP:, :] = extra


def forward(place, x, block, gain, wk, wv, arrived=None):
    own = arrived is not None

    def columns(d, s):
        core = s[1] if own else 1 - s[1]
        return (0, 2 * lax.rem(s[0] + d, RINGS) + core)

    in_specs = [
        pl.BlockSpec((GROUP, x.shape[1]), lambda d, s: (block, 0)),
        pl.BlockSpec((1, x.shape[1]), lambda d, s: (0, 0)),
        pl.BlockSpec((wk.shape[0], HEAD), columns),
        pl.BlockSpec((wk.shape[0], HEAD), columns),
    ]
    operands = [x, gain, wk, wv]
    rows = GROUP + EXTRA
    if own:
        in_specs.append(pl.BlockSpec((1, rows, PAIR), lambda d, s: (d, 0, 0)))
        operands.append(arrived)
        out_shape = [jax.ShapeDtypeStruct((rows, PAIR), BF16)] * RINGS
        out_specs = [pl.BlockSpec((rows, PAIR), lambda d, s: (0, 0))] * RINGS
    else:
        out_shape = jax.ShapeDtypeStruct((RINGS, rows, PAIR), BF16)
        out_specs = pl.BlockSpec((1, rows, PAIR), lambda d, s: (d, 0, 0))
    return pl.pallas_call(
        forward_own_kernel if own else forward_other_kernel,
        grid_spec=pltpu.PrefetchScalarGridSpec(
            num_scalar_prefetch=1,
            grid=(RINGS,),
            in_specs=in_specs,
            out_specs=out_specs,
            scratch_shapes=[pltpu.VMEM((GROUP, x.shape[1]), BF16), pltpu.VMEM((8, HEAD), F32)],
        ),
        out_shape=out_shape,
        compiler_params=PARAMS,
        cost_estimate=pl.CostEstimate(
            flops=2 * GROUP * x.shape[1] * RINGS * PAIR, bytes_accessed=5 * 2**20, transcendentals=0
        ),
        name="forward_own" if own else "forward_other",
    )(place, *operands)


def gathered(refs):
    total = refs[0][0:GROUP, :].astype(F32)
    lanes = join_extra(refs[0][GROUP:, :])
    for ref in refs[1:]:
        total = total + ref[0:GROUP, :].astype(F32)
        lanes = lanes + join_extra(ref[GROUP:, :])
    inverse = lax.rsqrt(lanes_to_column(lanes) / WIDTH + EPSILON)
    return (inverse * total).astype(BF16), inverse


def residual(both, target, inverse, resid_ref, inverse_ref):
    resid = (both.astype(F32) - target).astype(BF16)
    dots = jnp.sum(resid.astype(F32) * both.astype(F32), axis=1, keepdims=True)
    resid_ref[0:GROUP, :] = resid
    resid_ref[GROUP:, :] = split_extra(column_to_lanes(dots))
    inverse_ref[...] = jnp.broadcast_to(inverse, (GROUP, HEAD))


def text_combine_kernel(a, b, c, d, kt_ref, vt_ref, keys_ref, values_ref, resid_ref, inverse_ref):
    both, inverse = gathered((a, b, c, d))
    target = jnp.concatenate([kt_ref[...], vt_ref[...]], axis=1).astype(F32)
    keys_ref[...] = both[:, 0:HEAD]
    values_ref[...] = both[:, HEAD:]
    residual(both, target, inverse, resid_ref, inverse_ref)


def one_hot(shape, match):
    return jnp.where(match, jnp.ones(shape, F32), jnp.zeros(shape, F32)).astype(BF16)


def slot_columns(rows, first, count, lanes_ref):
    row = first + lax.broadcasted_iota(jnp.int32, (rows, count), 0)
    begin = IMAGE_LEN * lax.broadcasted_iota(jnp.int32, (rows, count), 1)
    inside = (row >= begin) & (row < begin + IMAGE_LEN)
    value = lanes_ref[...] + (row - begin).astype(F32)
    return jnp.sum(jnp.where(inside, value, 0.0), axis=1, keepdims=True)


def slot_lanes(rows, count, column_ref):
    row = lax.broadcasted_iota(jnp.int32, (count, rows), 1)
    begin = IMAGE_LEN * lax.broadcasted_iota(jnp.int32, (count, rows), 0)
    inside = (row >= begin) & (row < begin + IMAGE_LEN)
    value = column_ref[...] + (row - begin).astype(F32)
    return jnp.sum(jnp.where(inside, value, 0.0), axis=0, keepdims=True)


def image_combine_kernel(
    a, b, c, d, arrived_ref, dest_lanes, dest_column, send_ref, resid_ref, inverse_ref
):
    slots = arrived_ref.shape[0]
    images = GROUP // IMAGE_LEN
    both, inverse = gathered((a, b, c, d))
    slot = slot_columns(GROUP, 0, images, dest_lanes)
    shape = (GROUP, slots)
    match = lax.broadcasted_iota(jnp.int32, shape, 1).astype(F32) == slot
    target = jnp.dot(one_hot(shape, match), arrived_ref[...], preferred_element_type=F32)
    residual(both, target, inverse, resid_ref, inverse_ref)
    shape = (slots, GROUP)
    match = lax.broadcasted_iota(jnp.int32, shape, 0).astype(F32) == slot_lanes(
        GROUP, images, dest_column
    )
    send_ref[...] = jnp.dot(one_hot(shape, match), both, preferred_element_type=F32).astype(BF16)


def combine(parts, targets, block):
    rows = GROUP + EXTRA
    part = pl.BlockSpec((rows, PAIR), lambda i: (0, 0))
    target = pl.BlockSpec((GROUP, HEAD), lambda i: (block, 0))
    head = pl.BlockSpec((GROUP, HEAD), lambda i: (0, 0))
    return pl.pallas_call(
        text_combine_kernel,
        grid=(1,),
        in_specs=[part] * RINGS + [target] * 2,
        out_specs=[head, head, part, head],
        out_shape=[
            jax.ShapeDtypeStruct((GROUP, HEAD), BF16),
            jax.ShapeDtypeStruct((GROUP, HEAD), BF16),
            jax.ShapeDtypeStruct((rows, PAIR), BF16),
            jax.ShapeDtypeStruct((GROUP, HEAD), F32),
        ],
        compiler_params=PARAMS,
        cost_estimate=pl.CostEstimate(flops=2**22, bytes_accessed=2**21, transcendentals=0),
        name="text_combine",
    )(*parts, *targets)


def image_combine(parts, arrived, dest):
    rows = GROUP + EXTRA
    return pl.pallas_call(
        image_combine_kernel,
        out_shape=[
            jax.ShapeDtypeStruct(arrived.shape, BF16),
            jax.ShapeDtypeStruct((rows, PAIR), BF16),
            jax.ShapeDtypeStruct((GROUP, HEAD), F32),
        ],
        compiler_params=PARAMS,
        cost_estimate=pl.CostEstimate(flops=2**28, bytes_accessed=2**21, transcendentals=0),
        name="image_combine",
    )(*parts, arrived, dest[None, :], dest[:, None])


def gather_kernel(first_ref, kt_ref, vt_ref, out_ref):
    rows, slots = kt_ref.shape[0], first_ref.shape[1]
    step = HEAD
    both = jnp.concatenate([kt_ref[...], vt_ref[...]], axis=1)
    for begin in range(0, out_ref.shape[0], step):
        place = slot_columns(step, begin, slots, first_ref)
        shape = (step, rows)
        match = lax.broadcasted_iota(jnp.int32, shape, 1).astype(F32) == place
        picked = jnp.dot(one_hot(shape, match), both, preferred_element_type=F32)
        out_ref[begin : begin + step, :] = picked.astype(BF16)


def gather_targets(first, key_target, value_target):
    slots = first.shape[0] * IMAGE_LEN
    return pl.pallas_call(
        gather_kernel,
        out_shape=jax.ShapeDtypeStruct((slots, PAIR), BF16),
        compiler_params=PARAMS,
        cost_estimate=pl.CostEstimate(flops=2**28, bytes_accessed=2**20, transcendentals=0),
        name="gather_targets",
    )(first[None, :], key_target, value_target)


def image_rows_mask(first_row, first_lanes):
    shape = (GROUP, first_lanes.shape[1])
    row = (first_row + lax.broadcasted_iota(jnp.int32, shape, 0)).astype(F32)
    begin = first_lanes[...]
    inside = (row >= begin) & (row < begin + IMAGE_LEN)
    return jnp.sum(jnp.where(inside, 1.0, 0.0), axis=1, keepdims=True) > 0.5


def merge_kernel(
    first_lanes, first_column, arrived_ref, k0, k1, v0, v1, keys_ref, values_ref
):
    slots = arrived_ref.shape[0]
    place = slot_lanes(slots, first_column.shape[0], first_column)
    for g, (k_ref, v_ref) in enumerate(((k0, v0), (k1, v1))):
        shape = (GROUP, slots)
        row = g * GROUP + lax.broadcasted_iota(jnp.int32, shape, 0)
        match = row.astype(F32) == place
        landed = jnp.dot(one_hot(shape, match), arrived_ref[...], preferred_element_type=F32)
        mask = image_rows_mask(g * GROUP, first_lanes)
        here = slice(g * GROUP, (g + 1) * GROUP)
        keys_ref[here, :] = jnp.where(mask, landed[:, 0:HEAD], k_ref[...].astype(F32)).astype(BF16)
        values_ref[here, :] = jnp.where(mask, landed[:, HEAD:], v_ref[...].astype(F32)).astype(BF16)


def merge(first, arrived, keys, values):
    rows = 2 * GROUP
    return pl.pallas_call(
        merge_kernel,
        out_shape=[jax.ShapeDtypeStruct((rows, HEAD), BF16)] * 2,
        compiler_params=PARAMS,
        cost_estimate=pl.CostEstimate(flops=2**28, bytes_accessed=2**21, transcendentals=0),
        name="merge",
    )(first[None, :], first[:, None], arrived, *keys, *values)


def backward_kernel(
    masked,
    aliased,
    block,
    place,
    x_ref,
    gain_ref,
    inverse_ref,
    first_lanes,
    wk_own,
    wv_own,
    wk_other,
    wv_other,
    *rest,
):
    resids = rest[0 : 2 * RINGS]
    out_ref, stacked, total, coefficient = rest[-4:]
    step = pl.program_id(0)

    @pl.when(step == 0)
    def _():
        lanes = jnp.zeros((8, HEAD), F32)
        for n, ref in enumerate(resids):
            core, d = n // RINGS, n % RINGS
            stacked[d, :, core * PAIR : (core + 1) * PAIR] = ref[0:GROUP, :]
            lanes = lanes + join_extra(ref[GROUP:, :])
        inverse = inverse_ref[...]
        column = lanes_to_column(lanes)
        coefficient[...] = inverse * inverse * column / WIDTH

    weight = jnp.concatenate([wk_own[...], wv_own[...], wk_other[...], wv_other[...]], axis=1)
    contract = (((1,), (1,)), ((), ()))
    back = lax.dot_general(stacked[step], weight, contract, preferred_element_type=F32)

    @pl.when(step == 0)
    def _():
        total[...] = back

    @pl.when((step > 0) & (step < RINGS - 1))
    def _():
        total[...] += back

    @pl.when(step == RINGS - 1)
    def _():
        inverse = inverse_ref[:, 0:1]
        grad = gain_ref[...] * inverse * (total[...] + back) - coefficient[:, 0:1] * x_ref[
            ...
        ].astype(F32)
        if masked:
            grad = jnp.where(image_rows_mask(block * GROUP, first_lanes), 0.0, grad)
        out_ref[...] = grad.astype(BF16)


def backward(place, x, block, gain, inverse, first, wk, wv, resids, masked, before=None):
    rows, width = GROUP + EXTRA, x.shape[1]

    def columns(other):
        def index(d, s):
            core = 1 - s[1] if other else s[1]
            return (0, 2 * lax.rem(s[0] + RINGS - d, RINGS) + core)

        return index

    weights = [pl.BlockSpec((width, HEAD), columns(other)) for other in (False, False, True, True)]
    in_specs = [
        pl.BlockSpec((GROUP, width), lambda d, s: (block, 0)),
        pl.BlockSpec((1, width), lambda d, s: (0, 0)),
        pl.BlockSpec((GROUP, HEAD), lambda d, s: (0, 0)),
        pl.BlockSpec((1, first.shape[0]), lambda d, s: (0, 0)),
        *weights,
        *[pl.BlockSpec((rows, PAIR), lambda d, s: (0, 0))] * (2 * RINGS),
    ]
    operands = [place, x, gain, inverse, first[None, :], wk, wv, wk, wv, *resids]
    aliases = {}
    if before is not None:
        in_specs.append(pl.BlockSpec(memory_space=pl.ANY))
        aliases = {len(operands): 0}
        operands.append(before)
    return pl.pallas_call(
        functools.partial(backward_kernel, masked, before is not None, block),
        grid_spec=pltpu.PrefetchScalarGridSpec(
            num_scalar_prefetch=1,
            grid=(RINGS,),
            in_specs=in_specs,
            out_specs=pl.BlockSpec((GROUP, width), lambda d, s: (block, 0)),
            scratch_shapes=[
                pltpu.VMEM((RINGS, GROUP, 2 * PAIR), BF16),
                pltpu.VMEM((GROUP, width), F32),
                pltpu.VMEM((GROUP, HEAD), F32),
            ],
        ),
        out_shape=jax.ShapeDtypeStruct(x.shape, BF16),
        input_output_aliases=aliases,
        compiler_params=PARAMS,
        cost_estimate=pl.CostEstimate(
            flops=2 * GROUP * width * 2 * RINGS * PAIR, bytes_accessed=8 * 2**20, transcendentals=0
        ),
        name="backward",
    )(*operands)


def around(x, shift):
    return lax.ppermute(
        x, "tp", [(2 * y + c, 2 * ((y + shift) % RINGS) + c) for y in range(RINGS) for c in range(2)]
    )


def across(x):
    return lax.ppermute(x, "tp", [(i, i ^ 1) for i in range(2 * RINGS)])


def on_device(
    text_embed,
    image_embed,
    image_start,
    norm_gain,
    key_weight,
    value_weight,
    key_target,
    value_target,
):
    shards = lax.axis_size("rows")
    myself = lax.axis_index("rows")
    mine = lax.axis_index("tp").astype(jnp.int32)
    place = jnp.stack([mine // 2, mine % 2])
    gain = norm_gain[None, :]
    starts = image_start.reshape(shards, -1)
    block_of = starts // text_embed.shape[0]
    offset = (starts - block_of * text_embed.shape[0]).astype(F32)
    here = jnp.where(block_of == myself, offset + 8192.0, 0.0)
    first = jnp.sum(here, axis=1) - 8192.0
    dest = IMAGE_LEN * lax.dynamic_index_in_dim(block_of, myself, 0, keepdims=False).astype(F32)

    inputs = [(text_embed, 0), (text_embed, 1), (image_embed, 0)]
    parts = []
    for x, block in inputs:
        other = forward(place, x, block, gain, key_weight, value_weight)
        own = forward(place, x, block, gain, key_weight, value_weight, across(other))
        parts.append([own[0]] + [around(own[d], d) for d in range(1, RINGS)])

    goals = gather_targets(first, key_target, value_target)
    goals = lax.all_to_all(goals, "rows", split_axis=0, concat_axis=0, tiled=True)
    k0, v0, *state0 = combine(parts[0], (key_target, value_target), 0)
    k1, v1, *state1 = combine(parts[1], (key_target, value_target), 1)
    send, *state2 = image_combine(parts[2], goals, dest)
    landed = lax.all_to_all(send, "rows", split_axis=0, concat_axis=0, tiled=True)

    grads = []
    for (x, block), (resid, inverse) in zip(inputs, (state0, state1, state2)):
        own = [resid] + [around(resid, d) for d in range(1, RINGS)]
        resids = own + [across(r) for r in own]
        before = grads[0] if len(grads) == 1 else None
        grads.append(
            backward(
                place, x, block, gain, inverse, first, key_weight, value_weight, resids,
                len(grads) < 2, before,
            )
        )
    keys, values = merge(first, landed, (k0, k1), (v0, v1))
    return (keys, values, grads[1], grads[2])


def solution(mesh):
    in_specs = (
        P("rows", "tp"),
        P("rows", "tp"),
        P(),
        P("tp"),
        P("tp", None),
        P("tp", None),
        P("rows", "tp"),
        P("rows", "tp"),
    )
    out_specs = (P("rows", "tp"), P("rows", "tp"), P("rows", "tp"), P("rows", "tp"))
    return jax.shard_map(
        on_device, mesh=mesh, in_specs=in_specs, out_specs=out_specs, check_vma=False
    )
```

time: 354 us -> 145 us (0.41)
  waiting for transfers between devices: 244 us -> 0.4 us
  Pallas kernels: 0 us -> 56.9 us
  starting transfers between devices: 21.8 us -> 53.1 us
  matrix products: 16.1 us -> 0 us
  blocking collectives: 15.5 us -> 0 us
  between operations: 14.3 us -> 0.94 us
  other arithmetic: 11.2 us -> 0.24 us
  local copies, waits for them, and re-layouts: 29.2 us -> 32.8 us
    all_gather x4 -> x0, waiting for transfers between devices: 117 us -> none  [the longest x1 31 us: on_device(): lax.all_gather(value_resid, 'tp', axis=1, tiled=True)]
    all_to_all x2, waiting for transfers between devices: 72.9 us -> 0.01 us  [the longest x1 0.01 us: on_device(): lax.all_to_all(goals, 'rows', split_axis=0, concat_axis=0, tiled=True)]
    pallas_call x0 -> x14, Pallas kernels: none -> 56.9 us  [the longest x6 26.7 us: forward(): pl.pallas_call(forward_own_kernel if own else forward_other_kernel, grid_...]
    reduce_scatter x2 -> x0, waiting for transfers between devices: 52.6 us -> none  [the longest x1 39.8 us: on_device(): lax.psum_scatter(key_part, 'tp', scatter_dimension=1, tiled=True)]
    ppermute x0 -> x33, starting transfers between devices: none -> 33.9 us  [the longest x18 21.1 us: around(): lax.ppermute(x, 'tp', [(2 * y + c, 2 * ((y + shift) % RINGS) + c) for y i...]
    unnamed x21 -> x106, local copies, waits for them, and re-layouts: 2.92 us -> 32.6 us
    dot_general x4 -> x0, matrix products: 16.1 us -> none  [the longest x1 5.53 us: on_device(): key_part = jnp.dot(scaled, key_weight, preferred_element_type=jnp.float32)]
    scatter x3 -> x0, local copies, waits for them, and re-layouts: 15.5 us -> none  [the longest x1 9.14 us: on_device(): text_embed.at[landing].set(incoming.reshape(-1, columns), mode='drop')]
  transfers between devices with their start and end apart: 8 -> 35, of which waited for: 8 -> 1; matrix products, arithmetic and copies ran while one was open for 3% -> 0% of each run, Pallas kernels for 0% -> 36%
where the time goes in v1:
time: 145 us; the launch traced here: 144 us
  Pallas kernels  56.9 us (39%)
  starting transfers between devices  53.1 us (37%)
  local copies, waits for them, and re-layouts  32.8 us (23%)
    unnamed x106, local copies, waits for them, and re-layouts  32.6 us
    pallas_call x6, Pallas kernels, forward(): pl.pallas_call(forward_own_kernel if own else forward_other_kernel, grid_...  26.7 us
    pallas_call x3, Pallas kernels, backward(): pl.pallas_call(functools.partial(backward_kernel, masked, before is not N...  22.6 us
    ppermute x18, starting transfers between devices, around(): lax.ppermute(x, 'tp', [(2 * y + c, 2 * ((y + shift) % RINGS) + c) for y i...  21.1 us
    ppermute x15, starting transfers between devices, across(): return lax.ppermute(x, 'tp', [(i, i ^ 1) for i in range(2 * RINGS)])  12.8 us
    all_to_all x1, starting transfers between devices, on_device(): lax.all_to_all(goals, 'rows', split_axis=0, concat_axis=0, tiled=True)  10.3 us
    all_to_all x1, starting transfers between devices, on_device(): lax.all_to_all(send, 'rows', split_axis=0, concat_axis=0, tiled=True)  8.82 us
    pallas_call x2, Pallas kernels, combine(): pl.pallas_call(text_combine_kernel, grid=(1,), in_specs=[part] * RINGS +...  3.16 us
  transfers between devices with their start and end apart: 35, of which 1 were waited for; matrix products, arithmetic and copies ran while one was open for 0% of the time, Pallas kernels for 36%

profile of v1, /device:TPU:1, one launch (start us, length us, event | category | flops | bytes accessed | tf_op | source)
XLA Modules:
  0.0 144.4 jit_solution(9219517824929918566)
XLA Ops:
  0.7 1.6 %copy-done = bf16[1024,1024]{1,0:T(8,128)(2,1)S(1)} copy-done((bf16[1024,1024]{1,0:T(8,128)(2,1)S(1)}, bf16[1024,1024]{1,0:T(8,128)(2,1)}, u32[]{:S(2)}) %copy-start) | copy-done | bytes 2097176
  2.3 1.6 %copy-done.2 = bf16[1024,1024]{1,0:T(8,128)(2,1)S(1)} copy-done((bf16[1024,1024]{1,0:T(8,128)(2,1)S(1)}, bf16[1024,1024]{1,0:T(8,128)(2,1)}, u32[]{:S(2)}) %copy-start.2) | copy-done | bytes 2097176
  3.9 1.4 copy-done.8
  5.3 0.7 copy-done.20
  6.0 3.9 %forward_other.5 = bf16[4,400,256]{2,1,0:T(8,128)(2,1)} custom-call(s32[2]{0:T(128)S(1)} %pad_add_fusion.place, bf16[768,1024]{1,0:T(8,128)(2,1)S(1)} %copy-done.8, f32[1,1024]{1,0:T(1,128)S(1)} %bitcast.17, bf16[1024,1024]{1,0:T(8,128)(2,1)S(1)} %copy-done, bf16[1024,1024]{1,0:T(8,128)(2,1)S(1)} %copy-done.2), custom_call_target="tpu_custom_call" | custom-call | flops 805306368 | bytes 5242880 | tf_op jit(solution)/shard_map/forward_other/pallas_call | solution.py:122
  9.9 3.2 %collective-permute-start.8 = (bf16[4,400,256]{2,1,0:T(8,128)(2,1)}, bf16[4,400,256]{2,1,0:T(8,128)(2,1)}, u32[]{:S(2)}, u32[]{:S(2)}) collective-permute-start(bf16[4,400,256]{2,1,0:T(8,128)(2,1)} %forward_other.5), channel_id=1, source_target_pairs={{0,1},{1,0},{2,3},{3,2},{4,5},{5,4},{6,7},{7,6},{8,9},{9,8},{10,11... | collective-permute-start | bytes 2457608 | tf_op jit(solution)/shard_map/ppermute | solution.py:407
  13.2 3.9 %forward_other.4 = bf16[4,400,256]{2,1,0:T(8,128)(2,1)} custom-call(s32[2]{0:T(128)S(1)} %pad_add_fusion.place, bf16[768,1024]{1,0:T(8,128)(2,1)S(1)} %copy-done.8, f32[1,1024]{1,0:T(1,128)S(1)} %bitcast.18, bf16[1024,1024]{1,0:T(8,128)(2,1)S(1)} %copy-done, bf16[1024,1024]{1,0:T(8,128)(2,1)S(1)} %copy-done.2), custom_call_target="tpu_custom_call" | custom-call | flops 805306368 | bytes 5242880 | tf_op jit(solution)/shard_map/forward_other/pallas_call | solution.py:122
  17.1 3.9 %forward_other.3 = bf16[4,400,256]{2,1,0:T(8,128)(2,1)} custom-call(s32[2]{0:T(128)S(1)} %pad_add_fusion.place, bf16[384,1024]{1,0:T(8,128)(2,1)S(1)} %copy-done.13, f32[1,1024]{1,0:T(1,128)S(1)} %bitcast.19, bf16[1024,1024]{1,0:T(8,128)(2,1)S(1)} %copy-done.1, bf16[1024,1024]{1,0:T(8,128)(2,1)S(1)} %copy-done.2), custom_call_target="tpu_custom_call" | custom-call | flops 805306368 | bytes 5242880 | tf_op jit(solution)/shard_map/forward_other/pallas_call | solution.py:122
  21.7 1.6 %copy-done.3 = bf16[1024,1024]{1,0:T(8,128)(2,1)S(1)} copy-done((bf16[1024,1024]{1,0:T(8,128)(2,1)S(1)}, bf16[1024,1024]{1,0:T(8,128)(2,1)}, u32[]{:S(2)}) %copy-start.3) | copy-done | bytes 2097176
  23.3 1.4 copy-done.9
  24.7 5.2 %forward_own.5 = (bf16[400,256]{1,0:T(8,128)(2,1)S(1)}, bf16[400,256]{1,0:T(8,128)(2,1)}, bf16[400,256]{1,0:T(8,128)(2,1)S(1)}, bf16[400,256]{1,0:T(8,128)(2,1)S(1)}) custom-call(s32[2]{0:T(128)S(1)} %pad_add_fusion.place, bf16[768,1024]{1,0:T(8,128)(2,1)S(1)} %copy-done.9, f32[1,1024]{1,0:T(1,128)S(1)} %bitcast.20, bf16[1024,1024]{1,0:T(8,128)(2,1)S(1)} %copy-done.1, ...), custom_call_target="tpu_custom_call" | custom-call | flops 805306368 | bytes 5242880 | tf_op jit(solution)/shard_map/forward_own/pallas_call | solution.py:122
  30.8 0.7 copy-done.18
  31.5 10.3 %all-to-all-start = ((bf16[32,24,256]{2,1,0:T(8,128)(2,1)}), bf16[32,24,256]{2,1,0:T(8,128)(2,1)S(1)}, u32[]{:S(2)}, u32[]{:S(2)}) async-start(bf16[32,24,256]{2,1,0:T(8,128)(2,1)} %bitcast.14), calls=%async_computation | async-start | bytes 786432 | tf_op jit(solution)/shard_map/all_to_all | solution.py:440
  41.8 2.7 %collective-permute-start.10 = (bf16[400,256]{1,0:T(8,128)(2,1)}, bf16[400,256]{1,0:T(8,128)(2,1)S(1)}, u32[]{:S(2)}, u32[]{:S(2)}) collective-permute-start(bf16[400,256]{1,0:T(8,128)(2,1)} %copy-done.43), channel_id=1, source_target_pairs={{0,4},{1,5},{2,6},{3,7},{4,0},{5,1},{6,2},{7,3},{8,12},{9,13},{10,... | collective-permute-start | bytes 614408 | tf_op jit(solution)/shard_map/ppermute | solution.py:401
  44.6 1.0 collective-permute-start.11
  45.6 1.6 %copy-done.4 = bf16[1024,1024]{1,0:T(8,128)(2,1)S(1)} copy-done((bf16[1024,1024]{1,0:T(8,128)(2,1)S(1)}, bf16[1024,1024]{1,0:T(8,128)(2,1)}, u32[]{:S(2)}) %copy-start.4) | copy-done | bytes 2097176
  47.2 1.4 copy-done.10
  48.6 4.5 %forward_own.4 = (bf16[400,256]{1,0:T(8,128)(2,1)S(1)}, bf16[400,256]{1,0:T(8,128)(2,1)S(1)}, bf16[400,256]{1,0:T(8,128)(2,1)S(1)}, bf16[400,256]{1,0:T(8,128)(2,1)S(1)}) custom-call(s32[2]{0:T(128)S(1)} %pad_add_fusion.place, bf16[768,1024]{1,0:T(8,128)(2,1)S(1)} %copy-done.10, f32[1,1024]{1,0:T(1,128)S(1)} %bitcast.21, bf16[1024,1024]{1,0:T(8,128)(2,1)S(1)} %copy-done.1, ...), custom_call_target="tpu_custom_call" | custom-call | flops 805306368 | bytes 5242880 | tf_op jit(solution)/shard_map/forward_own/pallas_call | solution.py:122
  53.6 0.8 collective-permute-start.6
  54.4 1.8 %collective-permute-start.7 = (bf16[400,256]{1,0:T(8,128)(2,1)S(1)}, bf16[400,256]{1,0:T(8,128)(2,1)S(1)}, u32[]{:S(2)}, u32[]{:S(2)}) collective-permute-start(bf16[400,256]{1,0:T(8,128)(2,1)S(1)} %get-tuple-element.37), channel_id=1, source_target_pairs={{0,6},{1,7},{2,0},{3,1},{4,2},{5,3},{6,4},{7,5},{8,14},{9,15},{10,... | collective-permute-start | bytes 614408 | tf_op jit(solution)/shard_map/ppermute | solution.py:401
  56.1 5.3 %forward_own.3 = (bf16[400,256]{1,0:T(8,128)(2,1)S(1)}, bf16[400,256]{1,0:T(8,128)(2,1)}, bf16[400,256]{1,0:T(8,128)(2,1)}, bf16[400,256]{1,0:T(8,128)(2,1)}) custom-call(s32[2]{0:T(128)S(1)} %pad_add_fusion.place, bf16[384,1024]{1,0:T(8,128)(2,1)S(1)} %copy-done.13, f32[1,1024]{1,0:T(1,128)S(1)} %bitcast.22, bf16[1024,1024]{1,0:T(8,128)(2,1)S(1)} %copy-done.1, ...), custom_call_target="tpu_custom_call" | custom-call | flops 805306368 | bytes 5242880 | tf_op jit(solution)/shard_map/forward_own/pallas_call | solution.py:122
  61.4 0.6 collective-permute-start.1
  62.0 1.9 %collective-permute-start.2 = (bf16[400,256]{1,0:T(8,128)(2,1)}, bf16[400,256]{1,0:T(8,128)(2,1)}, u32[]{:S(2)}, u32[]{:S(2)}) collective-permute-start(bf16[400,256]{1,0:T(8,128)(2,1)} %get-tuple-element.31), channel_id=1, source_target_pairs={{0,4},{1,5},{2,6},{3,7},{4,0},{5,1},{6,2},{7,3},{8,12},{9,13},{10,... | collective-permute-start | bytes 614408 | tf_op jit(solution)/shard_map/ppermute | solution.py:401
  63.9 2.0 %text_combine.3 = (bf16[384,128]{1,0:T(8,128)(2,1)S(1)}, bf16[384,128]{1,0:T(8,128)(2,1)S(1)}, bf16[400,256]{1,0:T(8,128)(2,1)}, f32[384,128]{1,0:T(8,128)S(1)}) custom-call(bf16[400,256]{1,0:T(8,128)(2,1)S(1)} %copy-done.31, bf16[400,256]{1,0:T(8,128)(2,1)} %collective-permute-done.9.b, bf16[400,256]{1,0:T(8,128)(2,1)S(1)} %collective-permute-done.10.c, ...), custom_call_target="tpu_custom_call" | custom-call | flops 4194304 | bytes 2097152 | tf_op jit(solution)/shard_map/text_combine/pallas_call | solution.py:209
  66.0 0.7 copy-done.36
  66.6 0.6 copy-done.44
  67.3 0.6 copy-done.46
  67.9 0.7 copy-done.26
  68.6 2.0 %collective-permute-start.3 = (bf16[400,256]{1,0:T(8,128)(2,1)}, bf16[400,256]{1,0:T(8,128)(2,1)}, u32[]{:S(2)}, u32[]{:S(2)}) collective-permute-start(bf16[400,256]{1,0:T(8,128)(2,1)} %get-tuple-element.32), channel_id=1, source_target_pairs={{0,6},{1,7},{2,0},{3,1},{4,2},{5,3},{6,4},{7,5},{8,14},{9,15},{10,... | collective-permute-start | bytes 614408 | tf_op jit(solution)/shard_map/ppermute | solution.py:401
  70.6 0.7 copy-done.28
  71.3 0.7 copy-done.32
  71.9 1.2 collective-permute-start.13
  73.2 0.9 copy-done.17
  74.1 0.9 copy-done.25
  75.0 0.9 copy-done.27
  75.9 0.9 copy-done.29
  76.9 0.9 copy-done.33
  77.8 1.1 text_combine.2
  78.9 0.7 copy-done.38
  79.6 0.6 copy-done.48
  80.2 0.6 copy-done.50
  80.9 1.7 %collective-permute-start.14 = (bf16[400,256]{1,0:T(8,128)(2,1)}, bf16[400,256]{1,0:T(8,128)(2,1)}, u32[]{:S(2)}, u32[]{:S(2)}) collective-permute-start(bf16[400,256]{1,0:T(8,128)(2,1)} %get-tuple-element.49.rest_0_), channel_id=1, source_target_pairs={{0,6},{1,7},{2,0},{3,1},{4,2},{5,3},{6,4},{7,5},{8,14},{9,15},{10,... | collective-permute-start | bytes 614408 | tf_op jit(solution)/shard_map/ppermute | solution.py:401
  83.0 1.8 %collective-permute-start.20 = (bf16[400,256]{1,0:T(8,128)(2,1)}, bf16[400,256]{1,0:T(8,128)(2,1)}, u32[]{:S(2)}, u32[]{:S(2)}) collective-permute-start(bf16[400,256]{1,0:T(8,128)(2,1)} %get-tuple-element.51.rest_0_), channel_id=1, source_target_pairs={{0,4},{1,5},{2,6},{3,7},{4,0},{5,1},{6,2},{7,3},{8,12},{9,13},{10,... | collective-permute-start | bytes 614408 | tf_op jit(solution)/shard_map/ppermute | solution.py:401
  84.8 2.0 %collective-permute-start.21 = (bf16[400,256]{1,0:T(8,128)(2,1)}, bf16[400,256]{1,0:T(8,128)(2,1)}, u32[]{:S(2)}, u32[]{:S(2)}) collective-permute-start(bf16[400,256]{1,0:T(8,128)(2,1)} %get-tuple-element.51.rest_0_), channel_id=1, source_target_pairs={{0,6},{1,7},{2,0},{3,1},{4,2},{5,3},{6,4},{7,5},{8,14},{9,15},{10,... | collective-permute-start | bytes 614408 | tf_op jit(solution)/shard_map/ppermute | solution.py:401
  86.8 4.6 %collective-permute-start.22 = (bf16[400,256]{1,0:T(8,128)(2,1)}, bf16[400,256]{1,0:T(8,128)(2,1)}, u32[]{:S(2)}, u32[]{:S(2)}) collective-permute-start(bf16[400,256]{1,0:T(8,128)(2,1)} %get-tuple-element.51.rest_0_), channel_id=1, source_target_pairs={{0,1},{1,0},{2,3},{3,2},{4,5},{5,4},{6,7},{7,6},{8,9},{9,8},{10,11... | collective-permute-start | bytes 614408 | tf_op jit(solution)/shard_map/ppermute | solution.py:407
  91.5 0.9 copy-done.35
  92.5 2.7 %image_combine.1 = (bf16[768,256]{1,0:T(8,128)(2,1)S(1)}, bf16[400,256]{1,0:T(8,128)(2,1)}, f32[384,128]{1,0:T(8,128)S(1)}) custom-call(bf16[400,256]{1,0:T(8,128)(2,1)S(1)} %copy-done.35, bf16[400,256]{1,0:T(8,128)(2,1)} %collective-permute-done.1.b, bf16[400,256]{1,0:T(8,128)(2,1)} %collective-permute-done.2.c, bf16[400,256]{1,0:T(8,128)(2,1)} %collective-permute-done.3.d, ...), custom_call_target="tpu_custom_call" | custom-call | flops 268435456 | bytes 2097152 | tf_op jit(solution)/shard_map/image_combine/pallas_call | solution.py:228
  95.1 0.7 copy-done.19
  95.8 0.7 copy-done.40
  96.6 0.9 collective-permute-start.27
  97.5 1.8 %collective-permute-start.28 = (bf16[400,256]{1,0:T(8,128)(2,1)}, bf16[400,256]{1,0:T(8,128)(2,1)}, u32[]{:S(2)}, u32[]{:S(2)}) collective-permute-start(bf16[400,256]{1,0:T(8,128)(2,1)} %get-tuple-element.53.rest_0_), channel_id=1, source_target_pairs={{0,6},{1,7},{2,0},{3,1},{4,2},{5,3},{6,4},{7,5},{8,14},{9,15},{10,... | collective-permute-start | bytes 614408 | tf_op jit(solution)/shard_map/ppermute | solution.py:401
  99.3 1.7 %collective-permute-start.29 = (bf16[400,256]{1,0:T(8,128)(2,1)}, bf16[400,256]{1,0:T(8,128)(2,1)}, u32[]{:S(2)}, u32[]{:S(2)}) collective-permute-start(bf16[400,256]{1,0:T(8,128)(2,1)} %get-tuple-element.53.rest_0_), channel_id=1, source_target_pairs={{0,1},{1,0},{2,3},{3,2},{4,5},{5,4},{6,7},{7,6},{8,9},{9,8},{10,11... | collective-permute-start | bytes 614408 | tf_op jit(solution)/shard_map/ppermute | solution.py:407
  101.1 8.8 %all-to-all-start.1 = ((bf16[32,24,256]{2,1,0:T(8,128)(2,1)}), bf16[32,24,256]{2,1,0:T(8,128)(2,1)S(1)}, u32[]{:S(2)}, u32[]{:S(2)}) async-start(bf16[32,24,256]{2,1,0:T(8,128)(2,1)} %bitcast.15), calls=%async_computation.1 | async-start | bytes 786432 | tf_op jit(solution)/shard_map/all_to_all | solution.py:444
  111.7 0.7 copy-done.22
  113.8 1.6 %copy-done.6 = bf16[1024,1024]{1,0:T(8,128)(2,1)S(1)} copy-done((bf16[1024,1024]{1,0:T(8,128)(2,1)S(1)}, bf16[1024,1024]{1,0:T(8,128)(2,1)}, u32[]{:S(2)}) %copy-start.6) | copy-done | bytes 2097176
  115.4 1.4 copy-done.11
  116.8 0.9 copy-done.23
  117.7 7.6 %backward.3.rest_8_ = bf16[768,1024]{1,0:T(8,128)(2,1)} custom-call(s32[2]{0:T(128)S(1)} %pad_add_fusion.place, bf16[768,1024]{1,0:T(8,128)(2,1)S(1)} %copy-done.11, f32[1,1024]{1,0:T(1,128)S(1)} %bitcast.23, f32[384,128]{1,0:T(8,128)S(1)} %copy-done.39, f32[1,32]{1,0:T(1,128)S(1)} %get-tuple-element.55.first_ref.first_lanes, ...), custom_call_target="tpu_custom_call" | custom-call | flops 1610612736 | bytes 8388608 | tf_op jit(solution)/shard_map/backward/pallas_call | solution.py:377
  125.3 7.6 %backward.5 = bf16[384,1024]{1,0:T(8,128)(2,1)} custom-call(s32[2]{0:T(128)S(1)} %pad_add_fusion.place, bf16[384,1024]{1,0:T(8,128)(2,1)S(1)} %copy-done.13, f32[1,1024]{1,0:T(1,128)S(1)} %bitcast.24, f32[384,128]{1,0:T(8,128)S(1)} %copy-done.41, f32[1,32]{1,0:T(1,128)S(1)} %get-tuple-element.55.first_ref.first_lanes, bf16[1024,1024]{1,0:T(8,128)(2,1)S(1)} %copy-done.1, ...), custom_call_target="tpu_custom_call" | custom-call | flops 1610612736 | bytes 8388608 | tf_op jit(solution)/shard_map/backward/pallas_call | solution.py:377
  133.0 7.4 %backward.4 = bf16[768,1024]{1,0:T(8,128)(2,1)} custom-call(s32[2]{0:T(128)S(1)} %pad_add_fusion.place, bf16[768,1024]{1,0:T(8,128)(2,1)S(1)} %copy-done.12, f32[1,1024]{1,0:T(1,128)S(1)} %bitcast.25, f32[384,128]{1,0:T(8,128)S(1)} %copy-done.37, f32[1,32]{1,0:T(1,128)S(1)} %get-tuple-element.55.first_ref.first_lanes, ...), custom_call_target="tpu_custom_call", output_to_operand_aliasing={{}: (17, {})} | custom-call | flops 1610612736 | bytes 8388608 | tf_op jit(solution)/shard_map/backward/pallas_call | solution.py:377
  140.4 0.9 copy-done.47
  141.3 0.9 copy-done.49
  142.2 0.9 copy-done.51
  143.1 1.3 merge.1
  (135 shorter events, 6.0 us)
Async XLA Ops:
  0.7 1.6 %copy-start = (bf16[1024,1024]{1,0:T(8,128)(2,1)S(1)}, bf16[1024,1024]{1,0:T(8,128)(2,1)}, u32[]{:S(2)}) copy-start(bf16[1024,1024]{1,0:T(8,128)(2,1)} %wk_other.5) | copy-start | bytes 6291460
  2.3 1.6 %copy-start.2 = (bf16[1024,1024]{1,0:T(8,128)(2,1)S(1)}, bf16[1024,1024]{1,0:T(8,128)(2,1)}, u32[]{:S(2)}) copy-start(bf16[1024,1024]{1,0:T(8,128)(2,1)} %wv_other.5) | copy-start | bytes 6291460
  3.9 1.4 copy-start.8
  9.9 7.2 %copy-start.1 = (bf16[1024,1024]{1,0:T(8,128)(2,1)S(1)}, bf16[1024,1024]{1,0:T(8,128)(2,1)}, u32[]{:S(2)}) copy-start(bf16[1024,1024]{1,0:T(8,128)(2,1)} %wk_other.5) | copy-start | bytes 6291460
  9.9 7.2 %copy-start.13 = (bf16[384,1024]{1,0:T(8,128)(2,1)S(1)}, bf16[384,1024]{1,0:T(8,128)(2,1)}, u32[]{:S(2)}) copy-start(bf16[384,1024]{1,0:T(8,128)(2,1)} %x_ref.17) | copy-start | bytes 2359300
  9.9 11.8 %collective-permute-start.8 = (bf16[4,400,256]{2,1,0:T(8,128)(2,1)}, bf16[4,400,256]{2,1,0:T(8,128)(2,1)}, u32[]{:S(2)}, u32[]{:S(2)}) collective-permute-start(bf16[4,400,256]{2,1,0:T(8,128)(2,1)} %forward_other.5), channel_id=1, source_target_pairs={{0,1},{1,0},{2,3},{3,2},{4,5},{5,4},{6,7},{7,6},{8,9},{9,8},{10,11... | collective-permute-start | bytes 2457608 | tf_op jit(solution)/shard_map/ppermute | solution.py:407
  17.1 4.4 %copy-start.52 = (s32[512]{0:T(512)S(1)}, s32[512]{0:T(512)}, u32[]{:S(2)}) copy-start(s32[512]{0:T(512)} %param.10) | copy-start | bytes 6148
  17.1 4.6 %copy-start.21 = (f32[1024]{0:T(1024)S(1)}, f32[1024]{0:T(1024)}, u32[]{:S(2)}) copy-start(f32[1024]{0:T(1024)} %param.11) | copy-start | bytes 12292
  17.1 28.5 %collective-permute-start.4 = (bf16[4,400,256]{2,1,0:T(8,128)(2,1)}, bf16[4,400,256]{2,1,0:T(8,128)(2,1)}, u32[]{:S(2)}, u32[]{:S(2)}) collective-permute-start(bf16[4,400,256]{2,1,0:T(8,128)(2,1)} %forward_other.4), channel_id=1, source_target_pairs={{0,1},{1,0},{2,3},{3,2},{4,5},{5,4},{6,7},{7,6},{8,9},{9,8},{10,11... | collective-permute-start | bytes 2457608 | tf_op jit(solution)/shard_map/ppermute | solution.py:407
  21.0 32.6 %collective-permute-start = (bf16[4,400,256]{2,1,0:T(8,128)(2,1)}, bf16[4,400,256]{2,1,0:T(8,128)(2,1)}, u32[]{:S(2)}, u32[]{:S(2)}) collective-permute-start(bf16[4,400,256]{2,1,0:T(8,128)(2,1)} %forward_other.3), channel_id=1, source_target_pairs={{0,1},{1,0},{2,3},{3,2},{4,5},{5,4},{6,7},{7,6},{8,9},{9,8},{10,11... | collective-permute-start | bytes 2457608 | tf_op jit(solution)/shard_map/ppermute | solution.py:407
  21.7 1.6 %copy-start.3 = (bf16[1024,1024]{1,0:T(8,128)(2,1)S(1)}, bf16[1024,1024]{1,0:T(8,128)(2,1)}, u32[]{:S(2)}) copy-start(bf16[1024,1024]{1,0:T(8,128)(2,1)} %wv_other.5) | copy-start | bytes 6291460
  23.3 1.4 copy-start.9
  24.7 5.2 %copy-start.14 = (bf16[768,128]{1,0:T(8,128)(2,1)S(1)}, bf16[768,128]{1,0:T(8,128)(2,1)}, u32[]{:S(2)}) copy-start(bf16[768,128]{1,0:T(8,128)(2,1)} %kt_ref.5) | copy-start | bytes 589828
  24.7 5.2 %copy-start.15 = (bf16[768,128]{1,0:T(8,128)(2,1)S(1)}, bf16[768,128]{1,0:T(8,128)(2,1)}, u32[]{:S(2)}) copy-start(bf16[768,128]{1,0:T(8,128)(2,1)} %vt_ref.5) | copy-start | bytes 589828
  29.9 24.5 %collective-permute-start.9 = (bf16[400,256]{1,0:T(8,128)(2,1)}, bf16[400,256]{1,0:T(8,128)(2,1)}, u32[]{:S(2)}, u32[]{:S(2)}) collective-permute-start(bf16[400,256]{1,0:T(8,128)(2,1)} %get-tuple-element.40), channel_id=1, source_target_pairs={{0,2},{1,3},{2,4},{3,5},{4,6},{5,7},{6,0},{7,1},{8,10},{9,11},{10,... | collective-permute-start | bytes 614408 | tf_op jit(solution)/shard_map/ppermute | solution.py:401
  31.5 60.0 %all-to-all-start = ((bf16[32,24,256]{2,1,0:T(8,128)(2,1)}), bf16[32,24,256]{2,1,0:T(8,128)(2,1)S(1)}, u32[]{:S(2)}, u32[]{:S(2)}) async-start(bf16[32,24,256]{2,1,0:T(8,128)(2,1)} %bitcast.14), calls=%async_computation | async-start | bytes 786432 | tf_op jit(solution)/shard_map/all_to_all | solution.py:440
  41.8 19.6 %collective-permute-start.10 = (bf16[400,256]{1,0:T(8,128)(2,1)}, bf16[400,256]{1,0:T(8,128)(2,1)S(1)}, u32[]{:S(2)}, u32[]{:S(2)}) collective-permute-start(bf16[400,256]{1,0:T(8,128)(2,1)} %copy-done.43), channel_id=1, source_target_pairs={{0,4},{1,5},{2,6},{3,7},{4,0},{5,1},{6,2},{7,3},{8,12},{9,13},{10,... | collective-permute-start | bytes 614408 | tf_op jit(solution)/shard_map/ppermute | solution.py:401
  44.6 17.5 %collective-permute-start.11 = (bf16[400,256]{1,0:T(8,128)(2,1)}, bf16[400,256]{1,0:T(8,128)(2,1)S(1)}, u32[]{:S(2)}, u32[]{:S(2)}) collective-permute-start(bf16[400,256]{1,0:T(8,128)(2,1)} %copy-done.42), channel_id=1, source_target_pairs={{0,6},{1,7},{2,0},{3,1},{4,2},{5,3},{6,4},{7,5},{8,14},{9,15},{10,... | collective-permute-start | bytes 614408 | tf_op jit(solution)/shard_map/ppermute | solution.py:401
  45.6 1.6 %copy-start.4 = (bf16[1024,1024]{1,0:T(8,128)(2,1)S(1)}, bf16[1024,1024]{1,0:T(8,128)(2,1)}, u32[]{:S(2)}) copy-start(bf16[1024,1024]{1,0:T(8,128)(2,1)} %wv_other.5) | copy-start | bytes 6291460
  47.2 1.4 copy-start.10
  48.6 7.5 %copy-start.5 = (bf16[1024,1024]{1,0:T(8,128)(2,1)S(1)}, bf16[1024,1024]{1,0:T(8,128)(2,1)}, u32[]{:S(2)}) copy-start(bf16[1024,1024]{1,0:T(8,128)(2,1)} %wv_other.5) | copy-start | bytes 6291460
  53.1 8.3 %copy-start.24 = (bf16[400,256]{1,0:T(8,128)(2,1)}, bf16[400,256]{1,0:T(8,128)(2,1)S(1)}, u32[]{:S(2)}) copy-start(bf16[400,256]{1,0:T(8,128)(2,1)S(1)} %get-tuple-element.34.a) | copy-start | bytes 614404
  53.1 14.8 %collective-permute-start.5 = (bf16[400,256]{1,0:T(8,128)(2,1)S(1)}, bf16[400,256]{1,0:T(8,128)(2,1)S(1)}, u32[]{:S(2)}, u32[]{:S(2)}) collective-permute-start(bf16[400,256]{1,0:T(8,128)(2,1)S(1)} %get-tuple-element.35), channel_id=1, source_target_pairs={{0,2},{1,3},{2,4},{3,5},{4,6},{5,7},{6,0},{7,1},{8,10},{9,11},{10,... | collective-permute-start | bytes 614408 | tf_op jit(solution)/shard_map/ppermute | solution.py:401
  53.6 17.0 %collective-permute-start.6 = (bf16[400,256]{1,0:T(8,128)(2,1)S(1)}, bf16[400,256]{1,0:T(8,128)(2,1)S(1)}, u32[]{:S(2)}, u32[]{:S(2)}) collective-permute-start(bf16[400,256]{1,0:T(8,128)(2,1)S(1)} %get-tuple-element.36), channel_id=1, source_target_pairs={{0,4},{1,5},{2,6},{3,7},{4,0},{5,1},{6,2},{7,3},{8,12},{9,13},{10,... | collective-permute-start | bytes 614408 | tf_op jit(solution)/shard_map/ppermute | solution.py:401
  54.4 9.5 %copy-start.16 = (bf16[768,128]{1,0:T(8,128)(2,1)S(1)}, bf16[768,128]{1,0:T(8,128)(2,1)}, u32[]{:S(2)}) copy-start(bf16[768,128]{1,0:T(8,128)(2,1)} %vt_ref.5) | copy-start | bytes 589828
  54.4 9.5 %copy-start.31 = (bf16[400,256]{1,0:T(8,128)(2,1)S(1)}, bf16[400,256]{1,0:T(8,128)(2,1)}, u32[]{:S(2)}) copy-start(bf16[400,256]{1,0:T(8,128)(2,1)} %copy-done.30) | copy-start | bytes 614404
  54.4 16.9 %collective-permute-start.7 = (bf16[400,256]{1,0:T(8,128)(2,1)S(1)}, bf16[400,256]{1,0:T(8,128)(2,1)S(1)}, u32[]{:S(2)}, u32[]{:S(2)}) collective-permute-start(bf16[400,256]{1,0:T(8,128)(2,1)S(1)} %get-tuple-element.37), channel_id=1, source_target_pairs={{0,6},{1,7},{2,0},{3,1},{4,2},{5,3},{6,4},{7,5},{8,14},{9,15},{10,... | collective-permute-start | bytes 614408 | tf_op jit(solution)/shard_map/ppermute | solution.py:401
  61.4 9.8 %copy-start.34 = (bf16[400,256]{1,0:T(8,128)(2,1)}, bf16[400,256]{1,0:T(8,128)(2,1)S(1)}, u32[]{:S(2)}) copy-start(bf16[400,256]{1,0:T(8,128)(2,1)S(1)} %get-tuple-element.29.a) | copy-start | bytes 614404
  61.4 19.4 %collective-permute-start.1 = (bf16[400,256]{1,0:T(8,128)(2,1)}, bf16[400,256]{1,0:T(8,128)(2,1)}, u32[]{:S(2)}, u32[]{:S(2)}) collective-permute-start(bf16[400,256]{1,0:T(8,128)(2,1)} %get-tuple-element.30), channel_id=1, source_target_pairs={{0,2},{1,3},{2,4},{3,5},{4,6},{5,7},{6,0},{7,1},{8,10},{9,11},{10,... | collective-permute-start | bytes 614408 | tf_op jit(solution)/shard_map/ppermute | solution.py:401
  62.0 20.6 %collective-permute-start.2 = (bf16[400,256]{1,0:T(8,128)(2,1)}, bf16[400,256]{1,0:T(8,128)(2,1)}, u32[]{:S(2)}, u32[]{:S(2)}) collective-permute-start(bf16[400,256]{1,0:T(8,128)(2,1)} %get-tuple-element.31), channel_id=1, source_target_pairs={{0,4},{1,5},{2,6},{3,7},{4,0},{5,1},{6,2},{7,3},{8,12},{9,13},{10,... | collective-permute-start | bytes 614408 | tf_op jit(solution)/shard_map/ppermute | solution.py:401
  68.6 14.4 %collective-permute-start.3 = (bf16[400,256]{1,0:T(8,128)(2,1)}, bf16[400,256]{1,0:T(8,128)(2,1)}, u32[]{:S(2)}, u32[]{:S(2)}) collective-permute-start(bf16[400,256]{1,0:T(8,128)(2,1)} %get-tuple-element.32), channel_id=1, source_target_pairs={{0,6},{1,7},{2,0},{3,1},{4,2},{5,3},{6,4},{7,5},{8,14},{9,15},{10,... | collective-permute-start | bytes 614408 | tf_op jit(solution)/shard_map/ppermute | solution.py:401
  71.2 13.6 %collective-permute-start.12 = (bf16[400,256]{1,0:T(8,128)(2,1)}, bf16[400,256]{1,0:T(8,128)(2,1)}, u32[]{:S(2)}, u32[]{:S(2)}) collective-permute-start(bf16[400,256]{1,0:T(8,128)(2,1)} %get-tuple-element.49.rest_0_), channel_id=1, source_target_pairs={{0,2},{1,3},{2,4},{3,5},{4,6},{5,7},{6,0},{7,1},{8,10},{9,11},{10,... | collective-permute-start | bytes 614408 | tf_op jit(solution)/shard_map/ppermute | solution.py:401
  71.9 14.9 %collective-permute-start.13 = (bf16[400,256]{1,0:T(8,128)(2,1)}, bf16[400,256]{1,0:T(8,128)(2,1)}, u32[]{:S(2)}, u32[]{:S(2)}) collective-permute-start(bf16[400,256]{1,0:T(8,128)(2,1)} %get-tuple-element.49.rest_0_), channel_id=1, source_target_pairs={{0,4},{1,5},{2,6},{3,7},{4,0},{5,1},{6,2},{7,3},{8,12},{9,13},{10,... | collective-permute-start | bytes 614408 | tf_op jit(solution)/shard_map/ppermute | solution.py:401
  73.1 0.9 copy-start.17
  74.1 0.9 copy-start.25
  80.9 15.7 %collective-permute-start.14 = (bf16[400,256]{1,0:T(8,128)(2,1)}, bf16[400,256]{1,0:T(8,128)(2,1)}, u32[]{:S(2)}, u32[]{:S(2)}) collective-permute-start(bf16[400,256]{1,0:T(8,128)(2,1)} %get-tuple-element.49.rest_0_), channel_id=1, source_target_pairs={{0,6},{1,7},{2,0},{3,1},{4,2},{5,3},{6,4},{7,5},{8,14},{9,15},{10,... | collective-permute-start | bytes 614408 | tf_op jit(solution)/shard_map/ppermute | solution.py:401
  82.6 13.9 %collective-permute-start.19 = (bf16[400,256]{1,0:T(8,128)(2,1)}, bf16[400,256]{1,0:T(8,128)(2,1)}, u32[]{:S(2)}, u32[]{:S(2)}) collective-permute-start(bf16[400,256]{1,0:T(8,128)(2,1)} %get-tuple-element.51.rest_0_), channel_id=1, source_target_pairs={{0,2},{1,3},{2,4},{3,5},{4,6},{5,7},{6,0},{7,1},{8,10},{9,11},{10,... | collective-permute-start | bytes 614408 | tf_op jit(solution)/shard_map/ppermute | solution.py:401
  83.0 14.4 %collective-permute-start.20 = (bf16[400,256]{1,0:T(8,128)(2,1)}, bf16[400,256]{1,0:T(8,128)(2,1)}, u32[]{:S(2)}, u32[]{:S(2)}) collective-permute-start(bf16[400,256]{1,0:T(8,128)(2,1)} %get-tuple-element.51.rest_0_), channel_id=1, source_target_pairs={{0,4},{1,5},{2,6},{3,7},{4,0},{5,1},{6,2},{7,3},{8,12},{9,13},{10,... | collective-permute-start | bytes 614408 | tf_op jit(solution)/shard_map/ppermute | solution.py:401
  84.8 14.5 %collective-permute-start.21 = (bf16[400,256]{1,0:T(8,128)(2,1)}, bf16[400,256]{1,0:T(8,128)(2,1)}, u32[]{:S(2)}, u32[]{:S(2)}) collective-permute-start(bf16[400,256]{1,0:T(8,128)(2,1)} %get-tuple-element.51.rest_0_), channel_id=1, source_target_pairs={{0,6},{1,7},{2,0},{3,1},{4,2},{5,3},{6,4},{7,5},{8,14},{9,15},{10,... | collective-permute-start | bytes 614408 | tf_op jit(solution)/shard_map/ppermute | solution.py:401
  86.8 23.1 %collective-permute-start.22 = (bf16[400,256]{1,0:T(8,128)(2,1)}, bf16[400,256]{1,0:T(8,128)(2,1)}, u32[]{:S(2)}, u32[]{:S(2)}) collective-permute-start(bf16[400,256]{1,0:T(8,128)(2,1)} %get-tuple-element.51.rest_0_), channel_id=1, source_target_pairs={{0,1},{1,0},{2,3},{3,2},{4,5},{5,4},{6,7},{7,6},{8,9},{9,8},{10,11... | collective-permute-start | bytes 614408 | tf_op jit(solution)/shard_map/ppermute | solution.py:407
  91.5 0.9 copy-start.35
  92.5 21.3 %copy-start.39 = (f32[384,128]{1,0:T(8,128)S(1)}, f32[384,128]{1,0:T(8,128)}, u32[]{:S(2)}) copy-start(f32[384,128]{1,0:T(8,128)} %copy-done.38) | copy-start | bytes 589828
  96.5 13.7 %collective-permute-start.26 = (bf16[400,256]{1,0:T(8,128)(2,1)}, bf16[400,256]{1,0:T(8,128)(2,1)}, u32[]{:S(2)}, u32[]{:S(2)}) collective-permute-start(bf16[400,256]{1,0:T(8,128)(2,1)} %get-tuple-element.53.rest_0_), channel_id=1, source_target_pairs={{0,2},{1,3},{2,4},{3,5},{4,6},{5,7},{6,0},{7,1},{8,10},{9,11},{10,... | collective-permute-start | bytes 614408 | tf_op jit(solution)/shard_map/ppermute | solution.py:401
  96.6 13.9 %collective-permute-start.27 = (bf16[400,256]{1,0:T(8,128)(2,1)}, bf16[400,256]{1,0:T(8,128)(2,1)}, u32[]{:S(2)}, u32[]{:S(2)}) collective-permute-start(bf16[400,256]{1,0:T(8,128)(2,1)} %get-tuple-element.53.rest_0_), channel_id=1, source_target_pairs={{0,4},{1,5},{2,6},{3,7},{4,0},{5,1},{6,2},{7,3},{8,12},{9,13},{10,... | collective-permute-start | bytes 614408 | tf_op jit(solution)/shard_map/ppermute | solution.py:401
  97.5 13.4 %collective-permute-start.28 = (bf16[400,256]{1,0:T(8,128)(2,1)}, bf16[400,256]{1,0:T(8,128)(2,1)}, u32[]{:S(2)}, u32[]{:S(2)}) collective-permute-start(bf16[400,256]{1,0:T(8,128)(2,1)} %get-tuple-element.53.rest_0_), channel_id=1, source_target_pairs={{0,6},{1,7},{2,0},{3,1},{4,2},{5,3},{6,4},{7,5},{8,14},{9,15},{10,... | collective-permute-start | bytes 614408 | tf_op jit(solution)/shard_map/ppermute | solution.py:401
  99.3 11.8 %collective-permute-start.29 = (bf16[400,256]{1,0:T(8,128)(2,1)}, bf16[400,256]{1,0:T(8,128)(2,1)}, u32[]{:S(2)}, u32[]{:S(2)}) collective-permute-start(bf16[400,256]{1,0:T(8,128)(2,1)} %get-tuple-element.53.rest_0_), channel_id=1, source_target_pairs={{0,1},{1,0},{2,3},{3,2},{4,5},{5,4},{6,7},{7,6},{8,9},{9,8},{10,11... | collective-permute-start | bytes 614408 | tf_op jit(solution)/shard_map/ppermute | solution.py:407
  101.1 39.3 %all-to-all-start.1 = ((bf16[32,24,256]{2,1,0:T(8,128)(2,1)}), bf16[32,24,256]{2,1,0:T(8,128)(2,1)S(1)}, u32[]{:S(2)}, u32[]{:S(2)}) async-start(bf16[32,24,256]{2,1,0:T(8,128)(2,1)} %bitcast.15), calls=%async_computation.1 | async-start | bytes 786432 | tf_op jit(solution)/shard_map/all_to_all | solution.py:444
  109.9 1.8 %collective-permute-start.23 = (bf16[400,256]{1,0:T(8,128)(2,1)}, bf16[400,256]{1,0:T(8,128)(2,1)S(1)}, u32[]{:S(2)}, u32[]{:S(2)}) collective-permute-start(bf16[400,256]{1,0:T(8,128)(2,1)} %collective-permute-done.19.rest_1_), channel_id=1, source_target_pairs={{0,1},{1,0},{2,3},{3,2},{4,5},{5,4},{6,7},{7,6},{8,9},{9,8},{10,11... | collective-permute-start | bytes 614408 | tf_op jit(solution)/shard_map/ppermute | solution.py:407
  110.3 2.4 %collective-permute-start.24 = (bf16[400,256]{1,0:T(8,128)(2,1)}, bf16[400,256]{1,0:T(8,128)(2,1)}, u32[]{:S(2)}, u32[]{:S(2)}) collective-permute-start(bf16[400,256]{1,0:T(8,128)(2,1)} %collective-permute-done.20.rest_2_), channel_id=1, source_target_pairs={{0,1},{1,0},{2,3},{3,2},{4,5},{5,4},{6,7},{7,6},{8,9},{9,8},{10,11... | collective-permute-start | bytes 614408 | tf_op jit(solution)/shard_map/ppermute | solution.py:407
  110.5 2.4 %collective-permute-start.25 = (bf16[400,256]{1,0:T(8,128)(2,1)}, bf16[400,256]{1,0:T(8,128)(2,1)}, u32[]{:S(2)}, u32[]{:S(2)}) collective-permute-start(bf16[400,256]{1,0:T(8,128)(2,1)} %collective-permute-done.21.rest_3_), channel_id=1, source_target_pairs={{0,1},{1,0},{2,3},{3,2},{4,5},{5,4},{6,7},{7,6},{8,9},{9,8},{10,11... | collective-permute-start | bytes 614408 | tf_op jit(solution)/shard_map/ppermute | solution.py:407
  110.8 2.4 %collective-permute-start.30 = (bf16[400,256]{1,0:T(8,128)(2,1)}, bf16[400,256]{1,0:T(8,128)(2,1)}, u32[]{:S(2)}, u32[]{:S(2)}) collective-permute-start(bf16[400,256]{1,0:T(8,128)(2,1)} %collective-permute-done.26.rest_1_), channel_id=1, source_target_pairs={{0,1},{1,0},{2,3},{3,2},{4,5},{5,4},{6,7},{7,6},{8,9},{9,8},{10,11... | collective-permute-start | bytes 614408 | tf_op jit(solution)/shard_map/ppermute | solution.py:407
  111.1 2.4 %collective-permute-start.31 = (bf16[400,256]{1,0:T(8,128)(2,1)}, bf16[400,256]{1,0:T(8,128)(2,1)}, u32[]{:S(2)}, u32[]{:S(2)}) collective-permute-start(bf16[400,256]{1,0:T(8,128)(2,1)} %collective-permute-done.27.rest_2_), channel_id=1, source_target_pairs={{0,1},{1,0},{2,3},{3,2},{4,5},{5,4},{6,7},{7,6},{8,9},{9,8},{10,11... | collective-permute-start | bytes 614408 | tf_op jit(solution)/shard_map/ppermute | solution.py:407
  112.3 13.0 %collective-permute-start.32 = (bf16[400,256]{1,0:T(8,128)(2,1)}, bf16[400,256]{1,0:T(8,128)(2,1)}, u32[]{:S(2)}, u32[]{:S(2)}) collective-permute-start(bf16[400,256]{1,0:T(8,128)(2,1)} %collective-permute-done.28.rest_3_), channel_id=1, source_target_pairs={{0,1},{1,0},{2,3},{3,2},{4,5},{5,4},{6,7},{7,6},{8,9},{9,8},{10,11... | collective-permute-start | bytes 614408 | tf_op jit(solution)/shard_map/ppermute | solution.py:407
  112.7 20.2 %collective-permute-start.15 = (bf16[400,256]{1,0:T(8,128)(2,1)}, bf16[400,256]{1,0:T(8,128)(2,1)S(1)}, u32[]{:S(2)}, u32[]{:S(2)}) collective-permute-start(bf16[400,256]{1,0:T(8,128)(2,1)} %get-tuple-element.49.rest_0_), channel_id=1, source_target_pairs={{0,1},{1,0},{2,3},{3,2},{4,5},{5,4},{6,7},{7,6},{8,9},{9,8},{10,11... | collective-permute-start | bytes 614408 | tf_op jit(solution)/shard_map/ppermute | solution.py:407
  113.0 20.0 %collective-permute-start.16 = (bf16[400,256]{1,0:T(8,128)(2,1)}, bf16[400,256]{1,0:T(8,128)(2,1)S(1)}, u32[]{:S(2)}, u32[]{:S(2)}) collective-permute-start(bf16[400,256]{1,0:T(8,128)(2,1)} %collective-permute-done.12.rest_1_), channel_id=1, source_target_pairs={{0,1},{1,0},{2,3},{3,2},{4,5},{5,4},{6,7},{7,6},{8,9},{9,8},{10,11... | collective-permute-start | bytes 614408 | tf_op jit(solution)/shard_map/ppermute | solution.py:407
  113.2 19.7 %collective-permute-start.17 = (bf16[400,256]{1,0:T(8,128)(2,1)}, bf16[400,256]{1,0:T(8,128)(2,1)S(1)}, u32[]{:S(2)}, u32[]{:S(2)}) collective-permute-start(bf16[400,256]{1,0:T(8,128)(2,1)} %collective-permute-done.13.rest_2_), channel_id=1, source_target_pairs={{0,1},{1,0},{2,3},{3,2},{4,5},{5,4},{6,7},{7,6},{8,9},{9,8},{10,11... | collective-permute-start | bytes 614408 | tf_op jit(solution)/shard_map/ppermute | solution.py:407
  113.5 19.5 %collective-permute-start.18 = (bf16[400,256]{1,0:T(8,128)(2,1)}, bf16[400,256]{1,0:T(8,128)(2,1)S(1)}, u32[]{:S(2)}, u32[]{:S(2)}) collective-permute-start(bf16[400,256]{1,0:T(8,128)(2,1)} %collective-permute-done.14.rest_3_), channel_id=1, source_target_pairs={{0,1},{1,0},{2,3},{3,2},{4,5},{5,4},{6,7},{7,6},{8,9},{9,8},{10,11... | collective-permute-start | bytes 614408 | tf_op jit(solution)/shard_map/ppermute | solution.py:407
  113.8 1.6 %copy-start.6 = (bf16[1024,1024]{1,0:T(8,128)(2,1)S(1)}, bf16[1024,1024]{1,0:T(8,128)(2,1)}, u32[]{:S(2)}) copy-start(bf16[1024,1024]{1,0:T(8,128)(2,1)} %wv_other.5) | copy-start | bytes 6291460
  115.4 1.4 copy-start.11
  117.7 7.6 %copy-start.7 = (bf16[1024,1024]{1,0:T(8,128)(2,1)S(1)}, bf16[1024,1024]{1,0:T(8,128)(2,1)}, u32[]{:S(2)}) copy-start(bf16[1024,1024]{1,0:T(8,128)(2,1)} %wv_other.5) | copy-start | bytes 6291460
  117.7 7.6 %copy-start.41 = (f32[384,128]{1,0:T(8,128)S(1)}, f32[384,128]{1,0:T(8,128)}, u32[]{:S(2)}) copy-start(f32[384,128]{1,0:T(8,128)} %copy-done.40) | copy-start | bytes 589828
  125.3 7.6 %copy-start.12 = (bf16[768,1024]{1,0:T(8,128)(2,1)S(1)}, bf16[768,1024]{1,0:T(8,128)(2,1)}, u32[]{:S(2)}) copy-start(bf16[768,1024]{1,0:T(8,128)(2,1)} %x_ref.16) | copy-start | bytes 4718596
  125.3 7.6 %copy-start.37 = (f32[384,128]{1,0:T(8,128)S(1)}, f32[384,128]{1,0:T(8,128)}, u32[]{:S(2)}) copy-start(f32[384,128]{1,0:T(8,128)} %copy-done.36) | copy-start | bytes 589828
  133.0 7.4 %copy-start.45 = (bf16[384,128]{1,0:T(8,128)(2,1)S(1)}, bf16[384,128]{1,0:T(8,128)(2,1)}, u32[]{:S(2)}) copy-start(bf16[384,128]{1,0:T(8,128)(2,1)} %copy-done.44) | copy-start | bytes 294916
  (24 other events, 18.2 us)

commit v2 on v1

v2 whole, which is shorter than its diff:
```python
import functools

import jax
import jax.numpy as jnp
from jax import lax
from jax.experimental import pallas as pl
from jax.experimental.pallas import tpu as pltpu
from jax.sharding import PartitionSpec as P

WIDTH = 8192
EPSILON = 1e-06
IMAGE_LEN = 24
EXTRA = 16
HEAD = 128
PAIR = 2 * HEAD
RINGS = 4

F32 = jnp.float32
BF16 = jnp.bfloat16
PARAMS = pltpu.CompilerParams(vmem_limit_bytes=60 * 2**20)


def identity_mask():
    shape = (HEAD, HEAD)
    return lax.broadcasted_iota(jnp.int32, shape, 0) == lax.broadcasted_iota(jnp.int32, shape, 1)


def column_to_lanes(column):
    eye = identity_mask()
    row = lax.broadcasted_iota(jnp.int32, (8, HEAD), 0)
    out = jnp.zeros((8, HEAD), F32)
    for p in range(column.shape[0] // HEAD):
        piece = column[p * HEAD : (p + 1) * HEAD, :]
        lanes = jnp.sum(jnp.where(eye, piece, 0.0), axis=0, keepdims=True)
        out = jnp.where(row == p, lanes, out)
    return out


def lanes_to_column(lanes, rows):
    eye = identity_mask()
    pieces = [
        jnp.sum(jnp.where(eye, lanes[p : p + 1, :], 0.0), axis=1, keepdims=True)
        for p in range(rows // HEAD)
    ]
    return jnp.concatenate(pieces, axis=0)


def split_extra(lanes):
    high = lanes.astype(BF16).astype(F32)
    both = jnp.concatenate([high, lanes - high], axis=0)
    return jnp.concatenate([both, jnp.zeros((EXTRA, HEAD), F32)], axis=1).astype(BF16)


def join_extra(block):
    block = block.astype(F32)
    return block[0:8, 0:HEAD] + block[8:16, 0:HEAD]


def product(scaled_ref, wk_ref, wv_ref):
    weight = jnp.concatenate([wk_ref[...], wv_ref[...]], axis=1)
    return jnp.dot(scaled_ref[...], weight, preferred_element_type=F32)


def forward_other_kernel(place, x_ref, gain_ref, wk_ref, wv_ref, out_ref, scaled_ref, lanes_ref):
    @pl.when(pl.program_id(0) == 0)
    def _():
        x = x_ref[...].astype(F32)
        scaled_ref[...] = (gain_ref[...] * x).astype(BF16)
        lanes_ref[...] = column_to_lanes(jnp.sum(x * x, axis=1, keepdims=True))

    rows = x_ref.shape[0]
    out_ref[0, 0:rows, :] = product(scaled_ref, wk_ref, wv_ref).astype(BF16)
    out_ref[0, rows:, :] = split_extra(lanes_ref[...])


def forward_own_kernel(
    place, scaled_ref, lanes_ref, wk_ref, wv_ref, in_ref, out0, out1, out2, out3
):
    step, rows = pl.program_id(0), scaled_ref.shape[0]
    total = product(scaled_ref, wk_ref, wv_ref) + in_ref[0, 0:rows, :].astype(F32)
    total = total.astype(BF16)
    extra = split_extra(lanes_ref[...] + join_extra(in_ref[0, rows:, :]))
    for d, out_ref in enumerate((out0, out1, out2, out3)):

        @pl.when(step == d)
        def _(out_ref=out_ref):
            out_ref[0:rows, :] = total
            out_ref[rows:, :] = extra


def forward_call(kernel, own, place, operands, in_specs, out_specs, out_shape, rows, wk, wv):
    depth = wk.shape[0]

    def columns(d, s):
        core = s[1] if own else 1 - s[1]
        return (0, 2 * lax.rem(s[0] + d, RINGS) + core)

    weights = [pl.BlockSpec((depth, HEAD), columns)] * 2
    return pl.pallas_call(
        kernel,
        grid_spec=pltpu.PrefetchScalarGridSpec(
            num_scalar_prefetch=1,
            grid=(RINGS,),
            in_specs=in_specs[0:2] + weights + in_specs[2:],
            out_specs=out_specs,
        ),
        out_shape=out_shape,
        compiler_params=PARAMS,
        cost_estimate=pl.CostEstimate(
            flops=2 * rows * depth * RINGS * PAIR, bytes_accessed=rows * 2**13 + 2**21, transcendentals=0
        ),
        name="forward_own" if own else "forward_other",
    )(place, *operands[0:2], wk, wv, *operands[2:])


def whole(shape):
    return pl.BlockSpec(shape, lambda *_: (0,) * len(shape))


def stepwise(shape):
    return pl.BlockSpec((1,) + shape, lambda d, s: (d, 0, 0))


def forward_other(place, x, gain, wk, wv):
    rows, width = x.shape
    block = (rows + EXTRA, PAIR)
    return forward_call(
        forward_other_kernel,
        False,
        place,
        (x, gain),
        [whole(x.shape), whole(gain.shape)],
        [stepwise(block), whole(x.shape), whole((8, HEAD))],
        [
            jax.ShapeDtypeStruct((RINGS,) + block, BF16),
            jax.ShapeDtypeStruct(x.shape, BF16),
            jax.ShapeDtypeStruct((8, HEAD), F32),
        ],
        rows,
        wk,
        wv,
    )


def forward_own(place, scaled, lanes, wk, wv, arrived):
    rows = scaled.shape[0]
    block = (rows + EXTRA, PAIR)
    return forward_call(
        forward_own_kernel,
        True,
        place,
        (scaled, lanes, arrived),
        [whole(scaled.shape), whole(lanes.shape), stepwise(block)],
        [whole(block)] * RINGS,
        [jax.ShapeDtypeStruct(block, BF16)] * RINGS,
        rows,
        wk,
        wv,
    )


def gathered(refs):
    rows = refs[0].shape[0] - EXTRA
    total = refs[0][0:rows, :].astype(F32)
    lanes = join_extra(refs[0][rows:, :])
    for ref in refs[1:]:
        total = total + ref[0:rows, :].astype(F32)
        lanes = lanes + join_extra(ref[rows:, :])
    inverse = lax.rsqrt(lanes_to_column(lanes, rows) / WIDTH + EPSILON)
    return (inverse * total).astype(BF16), inverse


def residual(both, target, inverse, resid_ref, inverse_ref):
    rows = both.shape[0]
    resid = (both.astype(F32) - target).astype(BF16)
    dots = jnp.sum(resid.astype(F32) * both.astype(F32), axis=1, keepdims=True)
    resid_ref[0:rows, :] = resid
    resid_ref[rows:, :] = split_extra(column_to_lanes(dots))
    inverse_ref[...] = jnp.broadcast_to(inverse, (rows, HEAD))


def text_combine_kernel(a, b, c, d, kt_ref, vt_ref, keys_ref, values_ref, resid_ref, inverse_ref):
    both, inverse = gathered((a, b, c, d))
    target = jnp.concatenate([kt_ref[...], vt_ref[...]], axis=1).astype(F32)
    keys_ref[...] = both[:, 0:HEAD]
    values_ref[...] = both[:, HEAD:]
    residual(both, target, inverse, resid_ref, inverse_ref)


def one_hot(shape, match):
    return jnp.where(match, jnp.ones(shape, F32), jnp.zeros(shape, F32)).astype(BF16)


def slot_columns(rows, first, count, lanes_ref):
    row = first + lax.broadcasted_iota(jnp.int32, (rows, count), 0)
    begin = IMAGE_LEN * lax.broadcasted_iota(jnp.int32, (rows, count), 1)
    inside = (row >= begin) & (row < begin + IMAGE_LEN)
    value = lanes_ref[...] + (row - begin).astype(F32)
    return jnp.sum(jnp.where(inside, value, 0.0), axis=1, keepdims=True)


def slot_lanes(rows, count, column_ref):
    row = lax.broadcasted_iota(jnp.int32, (count, rows), 1)
    begin = IMAGE_LEN * lax.broadcasted_iota(jnp.int32, (count, rows), 0)
    inside = (row >= begin) & (row < begin + IMAGE_LEN)
    value = column_ref[...] + (row - begin).astype(F32)
    return jnp.sum(jnp.where(inside, value, 0.0), axis=0, keepdims=True)


def image_combine_kernel(
    a, b, c, d, arrived_ref, dest_lanes, dest_column, send_ref, resid_ref, inverse_ref
):
    slots, images = arrived_ref.shape[0], dest_lanes.shape[1]
    rows = images * IMAGE_LEN
    both, inverse = gathered((a, b, c, d))
    slot = slot_columns(rows, 0, images, dest_lanes)
    shape = (rows, slots)
    match = lax.broadcasted_iota(jnp.int32, shape, 1).astype(F32) == slot
    target = jnp.dot(one_hot(shape, match), arrived_ref[...], preferred_element_type=F32)
    residual(both, target, inverse, resid_ref, inverse_ref)
    shape = (slots, rows)
    match = lax.broadcasted_iota(jnp.int32, shape, 0).astype(F32) == slot_lanes(
        rows, images, dest_column
    )
    send_ref[...] = jnp.dot(one_hot(shape, match), both, preferred_element_type=F32).astype(BF16)


def text_combine(parts, targets):
    rows = targets[0].shape[0]
    return pl.pallas_call(
        text_combine_kernel,
        out_shape=[
            jax.ShapeDtypeStruct((rows, HEAD), BF16),
            jax.ShapeDtypeStruct((rows, HEAD), BF16),
            jax.ShapeDtypeStruct(parts[0].shape, BF16),
            jax.ShapeDtypeStruct((rows, HEAD), F32),
        ],
        compiler_params=PARAMS,
        cost_estimate=pl.CostEstimate(flops=2**22, bytes_accessed=2**22, transcendentals=0),
        name="text_combine",
    )(*parts, *targets)


def image_combine(parts, arrived, dest):
    rows = parts[0].shape[0] - EXTRA
    return pl.pallas_call(
        image_combine_kernel,
        out_shape=[
            jax.ShapeDtypeStruct(arrived.shape, BF16),
            jax.ShapeDtypeStruct(parts[0].shape, BF16),
            jax.ShapeDtypeStruct((rows, HEAD), F32),
        ],
        compiler_params=PARAMS,
        cost_estimate=pl.CostEstimate(flops=2**28, bytes_accessed=2**21, transcendentals=0),
        name="image_combine",
    )(*parts, arrived, dest[None, :], dest[:, None])


def gather_kernel(first_ref, kt_ref, vt_ref, out_ref):
    rows, slots = kt_ref.shape[0], first_ref.shape[1]
    step = HEAD
    both = jnp.concatenate([kt_ref[...], vt_ref[...]], axis=1)
    for begin in range(0, out_ref.shape[0], step):
        place = slot_columns(step, begin, slots, first_ref)
        shape = (step, rows)
        match = lax.broadcasted_iota(jnp.int32, shape, 1).astype(F32) == place
        picked = jnp.dot(one_hot(shape, match), both, preferred_element_type=F32)
        out_ref[begin : begin + step, :] = picked.astype(BF16)


def gather_targets(first, key_target, value_target):
    slots = first.shape[0] * IMAGE_LEN
    return pl.pallas_call(
        gather_kernel,
        out_shape=jax.ShapeDtypeStruct((slots, PAIR), BF16),
        compiler_params=PARAMS,
        cost_estimate=pl.CostEstimate(flops=2**28, bytes_accessed=2**20, transcendentals=0),
        name="gather_targets",
    )(first[None, :], key_target, value_target)


def image_rows_mask(rows, first_row, first_lanes):
    shape = (rows, first_lanes.shape[1])
    row = (first_row + lax.broadcasted_iota(jnp.int32, shape, 0)).astype(F32)
    begin = first_lanes[...]
    inside = (row >= begin) & (row < begin + IMAGE_LEN)
    return jnp.sum(jnp.where(inside, 1.0, 0.0), axis=1, keepdims=True) > 0.5


def merge_kernel(first_lanes, first_column, arrived_ref, k_ref, v_ref, keys_ref, values_ref):
    slots = arrived_ref.shape[0]
    place = slot_lanes(slots, first_column.shape[0], first_column)
    step = 2 * HEAD
    for begin in range(0, k_ref.shape[0], step):
        shape = (step, slots)
        row = begin + lax.broadcasted_iota(jnp.int32, shape, 0)
        match = row.astype(F32) == place
        landed = jnp.dot(one_hot(shape, match), arrived_ref[...], preferred_element_type=F32)
        mask = image_rows_mask(step, begin, first_lanes)
        here = slice(begin, begin + step)
        keys = jnp.where(mask, landed[:, 0:HEAD], k_ref[here, :].astype(F32))
        values = jnp.where(mask, landed[:, HEAD:], v_ref[here, :].astype(F32))
        keys_ref[here, :] = keys.astype(BF16)
        values_ref[here, :] = values.astype(BF16)


def merge(first, arrived, keys, values):
    return pl.pallas_call(
        merge_kernel,
        out_shape=[jax.ShapeDtypeStruct(keys.shape, BF16)] * 2,
        compiler_params=PARAMS,
        cost_estimate=pl.CostEstimate(flops=2**28, bytes_accessed=2**21, transcendentals=0),
        name="merge",
    )(first[None, :], first[:, None], arrived, keys, values)


def backward_kernel(masked, place, x_ref, gain_ref, inverse_ref, first_lanes, wk_ref, wv_ref, *rest):
    resids = rest[0 : 2 * RINGS]
    out_ref, keys_all, values_all, coefficient, keep = rest[2 * RINGS :]
    rows = x_ref.shape[0]

    @pl.when(pl.program_id(0) == 0)
    def _():
        lanes = jnp.zeros((8, HEAD), F32)
        for n, ref in enumerate(resids):
            other, d = n // RINGS, n % RINGS
            core = 1 - place[1] if other else place[1]
            begin = HEAD * (2 * lax.rem(place[0] + RINGS - d, RINGS) + core)
            columns = pl.ds(pl.multiple_of(begin, HEAD), HEAD)
            keys_all[:, columns] = ref[0:rows, 0:HEAD]
            values_all[:, columns] = ref[0:rows, HEAD:]
            lanes = lanes + join_extra(ref[rows:, :])
        inverse = inverse_ref[...]
        coefficient[...] = inverse * inverse * lanes_to_column(lanes, rows) / WIDTH
        if masked:
            mask = image_rows_mask(rows, 0, first_lanes)
            keep[...] = jnp.broadcast_to(jnp.where(mask, 0.0, 1.0), keep.shape)

    contract = (((1,), (1,)), ((), ()))
    back = lax.dot_general(keys_all[...], wk_ref[...], contract, preferred_element_type=F32)
    back += lax.dot_general(values_all[...], wv_ref[...], contract, preferred_element_type=F32)
    grad = gain_ref[...] * inverse_ref[:, 0:1] * back
    grad = grad - coefficient[:, 0:1] * x_ref[...].astype(F32)
    if masked:
        grad = jnp.where(keep[:, 0:1] > 0.5, grad, 0.0)
    out_ref[...] = grad.astype(BF16)


def backward(place, x, gain, inverse, first, wk, wv, resids, masked):
    rows, width = x.shape
    columns = wk.shape[1]
    tile = 256
    across_tiles = lambda shape: pl.BlockSpec(shape, lambda i, s: (0, i))
    return pl.pallas_call(
        functools.partial(backward_kernel, masked),
        grid_spec=pltpu.PrefetchScalarGridSpec(
            num_scalar_prefetch=1,
            grid=(width // tile,),
            in_specs=[
                across_tiles((rows, tile)),
                across_tiles((1, tile)),
                whole((rows, HEAD)),
                whole((1, first.shape[0])),
                pl.BlockSpec((tile, columns), lambda i, s: (i, 0)),
                pl.BlockSpec((tile, columns), lambda i, s: (i, 0)),
                *[whole(resids[0].shape)] * (2 * RINGS),
            ],
            out_specs=across_tiles((rows, tile)),
            scratch_shapes=[
                pltpu.VMEM((rows, columns), BF16),
                pltpu.VMEM((rows, columns), BF16),
                pltpu.VMEM((rows, HEAD), F32),
                pltpu.VMEM((rows, HEAD), F32),
            ],
        ),
        out_shape=jax.ShapeDtypeStruct(x.shape, BF16),
        compiler_params=PARAMS,
        cost_estimate=pl.CostEstimate(
            flops=4 * rows * width * columns, bytes_accessed=rows * 2**13 + 2**22, transcendentals=0
        ),
        name="backward",
    )(place, x, gain, inverse, first[None, :], wk, wv, *resids)


def around(x, shift):
    return lax.ppermute(
        x, "tp", [(2 * y + c, 2 * ((y + shift) % RINGS) + c) for y in range(RINGS) for c in range(2)]
    )


def across(x):
    return lax.ppermute(x, "tp", [(i, i ^ 1) for i in range(2 * RINGS)])


def on_device(
    text_embed,
    image_embed,
    image_start,
    norm_gain,
    key_weight,
    value_weight,
    key_target,
    value_target,
):
    shards = lax.axis_size("rows")
    myself = lax.axis_index("rows")
    mine = lax.axis_index("tp").astype(jnp.int32)
    place = jnp.stack([mine // 2, mine % 2])
    gain = norm_gain[None, :]
    starts = image_start.reshape(shards, -1)
    block_of = starts // text_embed.shape[0]
    offset = (starts - block_of * text_embed.shape[0]).astype(F32)
    here = jnp.where(block_of == myself, offset + 8192.0, 0.0)
    first = jnp.sum(here, axis=1) - 8192.0
    dest = IMAGE_LEN * lax.dynamic_index_in_dim(block_of, myself, 0, keepdims=False).astype(F32)

    inputs = (text_embed, image_embed)
    parts = []
    for x in inputs:
        other, scaled, lanes = forward_other(place, x, gain, key_weight, value_weight)
        own = forward_own(place, scaled, lanes, key_weight, value_weight, across(other))
        parts.append([own[0]] + [around(own[d], d) for d in range(1, RINGS)])

    goals = gather_targets(first, key_target, value_target)
    goals = lax.all_to_all(goals, "rows", split_axis=0, concat_axis=0, tiled=True)
    keys, values, *text_state = text_combine(parts[0], (key_target, value_target))
    send, *image_state = image_combine(parts[1], goals, dest)
    landed = lax.all_to_all(send, "rows", split_axis=0, concat_axis=0, tiled=True)

    grads = []
    for n, (x, (resid, inverse)) in enumerate(zip(inputs, (text_state, image_state))):
        own = [resid] + [around(resid, d) for d in range(1, RINGS)]
        resids = own + [across(r) for r in own]
        grads.append(
            backward(place, x, gain, inverse, first, key_weight, value_weight, resids, n == 0)
        )
    keys, values = merge(first, landed, keys, values)
    return (keys, values, *grads)


def solution(mesh):
    in_specs = (
        P("rows", "tp"),
        P("rows", "tp"),
        P(),
        P("tp"),
        P("tp", None),
        P("tp", None),
        P("rows", "tp"),
        P("rows", "tp"),
    )
    out_specs = (P("rows", "tp"), P("rows", "tp"), P("rows", "tp"), P("rows", "tp"))
    return jax.shard_map(
        on_device, mesh=mesh, in_specs=in_specs, out_specs=out_specs, check_vma=False
    )
```

time: 145 us -> 123 us (0.85)
  local copies, waits for them, and re-layouts: 32.8 us -> 7.28 us
  waiting for transfers between devices: 0.4 us -> 16.1 us
  starting transfers between devices: 53.1 us -> 43.9 us
  Pallas kernels: 56.9 us -> 52.3 us
  other arithmetic: 0.24 us -> 1.81 us
    unnamed x106 -> x46, local copies, waits for them, and re-layouts: 32.6 us -> 5.83 us
    ppermute x18 -> x12, waiting for transfers between devices: 0.05 us -> 14.2 us  [around(): lax.ppermute(x, 'tp', [(2 * y + c, 2 * ((y + shift) % RINGS) + c) for y i...]
    pallas_call x12 -> x8, Pallas kernels: 53.7 us -> 47 us  [the longest x4 24.4 us: forward_call(): pl.pallas_call(kernel, grid_spec=pltpu.PrefetchScalarGridSpec(num_scalar_...]
    ppermute x18 -> x12, starting transfers between devices: 21.1 us -> 15.7 us  [around(): lax.ppermute(x, 'tp', [(2 * y + c, 2 * ((y + shift) % RINGS) + c) for y i...]
    ppermute x15 -> x10, starting transfers between devices: 12.8 us -> 9.18 us  [across(): return lax.ppermute(x, 'tp', [(i, i ^ 1) for i in range(2 * RINGS)])]
    pallas_call x1, Pallas kernels: 0.55 us -> 2.32 us  [gather_targets(): pl.pallas_call(gather_kernel, out_shape=jax.ShapeDtypeStruct((slots, PAIR...]
    ppermute x15 -> x10, waiting for transfers between devices: 0.35 us -> 1.85 us  [across(): return lax.ppermute(x, 'tp', [(i, i ^ 1) for i in range(2 * RINGS)])]
  transfers between devices with their start and end apart: 35 -> 24, of which waited for: 1 -> 6; matrix products, arithmetic and copies ran while one was open for 0% -> 2% of each run, Pallas kernels for 36% -> 29%
where the time goes in v2:
time: 123 us; the launch traced here: 122 us
  Pallas kernels  52.3 us (43%)
  starting transfers between devices  43.9 us (36%)
  waiting for transfers between devices  16.1 us (13%)
  local copies, waits for them, and re-layouts  7.28 us (6%)
  other arithmetic  1.81 us (1%)
    pallas_call x4, Pallas kernels, forward_call(): pl.pallas_call(kernel, grid_spec=pltpu.PrefetchScalarGridSpec(num_scalar_...  24.4 us
    pallas_call x2, Pallas kernels, backward(): pl.pallas_call(functools.partial(backward_kernel, masked), grid_spec=pltp...  17.2 us
    ppermute x12, starting transfers between devices, around(): lax.ppermute(x, 'tp', [(2 * y + c, 2 * ((y + shift) % RINGS) + c) for y i...  15.7 us
    ppermute x12, waiting for transfers between devices, around(): lax.ppermute(x, 'tp', [(2 * y + c, 2 * ((y + shift) % RINGS) + c) for y i...  14.2 us
    all_to_all x1, starting transfers between devices, on_device(): lax.all_to_all(send, 'rows', split_axis=0, concat_axis=0, tiled=True)  9.8 us
    all_to_all x1, starting transfers between devices, on_device(): lax.all_to_all(goals, 'rows', split_axis=0, concat_axis=0, tiled=True)  9.3 us
    ppermute x10, starting transfers between devices, across(): return lax.ppermute(x, 'tp', [(i, i ^ 1) for i in range(2 * RINGS)])  9.18 us
    unnamed x46, local copies, waits for them, and re-layouts  5.83 us
  transfers between devices with their start and end apart: 24, of which 6 were waited for; matrix products, arithmetic and copies ran while one was open for 2% of the time, Pallas kernels for 29%

profile of v2, /device:TPU:1, one launch (start us, length us, event | category | flops | bytes accessed | tf_op | source)
XLA Modules:
  0.0 122.3 jit_solution(12274974155365807749)
XLA Ops:
  0.6 0.6 pad_add_fusion.place
  1.3 6.6 %forward_other.3 = (bf16[4,784,256]{2,1,0:T(8,128)(2,1)}, bf16[768,1024]{1,0:T(8,128)(2,1)}, f32[8,128]{1,0:T(8,128)}) custom-call(s32[2]{0:T(128)} %pad_add_fusion.place, bf16[768,1024]{1,0:T(8,128)(2,1)} %x_ref.6, f32[1,1024]{1,0:T(1,128)} %bitcast.16, bf16[1024,1024]{1,0:T(8,128)(2,1)} %wk_ref.11, bf16[1024,1024]{1,0:T(8,128)(2,1)} %wv_ref.11), custom_call_target="tpu_custom_call" | custom-call | flops 1610612736 | bytes 8388608 | tf_op jit(solution)/shard_map/forward_other/pallas_call | solution.py:99
  7.9 3.3 %collective-permute-start.4 = (bf16[4,784,256]{2,1,0:T(8,128)(2,1)}, bf16[4,784,256]{2,1,0:T(8,128)(2,1)S(1)}, u32[]{:S(2)}, u32[]{:S(2)}) collective-permute-start(bf16[4,784,256]{2,1,0:T(8,128)(2,1)} %get-tuple-element.37), channel_id=1, source_target_pairs={{0,1},{1,0},{2,3},{3,2},{4,5},{5,4},{6,7},{7,6},{8,9},{9,8},{10,11... | collective-permute-start | bytes 4816904 | tf_op jit(solution)/shard_map/ppermute | solution.py:392
  11.1 5.5 %forward_other.2 = (bf16[4,400,256]{2,1,0:T(8,128)(2,1)}, bf16[384,1024]{1,0:T(8,128)(2,1)}, f32[8,128]{1,0:T(8,128)}) custom-call(s32[2]{0:T(128)} %pad_add_fusion.place, bf16[384,1024]{1,0:T(8,128)(2,1)} %x_ref.7, f32[1,1024]{1,0:T(1,128)} %bitcast.17, bf16[1024,1024]{1,0:T(8,128)(2,1)} %wk_ref.11, bf16[1024,1024]{1,0:T(8,128)(2,1)} %wv_ref.11), custom_call_target="tpu_custom_call" | custom-call | flops 805306368 | bytes 5242880 | tf_op jit(solution)/shard_map/forward_other/pallas_call | solution.py:99
  16.6 0.0 collective-permute-start
  16.7 0.1 reshape.49
  16.7 0.1 select_reduce_fusion
  16.9 0.5 add_bitcast_fusion
  17.4 2.3 %gather_targets.1 = bf16[768,256]{1,0:T(8,128)(2,1)} custom-call(f32[1,32]{1,0:T(1,128)} %get-tuple-element.51.first_ref.first_lanes, bf16[768,128]{1,0:T(8,128)(2,1)} %kt_ref.3, bf16[768,128]{1,0:T(8,128)(2,1)} %vt_ref.3), custom_call_target="tpu_custom_call" | custom-call | flops 268435456 | bytes 1048576 | tf_op jit(solution)/shard_map/gather_targets/pallas_call | solution.py:273
  19.7 9.3 %all-to-all-start = ((bf16[32,24,256]{2,1,0:T(8,128)(2,1)}), bf16[32,24,256]{2,1,0:T(8,128)(2,1)S(1)}, u32[]{:S(2)}, u32[]{:S(2)}) async-start(bf16[32,24,256]{2,1,0:T(8,128)(2,1)} %bitcast.15), calls=%async_computation | async-start | bytes 786432 | tf_op jit(solution)/shard_map/all_to_all | solution.py:425
  29.1 0.9 copy-done.2
  29.9 5.5 %forward_own.2 = (bf16[400,256]{1,0:T(8,128)(2,1)}, bf16[400,256]{1,0:T(8,128)(2,1)}, bf16[400,256]{1,0:T(8,128)(2,1)}, bf16[400,256]{1,0:T(8,128)(2,1)}) custom-call(s32[2]{0:T(128)} %pad_add_fusion.place, bf16[384,1024]{1,0:T(8,128)(2,1)} %get-tuple-element.27.scaled_ref, f32[8,128]{1,0:T(8,128)} %get-tuple-element.28.lanes_ref, ...), custom_call_target="tpu_custom_call" | custom-call | flops 805306368 | bytes 5242880 | tf_op jit(solution)/shard_map/forward_own/pallas_call | solution.py:99
  35.4 1.3 %collective-permute-start.1 = (bf16[400,256]{1,0:T(8,128)(2,1)}, bf16[400,256]{1,0:T(8,128)(2,1)S(1)}, u32[]{:S(2)}, u32[]{:S(2)}) collective-permute-start(bf16[400,256]{1,0:T(8,128)(2,1)} %get-tuple-element.31), channel_id=1, source_target_pairs={{0,2},{1,3},{2,4},{3,5},{4,6},{5,7},{6,0},{7,1},{8,10},{9,11},{10,... | collective-permute-start | bytes 614408 | tf_op jit(solution)/shard_map/ppermute | solution.py:386
  36.7 2.7 %collective-permute-start.2 = (bf16[400,256]{1,0:T(8,128)(2,1)}, bf16[400,256]{1,0:T(8,128)(2,1)S(1)}, u32[]{:S(2)}, u32[]{:S(2)}) collective-permute-start(bf16[400,256]{1,0:T(8,128)(2,1)} %get-tuple-element.32), channel_id=1, source_target_pairs={{0,4},{1,5},{2,6},{3,7},{4,0},{5,1},{6,2},{7,3},{8,12},{9,13},{10,... | collective-permute-start | bytes 614408 | tf_op jit(solution)/shard_map/ppermute | solution.py:386
  39.5 1.1 collective-permute-start.3
  40.5 1.2 copy-done
  41.7 6.8 %forward_own.3 = (bf16[784,256]{1,0:T(8,128)(2,1)}, bf16[784,256]{1,0:T(8,128)(2,1)}, bf16[784,256]{1,0:T(8,128)(2,1)}, bf16[784,256]{1,0:T(8,128)(2,1)}) custom-call(s32[2]{0:T(128)} %pad_add_fusion.place, bf16[768,1024]{1,0:T(8,128)(2,1)} %get-tuple-element.35.scaled_ref, f32[8,128]{1,0:T(8,128)} %get-tuple-element.36.lanes_ref, ...), custom_call_target="tpu_custom_call" | custom-call | flops 1610612736 | bytes 8388608 | tf_op jit(solution)/shard_map/forward_own/pallas_call | solution.py:99
  48.5 0.4 collective-permute-start.5
  48.9 0.8 collective-permute-start.6
  49.7 1.7 %collective-permute-start.7 = (bf16[784,256]{1,0:T(8,128)(2,1)}, bf16[784,256]{1,0:T(8,128)(2,1)S(1)}, u32[]{:S(2)}, u32[]{:S(2)}) collective-permute-start(bf16[784,256]{1,0:T(8,128)(2,1)} %get-tuple-element.41), channel_id=1, source_target_pairs={{0,6},{1,7},{2,0},{3,1},{4,2},{5,3},{6,4},{7,5},{8,14},{9,15},{10,... | collective-permute-start | bytes 1204232 | tf_op jit(solution)/shard_map/ppermute | solution.py:386
  51.4 0.7 copy.14.dest_column
  52.1 0.5 convert_multiply_fusion.dest_lanes
  52.6 0.0 all-to-all-done
  52.6 0.0 collective-permute-done.3.d
  52.6 0.7 copy-done.1
  53.3 0.1 copy-done.16
  53.4 0.1 copy-done.17
  53.5 3.0 %image_combine.1 = (bf16[768,256]{1,0:T(8,128)(2,1)}, bf16[400,256]{1,0:T(8,128)(2,1)}, f32[384,128]{1,0:T(8,128)}) custom-call(bf16[400,256]{1,0:T(8,128)(2,1)} %get-tuple-element.30.a, bf16[400,256]{1,0:T(8,128)(2,1)} %copy-done.15, bf16[400,256]{1,0:T(8,128)(2,1)} %copy-done.16, bf16[400,256]{1,0:T(8,128)(2,1)} %copy-done.17, bf16[768,256]{1,0:T(8,128)(2,1)} %bitcast.13, ...), custom_call_target="tpu_custom_call" | custom-call | flops 268435456 | bytes 2097152 | tf_op jit(solution)/shard_map/image_combine/pallas_call | solution.py:246
  56.5 0.4 collective-permute-start.15
  56.9 1.9 %collective-permute-start.16 = (bf16[400,256]{1,0:T(8,128)(2,1)}, bf16[400,256]{1,0:T(8,128)(2,1)S(1)}, u32[]{:S(2)}, u32[]{:S(2)}) collective-permute-start(bf16[400,256]{1,0:T(8,128)(2,1)} %get-tuple-element.49.rest_0_), channel_id=1, source_target_pairs={{0,4},{1,5},{2,6},{3,7},{4,0},{5,1},{6,2},{7,3},{8,12},{9,13},{10,... | collective-permute-start | bytes 614408 | tf_op jit(solution)/shard_map/ppermute | solution.py:386
  58.8 1.5 %collective-permute-done.5.b = bf16[784,256]{1,0:T(8,128)(2,1)S(1)} collective-permute-done((bf16[784,256]{1,0:T(8,128)(2,1)}, bf16[784,256]{1,0:T(8,128)(2,1)S(1)}, u32[]{:S(2)}, u32[]{:S(2)}) %collective-permute-start.5) | collective-permute-done | bytes 401440 | tf_op jit(solution)/shard_map/ppermute | solution.py:386
  60.3 0.5 collective-permute-start.17
  60.8 5.8 %collective-permute-done.6.c = bf16[784,256]{1,0:T(8,128)(2,1)S(1)} collective-permute-done((bf16[784,256]{1,0:T(8,128)(2,1)}, bf16[784,256]{1,0:T(8,128)(2,1)S(1)}, u32[]{:S(2)}, u32[]{:S(2)}) %collective-permute-start.6) | collective-permute-done | bytes 401440 | tf_op jit(solution)/shard_map/ppermute | solution.py:386
  66.6 4.1 %collective-permute-done.7.d = bf16[784,256]{1,0:T(8,128)(2,1)S(1)} collective-permute-done((bf16[784,256]{1,0:T(8,128)(2,1)}, bf16[784,256]{1,0:T(8,128)(2,1)S(1)}, u32[]{:S(2)}, u32[]{:S(2)}) %collective-permute-start.7) | collective-permute-done | bytes 401440 | tf_op jit(solution)/shard_map/ppermute | solution.py:386
  70.7 0.8 copy-done.5
  71.4 2.9 %text_combine.1 = (bf16[768,128]{1,0:T(8,128)(2,1)}, bf16[768,128]{1,0:T(8,128)(2,1)}, bf16[784,256]{1,0:T(8,128)(2,1)}, f32[768,128]{1,0:T(8,128)}) custom-call(bf16[784,256]{1,0:T(8,128)(2,1)} %get-tuple-element.38.a, bf16[784,256]{1,0:T(8,128)(2,1)} %copy-done.3, bf16[784,256]{1,0:T(8,128)(2,1)} %copy-done.4, bf16[784,256]{1,0:T(8,128)(2,1)} %copy-done.5, ...), custom_call_target="tpu_custom_call" | custom-call | flops 4194304 | bytes 4194304 | tf_op jit(solution)/shard_map/text_combine/pallas_call | solution.py:230
  74.3 1.8 %collective-permute-start.8 = (bf16[784,256]{1,0:T(8,128)(2,1)}, bf16[784,256]{1,0:T(8,128)(2,1)S(1)}, u32[]{:S(2)}, u32[]{:S(2)}) collective-permute-start(bf16[784,256]{1,0:T(8,128)(2,1)} %get-tuple-element.47.rest_0_), channel_id=1, source_target_pairs={{0,2},{1,3},{2,4},{3,5},{4,6},{5,7},{6,0},{7,1},{8,10},{9,11},{10,... | collective-permute-start | bytes 1204232 | tf_op jit(solution)/shard_map/ppermute | solution.py:386
  76.2 3.1 %collective-permute-start.9 = (bf16[784,256]{1,0:T(8,128)(2,1)}, bf16[784,256]{1,0:T(8,128)(2,1)S(1)}, u32[]{:S(2)}, u32[]{:S(2)}) collective-permute-start(bf16[784,256]{1,0:T(8,128)(2,1)} %get-tuple-element.47.rest_0_), channel_id=1, source_target_pairs={{0,4},{1,5},{2,6},{3,7},{4,0},{5,1},{6,2},{7,3},{8,12},{9,13},{10,... | collective-permute-start | bytes 1204232 | tf_op jit(solution)/shard_map/ppermute | solution.py:386
  79.3 0.0 collective-permute-done.15.rest_1_
  79.3 0.0 collective-permute-start.10
  79.4 2.3 %collective-permute-start.18 = (bf16[400,256]{1,0:T(8,128)(2,1)S(1)}, bf16[400,256]{1,0:T(8,128)(2,1)S(1)}, u32[]{:S(2)}, u32[]{:S(2)}) collective-permute-start(bf16[400,256]{1,0:T(8,128)(2,1)S(1)} %copy-done.7), channel_id=1, source_target_pairs={{0,1},{1,0},{2,3},{3,2},{4,5},{5,4},{6,7},{7,6},{8,9},{9,8},{10,11... | collective-permute-start | bytes 614408 | tf_op jit(solution)/shard_map/ppermute | solution.py:392
  81.7 9.8 %all-to-all-start.1 = ((bf16[32,24,256]{2,1,0:T(8,128)(2,1)}), bf16[32,24,256]{2,1,0:T(8,128)(2,1)S(1)}, u32[]{:S(2)}, u32[]{:S(2)}) async-start(bf16[32,24,256]{2,1,0:T(8,128)(2,1)} %bitcast.8), calls=%async_computation.1 | async-start | bytes 786432 | tf_op jit(solution)/shard_map/all_to_all | solution.py:428
  91.5 0.0 collective-permute-done.17.rest_3_
  91.5 0.4 collective-permute-start.19
  91.9 0.0 collective-permute-done.18.rest_4_
  91.9 0.2 collective-permute-start.20
  92.1 0.9 collective-permute-done.19.rest_5_
  93.0 0.3 collective-permute-start.11
  93.3 0.2 collective-permute-start.12
  93.6 2.8 %collective-permute-done.9.rest_2_ = bf16[784,256]{1,0:T(8,128)(2,1)S(1)} collective-permute-done((bf16[784,256]{1,0:T(8,128)(2,1)}, bf16[784,256]{1,0:T(8,128)(2,1)S(1)}, u32[]{:S(2)}, u32[]{:S(2)}) %collective-permute-start.9) | collective-permute-done | bytes 401440 | tf_op jit(solution)/shard_map/ppermute | solution.py:386
  96.4 2.0 %collective-permute-start.13 = (bf16[784,256]{1,0:T(8,128)(2,1)S(1)}, bf16[784,256]{1,0:T(8,128)(2,1)}, u32[]{:S(2)}, u32[]{:S(2)}) collective-permute-start(bf16[784,256]{1,0:T(8,128)(2,1)S(1)} %collective-permute-done.9.rest_2_), channel_id=1, source_target_pairs={{0,1},{1,0},{2,3},{3,2},{4,5},{5,4},{6,7},{7,6},{8,9},{9,8},{10,11... | collective-permute-start | bytes 1204232 | tf_op jit(solution)/shard_map/ppermute | solution.py:392
  98.4 0.0 collective-permute-done.10.rest_3_
  98.4 0.1 collective-permute-start.14
  98.5 0.0 collective-permute-done.20.rest_6_
  98.5 0.4 collective-permute-start.21
  98.9 0.7 copy.15.first_column
  99.6 0.9 collective-permute-done.21.rest_7_
  100.5 0.6 copy-done.14
  101.2 7.2 %backward.3 = bf16[384,1024]{1,0:T(8,128)(2,1)} custom-call(s32[2]{0:T(128)} %pad_add_fusion.place, bf16[384,1024]{1,0:T(8,128)(2,1)} %x_ref.7, f32[1,1024]{1,0:T(1,128)} %bitcast.18, f32[384,128]{1,0:T(8,128)} %get-tuple-element.48.inverse_ref, f32[1,32]{1,0:T(1,128)} %get-tuple-element.51.first_ref.first_lanes, bf16[1024,1024]{1,0:T(8,128)(2,1)} %wk_ref.11, ...), custom_call_target="tpu_custom_call" | custom-call | flops 1610612736 | bytes 7340032 | tf_op jit(solution)/shard_map/backward/pallas_call | solution.py:354
  108.4 0.0 copy-start.6
  108.4 0.7 copy-done.6
  109.1 2.5 %merge.1 = (bf16[768,128]{1,0:T(8,128)(2,1)}, bf16[768,128]{1,0:T(8,128)(2,1)}) custom-call(f32[1,32]{1,0:T(1,128)} %get-tuple-element.51.first_ref.first_lanes, f32[32,1]{1,0:T(8,128)} %copy.15.first_column, bf16[768,256]{1,0:T(8,128)(2,1)} %bitcast.14, bf16[768,128]{1,0:T(8,128)(2,1)} %get-tuple-element.42.k_ref, bf16[768,128]{1,0:T(8,128)(2,1)} %get-tuple-element.43.v_ref), custom_call_target="tpu_custom_call" | custom-call | flops 268435456 | bytes 2097152 | tf_op jit(solution)/shard_map/merge/pallas_call | solution.py:308
  111.6 0.7 copy-done.22
  112.3 10.0 %backward.2 = bf16[768,1024]{1,0:T(8,128)(2,1)} custom-call(s32[2]{0:T(128)} %pad_add_fusion.place, bf16[768,1024]{1,0:T(8,128)(2,1)} %x_ref.6, f32[1,1024]{1,0:T(1,128)} %bitcast.19, f32[768,128]{1,0:T(8,128)} %get-tuple-element.46.inverse_ref, f32[1,32]{1,0:T(1,128)} %get-tuple-element.51.first_ref.first_lanes, bf16[1024,1024]{1,0:T(8,128)(2,1)} %wk_ref.11, ...), custom_call_target="tpu_custom_call" | custom-call | flops 3221225472 | bytes 10485760 | tf_op jit(solution)/shard_map/backward/pallas_call | solution.py:354
  (49 shorter events, 0.1 us)
Async XLA Ops:
  7.9 8.8 %copy-start.18 = (s32[512]{0:T(512)S(1)}, s32[512]{0:T(512)}, u32[]{:S(2)}) copy-start(s32[512]{0:T(512)} %param.10) | copy-start | bytes 6148
  7.9 32.7 %collective-permute-start.4 = (bf16[4,784,256]{2,1,0:T(8,128)(2,1)}, bf16[4,784,256]{2,1,0:T(8,128)(2,1)S(1)}, u32[]{:S(2)}, u32[]{:S(2)}) collective-permute-start(bf16[4,784,256]{2,1,0:T(8,128)(2,1)} %get-tuple-element.37), channel_id=1, source_target_pairs={{0,1},{1,0},{2,3},{3,2},{4,5},{5,4},{6,7},{7,6},{8,9},{9,8},{10,11... | collective-permute-start | bytes 4816904 | tf_op jit(solution)/shard_map/ppermute | solution.py:392
  16.6 12.4 %collective-permute-start = (bf16[4,400,256]{2,1,0:T(8,128)(2,1)}, bf16[4,400,256]{2,1,0:T(8,128)(2,1)S(1)}, u32[]{:S(2)}, u32[]{:S(2)}) collective-permute-start(bf16[4,400,256]{2,1,0:T(8,128)(2,1)} %get-tuple-element.29), channel_id=1, source_target_pairs={{0,1},{1,0},{2,3},{3,2},{4,5},{5,4},{6,7},{7,6},{8,9},{9,8},{10,11... | collective-permute-start | bytes 2457608 | tf_op jit(solution)/shard_map/ppermute | solution.py:392
  19.7 32.9 %all-to-all-start = ((bf16[32,24,256]{2,1,0:T(8,128)(2,1)}), bf16[32,24,256]{2,1,0:T(8,128)(2,1)S(1)}, u32[]{:S(2)}, u32[]{:S(2)}) async-start(bf16[32,24,256]{2,1,0:T(8,128)(2,1)} %bitcast.15), calls=%async_computation | async-start | bytes 786432 | tf_op jit(solution)/shard_map/all_to_all | solution.py:425
  29.0 0.9 copy-start.2
  35.4 14.3 %collective-permute-start.1 = (bf16[400,256]{1,0:T(8,128)(2,1)}, bf16[400,256]{1,0:T(8,128)(2,1)S(1)}, u32[]{:S(2)}, u32[]{:S(2)}) collective-permute-start(bf16[400,256]{1,0:T(8,128)(2,1)} %get-tuple-element.31), channel_id=1, source_target_pairs={{0,2},{1,3},{2,4},{3,5},{4,6},{5,7},{6,0},{7,1},{8,10},{9,11},{10,... | collective-permute-start | bytes 614408 | tf_op jit(solution)/shard_map/ppermute | solution.py:386
  36.7 15.9 %collective-permute-start.2 = (bf16[400,256]{1,0:T(8,128)(2,1)}, bf16[400,256]{1,0:T(8,128)(2,1)S(1)}, u32[]{:S(2)}, u32[]{:S(2)}) collective-permute-start(bf16[400,256]{1,0:T(8,128)(2,1)} %get-tuple-element.32), channel_id=1, source_target_pairs={{0,4},{1,5},{2,6},{3,7},{4,0},{5,1},{6,2},{7,3},{8,12},{9,13},{10,... | collective-permute-start | bytes 614408 | tf_op jit(solution)/shard_map/ppermute | solution.py:386
  39.5 13.2 %collective-permute-start.3 = (bf16[400,256]{1,0:T(8,128)(2,1)}, bf16[400,256]{1,0:T(8,128)(2,1)S(1)}, u32[]{:S(2)}, u32[]{:S(2)}) collective-permute-start(bf16[400,256]{1,0:T(8,128)(2,1)} %get-tuple-element.33), channel_id=1, source_target_pairs={{0,6},{1,7},{2,0},{3,1},{4,2},{5,3},{6,4},{7,5},{8,14},{9,15},{10,... | collective-permute-start | bytes 614408 | tf_op jit(solution)/shard_map/ppermute | solution.py:386
  40.5 1.2 copy-start
  48.5 11.8 %collective-permute-start.5 = (bf16[784,256]{1,0:T(8,128)(2,1)}, bf16[784,256]{1,0:T(8,128)(2,1)S(1)}, u32[]{:S(2)}, u32[]{:S(2)}) collective-permute-start(bf16[784,256]{1,0:T(8,128)(2,1)} %get-tuple-element.39), channel_id=1, source_target_pairs={{0,2},{1,3},{2,4},{3,5},{4,6},{5,7},{6,0},{7,1},{8,10},{9,11},{10,... | collective-permute-start | bytes 1204232 | tf_op jit(solution)/shard_map/ppermute | solution.py:386
  48.9 17.6 %collective-permute-start.6 = (bf16[784,256]{1,0:T(8,128)(2,1)}, bf16[784,256]{1,0:T(8,128)(2,1)S(1)}, u32[]{:S(2)}, u32[]{:S(2)}) collective-permute-start(bf16[784,256]{1,0:T(8,128)(2,1)} %get-tuple-element.40), channel_id=1, source_target_pairs={{0,4},{1,5},{2,6},{3,7},{4,0},{5,1},{6,2},{7,3},{8,12},{9,13},{10,... | collective-permute-start | bytes 1204232 | tf_op jit(solution)/shard_map/ppermute | solution.py:386
  49.7 2.9 %copy-start.15 = (bf16[400,256]{1,0:T(8,128)(2,1)}, bf16[400,256]{1,0:T(8,128)(2,1)S(1)}, u32[]{:S(2)}) copy-start(bf16[400,256]{1,0:T(8,128)(2,1)S(1)} %collective-permute-done.1.b) | copy-start | bytes 614404
  49.7 20.9 %collective-permute-start.7 = (bf16[784,256]{1,0:T(8,128)(2,1)}, bf16[784,256]{1,0:T(8,128)(2,1)S(1)}, u32[]{:S(2)}, u32[]{:S(2)}) collective-permute-start(bf16[784,256]{1,0:T(8,128)(2,1)} %get-tuple-element.41), channel_id=1, source_target_pairs={{0,6},{1,7},{2,0},{3,1},{4,2},{5,3},{6,4},{7,5},{8,14},{9,15},{10,... | collective-permute-start | bytes 1204232 | tf_op jit(solution)/shard_map/ppermute | solution.py:386
  52.6 0.7 copy-start.1
  52.6 0.8 copy-start.16
  52.6 0.9 copy-start.17
  56.5 22.8 %copy-start.7 = (bf16[400,256]{1,0:T(8,128)(2,1)S(1)}, bf16[400,256]{1,0:T(8,128)(2,1)}, u32[]{:S(2)}) copy-start(bf16[400,256]{1,0:T(8,128)(2,1)} %get-tuple-element.49.rest_0_) | copy-start | bytes 614404
  56.5 22.8 %collective-permute-start.15 = (bf16[400,256]{1,0:T(8,128)(2,1)}, bf16[400,256]{1,0:T(8,128)(2,1)S(1)}, u32[]{:S(2)}, u32[]{:S(2)}) collective-permute-start(bf16[400,256]{1,0:T(8,128)(2,1)} %get-tuple-element.49.rest_0_), channel_id=1, source_target_pairs={{0,2},{1,3},{2,4},{3,5},{4,6},{5,7},{6,0},{7,1},{8,10},{9,11},{10,... | collective-permute-start | bytes 614408 | tf_op jit(solution)/shard_map/ppermute | solution.py:386
  56.9 22.4 %collective-permute-start.16 = (bf16[400,256]{1,0:T(8,128)(2,1)}, bf16[400,256]{1,0:T(8,128)(2,1)S(1)}, u32[]{:S(2)}, u32[]{:S(2)}) collective-permute-start(bf16[400,256]{1,0:T(8,128)(2,1)} %get-tuple-element.49.rest_0_), channel_id=1, source_target_pairs={{0,4},{1,5},{2,6},{3,7},{4,0},{5,1},{6,2},{7,3},{8,12},{9,13},{10,... | collective-permute-start | bytes 614408 | tf_op jit(solution)/shard_map/ppermute | solution.py:386
  60.3 10.4 %copy-start.3 = (bf16[784,256]{1,0:T(8,128)(2,1)}, bf16[784,256]{1,0:T(8,128)(2,1)S(1)}, u32[]{:S(2)}) copy-start(bf16[784,256]{1,0:T(8,128)(2,1)S(1)} %collective-permute-done.5.b) | copy-start | bytes 1204228
  60.3 31.2 %collective-permute-start.17 = (bf16[400,256]{1,0:T(8,128)(2,1)}, bf16[400,256]{1,0:T(8,128)(2,1)S(1)}, u32[]{:S(2)}, u32[]{:S(2)}) collective-permute-start(bf16[400,256]{1,0:T(8,128)(2,1)} %get-tuple-element.49.rest_0_), channel_id=1, source_target_pairs={{0,6},{1,7},{2,0},{3,1},{4,2},{5,3},{6,4},{7,5},{8,14},{9,15},{10,... | collective-permute-start | bytes 614408 | tf_op jit(solution)/shard_map/ppermute | solution.py:386
  66.6 4.1 %copy-start.4 = (bf16[784,256]{1,0:T(8,128)(2,1)}, bf16[784,256]{1,0:T(8,128)(2,1)S(1)}, u32[]{:S(2)}) copy-start(bf16[784,256]{1,0:T(8,128)(2,1)S(1)} %collective-permute-done.6.c) | copy-start | bytes 1204228
  70.7 0.8 copy-start.5
  74.3 19.0 %collective-permute-start.8 = (bf16[784,256]{1,0:T(8,128)(2,1)}, bf16[784,256]{1,0:T(8,128)(2,1)S(1)}, u32[]{:S(2)}, u32[]{:S(2)}) collective-permute-start(bf16[784,256]{1,0:T(8,128)(2,1)} %get-tuple-element.47.rest_0_), channel_id=1, source_target_pairs={{0,2},{1,3},{2,4},{3,5},{4,6},{5,7},{6,0},{7,1},{8,10},{9,11},{10,... | collective-permute-start | bytes 1204232 | tf_op jit(solution)/shard_map/ppermute | solution.py:386
  76.2 20.2 %collective-permute-start.9 = (bf16[784,256]{1,0:T(8,128)(2,1)}, bf16[784,256]{1,0:T(8,128)(2,1)S(1)}, u32[]{:S(2)}, u32[]{:S(2)}) collective-permute-start(bf16[784,256]{1,0:T(8,128)(2,1)} %get-tuple-element.47.rest_0_), channel_id=1, source_target_pairs={{0,4},{1,5},{2,6},{3,7},{4,0},{5,1},{6,2},{7,3},{8,12},{9,13},{10,... | collective-permute-start | bytes 1204232 | tf_op jit(solution)/shard_map/ppermute | solution.py:386
  79.3 21.2 %copy-start.8 = (bf16[400,256]{1,0:T(8,128)(2,1)}, bf16[400,256]{1,0:T(8,128)(2,1)S(1)}, u32[]{:S(2)}) copy-start(bf16[400,256]{1,0:T(8,128)(2,1)S(1)} %collective-permute-done.15.rest_1_) | copy-start | bytes 614404
  79.3 19.1 %collective-permute-start.10 = (bf16[784,256]{1,0:T(8,128)(2,1)}, bf16[784,256]{1,0:T(8,128)(2,1)S(1)}, u32[]{:S(2)}, u32[]{:S(2)}) collective-permute-start(bf16[784,256]{1,0:T(8,128)(2,1)} %get-tuple-element.47.rest_0_), channel_id=1, source_target_pairs={{0,6},{1,7},{2,0},{3,1},{4,2},{5,3},{6,4},{7,5},{8,14},{9,15},{10,... | collective-permute-start | bytes 1204232 | tf_op jit(solution)/shard_map/ppermute | solution.py:386
  79.4 21.1 %copy-start.9 = (bf16[400,256]{1,0:T(8,128)(2,1)}, bf16[400,256]{1,0:T(8,128)(2,1)S(1)}, u32[]{:S(2)}) copy-start(bf16[400,256]{1,0:T(8,128)(2,1)S(1)} %collective-permute-done.16.rest_2_) | copy-start | bytes 614404
  79.4 12.5 %collective-permute-start.18 = (bf16[400,256]{1,0:T(8,128)(2,1)S(1)}, bf16[400,256]{1,0:T(8,128)(2,1)S(1)}, u32[]{:S(2)}, u32[]{:S(2)}) collective-permute-start(bf16[400,256]{1,0:T(8,128)(2,1)S(1)} %copy-done.7), channel_id=1, source_target_pairs={{0,1},{1,0},{2,3},{3,2},{4,5},{5,4},{6,7},{7,6},{8,9},{9,8},{10,11... | collective-permute-start | bytes 614408 | tf_op jit(solution)/shard_map/ppermute | solution.py:392
  81.7 26.7 %all-to-all-start.1 = ((bf16[32,24,256]{2,1,0:T(8,128)(2,1)}), bf16[32,24,256]{2,1,0:T(8,128)(2,1)S(1)}, u32[]{:S(2)}, u32[]{:S(2)}) async-start(bf16[32,24,256]{2,1,0:T(8,128)(2,1)} %bitcast.8), calls=%async_computation.1 | async-start | bytes 786432 | tf_op jit(solution)/shard_map/all_to_all | solution.py:428
  91.5 9.0 %copy-start.10 = (bf16[400,256]{1,0:T(8,128)(2,1)}, bf16[400,256]{1,0:T(8,128)(2,1)S(1)}, u32[]{:S(2)}) copy-start(bf16[400,256]{1,0:T(8,128)(2,1)S(1)} %collective-permute-done.17.rest_3_) | copy-start | bytes 614404
  91.5 1.5 %collective-permute-start.19 = (bf16[400,256]{1,0:T(8,128)(2,1)S(1)}, bf16[400,256]{1,0:T(8,128)(2,1)S(1)}, u32[]{:S(2)}, u32[]{:S(2)}) collective-permute-start(bf16[400,256]{1,0:T(8,128)(2,1)S(1)} %collective-permute-done.15.rest_1_), channel_id=1, source_target_pairs={{0,1},{1,0},{2,3},{3,2},{4,5},{5,4},{6,7},{7,6},{8,9},{9,8},{10,11... | collective-permute-start | bytes 614408 | tf_op jit(solution)/shard_map/ppermute | solution.py:392
  91.9 8.6 %copy-start.11 = (bf16[400,256]{1,0:T(8,128)(2,1)}, bf16[400,256]{1,0:T(8,128)(2,1)S(1)}, u32[]{:S(2)}) copy-start(bf16[400,256]{1,0:T(8,128)(2,1)S(1)} %collective-permute-done.18.rest_4_) | copy-start | bytes 614404
  91.9 6.6 %collective-permute-start.20 = (bf16[400,256]{1,0:T(8,128)(2,1)S(1)}, bf16[400,256]{1,0:T(8,128)(2,1)S(1)}, u32[]{:S(2)}, u32[]{:S(2)}) collective-permute-start(bf16[400,256]{1,0:T(8,128)(2,1)S(1)} %collective-permute-done.16.rest_2_), channel_id=1, source_target_pairs={{0,1},{1,0},{2,3},{3,2},{4,5},{5,4},{6,7},{7,6},{8,9},{9,8},{10,11... | collective-permute-start | bytes 614408 | tf_op jit(solution)/shard_map/ppermute | solution.py:392
  93.0 7.5 %copy-start.12 = (bf16[400,256]{1,0:T(8,128)(2,1)}, bf16[400,256]{1,0:T(8,128)(2,1)S(1)}, u32[]{:S(2)}) copy-start(bf16[400,256]{1,0:T(8,128)(2,1)S(1)} %collective-permute-done.19.rest_5_) | copy-start | bytes 614404
  93.0 18.5 %collective-permute-start.11 = (bf16[784,256]{1,0:T(8,128)(2,1)}, bf16[784,256]{1,0:T(8,128)(2,1)S(1)}, u32[]{:S(2)}, u32[]{:S(2)}) collective-permute-start(bf16[784,256]{1,0:T(8,128)(2,1)} %get-tuple-element.47.rest_0_), channel_id=1, source_target_pairs={{0,1},{1,0},{2,3},{3,2},{4,5},{5,4},{6,7},{7,6},{8,9},{9,8},{10,11... | collective-permute-start | bytes 1204232 | tf_op jit(solution)/shard_map/ppermute | solution.py:392
  93.3 18.3 %copy-start.19 = (bf16[784,256]{1,0:T(8,128)(2,1)}, bf16[784,256]{1,0:T(8,128)(2,1)S(1)}, u32[]{:S(2)}) copy-start(bf16[784,256]{1,0:T(8,128)(2,1)S(1)} %collective-permute-done.8.rest_1_) | copy-start | bytes 1204228
  93.3 18.2 %collective-permute-start.12 = (bf16[784,256]{1,0:T(8,128)(2,1)S(1)}, bf16[784,256]{1,0:T(8,128)(2,1)}, u32[]{:S(2)}, u32[]{:S(2)}) collective-permute-start(bf16[784,256]{1,0:T(8,128)(2,1)S(1)} %collective-permute-done.8.rest_1_), channel_id=1, source_target_pairs={{0,1},{1,0},{2,3},{3,2},{4,5},{5,4},{6,7},{7,6},{8,9},{9,8},{10,11... | collective-permute-start | bytes 1204232 | tf_op jit(solution)/shard_map/ppermute | solution.py:392
  96.4 15.2 %copy-start.20 = (bf16[784,256]{1,0:T(8,128)(2,1)}, bf16[784,256]{1,0:T(8,128)(2,1)S(1)}, u32[]{:S(2)}) copy-start(bf16[784,256]{1,0:T(8,128)(2,1)S(1)} %collective-permute-done.9.rest_2_) | copy-start | bytes 1204228
  96.4 15.2 %collective-permute-start.13 = (bf16[784,256]{1,0:T(8,128)(2,1)S(1)}, bf16[784,256]{1,0:T(8,128)(2,1)}, u32[]{:S(2)}, u32[]{:S(2)}) collective-permute-start(bf16[784,256]{1,0:T(8,128)(2,1)S(1)} %collective-permute-done.9.rest_2_), channel_id=1, source_target_pairs={{0,1},{1,0},{2,3},{3,2},{4,5},{5,4},{6,7},{7,6},{8,9},{9,8},{10,11... | collective-permute-start | bytes 1204232 | tf_op jit(solution)/shard_map/ppermute | solution.py:392
  98.4 13.2 %copy-start.21 = (bf16[784,256]{1,0:T(8,128)(2,1)}, bf16[784,256]{1,0:T(8,128)(2,1)S(1)}, u32[]{:S(2)}) copy-start(bf16[784,256]{1,0:T(8,128)(2,1)S(1)} %collective-permute-done.10.rest_3_) | copy-start | bytes 1204228
  98.4 13.2 %collective-permute-start.14 = (bf16[784,256]{1,0:T(8,128)(2,1)S(1)}, bf16[784,256]{1,0:T(8,128)(2,1)}, u32[]{:S(2)}, u32[]{:S(2)}) collective-permute-start(bf16[784,256]{1,0:T(8,128)(2,1)S(1)} %collective-permute-done.10.rest_3_), channel_id=1, source_target_pairs={{0,1},{1,0},{2,3},{3,2},{4,5},{5,4},{6,7},{7,6},{8,9},{9,8},{10,11... | collective-permute-start | bytes 1204232 | tf_op jit(solution)/shard_map/ppermute | solution.py:392
  98.5 2.0 %copy-start.13 = (bf16[400,256]{1,0:T(8,128)(2,1)}, bf16[400,256]{1,0:T(8,128)(2,1)S(1)}, u32[]{:S(2)}) copy-start(bf16[400,256]{1,0:T(8,128)(2,1)S(1)} %collective-permute-done.20.rest_6_) | copy-start | bytes 614404
  98.5 2.0 %collective-permute-start.21 = (bf16[400,256]{1,0:T(8,128)(2,1)S(1)}, bf16[400,256]{1,0:T(8,128)(2,1)S(1)}, u32[]{:S(2)}, u32[]{:S(2)}) collective-permute-start(bf16[400,256]{1,0:T(8,128)(2,1)S(1)} %collective-permute-done.17.rest_3_), channel_id=1, source_target_pairs={{0,1},{1,0},{2,3},{3,2},{4,5},{5,4},{6,7},{7,6},{8,9},{9,8},{10,11... | collective-permute-start | bytes 614408 | tf_op jit(solution)/shard_map/ppermute | solution.py:392
  100.5 0.7 copy-start.14
  108.4 0.7 copy-start.6
  111.6 0.8 copy-start.22

commit v3 on v0

v3 whole, which is shorter than its diff:
```python
import functools

import jax
import jax.numpy as jnp
from jax import lax
from jax.experimental import pallas as pl
from jax.experimental.pallas import tpu as pltpu
from jax.sharding import PartitionSpec as P

WIDTH = 8192
EPSILON = 1e-06
IMAGE_LEN = 24
EXTRA = 16
HEAD = 128
PAIR = 2 * HEAD
RINGS = 4
CHUNKS = 2 * RINGS
PIECE = 128
ABSENT = 8192.0

F32 = jnp.float32
BF16 = jnp.bfloat16
PARAMS = pltpu.CompilerParams(vmem_limit_bytes=20 * 2**20)
IN_VMEM = pl.BlockSpec(memory_space=pltpu.VMEM)
ANYWHERE = pl.BlockSpec(memory_space=pl.ANY)


def near(x):
    return pltpu.with_memory_space_constraint(x, pltpu.VMEM)


def cost(flops, nbytes):
    return pl.CostEstimate(flops=flops, bytes_accessed=nbytes, transcendentals=0)


def same_index(count):
    shape = (count, count)
    return lax.broadcasted_iota(jnp.int32, shape, 0) == lax.broadcasted_iota(jnp.int32, shape, 1)


def column_to_lanes(column):
    eye = same_index(HEAD)
    row = lax.broadcasted_iota(jnp.int32, (8, HEAD), 0)
    out = jnp.zeros((8, HEAD), F32)
    for p in range(column.shape[0] // HEAD):
        piece = column[p * HEAD : (p + 1) * HEAD, :]
        lanes = jnp.sum(jnp.where(eye, piece, 0.0), axis=0, keepdims=True)
        out = jnp.where(row == p, lanes, out)
    return out


def lanes_to_column(lanes, rows):
    eye = same_index(HEAD)
    pieces = [
        jnp.sum(jnp.where(eye, lanes[p : p + 1, :], 0.0), axis=1, keepdims=True)
        for p in range(rows // HEAD)
    ]
    return jnp.concatenate(pieces, axis=0)


def split_extra(lanes):
    high = lanes.astype(BF16).astype(F32)
    both = jnp.concatenate([high, lanes - high], axis=0)
    return jnp.concatenate([both, jnp.zeros((EXTRA, HEAD), F32)], axis=1).astype(BF16)


def join_extra(block):
    block = block.astype(F32)
    return block[0:8, 0:HEAD] + block[8:16, 0:HEAD]


def my_place():
    mine = lax.axis_index("tp")
    return lax.div(mine, 2), lax.rem(mine, 2)


def weight_copies(wk_ref, wv_ref, weight_ref, sems):
    ring, core = my_place()
    copies = []
    for j in range(CHUNKS):
        chip = lax.rem(ring + j % RINGS, RINGS)
        begin = pl.multiple_of(HEAD * (2 * chip + (core if j < RINGS else 1 - core)), HEAD)
        copies.append(
            [
                pltpu.make_async_copy(
                    ref.at[:, pl.ds(begin, HEAD)],
                    weight_ref.at[:, pl.ds(j * PAIR + n * HEAD, HEAD)],
                    sems.at[2 * j + n],
                )
                for n, ref in enumerate((wk_ref, wv_ref))
            ]
        )
    return copies


def forward_other_kernel(loads, x_ref, gain_ref, *refs):
    if loads:
        wk_ref, wv_ref, send_ref, scaled_ref, lanes_ref, held_ref, weight_ref, sems, more = refs
    else:
        weight_ref, send_ref, scaled_ref, lanes_ref, held_ref, sems = refs
    rows = x_ref.shape[0]
    x_copies = []
    for p in range(rows // PIECE):
        here = pl.ds(p * PIECE, PIECE)
        x_copies.append(pltpu.make_async_copy(x_ref.at[here], held_ref.at[here], sems.at[p]))
        x_copies[-1].start()
    weights = weight_copies(wk_ref, wv_ref, weight_ref, more) if loads else []
    for pair in weights[RINGS:] + weights[:RINGS]:
        for copy in pair:
            copy.start()
    row = lax.broadcasted_iota(jnp.int32, (8, HEAD), 0)
    eye = same_index(HEAD)
    lanes = jnp.zeros((8, HEAD), F32)
    for p, copy in enumerate(x_copies):
        copy.wait()
        here = slice(p * PIECE, (p + 1) * PIECE)
        x = held_ref[here, :].astype(F32)
        scaled_ref[here, :] = (gain_ref[...] * x).astype(BF16)
        squares = jnp.sum(x * x, axis=1, keepdims=True)
        line = jnp.sum(jnp.where(eye, squares, 0.0), axis=0, keepdims=True)
        lanes = jnp.where(row == p, line, lanes)
    lanes_ref[...] = lanes
    extra = split_extra(lanes)
    for d in range(RINGS):
        if loads:
            for copy in weights[RINGS + d]:
                copy.wait()
        weight = weight_ref[:, (RINGS + d) * PAIR : (RINGS + d + 1) * PAIR]
        product = jnp.dot(scaled_ref[...], weight, preferred_element_type=F32)
        send_ref[d, 0:rows, :] = product.astype(BF16)
        send_ref[d, rows:, :] = extra
    if loads:
        for pair in weights[:RINGS]:
            for copy in pair:
                copy.wait()


def forward_other(x, gain, weights):
    rows, width = x.shape
    loads = len(weights) == 2
    out_shape = [
        pltpu.VMEM((RINGS, rows + EXTRA, PAIR), BF16),
        pltpu.VMEM(x.shape, BF16),
        pltpu.VMEM((8, HEAD), F32),
        pltpu.VMEM(x.shape, BF16),
    ]
    scratch = [pltpu.SemaphoreType.DMA((rows // PIECE,))]
    if loads:
        out_shape.append(pltpu.VMEM((width, CHUNKS * PAIR), BF16))
        scratch.append(pltpu.SemaphoreType.DMA((2 * CHUNKS,)))
    else:
        weights = [near(w) for w in weights]
    return pl.pallas_call(
        functools.partial(forward_other_kernel, loads),
        in_specs=[ANYWHERE, IN_VMEM] + [ANYWHERE if loads else IN_VMEM] * len(weights),
        out_specs=[IN_VMEM] * len(out_shape),
        out_shape=out_shape,
        scratch_shapes=scratch,
        compiler_params=PARAMS,
        cost_estimate=cost(2 * rows * width * RINGS * PAIR, 2**22 if loads else 2**20),
        name="forward_other",
    )(x, gain, *weights)


def forward_own_kernel(scaled_ref, lanes_ref, weight_ref, in_ref, *out_refs):
    rows = scaled_ref.shape[0]
    extra = split_extra(lanes_ref[...] + join_extra(in_ref[0, rows:, :]))
    for d, out_ref in enumerate(out_refs):
        weight = weight_ref[:, d * PAIR : (d + 1) * PAIR]
        product = jnp.dot(scaled_ref[...], weight, preferred_element_type=F32)
        out_ref[0:rows, :] = (product + in_ref[d, 0:rows, :].astype(F32)).astype(BF16)
        out_ref[rows:, :] = extra


def forward_own(scaled, lanes, weight, arrived):
    rows, width = scaled.shape
    return pl.pallas_call(
        forward_own_kernel,
        in_specs=[IN_VMEM] * 4,
        out_specs=[IN_VMEM] * RINGS,
        out_shape=[pltpu.VMEM((rows + EXTRA, PAIR), BF16)] * RINGS,
        compiler_params=PARAMS,
        cost_estimate=cost(2 * rows * width * RINGS * PAIR, 2**20),
        name="forward_own",
    )(near(scaled), near(lanes), near(weight), near(arrived))


def gathered(refs):
    rows = refs[0].shape[0] - EXTRA
    total = refs[0][0:rows, :].astype(F32)
    lanes = join_extra(refs[0][rows:, :])
    for ref in refs[1:]:
        total = total + ref[0:rows, :].astype(F32)
        lanes = lanes + join_extra(ref[rows:, :])
    inverse = lax.rsqrt(lanes_to_column(lanes, rows) / WIDTH + EPSILON)
    return (inverse * total).astype(BF16), inverse


def residual(both, target, resid_ref):
    rows = both.shape[0]
    both = both.astype(F32)
    resid = (both - target.astype(F32)).astype(BF16)
    dots = jnp.sum(resid.astype(F32) * both, axis=1, keepdims=True)
    resid_ref[0:rows, :] = resid
    resid_ref[rows:, :] = split_extra(column_to_lanes(dots))


def text_combine_kernel(a, b, c, d, target_ref, both_ref, resid_ref, inverse_ref):
    both, inverse = gathered((a, b, c, d))
    both_ref[...] = both
    inverse_ref[...] = jnp.broadcast_to(inverse, inverse_ref.shape)
    residual(both, target_ref[...], resid_ref)


def text_combine(parts, target):
    rows = target.shape[0]
    return pl.pallas_call(
        text_combine_kernel,
        in_specs=[IN_VMEM] * 5,
        out_specs=[IN_VMEM] * 3,
        out_shape=[
            pltpu.VMEM((rows, PAIR), BF16),
            pltpu.VMEM(parts[0].shape, BF16),
            pltpu.VMEM((rows, HEAD), F32),
        ],
        compiler_params=PARAMS,
        cost_estimate=cost(2**22, 2**22),
        name="text_combine",
    )(*[near(p) for p in parts], near(target))


def one_hot(match):
    return jnp.where(match, jnp.ones(match.shape, F32), jnp.zeros(match.shape, F32)).astype(BF16)


def slot_columns(rows, first, lanes):
    shape = (rows, lanes.shape[1])
    row = first + lax.broadcasted_iota(jnp.int32, shape, 0)
    begin = IMAGE_LEN * lax.broadcasted_iota(jnp.int32, shape, 1)
    inside = (row >= begin) & (row < begin + IMAGE_LEN)
    value = lanes + (row - begin).astype(F32)
    return jnp.sum(jnp.where(inside, value, 0.0), axis=1, keepdims=True)


def slot_lanes(rows, column):
    shape = (column.shape[0], rows)
    row = lax.broadcasted_iota(jnp.int32, shape, 1)
    begin = IMAGE_LEN * lax.broadcasted_iota(jnp.int32, shape, 0)
    inside = (row >= begin) & (row < begin + IMAGE_LEN)
    value = column + (row - begin).astype(F32)
    return jnp.sum(jnp.where(inside, value, 0.0), axis=0, keepdims=True)


def first_rows(starts_ref, rows):
    start = starts_ref[...].astype(F32)
    offset = start - (lax.axis_index("rows") * rows).astype(F32)
    inside = (offset >= 0.0) & (offset < rows)
    column = jnp.sum(jnp.where(inside, offset + ABSENT, 0.0), axis=1, keepdims=True) - ABSENT
    eye = same_index(column.shape[0])
    return column, jnp.sum(jnp.where(eye, column, 0.0), axis=0, keepdims=True)


def destinations(starts_ref, rows):
    start = starts_ref[...].astype(F32)
    block = jnp.floor((start + 0.5) / rows)
    source = lax.broadcasted_iota(jnp.int32, start.shape, 0)
    mine = source == lax.axis_index("rows")
    lanes = IMAGE_LEN * jnp.sum(jnp.where(mine, block, 0.0), axis=0, keepdims=True)
    eye = same_index(lanes.shape[1])
    return lanes, jnp.sum(jnp.where(eye, lanes, 0.0), axis=1, keepdims=True)


def image_keys_kernel(seq_rows, a, b, c, d, starts_ref, send_ref, both_ref, inverse_ref):
    both, inverse = gathered((a, b, c, d))
    both_ref[...] = both
    inverse_ref[...] = jnp.broadcast_to(inverse, inverse_ref.shape)
    _, dest = destinations(starts_ref, seq_rows)
    shape = (send_ref.shape[0], both.shape[0])
    slot = lax.broadcasted_iota(jnp.int32, shape, 0).astype(F32)
    picks = one_hot(slot == slot_lanes(both.shape[0], dest))
    send_ref[...] = jnp.dot(picks, both, preferred_element_type=F32).astype(BF16)


def image_keys(parts, starts, seq_rows):
    rows = parts[0].shape[0] - EXTRA
    return pl.pallas_call(
        functools.partial(image_keys_kernel, seq_rows),
        in_specs=[IN_VMEM] * 5,
        out_specs=[IN_VMEM] * 3,
        out_shape=[
            jax.ShapeDtypeStruct((starts.shape[0] * IMAGE_LEN, PAIR), BF16),
            pltpu.VMEM((rows, PAIR), BF16),
            pltpu.VMEM((rows, HEAD), F32),
        ],
        compiler_params=PARAMS,
        cost_estimate=cost(2**28, 2**20),
        name="image_keys",
    )(*[near(p) for p in parts], starts)


def image_residual_kernel(seq_rows, both_ref, arrived_ref, starts_ref, resid_ref):
    rows = both_ref.shape[0]
    dest, _ = destinations(starts_ref, seq_rows)
    shape = (rows, arrived_ref.shape[0])
    slot = lax.broadcasted_iota(jnp.int32, shape, 1).astype(F32)
    picks = one_hot(slot == slot_columns(rows, 0, dest))
    target = jnp.dot(picks, arrived_ref[...], preferred_element_type=F32)
    residual(both_ref[...], target, resid_ref)


def image_residual(both, arrived, starts, seq_rows):
    return pl.pallas_call(
        functools.partial(image_residual_kernel, seq_rows),
        in_specs=[IN_VMEM] * 3,
        out_specs=IN_VMEM,
        out_shape=pltpu.VMEM((both.shape[0] + EXTRA, PAIR), BF16),
        compiler_params=PARAMS,
        cost_estimate=cost(2**28, 2**20),
        name="image_residual",
    )(near(both), near(arrived), starts)


def gather_kernel(starts_ref, kt_ref, vt_ref, out_ref, target_ref):
    rows = kt_ref.shape[0]
    target_ref[:, 0:HEAD] = kt_ref[...]
    target_ref[:, HEAD:] = vt_ref[...]
    _, first = first_rows(starts_ref, rows)
    for begin in range(0, out_ref.shape[0], PAIR):
        place = slot_columns(PAIR, begin, first)
        position = lax.broadcasted_iota(jnp.int32, (PAIR, rows), 1).astype(F32)
        picked = jnp.dot(
            one_hot(position == place), target_ref[...], preferred_element_type=F32
        )
        out_ref[begin : begin + PAIR, :] = picked.astype(BF16)


def gather_targets(starts, key_target, value_target):
    rows = key_target.shape[0]
    return pl.pallas_call(
        gather_kernel,
        in_specs=[IN_VMEM] * 3,
        out_specs=[IN_VMEM] * 2,
        out_shape=[
            jax.ShapeDtypeStruct((starts.shape[0] * IMAGE_LEN, PAIR), BF16),
            pltpu.VMEM((rows, PAIR), BF16),
        ],
        compiler_params=PARAMS,
        cost_estimate=cost(2**28, 2**20),
        name="gather_targets",
    )(starts, key_target, value_target)


def image_rows_mask(rows, first_row, first_lanes):
    shape = (rows, first_lanes.shape[1])
    row = (first_row + lax.broadcasted_iota(jnp.int32, shape, 0)).astype(F32)
    inside = (row >= first_lanes) & (row < first_lanes + IMAGE_LEN)
    return jnp.sum(jnp.where(inside, 1.0, 0.0), axis=1, keepdims=True) > 0.5


def merge_kernel(starts_ref, arrived_ref, both_ref, keys_ref, values_ref):
    slots, rows = arrived_ref.shape[0], both_ref.shape[0]
    column, lanes = first_rows(starts_ref, rows)
    place = slot_lanes(slots, column)
    for begin in range(0, rows, PAIR):
        row = begin + lax.broadcasted_iota(jnp.int32, (PAIR, slots), 0)
        picks = one_hot(row.astype(F32) == place)
        landed = jnp.dot(picks, arrived_ref[...], preferred_element_type=F32)
        here = slice(begin, begin + PAIR)
        mask = image_rows_mask(PAIR, begin, lanes)
        both = jnp.where(mask, landed, both_ref[here, :].astype(F32)).astype(BF16)
        keys_ref[here, :] = both[:, 0:HEAD]
        values_ref[here, :] = both[:, HEAD:]


def merge(starts, arrived, both):
    rows = both.shape[0]
    return pl.pallas_call(
        merge_kernel,
        in_specs=[IN_VMEM] * 3,
        out_specs=[IN_VMEM] * 2,
        out_shape=[jax.ShapeDtypeStruct((rows, HEAD), BF16)] * 2,
        compiler_params=PARAMS,
        cost_estimate=cost(2**28, 2**20),
        name="merge",
    )(starts, near(arrived), near(both))


def backward_kernel(masked, tile, x_ref, gain_ref, inverse_ref, weight_ref, *rest):
    rest = list(rest)
    starts_ref = rest.pop(0) if masked else None
    resids = rest[0:CHUNKS]
    out_ref, stacked, held, sems = rest[CHUNKS:]
    rows, width = x_ref.shape
    lanes = jnp.zeros((8, HEAD), F32)
    for n, ref in enumerate(resids):
        chunk = (RINGS - n) % RINGS + RINGS * (n // RINGS)
        stacked[:, chunk * PAIR : (chunk + 1) * PAIR] = ref[0:rows, :]
        lanes = lanes + join_extra(ref[rows:, :])
    inverse = inverse_ref[:, 0:1]
    coefficient = inverse * inverse * lanes_to_column(lanes, rows) / WIDTH
    if masked:
        mask = image_rows_mask(rows, 0, first_rows(starts_ref, rows)[1])
    contract = (((1,), (1,)), ((), ()))
    copies = []
    for n in range(width // tile):
        here = slice(n * tile, (n + 1) * tile)
        back = lax.dot_general(
            stacked[...], weight_ref[here, :], contract, preferred_element_type=F32
        )
        grad = gain_ref[:, here] * inverse * back - coefficient * x_ref[:, here].astype(F32)
        if masked:
            grad = jnp.where(mask, 0.0, grad)
        held[:, here] = grad.astype(BF16)
        span = pl.ds(n * tile, tile)
        copies.append(pltpu.make_async_copy(held.at[:, span], out_ref.at[:, span], sems.at[n]))
        copies[-1].start()
    for copy in copies:
        copy.wait()


def backward(x, gain, inverse, weight, starts, resids):
    rows, width = x.shape
    tile = 256
    masked = starts is not None
    operands = [near(x), gain, near(inverse), near(weight)] + ([starts] if masked else [])
    operands += [near(r) for r in resids]
    return pl.pallas_call(
        functools.partial(backward_kernel, masked, tile),
        in_specs=[IN_VMEM] * len(operands),
        out_specs=ANYWHERE,
        out_shape=jax.ShapeDtypeStruct(x.shape, BF16),
        scratch_shapes=[
            pltpu.VMEM((rows, CHUNKS * PAIR), BF16),
            pltpu.VMEM((rows, width), BF16),
            pltpu.SemaphoreType.DMA((width // tile,)),
        ],
        compiler_params=PARAMS,
        cost_estimate=cost(2 * rows * width * CHUNKS * PAIR, 2**21),
        name="backward",
    )(*operands)


def around(x, shift):
    return lax.ppermute(
        x, "tp", [(2 * y + c, 2 * ((y + shift) % RINGS) + c) for y in range(RINGS) for c in range(2)]
    )


def across(x):
    return lax.ppermute(x, "tp", [(i, i ^ 1) for i in range(2 * RINGS)])


def everyone(x):
    own = [x] + [around(x, d) for d in range(1, RINGS)]
    return own + [across(r) for r in own]


def route(x):
    return lax.all_to_all(x, "rows", split_axis=0, concat_axis=0, tiled=True)


def on_device(
    text_embed,
    image_embed,
    image_start,
    norm_gain,
    key_weight,
    value_weight,
    key_target,
    value_target,
):
    shards = lax.axis_size("rows")
    seq_rows = text_embed.shape[0]
    gain = norm_gain[None, :]
    starts = image_start.reshape(shards, -1)

    sent, scaled, lanes, text_held, weight = forward_other(
        text_embed, gain, (key_weight, value_weight)
    )
    arrived = across(sent)
    image_sent, image_scaled, image_lanes, image_held = forward_other(
        image_embed, gain, (weight,)
    )
    image_arrived = across(image_sent)
    goals, target = gather_targets(starts, key_target, value_target)
    own = forward_own(scaled, lanes, weight, arrived)
    parts = [own[0]] + [around(own[d], d) for d in range(1, RINGS)]
    own = forward_own(image_scaled, image_lanes, weight, image_arrived)
    image_parts = [own[0]] + [around(own[d], d) for d in range(1, RINGS)]
    goals, image_parts[0] = lax.optimization_barrier((goals, image_parts[0]))
    goals = route(goals)

    both, resid, inverse = text_combine(parts, target)
    resids = everyone(resid)
    image_send, image_both, image_inverse = image_keys(image_parts, starts, seq_rows)
    landed = route(image_send)
    image_resids = everyone(image_residual(image_both, goals, starts, seq_rows))

    text_grad = backward(text_held, gain, inverse, weight, starts, resids)
    image_grad = backward(image_held, gain, image_inverse, weight, None, image_resids)
    keys, values = merge(starts, landed, both)
    return (keys, values, text_grad, image_grad)


def solution(mesh):
    in_specs = (
        P("rows", "tp"),
        P("rows", "tp"),
        P(),
        P("tp"),
        P("tp", None),
        P("tp", None),
        P("rows", "tp"),
        P("rows", "tp"),
    )
    out_specs = (P("rows", "tp"), P("rows", "tp"), P("rows", "tp"), P("rows", "tp"))
    return jax.shard_map(
        on_device, mesh=mesh, in_specs=in_specs, out_specs=out_specs, check_vma=False
    )
```

time: 354 us -> 130 us (0.37)
  waiting for transfers between devices: 244 us -> 23.3 us
  Pallas kernels: 0 us -> 30.9 us
  starting transfers between devices: 21.8 us -> 44.3 us
  matrix products: 16.1 us -> 0 us
  blocking collectives: 15.5 us -> 0 us
  between operations: 14.3 us -> 1.03 us
  other arithmetic: 11.2 us -> 0 us
    all_gather x4 -> x0, waiting for transfers between devices: 117 us -> none  [the longest x1 31 us: on_device(): lax.all_gather(value_resid, 'tp', axis=1, tiled=True)]
    all_to_all x2, waiting for transfers between devices: 72.9 us -> 0.01 us  [route(): return lax.all_to_all(x, 'rows', split_axis=0, concat_axis=0, tiled=True)]
    reduce_scatter x2 -> x0, waiting for transfers between devices: 52.6 us -> none  [the longest x1 39.8 us: on_device(): lax.psum_scatter(key_part, 'tp', scatter_dimension=1, tiled=True)]
    pallas_call x0 -> x11, Pallas kernels: none -> 30.9 us  [the longest x2 10 us: forward_other(): pl.pallas_call(functools.partial(forward_other_kernel, loads), in_specs=[...]
    unnamed x21 -> x68, local copies, waits for them, and re-layouts: 2.92 us -> 29.3 us
    ppermute x0 -> x22, starting transfers between devices: none -> 25.7 us  [the longest x12 15.2 us: around(): lax.ppermute(x, 'tp', [(2 * y + c, 2 * ((y + shift) % RINGS) + c) for y i...]
    ppermute x0 -> x22, waiting for transfers between devices: none -> 23.3 us  [the longest x12 21.2 us: around(): lax.ppermute(x, 'tp', [(2 * y + c, 2 * ((y + shift) % RINGS) + c) for y i...]
    dot_general x4 -> x0, matrix products: 16.1 us -> none  [the longest x1 5.53 us: on_device(): key_part = jnp.dot(scaled, key_weight, preferred_element_type=jnp.float32)]
  transfers between devices with their start and end apart: 8 -> 24, of which waited for: 8 -> 6; matrix products, arithmetic and copies ran while one was open for 3% -> 0% of each run, Pallas kernels for 0% -> 13%
where the time goes in v3:
time: 130 us; the launch traced here: 129 us
  starting transfers between devices  44.3 us (34%)
  Pallas kernels  30.9 us (24%)
  local copies, waits for them, and re-layouts  29.4 us (23%)
  waiting for transfers between devices  23.3 us (18%)
    unnamed x68, local copies, waits for them, and re-layouts  29.3 us
    ppermute x12, waiting for transfers between devices, around(): lax.ppermute(x, 'tp', [(2 * y + c, 2 * ((y + shift) % RINGS) + c) for y i...  21.2 us
    all_to_all x2, starting transfers between devices, route(): return lax.all_to_all(x, 'rows', split_axis=0, concat_axis=0, tiled=True)  18.6 us
    ppermute x12, starting transfers between devices, around(): lax.ppermute(x, 'tp', [(2 * y + c, 2 * ((y + shift) % RINGS) + c) for y i...  15.2 us
    ppermute x10, starting transfers between devices, across(): return lax.ppermute(x, 'tp', [(i, i ^ 1) for i in range(2 * RINGS)])  10.5 us
    pallas_call x2, Pallas kernels, forward_other(): pl.pallas_call(functools.partial(forward_other_kernel, loads), in_specs=[...  10 us
    pallas_call x2, Pallas kernels, backward(): pl.pallas_call(functools.partial(backward_kernel, masked, tile), in_specs...  9.76 us
    pallas_call x2, Pallas kernels, forward_own(): pl.pallas_call(forward_own_kernel, in_specs=[IN_VMEM] * 4, out_specs=[IN_...  4.88 us
  transfers between devices with their start and end apart: 24, of which 6 were waited for; matrix products, arithmetic and copies ran while one was open for 0% of the time, Pallas kernels for 13%

profile of v3, /device:TPU:1, one launch (start us, length us, event | category | flops | bytes accessed | tf_op | source)
XLA Modules:
  0.0 129.0 jit_solution(1506659077775692972)
XLA Ops:
  0.6 0.7 copy-done.17
  1.3 1.6 %copy-done.19 = bf16[1024,1024]{1,0:T(8,128)(2,1)S(1)} copy-done((bf16[1024,1024]{1,0:T(8,128)(2,1)S(1)}, bf16[1024,1024]{1,0:T(8,128)(2,1)}, u32[]{:S(2)}) %copy-start.19) | copy-done | bytes 2097176
  2.9 1.6 %copy-done.20 = bf16[1024,1024]{1,0:T(8,128)(2,1)S(1)} copy-done((bf16[1024,1024]{1,0:T(8,128)(2,1)S(1)}, bf16[1024,1024]{1,0:T(8,128)(2,1)}, u32[]{:S(2)}) %copy-start.20) | copy-done | bytes 2097176
  4.5 1.4 %copy-done.21 = bf16[768,1024]{1,0:T(8,128)(2,1)S(1)} copy-done((bf16[768,1024]{1,0:T(8,128)(2,1)S(1)}, bf16[768,1024]{1,0:T(8,128)(2,1)}, u32[]{:S(2)}) %copy-start.21) | copy-done | bytes 1572888
  5.9 7.7 %forward_other.2 = (bf16[4,784,256]{2,1,0:T(8,128)(2,1)}, bf16[768,1024]{1,0:T(8,128)(2,1)S(1)}, f32[8,128]{1,0:T(8,128)S(1)}, bf16[768,1024]{1,0:T(8,128)(2,1)S(1)}, bf16[1024,2048]{1,0:T(8,128)(2,1)S(1)}) custom-call(bf16[768,1024]{1,0:T(8,128)(2,1)S(1)} %copy-done.21, f32[1,1024]{1,0:T(1,128)S(1)} %bitcast.7, bf16[1024,1024]{1,0:T(8,128)(2,1)S(1)} %copy-done.19, ...), custom_call_target="tpu_custom_call" | custom-call | flops 1610612736 | bytes 4194304 | tf_op jit(solution)/shard_map/forward_other/pallas_call | solution.py:153
  13.7 1.1 copy-done.31
  14.8 3.2 %collective-permute-start.4 = (bf16[4,784,256]{2,1,0:T(8,128)(2,1)}, bf16[4,784,256]{2,1,0:T(8,128)(2,1)S(1)}, u32[]{:S(2)}, u32[]{:S(2)}) collective-permute-start(bf16[4,784,256]{2,1,0:T(8,128)(2,1)} %get-tuple-element.46), channel_id=1, source_target_pairs={{0,1},{1,0},{2,3},{3,2},{4,5},{5,4},{6,7},{7,6},{8,9},{9,8},{10,11... | collective-permute-start | bytes 4816904 | tf_op jit(solution)/shard_map/ppermute | solution.py:450
  18.1 2.3 %forward_other.3 = (bf16[4,400,256]{2,1,0:T(8,128)(2,1)}, bf16[384,1024]{1,0:T(8,128)(2,1)S(1)}, f32[8,128]{1,0:T(8,128)S(1)}, bf16[384,1024]{1,0:T(8,128)(2,1)S(1)}) custom-call(bf16[384,1024]{1,0:T(8,128)(2,1)S(1)} %copy-done.9, f32[1,1024]{1,0:T(1,128)S(1)} %bitcast.8, bf16[1024,2048]{1,0:T(8,128)(2,1)S(1)} %get-tuple-element.34.refs_0_.weight_ref), custom_call_target="tpu_custom_call" | custom-call | flops 805306368 | bytes 1048576 | tf_op jit(solution)/shard_map/forward_other/pallas_call | solution.py:153
  20.4 0.9 copy-done.5
  21.3 0.9 copy-done.7
  22.2 0.1 reshape.15.starts_ref.rest_0_
  22.3 0.9 copy-done.30
  23.2 0.7 gather_targets.1
  23.9 0.8 copy-done.12
  24.7 0.8 copy-done.13
  25.5 2.2 %copy-done.1 = bf16[1024,2048]{1,0:T(8,128)(2,1)S(1)} copy-done((bf16[1024,2048]{1,0:T(8,128)(2,1)S(1)}, bf16[1024,2048]{1,0:T(8,128)(2,1)}, u32[]{:S(2)}) %copy-start.1) | copy-done | bytes 4194328
  27.6 1.1 copy-done.8
  28.8 2.1 %forward_own.2 = (bf16[400,256]{1,0:T(8,128)(2,1)S(1)}, bf16[400,256]{1,0:T(8,128)(2,1)S(1)}, bf16[400,256]{1,0:T(8,128)(2,1)S(1)}, bf16[400,256]{1,0:T(8,128)(2,1)S(1)}) custom-call(bf16[384,1024]{1,0:T(8,128)(2,1)S(1)} %copy-done.8, f32[8,128]{1,0:T(8,128)S(1)} %get-tuple-element.36.lanes_ref, bf16[1024,2048]{1,0:T(8,128)(2,1)S(1)} %copy-done.1, ...), custom_call_target="tpu_custom_call" | custom-call | flops 805306368 | bytes 1048576 | tf_op jit(solution)/shard_map/forward_own/pallas_call | solution.py:177
  30.9 0.7 copy-done.26
  31.6 0.7 copy-done.27
  32.3 9.4 %all-to-all-start.1 = ((bf16[32,24,256]{2,1,0:T(8,128)(2,1)}), bf16[32,24,256]{2,1,0:T(8,128)(2,1)}, u32[]{:S(2)}, u32[]{:S(2)}) async-start(bf16[32,24,256]{2,1,0:T(8,128)(2,1)} %bitcast.6), calls=%async_computation.1 | async-start | bytes 786432 | tf_op jit(solution)/shard_map/all_to_all | solution.py:459
  41.8 1.1 collective-permute-start.1
  42.9 2.6 %collective-permute-start.2 = (bf16[400,256]{1,0:T(8,128)(2,1)}, bf16[400,256]{1,0:T(8,128)(2,1)S(1)}, u32[]{:S(2)}, u32[]{:S(2)}) collective-permute-start(bf16[400,256]{1,0:T(8,128)(2,1)} %copy-done.27), channel_id=1, source_target_pairs={{0,4},{1,5},{2,6},{3,7},{4,0},{5,1},{6,2},{7,3},{8,12},{9,13},{10,... | collective-permute-start | bytes 614408 | tf_op jit(solution)/shard_map/ppermute | solution.py:444
  45.5 1.1 collective-permute-start.3
  46.6 2.2 %copy-done.2 = bf16[1024,2048]{1,0:T(8,128)(2,1)S(1)} copy-done((bf16[1024,2048]{1,0:T(8,128)(2,1)S(1)}, bf16[1024,2048]{1,0:T(8,128)(2,1)}, u32[]{:S(2)}) %copy-start.2) | copy-done | bytes 4194328
  48.8 2.8 %forward_own.3 = (bf16[784,256]{1,0:T(8,128)(2,1)S(1)}, bf16[784,256]{1,0:T(8,128)(2,1)}, bf16[784,256]{1,0:T(8,128)(2,1)}, bf16[784,256]{1,0:T(8,128)(2,1)}) custom-call(bf16[768,1024]{1,0:T(8,128)(2,1)S(1)} %get-tuple-element.44.scaled_ref, f32[8,128]{1,0:T(8,128)S(1)} %get-tuple-element.45.lanes_ref, bf16[1024,2048]{1,0:T(8,128)(2,1)S(1)} %copy-done.2, ...), custom_call_target="tpu_custom_call" | custom-call | flops 1610612736 | bytes 1048576 | tf_op jit(solution)/shard_map/forward_own/pallas_call | solution.py:177
  51.5 0.8 copy-done.10
  52.3 0.4 collective-permute-start.5
  52.7 0.8 collective-permute-start.6
  53.5 1.7 %collective-permute-start.7 = (bf16[784,256]{1,0:T(8,128)(2,1)}, bf16[784,256]{1,0:T(8,128)(2,1)S(1)}, u32[]{:S(2)}, u32[]{:S(2)}) collective-permute-start(bf16[784,256]{1,0:T(8,128)(2,1)} %get-tuple-element.50), channel_id=1, source_target_pairs={{0,6},{1,7},{2,0},{3,1},{4,2},{5,3},{6,4},{7,5},{8,14},{9,15},{10,... | collective-permute-start | bytes 1204232 | tf_op jit(solution)/shard_map/ppermute | solution.py:444
  55.2 1.3 %image_keys.1 = (bf16[768,256]{1,0:T(8,128)(2,1)}, bf16[384,256]{1,0:T(8,128)(2,1)S(1)}, f32[384,128]{1,0:T(8,128)S(1)}) custom-call(bf16[400,256]{1,0:T(8,128)(2,1)S(1)} %get-tuple-element.39.a, bf16[400,256]{1,0:T(8,128)(2,1)S(1)} %collective-permute-done.1.b, bf16[400,256]{1,0:T(8,128)(2,1)S(1)} %collective-permute-done.2.c, ...), custom_call_target="tpu_custom_call" | custom-call | flops 268435456 | bytes 1048576 | tf_op jit(solution)/shard_map/image_keys/pallas_call | solution.py:286
  56.6 0.7 copy-done.15
  57.2 1.5 %image_residual.1.rest_0_ = bf16[400,256]{1,0:T(8,128)(2,1)S(1)} custom-call(bf16[384,256]{1,0:T(8,128)(2,1)S(1)} %get-tuple-element.60.both_ref, bf16[768,256]{1,0:T(8,128)(2,1)} %bitcast.4.arrived_ref, s32[32,16]{1,0:T(8,128)S(1)} %reshape.15.starts_ref.rest_0_), custom_call_target="tpu_custom_call" | custom-call | flops 268435456 | bytes 1048576 | tf_op jit(solution)/shard_map/image_residual/pallas_call | solution.py:312
  58.7 2.3 %collective-permute-start.18 = (bf16[400,256]{1,0:T(8,128)(2,1)S(1)}, bf16[400,256]{1,0:T(8,128)(2,1)S(1)}, u32[]{:S(2)}, u32[]{:S(2)}) collective-permute-start(bf16[400,256]{1,0:T(8,128)(2,1)S(1)} %image_residual.1.rest_0_), channel_id=1, source_target_pairs={{0,1},{1,0},{2,3},{3,2},{4,5},{5,4},{6,7},{7,6},{8,9},{9,8},{10,11... | collective-permute-start | bytes 614408 | tf_op jit(solution)/shard_map/ppermute | solution.py:450
  61.0 1.1 collective-permute-start.17
  62.1 0.9 collective-permute-done.5.b
  63.0 0.5 collective-permute-start.16
  63.5 8.5 %collective-permute-done.6.c = bf16[784,256]{1,0:T(8,128)(2,1)S(1)} collective-permute-done((bf16[784,256]{1,0:T(8,128)(2,1)}, bf16[784,256]{1,0:T(8,128)(2,1)S(1)}, u32[]{:S(2)}, u32[]{:S(2)}) %collective-permute-start.6) | collective-permute-done | bytes 401440 | tf_op jit(solution)/shard_map/ppermute | solution.py:444
  72.0 1.1 collective-permute-done.7.d
  73.0 1.4 %text_combine.1 = (bf16[768,256]{1,0:T(8,128)(2,1)S(1)}, bf16[784,256]{1,0:T(8,128)(2,1)}, f32[768,128]{1,0:T(8,128)S(1)}) custom-call(bf16[784,256]{1,0:T(8,128)(2,1)S(1)} %copy-done.11, bf16[784,256]{1,0:T(8,128)(2,1)S(1)} %collective-permute-done.5.b, bf16[784,256]{1,0:T(8,128)(2,1)S(1)} %collective-permute-done.6.c, ...), custom_call_target="tpu_custom_call" | custom-call | flops 4194304 | bytes 4194304 | tf_op jit(solution)/shard_map/text_combine/pallas_call | solution.py:217
  74.5 0.7 copy-done.22
  75.2 0.8 copy-done.24
  76.0 3.3 %collective-permute-start.10 = (bf16[784,256]{1,0:T(8,128)(2,1)}, bf16[784,256]{1,0:T(8,128)(2,1)S(1)}, u32[]{:S(2)}, u32[]{:S(2)}) collective-permute-start(bf16[784,256]{1,0:T(8,128)(2,1)} %get-tuple-element.57.rest_1_), channel_id=1, source_target_pairs={{0,6},{1,7},{2,0},{3,1},{4,2},{5,3},{6,4},{7,5},{8,14},{9,15},{10,... | collective-permute-start | bytes 1204232 | tf_op jit(solution)/shard_map/ppermute | solution.py:444
  79.3 0.6 collective-permute-start.8
  79.9 2.1 %collective-permute-start.15 = (bf16[400,256]{1,0:T(8,128)(2,1)S(1)}, bf16[400,256]{1,0:T(8,128)(2,1)S(1)}, u32[]{:S(2)}, u32[]{:S(2)}) collective-permute-start(bf16[400,256]{1,0:T(8,128)(2,1)S(1)} %image_residual.1.rest_0_), channel_id=1, source_target_pairs={{0,2},{1,3},{2,4},{3,5},{4,6},{5,7},{6,0},{7,1},{8,10},{9,11},{10,... | collective-permute-start | bytes 614408 | tf_op jit(solution)/shard_map/ppermute | solution.py:444
  82.0 9.2 %all-to-all-start = ((bf16[32,24,256]{2,1,0:T(8,128)(2,1)}), bf16[32,24,256]{2,1,0:T(8,128)(2,1)S(1)}, u32[]{:S(2)}, u32[]{:S(2)}) async-start(bf16[32,24,256]{2,1,0:T(8,128)(2,1)} %bitcast.1), calls=%async_computation | async-start | bytes 786432 | tf_op jit(solution)/shard_map/all_to_all | solution.py:459
  91.2 2.7 %collective-permute-start.21 = (bf16[400,256]{1,0:T(8,128)(2,1)S(1)}, bf16[400,256]{1,0:T(8,128)(2,1)S(1)}, u32[]{:S(2)}, u32[]{:S(2)}) collective-permute-start(bf16[400,256]{1,0:T(8,128)(2,1)S(1)} %collective-permute-done.17.rest_3_), channel_id=1, source_target_pairs={{0,1},{1,0},{2,3},{3,2},{4,5},{5,4},{6,7},{7,6},{8,9},{9,8},{10,11... | collective-permute-start | bytes 614408 | tf_op jit(solution)/shard_map/ppermute | solution.py:450
  93.9 10.7 %collective-permute-done.15.rest_1_ = bf16[400,256]{1,0:T(8,128)(2,1)S(1)} collective-permute-done((bf16[400,256]{1,0:T(8,128)(2,1)S(1)}, bf16[400,256]{1,0:T(8,128)(2,1)S(1)}, u32[]{:S(2)}, u32[]{:S(2)}) %collective-permute-start.15) | collective-permute-done | bytes 204832 | tf_op jit(solution)/shard_map/ppermute | solution.py:444
  104.6 0.8 collective-permute-start.20
  105.5 0.5 collective-permute-start.14
  106.0 0.1 collective-permute-start.13
  106.1 0.4 collective-permute-start.12
  106.5 0.5 collective-permute-done.20.rest_6_
  107.0 0.4 collective-permute-start.19
  107.3 1.6 %collective-permute-done.19.rest_5_ = bf16[400,256]{1,0:T(8,128)(2,1)S(1)} collective-permute-done((bf16[400,256]{1,0:T(8,128)(2,1)S(1)}, bf16[400,256]{1,0:T(8,128)(2,1)S(1)}, u32[]{:S(2)}, u32[]{:S(2)}) %collective-permute-start.19) | collective-permute-done | bytes 204832 | tf_op jit(solution)/shard_map/ppermute | solution.py:450
  108.9 2.2 %copy-done.3 = bf16[1024,2048]{1,0:T(8,128)(2,1)S(1)} copy-done((bf16[1024,2048]{1,0:T(8,128)(2,1)S(1)}, bf16[1024,2048]{1,0:T(8,128)(2,1)}, u32[]{:S(2)}) %copy-start.3) | copy-done | bytes 4194328
  111.1 0.9 copy-done.16
  112.1 3.7 %backward.3 = bf16[384,1024]{1,0:T(8,128)(2,1)} custom-call(bf16[384,1024]{1,0:T(8,128)(2,1)S(1)} %copy-done.6, f32[1,1024]{1,0:T(1,128)S(1)} %bitcast.9, f32[384,128]{1,0:T(8,128)S(1)} %copy-done.16, bf16[1024,2048]{1,0:T(8,128)(2,1)S(1)} %copy-done.3, bf16[400,256]{1,0:T(8,128)(2,1)S(1)} %image_residual.1.rest_0_, ...), custom_call_target="tpu_custom_call" | custom-call | flops 1610612736 | bytes 2097152 | tf_op jit(solution)/shard_map/backward/pallas_call | solution.py:427
  115.8 1.0 copy-done.25
  116.8 1.3 %merge.1 = (bf16[768,128]{1,0:T(8,128)(2,1)}, bf16[768,128]{1,0:T(8,128)(2,1)}) custom-call(s32[32,16]{1,0:T(8,128)S(1)} %reshape.15.starts_ref.rest_0_, bf16[768,256]{1,0:T(8,128)(2,1)S(1)} %bitcast.5, bf16[768,256]{1,0:T(8,128)(2,1)S(1)} %copy-done.25), custom_call_target="tpu_custom_call" | custom-call | flops 268435456 | bytes 1048576 | tf_op jit(solution)/shard_map/merge/pallas_call | solution.py:377
  118.1 2.2 %copy-done.4 = bf16[1024,2048]{1,0:T(8,128)(2,1)S(1)} copy-done((bf16[1024,2048]{1,0:T(8,128)(2,1)S(1)}, bf16[1024,2048]{1,0:T(8,128)(2,1)}, u32[]{:S(2)}) %copy-start.4) | copy-done | bytes 4194328
  120.3 1.0 copy-done.23
  121.3 1.4 %copy-done.32 = bf16[768,1024]{1,0:T(8,128)(2,1)S(1)} copy-done((bf16[768,1024]{1,0:T(8,128)(2,1)S(1)}, bf16[768,1024]{1,0:T(8,128)(2,1)}, u32[]{:S(2)}) %copy-start.32) | copy-done | bytes 1572888
  122.7 6.1 %backward.2 = bf16[768,1024]{1,0:T(8,128)(2,1)} custom-call(bf16[768,1024]{1,0:T(8,128)(2,1)S(1)} %copy-done.32, f32[1,1024]{1,0:T(1,128)S(1)} %bitcast.10, f32[768,128]{1,0:T(8,128)S(1)} %copy-done.23, bf16[1024,2048]{1,0:T(8,128)(2,1)S(1)} %copy-done.4, s32[32,16]{1,0:T(8,128)S(1)} %reshape.15.starts_ref.rest_0_, ...), custom_call_target="tpu_custom_call" | custom-call | flops 3221225472 | bytes 2097152 | tf_op jit(solution)/shard_map/backward/pallas_call | solution.py:427
  (64 shorter events, 0.2 us)
Async XLA Ops:
  0.6 0.7 copy-start.17
  1.3 1.6 %copy-start.19 = (bf16[1024,1024]{1,0:T(8,128)(2,1)S(1)}, bf16[1024,1024]{1,0:T(8,128)(2,1)}, u32[]{:S(2)}) copy-start(bf16[1024,1024]{1,0:T(8,128)(2,1)} %refs_0_.1) | copy-start | bytes 6291460
  2.9 1.6 %copy-start.20 = (bf16[1024,1024]{1,0:T(8,128)(2,1)S(1)}, bf16[1024,1024]{1,0:T(8,128)(2,1)}, u32[]{:S(2)}) copy-start(bf16[1024,1024]{1,0:T(8,128)(2,1)} %refs_1_.1) | copy-start | bytes 6291460
  4.5 1.4 %copy-start.21 = (bf16[768,1024]{1,0:T(8,128)(2,1)S(1)}, bf16[768,1024]{1,0:T(8,128)(2,1)}, u32[]{:S(2)}) copy-start(bf16[768,1024]{1,0:T(8,128)(2,1)} %x_ref.2) | copy-start | bytes 4718596
  5.9 12.1 %copy-start.9 = (bf16[384,1024]{1,0:T(8,128)(2,1)S(1)}, bf16[384,1024]{1,0:T(8,128)(2,1)}, u32[]{:S(2)}) copy-start(bf16[384,1024]{1,0:T(8,128)(2,1)} %x_ref.3) | copy-start | bytes 2359300
  13.7 1.1 copy-start.31
  14.8 5.5 %copy-start = (bf16[1024,2048]{1,0:T(8,128)(2,1)}, bf16[1024,2048]{1,0:T(8,128)(2,1)S(1)}, u32[]{:S(2)}) copy-start(bf16[1024,2048]{1,0:T(8,128)(2,1)S(1)} %get-tuple-element.34.refs_0_.weight_ref) | copy-start | bytes 12582916
  14.8 31.8 %collective-permute-start.4 = (bf16[4,784,256]{2,1,0:T(8,128)(2,1)}, bf16[4,784,256]{2,1,0:T(8,128)(2,1)S(1)}, u32[]{:S(2)}, u32[]{:S(2)}) collective-permute-start(bf16[4,784,256]{2,1,0:T(8,128)(2,1)} %get-tuple-element.46), channel_id=1, source_target_pairs={{0,1},{1,0},{2,3},{3,2},{4,5},{5,4},{6,7},{7,6},{8,9},{9,8},{10,11... | collective-permute-start | bytes 4816904 | tf_op jit(solution)/shard_map/ppermute | solution.py:450
  18.1 4.2 %copy-start.33 = (s32[512]{0:T(512)S(1)}, s32[512]{0:T(512)}, u32[]{:S(2)}) copy-start(s32[512]{0:T(512)} %param.10) | copy-start | bytes 6148
  18.1 4.2 %copy-start.29 = (bf16[768,128]{1,0:T(8,128)(2,1)S(1)}, bf16[768,128]{1,0:T(8,128)(2,1)}, u32[]{:S(2)}) copy-start(bf16[768,128]{1,0:T(8,128)(2,1)} %kt_ref.1) | copy-start | bytes 589828
  20.4 0.9 copy-start.5
  21.3 0.9 copy-start.7
  22.2 3.3 %collective-permute-start = (bf16[4,400,256]{2,1,0:T(8,128)(2,1)}, bf16[4,400,256]{2,1,0:T(8,128)(2,1)}, u32[]{:S(2)}, u32[]{:S(2)}) collective-permute-start(bf16[4,400,256]{2,1,0:T(8,128)(2,1)} %get-tuple-element.37), channel_id=1, source_target_pairs={{0,1},{1,0},{2,3},{3,2},{4,5},{5,4},{6,7},{7,6},{8,9},{9,8},{10,11... | collective-permute-start | bytes 2457608 | tf_op jit(solution)/shard_map/ppermute | solution.py:450
  22.3 0.9 copy-start.30
  23.9 0.8 copy-start.12
  24.7 0.8 copy-start.13
  25.5 2.2 %copy-start.1 = (bf16[1024,2048]{1,0:T(8,128)(2,1)S(1)}, bf16[1024,2048]{1,0:T(8,128)(2,1)}, u32[]{:S(2)}) copy-start(bf16[1024,2048]{1,0:T(8,128)(2,1)} %copy-done) | copy-start | bytes 12582916
  27.6 1.1 copy-start.8
  30.9 0.7 copy-start.26
  31.6 0.7 copy-start.27
  31.6 0.7 copy-start.28
  32.3 24.9 %all-to-all-start.1 = ((bf16[32,24,256]{2,1,0:T(8,128)(2,1)}), bf16[32,24,256]{2,1,0:T(8,128)(2,1)}, u32[]{:S(2)}, u32[]{:S(2)}) async-start(bf16[32,24,256]{2,1,0:T(8,128)(2,1)} %bitcast.6), calls=%async_computation.1 | async-start | bytes 786432 | tf_op jit(solution)/shard_map/all_to_all | solution.py:459
  41.8 11.8 %collective-permute-start.1 = (bf16[400,256]{1,0:T(8,128)(2,1)}, bf16[400,256]{1,0:T(8,128)(2,1)S(1)}, u32[]{:S(2)}, u32[]{:S(2)}) collective-permute-start(bf16[400,256]{1,0:T(8,128)(2,1)} %copy-done.28), channel_id=1, source_target_pairs={{0,2},{1,3},{2,4},{3,5},{4,6},{5,7},{6,0},{7,1},{8,10},{9,11},{10,... | collective-permute-start | bytes 614408 | tf_op jit(solution)/shard_map/ppermute | solution.py:444
  42.9 12.3 %collective-permute-start.2 = (bf16[400,256]{1,0:T(8,128)(2,1)}, bf16[400,256]{1,0:T(8,128)(2,1)S(1)}, u32[]{:S(2)}, u32[]{:S(2)}) collective-permute-start(bf16[400,256]{1,0:T(8,128)(2,1)} %copy-done.27), channel_id=1, source_target_pairs={{0,4},{1,5},{2,6},{3,7},{4,0},{5,1},{6,2},{7,3},{8,12},{9,13},{10,... | collective-permute-start | bytes 614408 | tf_op jit(solution)/shard_map/ppermute | solution.py:444
  45.5 9.7 %collective-permute-start.3 = (bf16[400,256]{1,0:T(8,128)(2,1)}, bf16[400,256]{1,0:T(8,128)(2,1)S(1)}, u32[]{:S(2)}, u32[]{:S(2)}) collective-permute-start(bf16[400,256]{1,0:T(8,128)(2,1)} %copy-done.26), channel_id=1, source_target_pairs={{0,6},{1,7},{2,0},{3,1},{4,2},{5,3},{6,4},{7,5},{8,14},{9,15},{10,... | collective-permute-start | bytes 614408 | tf_op jit(solution)/shard_map/ppermute | solution.py:444
  46.6 2.2 %copy-start.2 = (bf16[1024,2048]{1,0:T(8,128)(2,1)S(1)}, bf16[1024,2048]{1,0:T(8,128)(2,1)}, u32[]{:S(2)}) copy-start(bf16[1024,2048]{1,0:T(8,128)(2,1)} %copy-done) | copy-start | bytes 12582916
  51.5 0.8 copy-start.10
  52.3 20.7 %copy-start.14 = (bf16[768,256]{1,0:T(8,128)(2,1)S(1)}, bf16[768,256]{1,0:T(8,128)(2,1)}, u32[]{:S(2)}) copy-start(bf16[768,256]{1,0:T(8,128)(2,1)} %copy-done.13) | copy-start | bytes 1179652
  52.3 20.7 %copy-start.11 = (bf16[784,256]{1,0:T(8,128)(2,1)S(1)}, bf16[784,256]{1,0:T(8,128)(2,1)}, u32[]{:S(2)}) copy-start(bf16[784,256]{1,0:T(8,128)(2,1)} %copy-done.10) | copy-start | bytes 1204228
  52.3 10.6 %collective-permute-start.5 = (bf16[784,256]{1,0:T(8,128)(2,1)}, bf16[784,256]{1,0:T(8,128)(2,1)S(1)}, u32[]{:S(2)}, u32[]{:S(2)}) collective-permute-start(bf16[784,256]{1,0:T(8,128)(2,1)} %get-tuple-element.48), channel_id=1, source_target_pairs={{0,2},{1,3},{2,4},{3,5},{4,6},{5,7},{6,0},{7,1},{8,10},{9,11},{10,... | collective-permute-start | bytes 1204232 | tf_op jit(solution)/shard_map/ppermute | solution.py:444
  52.7 19.2 %collective-permute-start.6 = (bf16[784,256]{1,0:T(8,128)(2,1)}, bf16[784,256]{1,0:T(8,128)(2,1)S(1)}, u32[]{:S(2)}, u32[]{:S(2)}) collective-permute-start(bf16[784,256]{1,0:T(8,128)(2,1)} %get-tuple-element.49), channel_id=1, source_target_pairs={{0,4},{1,5},{2,6},{3,7},{4,0},{5,1},{6,2},{7,3},{8,12},{9,13},{10,... | collective-permute-start | bytes 1204232 | tf_op jit(solution)/shard_map/ppermute | solution.py:444
  53.5 19.5 %collective-permute-start.7 = (bf16[784,256]{1,0:T(8,128)(2,1)}, bf16[784,256]{1,0:T(8,128)(2,1)S(1)}, u32[]{:S(2)}, u32[]{:S(2)}) collective-permute-start(bf16[784,256]{1,0:T(8,128)(2,1)} %get-tuple-element.50), channel_id=1, source_target_pairs={{0,6},{1,7},{2,0},{3,1},{4,2},{5,3},{6,4},{7,5},{8,14},{9,15},{10,... | collective-permute-start | bytes 1204232 | tf_op jit(solution)/shard_map/ppermute | solution.py:444
  56.5 0.7 copy-start.15
  58.7 50.2 %copy-start.6 = (bf16[384,1024]{1,0:T(8,128)(2,1)S(1)}, bf16[384,1024]{1,0:T(8,128)(2,1)}, u32[]{:S(2)}) copy-start(bf16[384,1024]{1,0:T(8,128)(2,1)} %copy-done.5) | copy-start | bytes 2359300
  58.7 50.2 %copy-start.18 = (f32[1024]{0:T(1024)S(1)}, f32[1024]{0:T(1024)}, u32[]{:S(2)}) copy-start(f32[1024]{0:T(1024)} %param.11) | copy-start | bytes 12292
  58.7 20.6 %collective-permute-start.18 = (bf16[400,256]{1,0:T(8,128)(2,1)S(1)}, bf16[400,256]{1,0:T(8,128)(2,1)S(1)}, u32[]{:S(2)}, u32[]{:S(2)}) collective-permute-start(bf16[400,256]{1,0:T(8,128)(2,1)S(1)} %image_residual.1.rest_0_), channel_id=1, source_target_pairs={{0,1},{1,0},{2,3},{3,2},{4,5},{5,4},{6,7},{7,6},{8,9},{9,8},{10,11... | collective-permute-start | bytes 614408 | tf_op jit(solution)/shard_map/ppermute | solution.py:450
  61.0 18.9 %collective-permute-start.17 = (bf16[400,256]{1,0:T(8,128)(2,1)S(1)}, bf16[400,256]{1,0:T(8,128)(2,1)S(1)}, u32[]{:S(2)}, u32[]{:S(2)}) collective-permute-start(bf16[400,256]{1,0:T(8,128)(2,1)S(1)} %image_residual.1.rest_0_), channel_id=1, source_target_pairs={{0,6},{1,7},{2,0},{3,1},{4,2},{5,3},{6,4},{7,5},{8,14},{9,15},{10,... | collective-permute-start | bytes 614408 | tf_op jit(solution)/shard_map/ppermute | solution.py:444
  63.0 28.2 %collective-permute-start.16 = (bf16[400,256]{1,0:T(8,128)(2,1)S(1)}, bf16[400,256]{1,0:T(8,128)(2,1)}, u32[]{:S(2)}, u32[]{:S(2)}) collective-permute-start(bf16[400,256]{1,0:T(8,128)(2,1)S(1)} %image_residual.1.rest_0_), channel_id=1, source_target_pairs={{0,4},{1,5},{2,6},{3,7},{4,0},{5,1},{6,2},{7,3},{8,12},{9,13},{10,... | collective-permute-start | bytes 614408 | tf_op jit(solution)/shard_map/ppermute | solution.py:444
  74.5 0.7 copy-start.22
  75.2 0.8 copy-start.24
  76.0 29.4 %collective-permute-start.10 = (bf16[784,256]{1,0:T(8,128)(2,1)}, bf16[784,256]{1,0:T(8,128)(2,1)S(1)}, u32[]{:S(2)}, u32[]{:S(2)}) collective-permute-start(bf16[784,256]{1,0:T(8,128)(2,1)} %get-tuple-element.57.rest_1_), channel_id=1, source_target_pairs={{0,6},{1,7},{2,0},{3,1},{4,2},{5,3},{6,4},{7,5},{8,14},{9,15},{10,... | collective-permute-start | bytes 1204232 | tf_op jit(solution)/shard_map/ppermute | solution.py:444
  79.3 26.6 %collective-permute-start.9 = (bf16[784,256]{1,0:T(8,128)(2,1)}, bf16[784,256]{1,0:T(8,128)(2,1)S(1)}, u32[]{:S(2)}, u32[]{:S(2)}) collective-permute-start(bf16[784,256]{1,0:T(8,128)(2,1)} %get-tuple-element.57.rest_1_), channel_id=1, source_target_pairs={{0,4},{1,5},{2,6},{3,7},{4,0},{5,1},{6,2},{7,3},{8,12},{9,13},{10,... | collective-permute-start | bytes 1204232 | tf_op jit(solution)/shard_map/ppermute | solution.py:444
  79.3 26.7 %collective-permute-start.8 = (bf16[784,256]{1,0:T(8,128)(2,1)}, bf16[784,256]{1,0:T(8,128)(2,1)S(1)}, u32[]{:S(2)}, u32[]{:S(2)}) collective-permute-start(bf16[784,256]{1,0:T(8,128)(2,1)} %get-tuple-element.57.rest_1_), channel_id=1, source_target_pairs={{0,2},{1,3},{2,4},{3,5},{4,6},{5,7},{6,0},{7,1},{8,10},{9,11},{10,... | collective-permute-start | bytes 1204232 | tf_op jit(solution)/shard_map/ppermute | solution.py:444
  79.9 24.7 %collective-permute-start.15 = (bf16[400,256]{1,0:T(8,128)(2,1)S(1)}, bf16[400,256]{1,0:T(8,128)(2,1)S(1)}, u32[]{:S(2)}, u32[]{:S(2)}) collective-permute-start(bf16[400,256]{1,0:T(8,128)(2,1)S(1)} %image_residual.1.rest_0_), channel_id=1, source_target_pairs={{0,2},{1,3},{2,4},{3,5},{4,6},{5,7},{6,0},{7,1},{8,10},{9,11},{10,... | collective-permute-start | bytes 614408 | tf_op jit(solution)/shard_map/ppermute | solution.py:444
  82.0 33.8 %all-to-all-start = ((bf16[32,24,256]{2,1,0:T(8,128)(2,1)}), bf16[32,24,256]{2,1,0:T(8,128)(2,1)S(1)}, u32[]{:S(2)}, u32[]{:S(2)}) async-start(bf16[32,24,256]{2,1,0:T(8,128)(2,1)} %bitcast.1), calls=%async_computation | async-start | bytes 786432 | tf_op jit(solution)/shard_map/all_to_all | solution.py:459
  91.2 14.3 %collective-permute-start.21 = (bf16[400,256]{1,0:T(8,128)(2,1)S(1)}, bf16[400,256]{1,0:T(8,128)(2,1)S(1)}, u32[]{:S(2)}, u32[]{:S(2)}) collective-permute-start(bf16[400,256]{1,0:T(8,128)(2,1)S(1)} %collective-permute-done.17.rest_3_), channel_id=1, source_target_pairs={{0,1},{1,0},{2,3},{3,2},{4,5},{5,4},{6,7},{7,6},{8,9},{9,8},{10,11... | collective-permute-start | bytes 614408 | tf_op jit(solution)/shard_map/ppermute | solution.py:450
  104.6 2.4 %collective-permute-start.20 = (bf16[400,256]{1,0:T(8,128)(2,1)}, bf16[400,256]{1,0:T(8,128)(2,1)S(1)}, u32[]{:S(2)}, u32[]{:S(2)}) collective-permute-start(bf16[400,256]{1,0:T(8,128)(2,1)} %collective-permute-done.16.rest_2_), channel_id=1, source_target_pairs={{0,1},{1,0},{2,3},{3,2},{4,5},{5,4},{6,7},{7,6},{8,9},{9,8},{10,11... | collective-permute-start | bytes 614408 | tf_op jit(solution)/shard_map/ppermute | solution.py:450
  105.5 12.6 %collective-permute-start.11 = (bf16[784,256]{1,0:T(8,128)(2,1)}, bf16[784,256]{1,0:T(8,128)(2,1)}, u32[]{:S(2)}, u32[]{:S(2)}) collective-permute-start(bf16[784,256]{1,0:T(8,128)(2,1)} %get-tuple-element.57.rest_1_), channel_id=1, source_target_pairs={{0,1},{1,0},{2,3},{3,2},{4,5},{5,4},{6,7},{7,6},{8,9},{9,8},{10,11... | collective-permute-start | bytes 1204232 | tf_op jit(solution)/shard_map/ppermute | solution.py:450
  105.5 12.6 %collective-permute-start.14 = (bf16[784,256]{1,0:T(8,128)(2,1)S(1)}, bf16[784,256]{1,0:T(8,128)(2,1)}, u32[]{:S(2)}, u32[]{:S(2)}) collective-permute-start(bf16[784,256]{1,0:T(8,128)(2,1)S(1)} %collective-permute-done.10.rest_4_), channel_id=1, source_target_pairs={{0,1},{1,0},{2,3},{3,2},{4,5},{5,4},{6,7},{7,6},{8,9},{9,8},{10,11... | collective-permute-start | bytes 1204232 | tf_op jit(solution)/shard_map/ppermute | solution.py:450
  106.0 12.1 %collective-permute-start.13 = (bf16[784,256]{1,0:T(8,128)(2,1)S(1)}, bf16[784,256]{1,0:T(8,128)(2,1)}, u32[]{:S(2)}, u32[]{:S(2)}) collective-permute-start(bf16[784,256]{1,0:T(8,128)(2,1)S(1)} %collective-permute-done.9.rest_3_), channel_id=1, source_target_pairs={{0,1},{1,0},{2,3},{3,2},{4,5},{5,4},{6,7},{7,6},{8,9},{9,8},{10,11... | collective-permute-start | bytes 1204232 | tf_op jit(solution)/shard_map/ppermute | solution.py:450
  106.1 12.0 %collective-permute-start.12 = (bf16[784,256]{1,0:T(8,128)(2,1)S(1)}, bf16[784,256]{1,0:T(8,128)(2,1)}, u32[]{:S(2)}, u32[]{:S(2)}) collective-permute-start(bf16[784,256]{1,0:T(8,128)(2,1)S(1)} %collective-permute-done.8.rest_2_), channel_id=1, source_target_pairs={{0,1},{1,0},{2,3},{3,2},{4,5},{5,4},{6,7},{7,6},{8,9},{9,8},{10,11... | collective-permute-start | bytes 1204232 | tf_op jit(solution)/shard_map/ppermute | solution.py:450
  107.0 2.0 %collective-permute-start.19 = (bf16[400,256]{1,0:T(8,128)(2,1)S(1)}, bf16[400,256]{1,0:T(8,128)(2,1)S(1)}, u32[]{:S(2)}, u32[]{:S(2)}) collective-permute-start(bf16[400,256]{1,0:T(8,128)(2,1)S(1)} %collective-permute-done.15.rest_1_), channel_id=1, source_target_pairs={{0,1},{1,0},{2,3},{3,2},{4,5},{5,4},{6,7},{7,6},{8,9},{9,8},{10,11... | collective-permute-start | bytes 614408 | tf_op jit(solution)/shard_map/ppermute | solution.py:450
  108.9 2.2 %copy-start.3 = (bf16[1024,2048]{1,0:T(8,128)(2,1)S(1)}, bf16[1024,2048]{1,0:T(8,128)(2,1)}, u32[]{:S(2)}) copy-start(bf16[1024,2048]{1,0:T(8,128)(2,1)} %copy-done) | copy-start | bytes 12582916
  111.1 0.9 copy-start.16
  115.8 1.0 copy-start.25
  118.1 2.2 %copy-start.4 = (bf16[1024,2048]{1,0:T(8,128)(2,1)S(1)}, bf16[1024,2048]{1,0:T(8,128)(2,1)}, u32[]{:S(2)}) copy-start(bf16[1024,2048]{1,0:T(8,128)(2,1)} %copy-done) | copy-start | bytes 12582916
  120.3 1.0 copy-start.23
  121.3 1.4 %copy-start.32 = (bf16[768,1024]{1,0:T(8,128)(2,1)S(1)}, bf16[768,1024]{1,0:T(8,128)(2,1)}, u32[]{:S(2)}) copy-start(bf16[768,1024]{1,0:T(8,128)(2,1)} %copy-done.31) | copy-start | bytes 4718596

commit v4 on v3

v4 whole, which is shorter than its diff:
```python
import functools

import jax
import jax.numpy as jnp
from jax import lax
from jax.experimental import pallas as pl
from jax.experimental.pallas import tpu as pltpu
from jax.sharding import PartitionSpec as P

WIDTH = 8192
EPSILON = 1e-06
IMAGE_LEN = 24
EXTRA = 16
HEAD = 128
PAIR = 2 * HEAD
RINGS = 4
CHUNKS = 2 * RINGS
PIECE = 128
ABSENT = 8192.0

F32 = jnp.float32
BF16 = jnp.bfloat16
PARAMS = pltpu.CompilerParams(vmem_limit_bytes=24 * 2**20)
IN_VMEM = pl.BlockSpec(memory_space=pltpu.VMEM)
ANYWHERE = pl.BlockSpec(memory_space=pl.ANY)


def near(x):
    return pltpu.with_memory_space_constraint(x, pltpu.VMEM)


def far(x):
    return pltpu.with_memory_space_constraint(x, pltpu.HBM)


def after(x, *others):
    return lax.optimization_barrier((x, *others))[0]


def fetch(pairs, sems, first=0):
    copies = [
        pltpu.make_async_copy(source, target, sems.at[first + n])
        for n, (source, target) in enumerate(pairs)
    ]
    for copy in copies:
        copy.start()
    return copies


def finish(copies):
    for copy in copies:
        copy.wait()


def cost(flops, nbytes):
    return pl.CostEstimate(flops=flops, bytes_accessed=nbytes, transcendentals=0)


def same_index(count):
    shape = (count, count)
    return lax.broadcasted_iota(jnp.int32, shape, 0) == lax.broadcasted_iota(jnp.int32, shape, 1)


def column_to_lanes(column):
    eye = same_index(HEAD)
    row = lax.broadcasted_iota(jnp.int32, (8, HEAD), 0)
    out = jnp.zeros((8, HEAD), F32)
    for p in range(column.shape[0] // HEAD):
        piece = column[p * HEAD : (p + 1) * HEAD, :]
        lanes = jnp.sum(jnp.where(eye, piece, 0.0), axis=0, keepdims=True)
        out = jnp.where(row == p, lanes, out)
    return out


def lanes_to_column(lanes, rows):
    eye = same_index(HEAD)
    pieces = [
        jnp.sum(jnp.where(eye, lanes[p : p + 1, :], 0.0), axis=1, keepdims=True)
        for p in range(rows // HEAD)
    ]
    return jnp.concatenate(pieces, axis=0)


def split_extra(lanes):
    high = lanes.astype(BF16).astype(F32)
    both = jnp.concatenate([high, lanes - high], axis=0)
    return jnp.concatenate([both, jnp.zeros((EXTRA, HEAD), F32)], axis=1).astype(BF16)


def join_extra(block):
    block = block.astype(F32)
    return block[0:8, 0:HEAD] + block[8:16, 0:HEAD]


def my_place():
    mine = lax.axis_index("tp")
    return lax.div(mine, 2), lax.rem(mine, 2)


def head_columns(d, other):
    ring, core = my_place()
    chip = lax.rem(ring + d, RINGS)
    return pl.ds(pl.multiple_of(HEAD * (2 * chip + (1 - core if other else core)), HEAD), HEAD)


def pair_weight(wk_ref, wv_ref, d, other):
    here = head_columns(d, other)
    return jnp.concatenate([wk_ref[:, here], wv_ref[:, here]], axis=1)


def forward_other_kernel(loads, splits, x_ref, gain_ref, *refs):
    from_refs, send_refs, refs = refs[0:2], refs[2 : 2 + len(splits)], refs[2 + len(splits) :]
    if loads:
        wk_from, wv_from = from_refs
        scaled_ref, lanes_ref, wk_ref, wv_ref, held, sems, more = refs
    else:
        wk_ref, wv_ref = from_refs
        scaled_ref, lanes_ref, held, sems = refs
    rows, depth = x_ref.shape[0], wk_ref.shape[0]
    pieces = [pl.ds(p * PIECE, PIECE) for p in range(rows // PIECE)]
    x_copies = fetch([(x_ref.at[p], held.at[p]) for p in pieces], sems)
    weights = []
    if loads:
        spans = [pl.ds(p * PAIR, PAIR) for p in range(depth // PAIR)]
        weights = [(wk_from.at[p], wk_ref.at[p]) for p in spans]
        weights += [(wv_from.at[p], wv_ref.at[p]) for p in spans]
        weights = fetch(weights, more)
    row = lax.broadcasted_iota(jnp.int32, (8, HEAD), 0)
    eye = same_index(HEAD)
    lanes = jnp.zeros((8, HEAD), F32)
    for p, copy in enumerate(x_copies):
        copy.wait()
        here = slice(p * PIECE, (p + 1) * PIECE)
        x = held[here, :].astype(F32)
        scaled_ref[here, :] = (gain_ref[...] * x).astype(BF16)
        squares = jnp.sum(x * x, axis=1, keepdims=True)
        line = jnp.sum(jnp.where(eye, squares, 0.0), axis=0, keepdims=True)
        lanes = jnp.where(row == p, line, lanes)
    lanes_ref[...] = lanes
    extra = split_extra(lanes)
    finish(weights)
    for split, send_ref in zip(splits, send_refs):
        for n, d in enumerate(split):
            weight = pair_weight(wk_ref, wv_ref, d, True)
            product = jnp.dot(scaled_ref[...], weight, preferred_element_type=F32)
            send_ref[n, 0:rows, :] = product.astype(BF16)
            send_ref[n, rows:, :] = extra


def forward_other(x, gain, weights, loads, splits):
    rows, width = x.shape
    out_shape = [pltpu.VMEM((len(split), rows + EXTRA, PAIR), BF16) for split in splits] + [
        pltpu.VMEM(x.shape, BF16),
        pltpu.VMEM((8, HEAD), F32),
    ]
    scratch = [pltpu.VMEM(x.shape, BF16), pltpu.SemaphoreType.DMA((rows // PIECE,))]
    if loads:
        out_shape += [pltpu.VMEM(w.shape, BF16) for w in weights]
        scratch.append(pltpu.SemaphoreType.DMA((2 * width // PAIR,)))
    weights = [far(w) if loads else near(w) for w in weights]
    return pl.pallas_call(
        functools.partial(forward_other_kernel, loads, splits),
        in_specs=[ANYWHERE, IN_VMEM] + [ANYWHERE if loads else IN_VMEM] * 2,
        out_specs=[IN_VMEM] * len(out_shape),
        out_shape=out_shape,
        scratch_shapes=scratch,
        compiler_params=PARAMS,
        cost_estimate=cost(2 * rows * width * RINGS * PAIR, 2**22 if loads else 2**20),
        name="forward_other",
    )(far(x), gain, *weights)


def forward_own_kernel(split, first, close, scaled_ref, lanes_ref, wk_ref, wv_ref, in_ref, *refs):
    out_refs, (held, sems) = refs[0 : len(split)], refs[len(split) :]
    rows = scaled_ref.shape[0]
    extra = split_extra(lanes_ref[...] + join_extra(in_ref[first, rows:, :]))
    copies = []
    for n, d in enumerate(split):
        weight = pair_weight(wk_ref, wv_ref, d, False)
        product = jnp.dot(scaled_ref[...], weight, preferred_element_type=F32)
        total = (product + in_ref[first + n, 0:rows, :].astype(F32)).astype(BF16)
        if d in close:
            out_refs[n][0:rows, :] = total
            out_refs[n][rows:, :] = extra
        else:
            held[n, 0:rows, :] = total
            held[n, rows:, :] = extra
            copies += fetch([(held.at[n], out_refs[n])], sems, n)
    finish(copies)


def forward_own(scaled, lanes, weights, arrived, split, first, close):
    rows, width = scaled.shape
    block = (rows + EXTRA, PAIR)
    sums = pl.pallas_call(
        functools.partial(forward_own_kernel, split, first, close),
        in_specs=[IN_VMEM] * 5,
        out_specs=[IN_VMEM if d in close else ANYWHERE for d in split],
        out_shape=[(pltpu.VMEM if d in close else pltpu.HBM)(block, BF16) for d in split],
        scratch_shapes=[
            pltpu.VMEM((len(split),) + block, BF16),
            pltpu.SemaphoreType.DMA((len(split),)),
        ],
        compiler_params=PARAMS,
        cost_estimate=cost(2 * rows * width * len(split) * PAIR, 2**20),
        name="forward_own",
    )(near(scaled), near(lanes), *[near(w) for w in weights], near(arrived))
    return dict(zip(split, sums))


def gathered(parts):
    rows = parts.shape[1] - EXTRA
    total = parts[0, 0:rows, :].astype(F32)
    lanes = join_extra(parts[0, rows:, :])
    for d in range(1, RINGS):
        total = total + parts[d, 0:rows, :].astype(F32)
        lanes = lanes + join_extra(parts[d, rows:, :])
    inverse = lax.rsqrt(lanes_to_column(lanes, rows) / WIDTH + EPSILON)
    return (inverse * total).astype(BF16), inverse


def residual(both, target, resid_ref):
    rows = both.shape[0]
    both = both.astype(F32)
    resid = (both - target.astype(F32)).astype(BF16)
    dots = jnp.sum(resid.astype(F32) * both, axis=1, keepdims=True)
    resid_ref[0:rows, :] = resid
    resid_ref[rows:, :] = split_extra(column_to_lanes(dots))


def text_combine_kernel(
    a, b, c, d, kt_ref, vt_ref, both_out, resid_out, inverse_out,
    parts, targets, both_ref, resid_ref, inverse_ref, sems,
):
    copies = fetch([(ref, parts.at[n]) for n, ref in enumerate((a, b, c, d))], sems)
    copies += fetch([(kt_ref, targets.at[0]), (vt_ref, targets.at[1])], sems, RINGS)
    finish(copies)
    both, inverse = gathered(parts)
    residual(both, jnp.concatenate([targets[0], targets[1]], axis=1), resid_ref)
    out = fetch([(resid_ref, resid_out)], sems)
    both_ref[...] = both
    inverse_ref[...] = jnp.broadcast_to(inverse, inverse_ref.shape)
    out += fetch([(both_ref, both_out), (inverse_ref, inverse_out)], sems, 1)
    finish(out)


def text_combine(parts, targets):
    rows = targets[0].shape[0]
    shapes = [((rows, PAIR), BF16), (parts[0].shape, BF16), ((rows, HEAD), F32)]
    return pl.pallas_call(
        text_combine_kernel,
        in_specs=[ANYWHERE] * 6,
        out_specs=[ANYWHERE] * 3,
        out_shape=[pltpu.HBM(*s) for s in shapes],
        scratch_shapes=[
            pltpu.VMEM((RINGS,) + parts[0].shape, BF16),
            pltpu.VMEM((2,) + targets[0].shape, BF16),
            *[pltpu.VMEM(*s) for s in shapes],
            pltpu.SemaphoreType.DMA((RINGS + 2,)),
        ],
        compiler_params=PARAMS,
        cost_estimate=cost(2**22, 2**22),
        name="text_combine",
    )(*parts, *[far(t) for t in targets])


def one_hot(match):
    return jnp.where(match, jnp.ones(match.shape, F32), jnp.zeros(match.shape, F32)).astype(BF16)


def slot_columns(rows, first, lanes):
    shape = (rows, lanes.shape[1])
    row = first + lax.broadcasted_iota(jnp.int32, shape, 0)
    begin = IMAGE_LEN * lax.broadcasted_iota(jnp.int32, shape, 1)
    inside = (row >= begin) & (row < begin + IMAGE_LEN)
    value = lanes + (row - begin).astype(F32)
    return jnp.sum(jnp.where(inside, value, 0.0), axis=1, keepdims=True)


def slot_lanes(rows, column):
    shape = (column.shape[0], rows)
    row = lax.broadcasted_iota(jnp.int32, shape, 1)
    begin = IMAGE_LEN * lax.broadcasted_iota(jnp.int32, shape, 0)
    inside = (row >= begin) & (row < begin + IMAGE_LEN)
    value = column + (row - begin).astype(F32)
    return jnp.sum(jnp.where(inside, value, 0.0), axis=0, keepdims=True)


def first_rows(starts_ref, rows):
    shards = lax.axis_size("rows")
    images = starts_ref.shape[1] // shards
    offset = starts_ref[...].astype(F32) - (lax.axis_index("rows") * rows).astype(F32)
    value = jnp.where((offset >= 0.0) & (offset < rows), offset + ABSENT, 0.0)
    shape = (shards, starts_ref.shape[1])
    lane = lax.broadcasted_iota(jnp.int32, shape, 1)
    begin = images * lax.broadcasted_iota(jnp.int32, shape, 0)
    mine = (lane >= begin) & (lane < begin + images)
    column = jnp.sum(jnp.where(mine, value, 0.0), axis=1, keepdims=True) - ABSENT
    return column, jnp.sum(jnp.where(same_index(shards), column, 0.0), axis=0, keepdims=True)


def destinations(starts_ref, rows):
    images = starts_ref.shape[1] // lax.axis_size("rows")
    slot = IMAGE_LEN * jnp.floor((starts_ref[...].astype(F32) + 0.5) / rows)
    shape = (images, starts_ref.shape[1])
    image = lax.axis_index("rows") * images + lax.broadcasted_iota(jnp.int32, shape, 0)
    mine = lax.broadcasted_iota(jnp.int32, shape, 1) == image
    column = jnp.sum(jnp.where(mine, slot, 0.0), axis=1, keepdims=True)
    return jnp.sum(jnp.where(same_index(images), column, 0.0), axis=0, keepdims=True), column


def image_keys_kernel(
    seq_rows, a, b, c, d, starts_ref, send_out, both_out, inverse_out,
    parts, send_ref, both_ref, inverse_ref, sems,
):
    copies = fetch([(ref, parts.at[n]) for n, ref in enumerate((a, b, c, d))], sems)
    rows, slots = both_ref.shape[0], send_ref.shape[0]
    _, dest = destinations(starts_ref, seq_rows)
    slot = lax.broadcasted_iota(jnp.int32, (slots, rows), 0).astype(F32)
    picks = one_hot(slot == slot_lanes(rows, dest))
    finish(copies)
    both, inverse = gathered(parts)
    send_ref[...] = jnp.dot(picks, both, preferred_element_type=F32).astype(BF16)
    out = fetch([(send_ref, send_out)], sems)
    both_ref[...] = both
    inverse_ref[...] = jnp.broadcast_to(inverse, inverse_ref.shape)
    out += fetch([(both_ref, both_out), (inverse_ref, inverse_out)], sems, 1)
    finish(out)


def image_keys(parts, starts, seq_rows):
    rows = parts[0].shape[0] - EXTRA
    slots = lax.axis_size("rows") * IMAGE_LEN
    shapes = [((slots, PAIR), BF16), ((rows, PAIR), BF16), ((rows, HEAD), F32)]
    return pl.pallas_call(
        functools.partial(image_keys_kernel, seq_rows),
        in_specs=[ANYWHERE] * RINGS + [IN_VMEM],
        out_specs=[ANYWHERE] * 3,
        out_shape=[pltpu.HBM(*s) for s in shapes],
        scratch_shapes=[
            pltpu.VMEM((RINGS,) + parts[0].shape, BF16),
            *[pltpu.VMEM(*s) for s in shapes],
            pltpu.SemaphoreType.DMA((RINGS,)),
        ],
        compiler_params=PARAMS,
        cost_estimate=cost(2**28, 2**20),
        name="image_keys",
    )(*parts, starts)


def image_residual_kernel(
    seq_rows, both_from, arrived_from, starts_ref, resid_out, both_ref, arrived_ref, resid_ref, sems
):
    copies = fetch([(both_from, both_ref), (arrived_from, arrived_ref)], sems)
    rows = both_ref.shape[0]
    dest, _ = destinations(starts_ref, seq_rows)
    shape = (rows, arrived_ref.shape[0])
    slot = lax.broadcasted_iota(jnp.int32, shape, 1).astype(F32)
    picks = one_hot(slot == slot_columns(rows, 0, dest))
    finish(copies)
    target = jnp.dot(picks, arrived_ref[...], preferred_element_type=F32)
    residual(both_ref[...], target, resid_ref)
    finish(fetch([(resid_ref, resid_out)], sems))


def image_residual(both, arrived, starts, seq_rows):
    shape = (both.shape[0] + EXTRA, PAIR)
    return pl.pallas_call(
        functools.partial(image_residual_kernel, seq_rows),
        in_specs=[ANYWHERE, ANYWHERE, IN_VMEM],
        out_specs=ANYWHERE,
        out_shape=pltpu.HBM(shape, BF16),
        scratch_shapes=[
            pltpu.VMEM(both.shape, BF16),
            pltpu.VMEM(arrived.shape, BF16),
            pltpu.VMEM(shape, BF16),
            pltpu.SemaphoreType.DMA((2,)),
        ],
        compiler_params=PARAMS,
        cost_estimate=cost(2**28, 2**20),
        name="image_residual",
    )(both, arrived, starts)


def gather_kernel(starts_ref, kt_from, vt_from, out_ref, halves, target_ref, held, sems):
    copies = fetch([(kt_from, halves.at[0]), (vt_from, halves.at[1])], sems)
    rows = target_ref.shape[0]
    _, first = first_rows(starts_ref, rows)
    finish(copies)
    target_ref[:, 0:HEAD] = halves[0]
    target_ref[:, HEAD:] = halves[1]
    for begin in range(0, out_ref.shape[0], PAIR):
        place = slot_columns(PAIR, begin, first)
        position = lax.broadcasted_iota(jnp.int32, (PAIR, rows), 1).astype(F32)
        picked = jnp.dot(
            one_hot(position == place), target_ref[...], preferred_element_type=F32
        )
        held[begin : begin + PAIR, :] = picked.astype(BF16)
    finish(fetch([(held, out_ref)], sems))


def gather_targets(starts, key_target, value_target):
    shape = (lax.axis_size("rows") * IMAGE_LEN, PAIR)
    return pl.pallas_call(
        gather_kernel,
        in_specs=[IN_VMEM, ANYWHERE, ANYWHERE],
        out_specs=ANYWHERE,
        out_shape=pltpu.HBM(shape, BF16),
        scratch_shapes=[
            pltpu.VMEM((2,) + key_target.shape, BF16),
            pltpu.VMEM((key_target.shape[0], PAIR), BF16),
            pltpu.VMEM(shape, BF16),
            pltpu.SemaphoreType.DMA((2,)),
        ],
        compiler_params=PARAMS,
        cost_estimate=cost(2**28, 2**20),
        name="gather_targets",
    )(starts, far(key_target), far(value_target))


def image_rows_mask(rows, first_row, first_lanes):
    shape = (rows, first_lanes.shape[1])
    row = (first_row + lax.broadcasted_iota(jnp.int32, shape, 0)).astype(F32)
    inside = (row >= first_lanes) & (row < first_lanes + IMAGE_LEN)
    return jnp.sum(jnp.where(inside, 1.0, 0.0), axis=1, keepdims=True) > 0.5


def merge_kernel(
    starts_ref, arrived_from, both_from, keys_out, values_out,
    arrived_ref, both_ref, keys_ref, values_ref, sems,
):
    copies = fetch([(arrived_from, arrived_ref), (both_from, both_ref)], sems)
    slots, rows = arrived_ref.shape[0], both_ref.shape[0]
    column, lanes = first_rows(starts_ref, rows)
    place = slot_lanes(slots, column)
    finish(copies)
    for begin in range(0, rows, PAIR):
        row = begin + lax.broadcasted_iota(jnp.int32, (PAIR, slots), 0)
        picks = one_hot(row.astype(F32) == place)
        landed = jnp.dot(picks, arrived_ref[...], preferred_element_type=F32)
        here = slice(begin, begin + PAIR)
        mask = image_rows_mask(PAIR, begin, lanes)
        both = jnp.where(mask, landed, both_ref[here, :].astype(F32)).astype(BF16)
        keys_ref[here, :] = both[:, 0:HEAD]
        values_ref[here, :] = both[:, HEAD:]
    finish(fetch([(keys_ref, keys_out), (values_ref, values_out)], sems))


def merge(starts, arrived, both):
    shape = (both.shape[0], HEAD)
    return pl.pallas_call(
        merge_kernel,
        in_specs=[IN_VMEM, ANYWHERE, ANYWHERE],
        out_specs=[ANYWHERE] * 2,
        out_shape=[jax.ShapeDtypeStruct(shape, BF16)] * 2,
        scratch_shapes=[
            pltpu.VMEM(arrived.shape, BF16),
            pltpu.VMEM(both.shape, BF16),
            pltpu.VMEM(shape, BF16),
            pltpu.VMEM(shape, BF16),
            pltpu.SemaphoreType.DMA((2,)),
        ],
        compiler_params=PARAMS,
        cost_estimate=cost(2**28, 2**20),
        name="merge",
    )(starts, arrived, both)


def stack_parts(resids, parts, stacked, sems):
    rows = stacked.shape[0]
    copies = fetch([(ref, parts.at[n]) for n, ref in enumerate(resids)], sems)
    lanes = jnp.zeros((8, HEAD), F32)
    for n, copy in enumerate(copies):
        copy.wait()
        stacked[:, n * PAIR : (n + 1) * PAIR] = parts[n, 0:rows, :]
        lanes = lanes + join_extra(parts[n, rows:, :])
    return lanes


def tile_product(stacked, wk_ref, wv_ref, here, other):
    pieces = []
    for n in range(RINGS):
        columns = head_columns((RINGS - n) % RINGS, other)
        pieces += [wk_ref[here, columns], wv_ref[here, columns]]
    contract = (((1,), (1,)), ((), ()))
    weight = jnp.concatenate(pieces, axis=1)
    return lax.dot_general(stacked[...], weight, contract, preferred_element_type=F32)


TILE = 256


def backward_own_kernel(loads, *refs):
    froms, resids, refs = refs[0:2], refs[2 : 2 + RINGS], refs[2 + RINGS :]
    if loads:
        total_ref, lanes_ref, wk_ref, wv_ref, parts, stacked, sems, more = refs
    else:
        wk_ref, wv_ref = froms
        total_ref, lanes_ref, parts, stacked, sems = refs
    tiles = total_ref.shape[1] // TILE
    weights = []
    for n in range(tiles if loads else 0):
        span = pl.ds(n * TILE, TILE)
        pairs = zip(froms, (wk_ref, wv_ref))
        weights.append(fetch([(source.at[span], to.at[span]) for source, to in pairs], more, 2 * n))
    lanes_ref[...] = stack_parts(resids, parts, stacked, sems)
    for n in range(tiles):
        here = slice(n * TILE, (n + 1) * TILE)
        finish(weights[n] if loads else [])
        total_ref[:, here] = tile_product(stacked, wk_ref, wv_ref, here, False)


def backward_own(weights, resids, rows, loads):
    width = weights[0].shape[0]
    out_shape = [pltpu.VMEM((rows, width), F32), pltpu.VMEM((8, HEAD), F32)]
    scratch = [
        pltpu.VMEM((RINGS,) + resids[0].shape, BF16),
        pltpu.VMEM((rows, RINGS * PAIR), BF16),
        pltpu.SemaphoreType.DMA((RINGS,)),
    ]
    if loads:
        out_shape += [pltpu.VMEM(w.shape, BF16) for w in weights]
        scratch.append(pltpu.SemaphoreType.DMA((2 * width // TILE,)))
    return pl.pallas_call(
        functools.partial(backward_own_kernel, loads),
        in_specs=[ANYWHERE if loads else IN_VMEM] * 2 + [ANYWHERE] * RINGS,
        out_specs=[IN_VMEM] * len(out_shape),
        out_shape=out_shape,
        scratch_shapes=scratch,
        compiler_params=PARAMS,
        cost_estimate=cost(2 * rows * width * RINGS * PAIR, 2**21),
        name="backward_own",
    )(*[far(w) if loads else near(w) for w in weights], *resids)


def backward_other_kernel(
    masked, x_from, gain_ref, starts_ref, inverse_from, wk_ref, wv_ref, total_ref, lanes_ref, *rest
):
    resids, rest = rest[0:RINGS], rest[RINGS:]
    out_ref, parts, stacked, inverse_ref, x_ref, held, sems = rest
    rows, width = x_ref.shape
    late = [(inverse_from, inverse_ref), (x_from, x_ref)]
    if masked:
        mask = image_rows_mask(rows, 0, first_rows(starts_ref, rows)[1])
    late = fetch(late, sems, RINGS)
    lanes = lanes_ref[...] + stack_parts(resids, parts, stacked, sems)
    finish(late)
    inverse = inverse_ref[:, 0:1]
    coefficient = inverse * inverse * lanes_to_column(lanes, rows) / WIDTH
    out = []
    for n in range(width // TILE):
        here = slice(n * TILE, (n + 1) * TILE)
        back = total_ref[:, here] + tile_product(stacked, wk_ref, wv_ref, here, True)
        grad = gain_ref[:, here] * inverse * back - coefficient * x_ref[:, here].astype(F32)
        if masked:
            grad = jnp.where(mask, 0.0, grad)
        held[:, here] = grad.astype(BF16)
        span = pl.ds(n * TILE, TILE)
        out += fetch([(held.at[:, span], out_ref.at[:, span])], sems, n)
    finish(out)


def backward_other(x, gain, inverse, weights, starts, before, resids, masked):
    rows, width = x.shape
    return pl.pallas_call(
        functools.partial(backward_other_kernel, masked),
        in_specs=[ANYWHERE] + [IN_VMEM] * 2 + [ANYWHERE] + [IN_VMEM] * 4 + [ANYWHERE] * RINGS,
        out_specs=ANYWHERE,
        out_shape=jax.ShapeDtypeStruct(x.shape, BF16),
        scratch_shapes=[
            pltpu.VMEM((RINGS,) + resids[0].shape, BF16),
            pltpu.VMEM((rows, RINGS * PAIR), BF16),
            pltpu.VMEM((rows, HEAD), F32),
            pltpu.VMEM(x.shape, BF16),
            pltpu.VMEM(x.shape, BF16),
            pltpu.SemaphoreType.DMA((RINGS + 2,)),
        ],
        compiler_params=PARAMS,
        cost_estimate=cost(2 * rows * width * RINGS * PAIR, 2**21),
        name="backward_other",
    )(far(x), gain, starts, inverse, *[near(w) for w in weights], *[near(b) for b in before], *resids)


def around(x, shift):
    return lax.ppermute(
        x, "tp", [(2 * y + c, 2 * ((y + shift) % RINGS) + c) for y in range(RINGS) for c in range(2)]
    )


def across(x):
    return lax.ppermute(x, "tp", [(i, i ^ 1) for i in range(2 * RINGS)])


def route(x):
    return lax.all_to_all(x, "rows", split_axis=0, concat_axis=0, tiled=True)


def on_device(
    text_embed,
    image_embed,
    image_start,
    norm_gain,
    key_weight,
    value_weight,
    key_target,
    value_target,
):
    seq_rows = text_embed.shape[0]
    gain = norm_gain[None, :]
    starts = image_start[None, :]
    weights = (key_weight, value_weight)
    targets = (key_target, value_target)

    early, late = (2, 1), (3, 0)
    sent_early, sent_late, scaled, lanes, *held = forward_other(
        text_embed, gain, weights, True, (early, late)
    )
    arrived_early, arrived_late = across(sent_early), across(sent_late)
    image_sent, image_scaled, image_lanes = forward_other(
        image_embed, gain, held, False, (early + late,)
    )
    image_arrived = across(image_sent)
    close = (2, 1, 3)
    sums = forward_own(after(scaled, image_sent), lanes, held, arrived_early, early, 0, close)
    sums |= forward_own(after(scaled, sums[1]), lanes, held, arrived_late, late, 0, close)
    part2, part1, part3 = [around(sums[d], d) for d in (2, 1, 3)]
    image_sums = forward_own(
        after(image_scaled, sums[0]), image_lanes, held, image_arrived, early, 0, ()
    )
    image2 = around(image_sums[2], 2)
    image_sums |= forward_own(
        after(image_scaled, image_sums[1]), image_lanes, held, image_arrived, late, 2, ()
    )
    goals = route(gather_targets(after(starts, image_sums[0]), *targets))
    image1 = around(after(image_sums[1], part1), 1)
    image3 = around(after(image_sums[3], part3), 3)

    both, resid, inverse = text_combine((sums[0], part1, part2, part3), targets)
    resid2 = around(after(resid, image2), 2)
    resid1 = around(after(resid, image1), 1)
    resid3 = around(after(resid, image3), 3)
    image_send, image_both, image_inverse = image_keys(
        (after(image_sums[0], resid), image1, image2, image3), starts, seq_rows
    )
    landed = route(image_send)
    image_resid = image_residual(image_both, goals, starts, seq_rows)
    image_resid2 = around(image_resid, 2)
    image_resid1 = around(after(image_resid, resid1), 1)
    image_resid3 = around(after(image_resid, resid3), 3)

    own = [resid, resid1, resid2, resid3]
    other = [across(r) for r in own]
    *before, wk, wv = backward_own(weights, own, seq_rows, True)
    held = (wk, wv)
    text_grad = backward_other(text_embed, gain, inverse, held, starts, before, other, True)
    own = [after(image_resid, text_grad), image_resid1, image_resid2, image_resid3]
    other = [across(r) for r in own]
    before = backward_own(held, own, image_embed.shape[0], False)
    image_grad = backward_other(
        image_embed, gain, image_inverse, held, starts, before, other, False
    )
    keys, values = merge(after(starts, image_grad), landed, both)
    return (keys, values, text_grad, image_grad)


def solution(mesh):
    in_specs = (
        P("rows", "tp"),
        P("rows", "tp"),
        P(),
        P("tp"),
        P("tp", None),
        P("tp", None),
        P("rows", "tp"),
        P("rows", "tp"),
    )
    out_specs = (P("rows", "tp"), P("rows", "tp"), P("rows", "tp"), P("rows", "tp"))
    return jax.shard_map(
        on_device, mesh=mesh, in_specs=in_specs, out_specs=out_specs, check_vma=False
    )
```

time: 130 us -> 101 us (0.78)
  local copies, waits for them, and re-layouts: 29.4 us -> 1.65 us
  waiting for transfers between devices: 23.3 us -> 2.64 us
  Pallas kernels: 30.9 us -> 42.3 us
  starting transfers between devices: 44.3 us -> 53.2 us
    unnamed x68 -> x22, local copies, waits for them, and re-layouts: 29.3 us -> 1.65 us
    ppermute x12, waiting for transfers between devices: 21.2 us -> 2.61 us  [around(): lax.ppermute(x, 'tp', [(2 * y + c, 2 * ((y + shift) % RINGS) + c) for y i...]
    pallas_call x9 -> x13, Pallas kernels: 28.1 us -> 37.8 us  [the longest x2 8.7 us: backward_own(): pl.pallas_call(functools.partial(backward_own_kernel, loads), in_specs=[A...]
    ppermute x10 -> x11, starting transfers between devices: 10.5 us -> 17.2 us  [across(): return lax.ppermute(x, 'tp', [(i, i ^ 1) for i in range(2 * RINGS)])]
    all_to_all x2, starting transfers between devices: 18.6 us -> 22.9 us  [route(): return lax.all_to_all(x, 'rows', split_axis=0, concat_axis=0, tiled=True)]
    ppermute x12, starting transfers between devices: 15.2 us -> 13.1 us  [around(): lax.ppermute(x, 'tp', [(2 * y + c, 2 * ((y + shift) % RINGS) + c) for y i...]
    ppermute x10 -> x11, waiting for transfers between devices: 2.08 us -> 0.03 us  [across(): return lax.ppermute(x, 'tp', [(i, i ^ 1) for i in range(2 * RINGS)])]
    pallas_call x1, Pallas kernels: 1.34 us -> 2.66 us  [image_keys(): pl.pallas_call(functools.partial(image_keys_kernel, seq_rows), in_specs=[...]
  transfers between devices with their start and end apart: 24 -> 25, of which waited for: 6 -> 2; matrix products, arithmetic and copies ran while one was open for 0% -> 0% of each run, Pallas kernels for 13% -> 36%
where the time goes in v4:
time: 101 us
  starting transfers between devices  53.2 us (53%)
  Pallas kernels  42.3 us (42%)
  waiting for transfers between devices  2.64 us (3%)
  local copies, waits for them, and re-layouts  1.65 us (2%)
  between operations  1.17 us (1%)
    all_to_all x2, starting transfers between devices, route(): return lax.all_to_all(x, 'rows', split_axis=0, concat_axis=0, tiled=True)  22.9 us
    ppermute x11, starting transfers between devices, across(): return lax.ppermute(x, 'tp', [(i, i ^ 1) for i in range(2 * RINGS)])  17.2 us
    ppermute x12, starting transfers between devices, around(): lax.ppermute(x, 'tp', [(2 * y + c, 2 * ((y + shift) % RINGS) + c) for y i...  13.1 us
    pallas_call x2, Pallas kernels, backward_own(): pl.pallas_call(functools.partial(backward_own_kernel, loads), in_specs=[A...  8.7 us
    pallas_call x2, Pallas kernels, backward_other(): pl.pallas_call(functools.partial(backward_other_kernel, masked), in_specs...  8.6 us
    pallas_call x2, Pallas kernels, forward_other(): pl.pallas_call(functools.partial(forward_other_kernel, loads, splits), in...  7.06 us
    pallas_call x4, Pallas kernels, forward_own(): pl.pallas_call(functools.partial(forward_own_kernel, split, first, close)...  5.75 us
    pallas_call x1, Pallas kernels, text_combine(): pl.pallas_call(text_combine_kernel, in_specs=[ANYWHERE] * 6, out_specs=[A...  3.54 us
  transfers between devices with their start and end apart: 25, of which 2 were waited for; matrix products, arithmetic and copies ran while one was open for 0% of the time, Pallas kernels for 36%

profile of v4, /device:TPU:1, one launch (start us, length us, event | category | flops | bytes accessed | tf_op | source)
XLA Modules:
  0.0 100.9 jit_solution(9044539604967518293)
XLA Ops:
  0.6 0.7 copy-done.4
  1.3 4.6 %forward_other.2 = (bf16[2,784,256]{2,1,0:T(8,128)(2,1)S(1)}, bf16[2,784,256]{2,1,0:T(8,128)(2,1)S(1)}, bf16[768,1024]{1,0:T(8,128)(2,1)S(1)}, f32[8,128]{1,0:T(...) custom-call(bf16[768,1024]{1,0:T(8,128)(2,1)} %x_from.2, f32[1,1024]{1,0:T(1,128)S(1)} %bitcast.8, ...), custom_call_target="tpu_custom_call" | custom-call | flops 1610612736 | bytes 4194304 | tf_op jit(solution)/shard_map/forward_other/pallas_call | solution.py:161
  5.9 3.3 %collective-permute-start = (bf16[2,784,256]{2,1,0:T(8,128)(2,1)S(1)}, bf16[2,784,256]{2,1,0:T(8,128)(2,1)S(1)}, u32[]{:S(2)}, u32[]{:S(2)}) collective-permute-start(bf16[2,784,256]{2,1,0:T(8,128)(2,1)S(1)} %get-tuple-element.57), channel_id=1, source_target_pairs={{0,1},{1,0},{2,3},{3,2},{4,5},{5,4},{6,7},{7,6},{8,9},{9,8},{10,11... | collective-permute-start | bytes 2408456 | tf_op jit(solution)/shard_map/ppermute | solution.py:591
  9.3 0.1 collective-permute-start.1
  9.4 2.4 %forward_other.3 = (bf16[4,400,256]{2,1,0:T(8,128)(2,1)S(1)}, bf16[384,1024]{1,0:T(8,128)(2,1)S(1)}, f32[8,128]{1,0:T(8,128)S(1)}) custom-call(bf16[384,1024]{1,0:T(8,128)(2,1)} %x_from.3, f32[1,1024]{1,0:T(1,128)S(1)} %bitcast.9, bf16[1024,1024]{1,0:T(8,128)(2,1)S(1)} %get-tuple-element.50.refs_0_.wk_ref, ...), custom_call_target="tpu_custom_call" | custom-call | flops 805306368 | bytes 1048576 | tf_op jit(solution)/shard_map/forward_other/pallas_call | solution.py:161
  11.8 0.5 collective-permute-start.2
  12.3 0.0 collective-permute-done.in_ref
  12.3 1.1 %forward_own.4 = (bf16[784,256]{1,0:T(8,128)(2,1)S(1)}, bf16[784,256]{1,0:T(8,128)(2,1)S(1)}) custom-call(bf16[768,1024]{1,0:T(8,128)(2,1)S(1)} %get-tuple-element.59.scaled_ref, f32[8,128]{1,0:T(8,128)S(1)} %get-tuple-element.56.lanes_ref, bf16[1024,1024]{1,0:T(8,128)(2,1)S(1)} %get-tuple-element.50.refs_0_.wk_ref, ...), custom_call_target="tpu_custom_call" | custom-call | flops 805306368 | bytes 1048576 | tf_op jit(solution)/shard_map/forward_own/pallas_call | solution.py:195
  13.4 0.0 collective-permute-done.1.in_ref
  13.4 1.8 %forward_own.5 = (bf16[784,256]{1,0:T(8,128)(2,1)S(1)}, bf16[784,256]{1,0:T(8,128)(2,1)}) custom-call(bf16[768,1024]{1,0:T(8,128)(2,1)S(1)} %get-tuple-element.59.scaled_ref, f32[8,128]{1,0:T(8,128)S(1)} %get-tuple-element.56.lanes_ref, bf16[1024,1024]{1,0:T(8,128)(2,1)S(1)} %get-tuple-element.50.refs_0_.wk_ref, ...), custom_call_target="tpu_custom_call" | custom-call | flops 805306368 | bytes 1048576 | tf_op jit(solution)/shard_map/forward_own/pallas_call | solution.py:195
  15.2 1.1 %collective-permute-start.5 = (bf16[784,256]{1,0:T(8,128)(2,1)S(1)}, bf16[784,256]{1,0:T(8,128)(2,1)S(1)}, u32[]{:S(2)}, u32[]{:S(2)}) collective-permute-start(bf16[784,256]{1,0:T(8,128)(2,1)S(1)} %get-tuple-element.68), channel_id=1, source_target_pairs={{0,6},{1,7},{2,0},{3,1},{4,2},{5,3},{6,4},{7,5},{8,14},{9,15},{10,... | collective-permute-start | bytes 1204232 | tf_op jit(solution)/shard_map/ppermute | solution.py:585
  16.3 0.5 collective-permute-start.3
  16.8 1.2 %collective-permute-start.4 = (bf16[784,256]{1,0:T(8,128)(2,1)S(1)}, bf16[784,256]{1,0:T(8,128)(2,1)S(1)}, u32[]{:S(2)}, u32[]{:S(2)}) collective-permute-start(bf16[784,256]{1,0:T(8,128)(2,1)S(1)} %get-tuple-element.67), channel_id=1, source_target_pairs={{0,4},{1,5},{2,6},{3,7},{4,0},{5,1},{6,2},{7,3},{8,12},{9,13},{10,... | collective-permute-start | bytes 1204232 | tf_op jit(solution)/shard_map/ppermute | solution.py:585
  17.9 1.4 %forward_own.6 = (bf16[400,256]{1,0:T(8,128)(2,1)}, bf16[400,256]{1,0:T(8,128)(2,1)}) custom-call(bf16[384,1024]{1,0:T(8,128)(2,1)S(1)} %get-tuple-element.65.scaled_ref, f32[8,128]{1,0:T(8,128)S(1)} %get-tuple-element.63.lanes_ref, bf16[1024,1024]{1,0:T(8,128)(2,1)S(1)} %get-tuple-element.50.refs_0_.wk_ref, ...), custom_call_target="tpu_custom_call" | custom-call | flops 402653184 | bytes 1048576 | tf_op jit(solution)/shard_map/forward_own/pallas_call | solution.py:195
  19.4 0.0 copy-start.6
  19.4 0.0 copy-start
  19.4 1.4 %forward_own.7 = (bf16[400,256]{1,0:T(8,128)(2,1)}, bf16[400,256]{1,0:T(8,128)(2,1)}) custom-call(bf16[384,1024]{1,0:T(8,128)(2,1)S(1)} %get-tuple-element.65.scaled_ref, f32[8,128]{1,0:T(8,128)S(1)} %get-tuple-element.63.lanes_ref, bf16[1024,1024]{1,0:T(8,128)(2,1)S(1)} %get-tuple-element.50.refs_0_.wk_ref, ...), custom_call_target="tpu_custom_call" | custom-call | flops 402653184 | bytes 1048576 | tf_op jit(solution)/shard_map/forward_own/pallas_call | solution.py:195
  20.9 2.4 %gather_targets.1 = bf16[768,256]{1,0:T(8,128)(2,1)} custom-call(s32[1,512]{1,0:T(1,128)S(1)} %bitcast.12, bf16[768,128]{1,0:T(8,128)(2,1)} %kt_from.1, bf16[768,128]{1,0:T(8,128)(2,1)} %vt_from.1), custom_call_target="tpu_custom_call" | custom-call | flops 268435456 | bytes 1048576 | tf_op jit(solution)/shard_map/gather_targets/pallas_call | solution.py:404
  23.3 11.0 %all-to-all-start = ((bf16[32,24,256]{2,1,0:T(8,128)(2,1)}), bf16[32,24,256]{2,1,0:T(8,128)(2,1)S(1)}, u32[]{:S(2)}, u32[]{:S(2)}) async-start(bf16[32,24,256]{2,1,0:T(8,128)(2,1)} %bitcast.19), calls=%async_computation | async-start | bytes 786432 | tf_op jit(solution)/shard_map/all_to_all | solution.py:595
  34.4 1.4 %collective-permute-start.7 = (bf16[400,256]{1,0:T(8,128)(2,1)}, bf16[400,256]{1,0:T(8,128)(2,1)S(1)}, u32[]{:S(2)}, u32[]{:S(2)}) collective-permute-start(bf16[400,256]{1,0:T(8,128)(2,1)} %get-tuple-element.72), channel_id=1, source_target_pairs={{0,4},{1,5},{2,6},{3,7},{4,0},{5,1},{6,2},{7,3},{8,12},{9,13},{10,... | collective-permute-start | bytes 614408 | tf_op jit(solution)/shard_map/ppermute | solution.py:585
  35.8 2.7 %collective-permute-start.8 = (bf16[400,256]{1,0:T(8,128)(2,1)}, bf16[400,256]{1,0:T(8,128)(2,1)S(1)}, u32[]{:S(2)}, u32[]{:S(2)}) collective-permute-start(bf16[400,256]{1,0:T(8,128)(2,1)} %get-tuple-element.74), channel_id=1, source_target_pairs={{0,6},{1,7},{2,0},{3,1},{4,2},{5,3},{6,4},{7,5},{8,14},{9,15},{10,... | collective-permute-start | bytes 614408 | tf_op jit(solution)/shard_map/ppermute | solution.py:585
  38.5 0.0 collective-permute-done.3.b
  38.5 0.0 collective-permute-start.6
  38.5 3.5 %text_combine.1 = (bf16[768,256]{1,0:T(8,128)(2,1)}, bf16[784,256]{1,0:T(8,128)(2,1)}, f32[768,128]{1,0:T(8,128)}) custom-call(bf16[784,256]{1,0:T(8,128)(2,1)S(1)} %copy-done, bf16[784,256]{1,0:T(8,128)(2,1)S(1)} %collective-permute-done.3.b, bf16[784,256]{1,0:T(8,128)(2,1)S(1)} %collective-permute-done.4.c, bf16[784,256]{1,0:T(8,128)(2,1)S(1)} %collective-permute-done.5.d, ...), custom_call_target="tpu_custom_call" | custom-call | flops 4194304 | bytes 4194304 | tf_op jit(solution)/shard_map/text_combine/pallas_call | solution.py:250
  42.0 0.0 copy-start.7
  42.0 1.3 %collective-permute-start.10 = (bf16[784,256]{1,0:T(8,128)(2,1)}, bf16[784,256]{1,0:T(8,128)(2,1)}, u32[]{:S(2)}, u32[]{:S(2)}) collective-permute-start(bf16[784,256]{1,0:T(8,128)(2,1)} %get-tuple-element.78.refs_2_), channel_id=1, source_target_pairs={{0,4},{1,5},{2,6},{3,7},{4,0},{5,1},{6,2},{7,3},{8,12},{9,13},{10,... | collective-permute-start | bytes 1204232 | tf_op jit(solution)/shard_map/ppermute | solution.py:585
  43.4 1.5 %collective-permute-done.8.d = bf16[400,256]{1,0:T(8,128)(2,1)S(1)} collective-permute-done((bf16[400,256]{1,0:T(8,128)(2,1)}, bf16[400,256]{1,0:T(8,128)(2,1)S(1)}, u32[]{:S(2)}, u32[]{:S(2)}) %collective-permute-start.8) | collective-permute-done | bytes 204832 | tf_op jit(solution)/shard_map/ppermute | solution.py:585
  44.9 2.9 %collective-permute-start.11 = (bf16[784,256]{1,0:T(8,128)(2,1)}, bf16[784,256]{1,0:T(8,128)(2,1)S(1)}, u32[]{:S(2)}, u32[]{:S(2)}) collective-permute-start(bf16[784,256]{1,0:T(8,128)(2,1)} %get-tuple-element.78.refs_2_), channel_id=1, source_target_pairs={{0,6},{1,7},{2,0},{3,1},{4,2},{5,3},{6,4},{7,5},{8,14},{9,15},{10,... | collective-permute-start | bytes 1204232 | tf_op jit(solution)/shard_map/ppermute | solution.py:585
  47.8 0.0 collective-permute-done.6.b
  47.8 0.0 collective-permute-start.9
  47.8 7.9 %collective-permute-start.12 = (bf16[784,256]{1,0:T(8,128)(2,1)}, bf16[784,256]{1,0:T(8,128)(2,1)S(1)}, u32[]{:S(2)}, u32[]{:S(2)}) collective-permute-start(bf16[784,256]{1,0:T(8,128)(2,1)} %get-tuple-element.78.refs_2_), channel_id=1, source_target_pairs={{0,1},{1,0},{2,3},{3,2},{4,5},{5,4},{6,7},{7,6},{8,9},{9,8},{10,11... | collective-permute-start | bytes 1204232 | tf_op jit(solution)/shard_map/ppermute | solution.py:591
  55.8 2.7 %image_keys.1 = (bf16[768,256]{1,0:T(8,128)(2,1)}, bf16[384,256]{1,0:T(8,128)(2,1)}, f32[384,128]{1,0:T(8,128)}) custom-call(bf16[400,256]{1,0:T(8,128)(2,1)S(1)} %copy-done.9, bf16[400,256]{1,0:T(8,128)(2,1)S(1)} %collective-permute-done.6.b, bf16[400,256]{1,0:T(8,128)(2,1)S(1)} %collective-permute-done.7.c, bf16[400,256]{1,0:T(8,128)(2,1)S(1)} %collective-permute-done.8.d, ...), custom_call_target="tpu_custom_call" | custom-call | flops 268435456 | bytes 1048576 | tf_op jit(solution)/shard_map/image_keys/pallas_call | solution.py:335
  58.4 0.0 copy-start.10
  58.4 0.9 copy-done.10
  59.4 1.8 %image_residual.1.refs_2_ = bf16[400,256]{1,0:T(8,128)(2,1)} custom-call(bf16[384,256]{1,0:T(8,128)(2,1)S(1)} %copy-done.10, bf16[768,256]{1,0:T(8,128)(2,1)S(1)} %bitcast.7, s32[1,512]{1,0:T(1,128)S(1)} %bitcast.14), custom_call_target="tpu_custom_call" | custom-call | flops 268435456 | bytes 1048576 | tf_op jit(solution)/shard_map/image_residual/pallas_call | solution.py:368
  61.2 0.4 collective-permute-start.17
  61.6 0.3 collective-permute-start.14
  61.9 1.1 %collective-permute-done.11.refs_5_ = bf16[784,256]{1,0:T(8,128)(2,1)S(1)} collective-permute-done((bf16[784,256]{1,0:T(8,128)(2,1)}, bf16[784,256]{1,0:T(8,128)(2,1)S(1)}, u32[]{:S(2)}, u32[]{:S(2)}) %collective-permute-start.11) | collective-permute-done | bytes 401440 | tf_op jit(solution)/shard_map/ppermute | solution.py:585
  63.0 1.4 %collective-permute-start.15 = (bf16[784,256]{1,0:T(8,128)(2,1)S(1)}, bf16[784,256]{1,0:T(8,128)(2,1)S(1)}, u32[]{:S(2)}, u32[]{:S(2)}) collective-permute-start(bf16[784,256]{1,0:T(8,128)(2,1)S(1)} %collective-permute-done.11.refs_5_), channel_id=1, source_target_pairs={{0,1},{1,0},{2,3},{3,2},{4,5},{5,4},{6,7},{7,6},{8,9},{9,8},{10,11... | collective-permute-start | bytes 1204232 | tf_op jit(solution)/shard_map/ppermute | solution.py:591
  64.5 0.0 collective-permute-done.9.refs_3_
  64.5 1.3 %collective-permute-start.13 = (bf16[784,256]{1,0:T(8,128)(2,1)S(1)}, bf16[784,256]{1,0:T(8,128)(2,1)S(1)}, u32[]{:S(2)}, u32[]{:S(2)}) collective-permute-start(bf16[784,256]{1,0:T(8,128)(2,1)S(1)} %collective-permute-done.9.refs_3_), channel_id=1, source_target_pairs={{0,1},{1,0},{2,3},{3,2},{4,5},{5,4},{6,7},{7,6},{8,9},{9,8},{10,11... | collective-permute-start | bytes 1204232 | tf_op jit(solution)/shard_map/ppermute | solution.py:591
  65.8 11.8 %all-to-all-start.1 = ((bf16[32,24,256]{2,1,0:T(8,128)(2,1)}), bf16[32,24,256]{2,1,0:T(8,128)(2,1)S(1)}, u32[]{:S(2)}, u32[]{:S(2)}) async-start(bf16[32,24,256]{2,1,0:T(8,128)(2,1)} %bitcast.18), calls=%async_computation.1 | async-start | bytes 786432 | tf_op jit(solution)/shard_map/all_to_all | solution.py:595
  77.6 0.0 copy-start.1
  77.6 1.4 %collective-permute-start.18 = (bf16[400,256]{1,0:T(8,128)(2,1)}, bf16[400,256]{1,0:T(8,128)(2,1)S(1)}, u32[]{:S(2)}, u32[]{:S(2)}) collective-permute-start(bf16[400,256]{1,0:T(8,128)(2,1)} %image_residual.1.refs_2_), channel_id=1, source_target_pairs={{0,6},{1,7},{2,0},{3,1},{4,2},{5,3},{6,4},{7,5},{8,14},{9,15},{10,... | collective-permute-start | bytes 614408 | tf_op jit(solution)/shard_map/ppermute | solution.py:585
  79.0 0.0 collective-permute-done.17.refs_4_
  79.0 0.2 collective-permute-start.16
  79.2 6.5 %backward_own.2 = (f32[768,1024]{1,0:T(8,128)S(1)}, f32[8,128]{1,0:T(8,128)S(1)}, bf16[1024,1024]{1,0:T(8,128)(2,1)S(1)}, bf16[1024,1024]{1,0:T(8,128)(2,1)S(1)}) custom-call(bf16[1024,1024]{1,0:T(8,128)(2,1)} %refs_0_.3, bf16[1024,1024]{1,0:T(8,128)(2,1)} %refs_1_.3, bf16[784,256]{1,0:T(8,128)(2,1)S(1)} %copy-done.7, ...), custom_call_target="tpu_custom_call" | custom-call | flops 1610612736 | bytes 2097152 | tf_op jit(solution)/shard_map/backward_own/pallas_call | solution.py:524
  85.7 0.0 collective-permute-done.14.rest_2_
  85.7 1.0 collective-permute-start.21
  86.7 0.0 collective-permute-done.18.refs_5_
  86.7 0.3 collective-permute-start.22
  87.0 0.0 collective-permute-done.16.refs_3_
  87.0 0.9 collective-permute-start.20
  87.9 0.0 collective-permute-done.15.rest_3_
  87.9 0.0 collective-permute-done.13.rest_1_
  87.9 5.1 %backward_other.2 = bf16[768,1024]{1,0:T(8,128)(2,1)} custom-call(bf16[768,1024]{1,0:T(8,128)(2,1)} %x_from.2, f32[1,1024]{1,0:T(1,128)S(1)} %bitcast.10, s32[1,512]{1,0:T(1,128)S(1)} %bitcast.15, f32[768,128]{1,0:T(8,128)S(1)} %copy-done.1, bf16[1024,1024]{1,0:T(8,128)(2,1)S(1)} %get-tuple-element.79.wk_ref.refs_0_, ...), custom_call_target="tpu_custom_call" | custom-call | flops 1610612736 | bytes 2097152 | tf_op jit(solution)/shard_map/backward_other/pallas_call | solution.py:565
  93.1 0.0 copy-start.3
  93.1 0.1 collective-permute-start.19
  93.2 2.2 %backward_own.3 = (f32[384,1024]{1,0:T(8,128)S(1)}, f32[8,128]{1,0:T(8,128)S(1)}) custom-call(bf16[1024,1024]{1,0:T(8,128)(2,1)S(1)} %get-tuple-element.79.wk_ref.refs_0_, bf16[1024,1024]{1,0:T(8,128)(2,1)S(1)} %get-tuple-element.80.wv_ref.refs_1_, bf16[400,256]{1,0:T(8,128)(2,1)S(1)} %copy-done.2, bf16[400,256]{1,0:T(8,128)(2,1)S(1)} %collective-permute-done.16.refs_3_, ...), custom_call_target="tpu_custom_call" | custom-call | flops 805306368 | bytes 2097152 | tf_op jit(solution)/shard_map/backward_own/pallas_call | solution.py:524
  95.4 0.0 collective-permute-done.21.rest_2_
  95.4 0.0 collective-permute-done.19.rest_0_
  95.4 3.5 %backward_other.3 = bf16[384,1024]{1,0:T(8,128)(2,1)} custom-call(bf16[384,1024]{1,0:T(8,128)(2,1)} %x_from.3, f32[1,1024]{1,0:T(1,128)S(1)} %bitcast.11, s32[1,512]{1,0:T(1,128)S(1)} %bitcast.16, f32[384,128]{1,0:T(8,128)S(1)} %copy-done.3, bf16[1024,1024]{1,0:T(8,128)(2,1)S(1)} %get-tuple-element.79.wk_ref.refs_0_, ...), custom_call_target="tpu_custom_call" | custom-call | flops 805306368 | bytes 2097152 | tf_op jit(solution)/shard_map/backward_other/pallas_call | solution.py:565
  98.9 0.0 all-to-all-done.1
  99.0 1.8 %merge.1 = (bf16[768,128]{1,0:T(8,128)(2,1)}, bf16[768,128]{1,0:T(8,128)(2,1)}) custom-call(s32[1,512]{1,0:T(1,128)S(1)} %bitcast.17, bf16[768,256]{1,0:T(8,128)(2,1)S(1)} %bitcast.6, bf16[768,256]{1,0:T(8,128)(2,1)S(1)} %copy-done.8), custom_call_target="tpu_custom_call" | custom-call | flops 268435456 | bytes 1048576 | tf_op jit(solution)/shard_map/merge/pallas_call | solution.py:451
  (23 shorter events, 0.1 us)
Async XLA Ops:
  0.6 0.7 copy-start.4
  1.3 8.1 %copy-start.5 = (f32[1024]{0:T(1024)S(1)}, f32[1024]{0:T(1024)}, u32[]{:S(2)}) copy-start(f32[1024]{0:T(1024)} %param.11) | copy-start | bytes 12292
  5.9 6.4 %collective-permute-start = (bf16[2,784,256]{2,1,0:T(8,128)(2,1)S(1)}, bf16[2,784,256]{2,1,0:T(8,128)(2,1)S(1)}, u32[]{:S(2)}, u32[]{:S(2)}) collective-permute-start(bf16[2,784,256]{2,1,0:T(8,128)(2,1)S(1)} %get-tuple-element.57), channel_id=1, source_target_pairs={{0,1},{1,0},{2,3},{3,2},{4,5},{5,4},{6,7},{7,6},{8,9},{9,8},{10,11... | collective-permute-start | bytes 2408456 | tf_op jit(solution)/shard_map/ppermute | solution.py:591
  9.3 4.1 %collective-permute-start.1 = (bf16[2,784,256]{2,1,0:T(8,128)(2,1)S(1)}, bf16[2,784,256]{2,1,0:T(8,128)(2,1)S(1)}, u32[]{:S(2)}, u32[]{:S(2)}) collective-permute-start(bf16[2,784,256]{2,1,0:T(8,128)(2,1)S(1)} %get-tuple-element.60), channel_id=1, source_target_pairs={{0,1},{1,0},{2,3},{3,2},{4,5},{5,4},{6,7},{7,6},{8,9},{9,8},{10,11... | collective-permute-start | bytes 2408456 | tf_op jit(solution)/shard_map/ppermute | solution.py:591
  11.8 6.1 %collective-permute-start.2 = (bf16[4,400,256]{2,1,0:T(8,128)(2,1)S(1)}, bf16[4,400,256]{2,1,0:T(8,128)(2,1)S(1)}, u32[]{:S(2)}, u32[]{:S(2)}) collective-permute-start(bf16[4,400,256]{2,1,0:T(8,128)(2,1)S(1)} %get-tuple-element.54), channel_id=1, source_target_pairs={{0,1},{1,0},{2,3},{3,2},{4,5},{5,4},{6,7},{7,6},{8,9},{9,8},{10,11... | collective-permute-start | bytes 2457608 | tf_op jit(solution)/shard_map/ppermute | solution.py:591
  15.2 20.6 %collective-permute-start.5 = (bf16[784,256]{1,0:T(8,128)(2,1)S(1)}, bf16[784,256]{1,0:T(8,128)(2,1)S(1)}, u32[]{:S(2)}, u32[]{:S(2)}) collective-permute-start(bf16[784,256]{1,0:T(8,128)(2,1)S(1)} %get-tuple-element.68), channel_id=1, source_target_pairs={{0,6},{1,7},{2,0},{3,1},{4,2},{5,3},{6,4},{7,5},{8,14},{9,15},{10,... | collective-permute-start | bytes 1204232 | tf_op jit(solution)/shard_map/ppermute | solution.py:585
  16.3 22.2 %collective-permute-start.3 = (bf16[784,256]{1,0:T(8,128)(2,1)S(1)}, bf16[784,256]{1,0:T(8,128)(2,1)S(1)}, u32[]{:S(2)}, u32[]{:S(2)}) collective-permute-start(bf16[784,256]{1,0:T(8,128)(2,1)S(1)} %get-tuple-element.58), channel_id=1, source_target_pairs={{0,2},{1,3},{2,4},{3,5},{4,6},{5,7},{6,0},{7,1},{8,10},{9,11},{10,... | collective-permute-start | bytes 1204232 | tf_op jit(solution)/shard_map/ppermute | solution.py:585
  16.8 21.7 %collective-permute-start.4 = (bf16[784,256]{1,0:T(8,128)(2,1)S(1)}, bf16[784,256]{1,0:T(8,128)(2,1)S(1)}, u32[]{:S(2)}, u32[]{:S(2)}) collective-permute-start(bf16[784,256]{1,0:T(8,128)(2,1)S(1)} %get-tuple-element.67), channel_id=1, source_target_pairs={{0,4},{1,5},{2,6},{3,7},{4,0},{5,1},{6,2},{7,3},{8,12},{9,13},{10,... | collective-permute-start | bytes 1204232 | tf_op jit(solution)/shard_map/ppermute | solution.py:585
  19.4 1.5 %copy-start.6 = (s32[512]{0:T(512)S(1)}, s32[512]{0:T(512)}, u32[]{:S(2)}) copy-start(s32[512]{0:T(512)} %param.10) | copy-start | bytes 6148
  19.4 19.1 %copy-start = (bf16[784,256]{1,0:T(8,128)(2,1)S(1)}, bf16[784,256]{1,0:T(8,128)(2,1)}, u32[]{:S(2)}) copy-start(bf16[784,256]{1,0:T(8,128)(2,1)} %get-tuple-element.61.a) | copy-start | bytes 1204228
  20.9 34.9 %copy-start.9 = (bf16[400,256]{1,0:T(8,128)(2,1)S(1)}, bf16[400,256]{1,0:T(8,128)(2,1)}, u32[]{:S(2)}) copy-start(bf16[400,256]{1,0:T(8,128)(2,1)} %get-tuple-element.70.a) | copy-start | bytes 614404
  23.3 35.1 %all-to-all-start = ((bf16[32,24,256]{2,1,0:T(8,128)(2,1)}), bf16[32,24,256]{2,1,0:T(8,128)(2,1)S(1)}, u32[]{:S(2)}, u32[]{:S(2)}) async-start(bf16[32,24,256]{2,1,0:T(8,128)(2,1)} %bitcast.19), calls=%async_computation | async-start | bytes 786432 | tf_op jit(solution)/shard_map/all_to_all | solution.py:595
  34.4 7.7 %collective-permute-start.7 = (bf16[400,256]{1,0:T(8,128)(2,1)}, bf16[400,256]{1,0:T(8,128)(2,1)S(1)}, u32[]{:S(2)}, u32[]{:S(2)}) collective-permute-start(bf16[400,256]{1,0:T(8,128)(2,1)} %get-tuple-element.72), channel_id=1, source_target_pairs={{0,4},{1,5},{2,6},{3,7},{4,0},{5,1},{6,2},{7,3},{8,12},{9,13},{10,... | collective-permute-start | bytes 614408 | tf_op jit(solution)/shard_map/ppermute | solution.py:585
  35.8 9.1 %collective-permute-start.8 = (bf16[400,256]{1,0:T(8,128)(2,1)}, bf16[400,256]{1,0:T(8,128)(2,1)S(1)}, u32[]{:S(2)}, u32[]{:S(2)}) collective-permute-start(bf16[400,256]{1,0:T(8,128)(2,1)} %get-tuple-element.74), channel_id=1, source_target_pairs={{0,6},{1,7},{2,0},{3,1},{4,2},{5,3},{6,4},{7,5},{8,14},{9,15},{10,... | collective-permute-start | bytes 614408 | tf_op jit(solution)/shard_map/ppermute | solution.py:585
  38.5 9.3 %collective-permute-start.6 = (bf16[400,256]{1,0:T(8,128)(2,1)}, bf16[400,256]{1,0:T(8,128)(2,1)S(1)}, u32[]{:S(2)}, u32[]{:S(2)}) collective-permute-start(bf16[400,256]{1,0:T(8,128)(2,1)} %get-tuple-element.71), channel_id=1, source_target_pairs={{0,2},{1,3},{2,4},{3,5},{4,6},{5,7},{6,0},{7,1},{8,10},{9,11},{10,... | collective-permute-start | bytes 614408 | tf_op jit(solution)/shard_map/ppermute | solution.py:585
  42.0 37.2 %copy-start.7 = (bf16[784,256]{1,0:T(8,128)(2,1)S(1)}, bf16[784,256]{1,0:T(8,128)(2,1)}, u32[]{:S(2)}) copy-start(bf16[784,256]{1,0:T(8,128)(2,1)} %get-tuple-element.78.refs_2_) | copy-start | bytes 1204228
  42.0 19.6 %collective-permute-start.10 = (bf16[784,256]{1,0:T(8,128)(2,1)}, bf16[784,256]{1,0:T(8,128)(2,1)}, u32[]{:S(2)}, u32[]{:S(2)}) collective-permute-start(bf16[784,256]{1,0:T(8,128)(2,1)} %get-tuple-element.78.refs_2_), channel_id=1, source_target_pairs={{0,4},{1,5},{2,6},{3,7},{4,0},{5,1},{6,2},{7,3},{8,12},{9,13},{10,... | collective-permute-start | bytes 1204232 | tf_op jit(solution)/shard_map/ppermute | solution.py:585
  44.9 18.2 %collective-permute-start.11 = (bf16[784,256]{1,0:T(8,128)(2,1)}, bf16[784,256]{1,0:T(8,128)(2,1)S(1)}, u32[]{:S(2)}, u32[]{:S(2)}) collective-permute-start(bf16[784,256]{1,0:T(8,128)(2,1)} %get-tuple-element.78.refs_2_), channel_id=1, source_target_pairs={{0,6},{1,7},{2,0},{3,1},{4,2},{5,3},{6,4},{7,5},{8,14},{9,15},{10,... | collective-permute-start | bytes 1204232 | tf_op jit(solution)/shard_map/ppermute | solution.py:585
  47.8 16.7 %collective-permute-start.9 = (bf16[784,256]{1,0:T(8,128)(2,1)}, bf16[784,256]{1,0:T(8,128)(2,1)S(1)}, u32[]{:S(2)}, u32[]{:S(2)}) collective-permute-start(bf16[784,256]{1,0:T(8,128)(2,1)} %get-tuple-element.78.refs_2_), channel_id=1, source_target_pairs={{0,2},{1,3},{2,4},{3,5},{4,6},{5,7},{6,0},{7,1},{8,10},{9,11},{10,... | collective-permute-start | bytes 1204232 | tf_op jit(solution)/shard_map/ppermute | solution.py:585
  47.8 29.8 %collective-permute-start.12 = (bf16[784,256]{1,0:T(8,128)(2,1)}, bf16[784,256]{1,0:T(8,128)(2,1)S(1)}, u32[]{:S(2)}, u32[]{:S(2)}) collective-permute-start(bf16[784,256]{1,0:T(8,128)(2,1)} %get-tuple-element.78.refs_2_), channel_id=1, source_target_pairs={{0,1},{1,0},{2,3},{3,2},{4,5},{5,4},{6,7},{7,6},{8,9},{9,8},{10,11... | collective-permute-start | bytes 1204232 | tf_op jit(solution)/shard_map/ppermute | solution.py:591
  58.4 0.9 copy-start.10
  61.2 17.8 %collective-permute-start.17 = (bf16[400,256]{1,0:T(8,128)(2,1)}, bf16[400,256]{1,0:T(8,128)(2,1)S(1)}, u32[]{:S(2)}, u32[]{:S(2)}) collective-permute-start(bf16[400,256]{1,0:T(8,128)(2,1)} %image_residual.1.refs_2_), channel_id=1, source_target_pairs={{0,4},{1,5},{2,6},{3,7},{4,0},{5,1},{6,2},{7,3},{8,12},{9,13},{10,... | collective-permute-start | bytes 614408 | tf_op jit(solution)/shard_map/ppermute | solution.py:585
  61.6 24.1 %collective-permute-start.14 = (bf16[784,256]{1,0:T(8,128)(2,1)}, bf16[784,256]{1,0:T(8,128)(2,1)S(1)}, u32[]{:S(2)}, u32[]{:S(2)}) collective-permute-start(bf16[784,256]{1,0:T(8,128)(2,1)} %collective-permute-done.10.refs_4_), channel_id=1, source_target_pairs={{0,1},{1,0},{2,3},{3,2},{4,5},{5,4},{6,7},{7,6},{8,9},{9,8},{10,11... | collective-permute-start | bytes 1204232 | tf_op jit(solution)/shard_map/ppermute | solution.py:591
  63.0 24.9 %collective-permute-start.15 = (bf16[784,256]{1,0:T(8,128)(2,1)S(1)}, bf16[784,256]{1,0:T(8,128)(2,1)S(1)}, u32[]{:S(2)}, u32[]{:S(2)}) collective-permute-start(bf16[784,256]{1,0:T(8,128)(2,1)S(1)} %collective-permute-done.11.refs_5_), channel_id=1, source_target_pairs={{0,1},{1,0},{2,3},{3,2},{4,5},{5,4},{6,7},{7,6},{8,9},{9,8},{10,11... | collective-permute-start | bytes 1204232 | tf_op jit(solution)/shard_map/ppermute | solution.py:591
  64.5 23.5 %collective-permute-start.13 = (bf16[784,256]{1,0:T(8,128)(2,1)S(1)}, bf16[784,256]{1,0:T(8,128)(2,1)S(1)}, u32[]{:S(2)}, u32[]{:S(2)}) collective-permute-start(bf16[784,256]{1,0:T(8,128)(2,1)S(1)} %collective-permute-done.9.refs_3_), channel_id=1, source_target_pairs={{0,1},{1,0},{2,3},{3,2},{4,5},{5,4},{6,7},{7,6},{8,9},{9,8},{10,11... | collective-permute-start | bytes 1204232 | tf_op jit(solution)/shard_map/ppermute | solution.py:591
  65.8 33.2 %all-to-all-start.1 = ((bf16[32,24,256]{2,1,0:T(8,128)(2,1)}), bf16[32,24,256]{2,1,0:T(8,128)(2,1)S(1)}, u32[]{:S(2)}, u32[]{:S(2)}) async-start(bf16[32,24,256]{2,1,0:T(8,128)(2,1)} %bitcast.18), calls=%async_computation.1 | async-start | bytes 786432 | tf_op jit(solution)/shard_map/all_to_all | solution.py:595
  77.6 10.3 %copy-start.1 = (f32[768,128]{1,0:T(8,128)S(1)}, f32[768,128]{1,0:T(8,128)}, u32[]{:S(2)}) copy-start(f32[768,128]{1,0:T(8,128)} %get-tuple-element.83.inverse_from) | copy-start | bytes 1179652
  77.6 9.1 %collective-permute-start.18 = (bf16[400,256]{1,0:T(8,128)(2,1)}, bf16[400,256]{1,0:T(8,128)(2,1)S(1)}, u32[]{:S(2)}, u32[]{:S(2)}) collective-permute-start(bf16[400,256]{1,0:T(8,128)(2,1)} %image_residual.1.refs_2_), channel_id=1, source_target_pairs={{0,6},{1,7},{2,0},{3,1},{4,2},{5,3},{6,4},{7,5},{8,14},{9,15},{10,... | collective-permute-start | bytes 614408 | tf_op jit(solution)/shard_map/ppermute | solution.py:585
  79.0 8.0 %collective-permute-start.16 = (bf16[400,256]{1,0:T(8,128)(2,1)}, bf16[400,256]{1,0:T(8,128)(2,1)S(1)}, u32[]{:S(2)}, u32[]{:S(2)}) collective-permute-start(bf16[400,256]{1,0:T(8,128)(2,1)} %image_residual.1.refs_2_), channel_id=1, source_target_pairs={{0,2},{1,3},{2,4},{3,5},{4,6},{5,7},{6,0},{7,1},{8,10},{9,11},{10,... | collective-permute-start | bytes 614408 | tf_op jit(solution)/shard_map/ppermute | solution.py:585
  85.7 9.6 %collective-permute-start.21 = (bf16[400,256]{1,0:T(8,128)(2,1)S(1)}, bf16[400,256]{1,0:T(8,128)(2,1)S(1)}, u32[]{:S(2)}, u32[]{:S(2)}) collective-permute-start(bf16[400,256]{1,0:T(8,128)(2,1)S(1)} %collective-permute-done.17.refs_4_), channel_id=1, source_target_pairs={{0,1},{1,0},{2,3},{3,2},{4,5},{5,4},{6,7},{7,6},{8,9},{9,8},{10,11... | collective-permute-start | bytes 614408 | tf_op jit(solution)/shard_map/ppermute | solution.py:591
  86.7 8.7 %collective-permute-start.22 = (bf16[400,256]{1,0:T(8,128)(2,1)S(1)}, bf16[400,256]{1,0:T(8,128)(2,1)S(1)}, u32[]{:S(2)}, u32[]{:S(2)}) collective-permute-start(bf16[400,256]{1,0:T(8,128)(2,1)S(1)} %collective-permute-done.18.refs_5_), channel_id=1, source_target_pairs={{0,1},{1,0},{2,3},{3,2},{4,5},{5,4},{6,7},{7,6},{8,9},{9,8},{10,11... | collective-permute-start | bytes 614408 | tf_op jit(solution)/shard_map/ppermute | solution.py:591
  87.0 8.4 %collective-permute-start.20 = (bf16[400,256]{1,0:T(8,128)(2,1)S(1)}, bf16[400,256]{1,0:T(8,128)(2,1)S(1)}, u32[]{:S(2)}, u32[]{:S(2)}) collective-permute-start(bf16[400,256]{1,0:T(8,128)(2,1)S(1)} %collective-permute-done.16.refs_3_), channel_id=1, source_target_pairs={{0,1},{1,0},{2,3},{3,2},{4,5},{5,4},{6,7},{7,6},{8,9},{9,8},{10,11... | collective-permute-start | bytes 614408 | tf_op jit(solution)/shard_map/ppermute | solution.py:591
  87.9 5.1 %copy-start.2 = (bf16[400,256]{1,0:T(8,128)(2,1)S(1)}, bf16[400,256]{1,0:T(8,128)(2,1)}, u32[]{:S(2)}) copy-start(bf16[400,256]{1,0:T(8,128)(2,1)} %image_residual.1.refs_2_) | copy-start | bytes 614404
  93.1 2.4 %copy-start.3 = (f32[384,128]{1,0:T(8,128)S(1)}, f32[384,128]{1,0:T(8,128)}, u32[]{:S(2)}) copy-start(f32[384,128]{1,0:T(8,128)} %get-tuple-element.75.inverse_from) | copy-start | bytes 589828
  93.1 2.3 %collective-permute-start.19 = (bf16[400,256]{1,0:T(8,128)(2,1)S(1)}, bf16[400,256]{1,0:T(8,128)(2,1)S(1)}, u32[]{:S(2)}, u32[]{:S(2)}) collective-permute-start(bf16[400,256]{1,0:T(8,128)(2,1)S(1)} %copy-done.2), channel_id=1, source_target_pairs={{0,1},{1,0},{2,3},{3,2},{4,5},{5,4},{6,7},{7,6},{8,9},{9,8},{10,11... | collective-permute-start | bytes 614408 | tf_op jit(solution)/shard_map/ppermute | solution.py:591
  95.4 3.5 %copy-start.8 = (bf16[768,256]{1,0:T(8,128)(2,1)S(1)}, bf16[768,256]{1,0:T(8,128)(2,1)}, u32[]{:S(2)}) copy-start(bf16[768,256]{1,0:T(8,128)(2,1)} %get-tuple-element.93.both_from) | copy-start | bytes 1179652

commit v5 on v4

v5 whole, which is shorter than its diff:
```python
import functools

import jax
import jax.numpy as jnp
from jax import lax
from jax.experimental import pallas as pl
from jax.experimental.pallas import tpu as pltpu
from jax.sharding import PartitionSpec as P

WIDTH = 8192
EPSILON = 1e-06
IMAGE_LEN = 24
EXTRA = 16
HEAD = 128
PAIR = 2 * HEAD
RINGS = 4
CHUNKS = 2 * RINGS
PIECE = 128
ABSENT = 8192.0

F32 = jnp.float32
BF16 = jnp.bfloat16
PARAMS = pltpu.CompilerParams(vmem_limit_bytes=24 * 2**20)
IN_VMEM = pl.BlockSpec(memory_space=pltpu.VMEM)
ANYWHERE = pl.BlockSpec(memory_space=pl.ANY)


def near(x):
    return pltpu.with_memory_space_constraint(x, pltpu.VMEM)


def far(x):
    return pltpu.with_memory_space_constraint(x, pltpu.HBM)


def after(x, *others):
    return lax.optimization_barrier((x, *others))[0]


def fetch(pairs, sems, first=0):
    copies = [
        pltpu.make_async_copy(source, target, sems.at[first + n])
        for n, (source, target) in enumerate(pairs)
    ]
    for copy in copies:
        copy.start()
    return copies


def finish(copies):
    for copy in copies:
        copy.wait()


SMALL = pl.CostEstimate(flops=2**20, bytes_accessed=2**16, transcendentals=0)


def same_index(count):
    shape = (count, count)
    return lax.broadcasted_iota(jnp.int32, shape, 0) == lax.broadcasted_iota(jnp.int32, shape, 1)


def with_piece(lanes, p, column):
    line = jnp.sum(jnp.where(same_index(HEAD), column, 0.0), axis=0, keepdims=True)
    return jnp.where(lax.broadcasted_iota(jnp.int32, lanes.shape, 0) == p, line, lanes)


def with_column(lanes, column, first=0):
    for p in range(column.shape[0] // HEAD):
        lanes = with_piece(lanes, first + p, column[p * HEAD : (p + 1) * HEAD, :])
    return lanes


def lanes_to_column(lanes, first, rows):
    eye = same_index(HEAD)
    pieces = [
        jnp.sum(jnp.where(eye, lanes[p : p + 1, :], 0.0), axis=1, keepdims=True)
        for p in range(first, first + rows // HEAD)
    ]
    return jnp.concatenate(pieces, axis=0)


def no_lanes():
    return jnp.zeros((EXTRA, HEAD), F32)


def split_extra(lanes):
    high = lanes.astype(BF16).astype(F32)
    return jnp.concatenate([high, lanes - high], axis=1).astype(BF16)


def join_extra(block):
    block = block.astype(F32)
    return block[:, 0:HEAD] + block[:, HEAD:]


def my_place():
    mine = lax.axis_index("tp")
    return lax.div(mine, 2), lax.rem(mine, 2)


def head_columns(d, other):
    ring, core = my_place()
    chip = lax.rem(ring + d, RINGS)
    return pl.ds(pl.multiple_of(HEAD * (2 * chip + (1 - core if other else core)), HEAD), HEAD)


def pair_weight(wk_ref, wv_ref, d, other):
    here = head_columns(d, other)
    return jnp.concatenate([wk_ref[:, here], wv_ref[:, here]], axis=1)


def forward_other_kernel(
    splits, text_ref, image_ref, gain_ref, wk_from, wv_from,
    early_ref, late_ref, scaled_ref, lanes_ref, wk_ref, wv_ref, held, sems, more,
):
    rows, depth = scaled_ref.shape
    pairs = []
    for ref in (text_ref, image_ref):
        for p in range(ref.shape[0] // PIECE):
            to = held.at[pl.ds(len(pairs) * PIECE, PIECE)]
            pairs.append((ref.at[pl.ds(p * PIECE, PIECE)], to))
    x_copies = fetch(pairs, sems)
    spans = [pl.ds(p * PAIR, PAIR) for p in range(depth // PAIR)]
    weights = [(wk_from.at[p], wk_ref.at[p]) for p in spans]
    weights += [(wv_from.at[p], wv_ref.at[p]) for p in spans]
    weights = fetch(weights, more)
    lanes = no_lanes()
    for p, copy in enumerate(x_copies):
        copy.wait()
        here = slice(p * PIECE, (p + 1) * PIECE)
        x = held[here, :].astype(F32)
        scaled_ref[here, :] = (gain_ref[...] * x).astype(BF16)
        lanes = with_piece(lanes, p, jnp.sum(x * x, axis=1, keepdims=True))
    lanes_ref[...] = lanes
    extra = split_extra(lanes)
    finish(weights)
    for split, send_ref in zip(splits, (early_ref, late_ref)):
        for n, d in enumerate(split):
            weight = pair_weight(wk_ref, wv_ref, d, True)
            product = jnp.dot(scaled_ref[...], weight, preferred_element_type=F32)
            send_ref[n, 0:rows, :] = product.astype(BF16)
            send_ref[n, rows:, :] = extra


def forward_other(text, image, gain, weights, splits):
    rows, width = text.shape[0] + image.shape[0], text.shape[1]
    out_shape = [pltpu.VMEM((len(split), rows + EXTRA, PAIR), BF16) for split in splits] + [
        pltpu.VMEM((rows, width), BF16),
        pltpu.VMEM((EXTRA, HEAD), F32),
    ]
    out_shape += [pltpu.VMEM(w.shape, BF16) for w in weights]
    return pl.pallas_call(
        functools.partial(forward_other_kernel, splits),
        in_specs=[ANYWHERE, ANYWHERE, IN_VMEM, ANYWHERE, ANYWHERE],
        out_specs=[IN_VMEM] * len(out_shape),
        out_shape=out_shape,
        scratch_shapes=[
            pltpu.VMEM((rows, width), BF16),
            pltpu.SemaphoreType.DMA((rows // PIECE,)),
            pltpu.SemaphoreType.DMA((2 * width // PAIR,)),
        ],
        compiler_params=PARAMS,
        cost_estimate=SMALL,
        name="forward_other",
    )(far(text), far(image), gain, *[far(w) for w in weights])


def forward_own_kernel(split, close, scaled_ref, lanes_ref, wk_ref, wv_ref, in_ref, *refs):
    out_refs, (held, sems) = refs[0 : len(split)], refs[len(split) :]
    rows = scaled_ref.shape[0]
    extra = split_extra(lanes_ref[...] + join_extra(in_ref[0, rows:, :]))
    copies = []
    for n, d in enumerate(split):
        weight = pair_weight(wk_ref, wv_ref, d, False)
        product = jnp.dot(scaled_ref[...], weight, preferred_element_type=F32)
        total = (product + in_ref[n, 0:rows, :].astype(F32)).astype(BF16)
        if d in close:
            out_refs[n][0:rows, :] = total
            out_refs[n][rows:, :] = extra
        else:
            held[n, 0:rows, :] = total
            held[n, rows:, :] = extra
            copies += fetch([(held.at[n], out_refs[n])], sems, n)
    finish(copies)


def forward_own(scaled, lanes, weights, arrived, split, close):
    rows, width = scaled.shape
    block = (rows + EXTRA, PAIR)
    sums = pl.pallas_call(
        functools.partial(forward_own_kernel, split, close),
        in_specs=[IN_VMEM] * 5,
        out_specs=[IN_VMEM if d in close else ANYWHERE for d in split],
        out_shape=[(pltpu.VMEM if d in close else pltpu.HBM)(block, BF16) for d in split],
        scratch_shapes=[
            pltpu.VMEM((len(split),) + block, BF16),
            pltpu.SemaphoreType.DMA((len(split),)),
        ],
        compiler_params=PARAMS,
        cost_estimate=SMALL,
        name="forward_own",
    )(near(scaled), near(lanes), *[near(w) for w in weights], near(arrived))
    return dict(zip(split, sums))


def inverse_of(squares, first, rows):
    return lax.rsqrt(lanes_to_column(squares, first, rows) / WIDTH + EPSILON)


def total_of(parts):
    total = parts[0].astype(F32)
    for d in range(1, RINGS):
        total = total + parts[d].astype(F32)
    return total


def residual(both, target):
    both = both.astype(F32)
    resid = (both - target.astype(F32)).astype(BF16)
    return resid, jnp.sum(resid.astype(F32) * both, axis=1, keepdims=True)


def text_combine_kernel(
    a, b, c, d, kt_ref, vt_ref, both_out, resid_out, squares_ref,
    parts, extras, targets, both_ref, resid_ref, sems, more, stores,
):
    rows, all_rows = both_ref.shape[0], a.shape[0] - EXTRA
    step = PAIR
    tail = pl.ds(all_rows, EXTRA)
    spare = fetch([(ref.at[tail], extras.at[n]) for n, ref in enumerate((a, b, c, d))], more)
    loads = []
    for begin in range(0, rows, step):
        span = pl.ds(begin, step)
        pairs = [(ref.at[span], parts.at[n, span]) for n, ref in enumerate((a, b, c, d))]
        pairs += [(ref.at[span], targets.at[n, span]) for n, ref in enumerate((kt_ref, vt_ref))]
        loads.append(fetch(pairs, sems, len(loads) * (RINGS + 2)))
    finish(spare)
    squares = total_of([join_extra(extras[n]) for n in range(RINGS)])
    squares_ref[...] = squares
    lanes, out = no_lanes(), []
    for n, begin in enumerate(range(0, rows, step)):
        here, span = slice(begin, begin + step), pl.ds(begin, step)
        inverse = inverse_of(squares, begin // HEAD, step)
        finish(loads[n])
        total = total_of([parts[m, here, :] for m in range(RINGS)])
        both = (inverse * total).astype(BF16)
        target = jnp.concatenate([targets[0, here, :], targets[1, here, :]], axis=1)
        resid, dots = residual(both, target)
        resid_ref[here, :] = resid
        both_ref[here, :] = both
        pairs = [(resid_ref.at[span], resid_out.at[span]), (both_ref.at[span], both_out.at[span])]
        out += fetch(pairs, stores, 2 * n)
        lanes = with_column(lanes, dots, begin // HEAD)
    resid_ref[rows:, :] = split_extra(lanes)
    tail = pl.ds(rows, EXTRA)
    out += fetch([(resid_ref.at[tail], resid_out.at[tail])], stores, len(out))
    finish(out)


def text_combine(parts, targets):
    rows = targets[0].shape[0]
    shapes = [((rows, PAIR), BF16), ((rows + EXTRA, PAIR), BF16)]
    steps = rows // PAIR
    return pl.pallas_call(
        text_combine_kernel,
        in_specs=[ANYWHERE] * 6,
        out_specs=[ANYWHERE] * 2 + [IN_VMEM],
        out_shape=[*[pltpu.HBM(*s) for s in shapes], jax.ShapeDtypeStruct((EXTRA, HEAD), F32)],
        scratch_shapes=[
            pltpu.VMEM((RINGS, rows, PAIR), BF16),
            pltpu.VMEM((RINGS, EXTRA, PAIR), BF16),
            pltpu.VMEM((2,) + targets[0].shape, BF16),
            *[pltpu.VMEM(*s) for s in shapes],
            pltpu.SemaphoreType.DMA((steps * (RINGS + 2),)),
            pltpu.SemaphoreType.DMA((RINGS,)),
            pltpu.SemaphoreType.DMA((2 * steps + 1,)),
        ],
        compiler_params=PARAMS,
        cost_estimate=SMALL,
        name="text_combine",
    )(far(parts[0]), *parts[1:], *[far(t) for t in targets])


def one_hot(match):
    return jnp.where(match, jnp.ones(match.shape, F32), jnp.zeros(match.shape, F32)).astype(BF16)


def slot_columns(rows, first, lanes):
    shape = (rows, lanes.shape[1])
    row = first + lax.broadcasted_iota(jnp.int32, shape, 0)
    begin = IMAGE_LEN * lax.broadcasted_iota(jnp.int32, shape, 1)
    inside = (row >= begin) & (row < begin + IMAGE_LEN)
    value = lanes + (row - begin).astype(F32)
    return jnp.sum(jnp.where(inside, value, 0.0), axis=1, keepdims=True)


def slot_lanes(rows, column):
    shape = (column.shape[0], rows)
    row = lax.broadcasted_iota(jnp.int32, shape, 1)
    begin = IMAGE_LEN * lax.broadcasted_iota(jnp.int32, shape, 0)
    inside = (row >= begin) & (row < begin + IMAGE_LEN)
    value = column + (row - begin).astype(F32)
    return jnp.sum(jnp.where(inside, value, 0.0), axis=0, keepdims=True)


def first_rows(starts_ref, rows):
    shards = lax.axis_size("rows")
    images = starts_ref.shape[1] // shards
    offset = starts_ref[...].astype(F32) - (lax.axis_index("rows") * rows).astype(F32)
    value = jnp.where((offset >= 0.0) & (offset < rows), offset + ABSENT, 0.0)
    shape = (shards, starts_ref.shape[1])
    lane = lax.broadcasted_iota(jnp.int32, shape, 1)
    begin = images * lax.broadcasted_iota(jnp.int32, shape, 0)
    mine = (lane >= begin) & (lane < begin + images)
    column = jnp.sum(jnp.where(mine, value, 0.0), axis=1, keepdims=True) - ABSENT
    return column, jnp.sum(jnp.where(same_index(shards), column, 0.0), axis=0, keepdims=True)


def destinations(starts_ref, rows):
    images = starts_ref.shape[1] // lax.axis_size("rows")
    slot = IMAGE_LEN * jnp.floor((starts_ref[...].astype(F32) + 0.5) / rows)
    shape = (images, starts_ref.shape[1])
    image = lax.axis_index("rows") * images + lax.broadcasted_iota(jnp.int32, shape, 0)
    mine = lax.broadcasted_iota(jnp.int32, shape, 1) == image
    column = jnp.sum(jnp.where(mine, slot, 0.0), axis=1, keepdims=True)
    return jnp.sum(jnp.where(same_index(images), column, 0.0), axis=0, keepdims=True), column


def image_keys_kernel(
    seq_rows, a, b, c, d, starts_ref, squares_ref, send_out, both_out,
    parts, send_ref, both_ref, sems,
):
    rows, slots = both_ref.shape[0], send_ref.shape[0]
    span = pl.ds(seq_rows, rows)
    copies = fetch([(ref.at[span], parts.at[n]) for n, ref in enumerate((a, b, c, d))], sems)
    _, dest = destinations(starts_ref, seq_rows)
    slot = lax.broadcasted_iota(jnp.int32, (slots, rows), 0).astype(F32)
    picks = one_hot(slot == slot_lanes(rows, dest))
    inverse = inverse_of(squares_ref[...], seq_rows // HEAD, rows)
    finish(copies)
    both = (inverse * total_of([parts[n] for n in range(RINGS)])).astype(BF16)
    both_ref[...] = both
    out = fetch([(both_ref, both_out)], sems)
    send_ref[...] = jnp.dot(picks, both, preferred_element_type=F32).astype(BF16)
    out += fetch([(send_ref, send_out)], sems, 1)
    finish(out)


def image_keys(parts, starts, squares, rows, seq_rows):
    slots = lax.axis_size("rows") * IMAGE_LEN
    shapes = [((slots, PAIR), BF16), ((rows, PAIR), BF16)]
    return pl.pallas_call(
        functools.partial(image_keys_kernel, seq_rows),
        in_specs=[ANYWHERE] * RINGS + [IN_VMEM] * 2,
        out_specs=[ANYWHERE] * 2,
        out_shape=[pltpu.HBM(*s) for s in shapes],
        scratch_shapes=[
            pltpu.VMEM((RINGS, rows, PAIR), BF16),
            *[pltpu.VMEM(*s) for s in shapes],
            pltpu.SemaphoreType.DMA((RINGS,)),
        ],
        compiler_params=PARAMS,
        cost_estimate=SMALL,
        name="image_keys",
    )(far(parts[0]), *parts[1:], starts, squares)


def image_residual_kernel(
    seq_rows, both_from, arrived_from, starts_ref, resid_out, both_ref, arrived_ref, resid_ref, sems
):
    copies = fetch([(both_from, both_ref), (arrived_from, arrived_ref)], sems)
    rows = both_ref.shape[0]
    dest, _ = destinations(starts_ref, seq_rows)
    shape = (rows, arrived_ref.shape[0])
    slot = lax.broadcasted_iota(jnp.int32, shape, 1).astype(F32)
    picks = one_hot(slot == slot_columns(rows, 0, dest))
    finish(copies)
    target = jnp.dot(picks, arrived_ref[...], preferred_element_type=F32)
    resid, dots = residual(both_ref[...], target)
    resid_ref[0:rows, :] = resid
    resid_ref[rows:, :] = split_extra(with_column(no_lanes(), dots))
    finish(fetch([(resid_ref, resid_out)], sems))


def image_residual(both, arrived, starts, seq_rows):
    shape = (both.shape[0] + EXTRA, PAIR)
    return pl.pallas_call(
        functools.partial(image_residual_kernel, seq_rows),
        in_specs=[ANYWHERE, ANYWHERE, IN_VMEM],
        out_specs=ANYWHERE,
        out_shape=pltpu.HBM(shape, BF16),
        scratch_shapes=[
            pltpu.VMEM(both.shape, BF16),
            pltpu.VMEM(arrived.shape, BF16),
            pltpu.VMEM(shape, BF16),
            pltpu.SemaphoreType.DMA((2,)),
        ],
        compiler_params=PARAMS,
        cost_estimate=SMALL,
        name="image_residual",
    )(far(both), arrived, starts)


def gather_kernel(starts_ref, kt_from, vt_from, out_ref, halves, target_ref, held, sems):
    copies = fetch([(kt_from, halves.at[0]), (vt_from, halves.at[1])], sems)
    rows = target_ref.shape[0]
    _, first = first_rows(starts_ref, rows)
    finish(copies)
    target_ref[:, 0:HEAD] = halves[0]
    target_ref[:, HEAD:] = halves[1]
    for begin in range(0, out_ref.shape[0], PAIR):
        place = slot_columns(PAIR, begin, first)
        position = lax.broadcasted_iota(jnp.int32, (PAIR, rows), 1).astype(F32)
        picked = jnp.dot(
            one_hot(position == place), target_ref[...], preferred_element_type=F32
        )
        held[begin : begin + PAIR, :] = picked.astype(BF16)
    finish(fetch([(held, out_ref)], sems))


def gather_targets(starts, key_target, value_target):
    shape = (lax.axis_size("rows") * IMAGE_LEN, PAIR)
    return pl.pallas_call(
        gather_kernel,
        in_specs=[IN_VMEM, ANYWHERE, ANYWHERE],
        out_specs=ANYWHERE,
        out_shape=pltpu.HBM(shape, BF16),
        scratch_shapes=[
            pltpu.VMEM((2,) + key_target.shape, BF16),
            pltpu.VMEM((key_target.shape[0], PAIR), BF16),
            pltpu.VMEM(shape, BF16),
            pltpu.SemaphoreType.DMA((2,)),
        ],
        compiler_params=PARAMS,
        cost_estimate=SMALL,
        name="gather_targets",
    )(starts, far(key_target), far(value_target))


def image_rows_mask(rows, first_row, first_lanes):
    shape = (rows, first_lanes.shape[1])
    row = (first_row + lax.broadcasted_iota(jnp.int32, shape, 0)).astype(F32)
    inside = (row >= first_lanes) & (row < first_lanes + IMAGE_LEN)
    return jnp.sum(jnp.where(inside, 1.0, 0.0), axis=1, keepdims=True) > 0.5


def merge_kernel(
    starts_ref, arrived_from, both_from, keys_out, values_out,
    arrived_ref, both_ref, keys_ref, values_ref, sems,
):
    copies = fetch([(arrived_from, arrived_ref), (both_from, both_ref)], sems)
    slots, rows = arrived_ref.shape[0], both_ref.shape[0]
    column, lanes = first_rows(starts_ref, rows)
    place = slot_lanes(slots, column)
    finish(copies)
    for begin in range(0, rows, PAIR):
        row = begin + lax.broadcasted_iota(jnp.int32, (PAIR, slots), 0)
        picks = one_hot(row.astype(F32) == place)
        landed = jnp.dot(picks, arrived_ref[...], preferred_element_type=F32)
        here = slice(begin, begin + PAIR)
        mask = image_rows_mask(PAIR, begin, lanes)
        both = jnp.where(mask, landed, both_ref[here, :].astype(F32)).astype(BF16)
        keys_ref[here, :] = both[:, 0:HEAD]
        values_ref[here, :] = both[:, HEAD:]
    finish(fetch([(keys_ref, keys_out), (values_ref, values_out)], sems))


def merge(starts, arrived, both):
    shape = (both.shape[0], HEAD)
    return pl.pallas_call(
        merge_kernel,
        in_specs=[IN_VMEM, ANYWHERE, ANYWHERE],
        out_specs=[ANYWHERE] * 2,
        out_shape=[jax.ShapeDtypeStruct(shape, BF16)] * 2,
        scratch_shapes=[
            pltpu.VMEM(arrived.shape, BF16),
            pltpu.VMEM(both.shape, BF16),
            pltpu.VMEM(shape, BF16),
            pltpu.VMEM(shape, BF16),
            pltpu.SemaphoreType.DMA((2,)),
        ],
        compiler_params=PARAMS,
        cost_estimate=SMALL,
        name="merge",
    )(starts, arrived, both)


def hold_kernel(*refs):
    count = (len(refs) - 1) // 2
    copies = []
    for n, (source, target) in enumerate(zip(refs[0:count], refs[count : 2 * count])):
        half = source.shape[0] // 2
        spans = [pl.ds(0, half), pl.ds(half, half)]
        copies += fetch([(source.at[p], target.at[p]) for p in spans], refs[-1], 2 * n)
    finish(copies)


def hold(*arrays):
    return pl.pallas_call(
        hold_kernel,
        in_specs=[ANYWHERE] * len(arrays),
        out_specs=[IN_VMEM] * len(arrays),
        out_shape=[pltpu.VMEM(x.shape, x.dtype) for x in arrays],
        scratch_shapes=[pltpu.SemaphoreType.DMA((2 * len(arrays),))],
        compiler_params=PARAMS,
        cost_estimate=SMALL,
        name="hold",
    )(*[far(x) for x in arrays])


TILE = 256


def backward_kernel(first, masked, x_ref, gain_ref, starts_ref, squares_ref, wk_ref, wv_ref, *rest):
    resids, (out_ref, keys_all, values_all, held, sems) = rest[0:CHUNKS], rest[CHUNKS:]
    rows, width = x_ref.shape
    if masked:
        mask = image_rows_mask(rows, 0, first_rows(starts_ref, rows)[1])
    inverse = inverse_of(squares_ref[...], first, rows)
    lanes = no_lanes()
    for n, ref in enumerate(resids):
        here = head_columns((RINGS - n) % RINGS, n >= RINGS)
        keys_all[:, here] = ref[0:rows, 0:HEAD]
        values_all[:, here] = ref[0:rows, HEAD:]
        lanes = lanes + join_extra(ref[rows:, :])
    coefficient = inverse * inverse * lanes_to_column(lanes, 0, rows) / WIDTH
    contract = (((1,), (1,)), ((), ()))
    out = []
    for n in range(width // TILE):
        here = slice(n * TILE, (n + 1) * TILE)
        back = lax.dot_general(
            keys_all[...], wk_ref[here, :], contract, preferred_element_type=F32
        ) + lax.dot_general(values_all[...], wv_ref[here, :], contract, preferred_element_type=F32)
        grad = gain_ref[:, here] * inverse * back - coefficient * x_ref[:, here].astype(F32)
        if masked:
            grad = jnp.where(mask, 0.0, grad)
        held[:, here] = grad.astype(BF16)
        span = pl.ds(n * TILE, TILE)
        out += fetch([(held.at[:, span], out_ref.at[:, span])], sems, n)
    finish(out)


def backward(x, gain, squares, first, weights, starts, resids, masked):
    rows, width = x.shape
    columns = weights[0].shape[1]
    return pl.pallas_call(
        functools.partial(backward_kernel, first, masked),
        in_specs=[IN_VMEM] * (6 + CHUNKS),
        out_specs=ANYWHERE,
        out_shape=jax.ShapeDtypeStruct(x.shape, BF16),
        scratch_shapes=[
            pltpu.VMEM((rows, columns), BF16),
            pltpu.VMEM((rows, columns), BF16),
            pltpu.VMEM(x.shape, BF16),
            pltpu.SemaphoreType.DMA((width // TILE,)),
        ],
        compiler_params=PARAMS,
        cost_estimate=SMALL,
        name="backward",
    )(near(x), gain, starts, squares, *[near(w) for w in weights], *[near(r) for r in resids])


def around(x, shift):
    return lax.ppermute(
        x, "tp", [(2 * y + c, 2 * ((y + shift) % RINGS) + c) for y in range(RINGS) for c in range(2)]
    )


def across(x):
    return lax.ppermute(x, "tp", [(i, i ^ 1) for i in range(2 * RINGS)])


def across_in_turn(own, before):
    other = []
    for x in own:
        before = across(after(x, before))
        other.append(before)
    return other


def route(x):
    return lax.all_to_all(x, "rows", split_axis=0, concat_axis=0, tiled=True)


def on_device(
    text_embed,
    image_embed,
    image_start,
    norm_gain,
    key_weight,
    value_weight,
    key_target,
    value_target,
):
    seq_rows = text_embed.shape[0]
    gain = norm_gain[None, :]
    starts = image_start[None, :]
    weights = (key_weight, value_weight)
    targets = (key_target, value_target)

    images = image_embed.shape[0]
    early, late = (2,), (1, 3, 0)
    sent_early, sent_late, scaled, lanes, *held = forward_other(
        text_embed, image_embed, gain, weights, (early, late)
    )
    arrived_early = across(sent_early)
    arrived_late = across(after(sent_late, arrived_early))
    close = (2, 1, 3)
    sums = forward_own(scaled, lanes, held, arrived_early, early, close)
    sums |= forward_own(after(scaled, sums[2]), lanes, held, arrived_late, late, close)
    parts = [sums[0]] + [around(sums[d], d) for d in (2, 1, 3)]
    goals = route(gather_targets(after(starts, sums[0]), *targets))

    both, resid, squares = text_combine(parts, targets)
    resid1, resid2, resid3 = [around(resid, d) for d in (1, 2, 3)]
    parts[0] = after(parts[0], resid)
    image_send, image_both = image_keys(parts, starts, squares, images, seq_rows)
    image_resid = image_residual(image_both, goals, starts, seq_rows)
    landed = route(after(image_send, image_resid))
    image_resid2 = around(image_resid, 2)
    image_resid1 = around(after(image_resid, resid1), 1)
    image_resid3 = around(after(image_resid, resid3), 3)

    *held, text_held, image_held = hold(
        *weights, after(text_embed, resid1, resid2, resid3), after(image_embed, image_resid)
    )
    own = [resid, resid1, resid3, resid2]
    other = [across(r) for r in own]
    resids = [x[n] for x in (own, other) for n in (0, 1, 3, 2)]
    text_grad = backward(text_held, gain, squares, 0, held, starts, resids, True)
    own = [image_resid, image_resid1, image_resid3, image_resid2]
    own[1], own[2] = after(own[1], text_grad), after(own[2], text_grad)
    other = [across(r) for r in own]
    resids = [x[n] for x in (own, other) for n in (0, 1, 3, 2)]
    resids[0] = after(resids[0], text_grad)
    image_grad = backward(
        image_held, gain, squares, seq_rows // HEAD, held, starts, resids, False
    )
    keys, values = merge(after(starts, image_grad), landed, both)
    return (keys, values, text_grad, image_grad)


def solution(mesh):
    in_specs = (
        P("rows", "tp"),
        P("rows", "tp"),
        P(),
        P("tp"),
        P("tp", None),
        P("tp", None),
        P("rows", "tp"),
        P("rows", "tp"),
    )
    out_specs = (P("rows", "tp"), P("rows", "tp"), P("rows", "tp"), P("rows", "tp"))
    return jax.shard_map(
        on_device, mesh=mesh, in_specs=in_specs, out_specs=out_specs, check_vma=False
    )
```

time: 101 us -> 96.4 us (0.954)
  waiting for transfers between devices: 2.64 us -> 18.6 us
  starting transfers between devices: 53.2 us -> 40.8 us
  Pallas kernels: 42.3 us -> 34.8 us
    ppermute x12 -> x9, waiting for transfers between devices: 2.61 us -> 14.4 us  [around(): lax.ppermute(x, 'tp', [(2 * y + c, 2 * ((y + shift) % RINGS) + c) for y i...]
    ppermute x11 -> x10, starting transfers between devices: 17.2 us -> 9.45 us  [across(): return lax.ppermute(x, 'tp', [(i, i ^ 1) for i in range(2 * RINGS)])]
    pallas_call x10 -> x6, Pallas kernels: 30.1 us -> 22.9 us  [the longest x2 9.72 us: backward(): pl.pallas_call(functools.partial(backward_kernel, first, masked), in_spec...]
    ppermute x11 -> x10, waiting for transfers between devices: 0.03 us -> 4.23 us  [across(): return lax.ppermute(x, 'tp', [(i, i ^ 1) for i in range(2 * RINGS)])]
    ppermute x12 -> x9, starting transfers between devices: 13.1 us -> 10.5 us  [around(): lax.ppermute(x, 'tp', [(2 * y + c, 2 * ((y + shift) % RINGS) + c) for y i...]
    all_to_all x2, starting transfers between devices: 22.9 us -> 20.9 us  [route(): return lax.all_to_all(x, 'rows', split_axis=0, concat_axis=0, tiled=True)]
  transfers between devices with their start and end apart: 25 -> 21, of which waited for: 2 -> 6; matrix products, arithmetic and copies ran while one was open for 0% -> 0% of each run, Pallas kernels for 36% -> 28%
where the time goes in v5:
time: 96.4 us; the launch traced here: 95.9 us
  starting transfers between devices  40.8 us (42%)
  Pallas kernels  34.8 us (36%)
  waiting for transfers between devices  18.6 us (19%)
  between operations  1.03 us (1%)
    all_to_all x2, starting transfers between devices, route(): return lax.all_to_all(x, 'rows', split_axis=0, concat_axis=0, tiled=True)  20.9 us
    ppermute x9, waiting for transfers between devices, around(): lax.ppermute(x, 'tp', [(2 * y + c, 2 * ((y + shift) % RINGS) + c) for y i...  14.4 us
    ppermute x9, starting transfers between devices, around(): lax.ppermute(x, 'tp', [(2 * y + c, 2 * ((y + shift) % RINGS) + c) for y i...  10.5 us
    pallas_call x2, Pallas kernels, backward(): pl.pallas_call(functools.partial(backward_kernel, first, masked), in_spec...  9.72 us
    ppermute x10, starting transfers between devices, across(): return lax.ppermute(x, 'tp', [(i, i ^ 1) for i in range(2 * RINGS)])  9.45 us
    pallas_call x1, Pallas kernels, forward_other(): pl.pallas_call(functools.partial(forward_other_kernel, splits), in_specs=...  5.7 us
    pallas_call x2, Pallas kernels, forward_own(): pl.pallas_call(functools.partial(forward_own_kernel, split, close), in_sp...  4.56 us
    ppermute x10, waiting for transfers between devices, across(): return lax.ppermute(x, 'tp', [(i, i ^ 1) for i in range(2 * RINGS)])  4.23 us
  transfers between devices with their start and end apart: 21, of which 6 were waited for; matrix products, arithmetic and copies ran while one was open for 0% of the time, Pallas kernels for 28%

profile of v5, /device:TPU:1, one launch (start us, length us, event | category | flops | bytes accessed | tf_op | source)
XLA Modules:
  0.0 95.9 jit_solution(6686247775404037835)
XLA Ops:
  0.6 0.0 copy-start.4
  0.6 0.7 copy-done.4
  1.3 5.7 %forward_other.1 = (bf16[1,1168,256]{2,1,0:T(8,128)(2,1)S(1)}, bf16[3,1168,256]{2,1,0:T(8,128)(2,1)S(1)}, bf16[1152,1024]{1,0:T(8,128)(2,1)S(1)}, f32[16,128]{1,...) custom-call(bf16[768,1024]{1,0:T(8,128)(2,1)} %refs_2_, bf16[384,1024]{1,0:T(8,128)(2,1)} %refs_3_, ...), custom_call_target="tpu_custom_call" | custom-call | flops 1048576 | bytes 65536 | tf_op jit(solution)/shard_map/forward_other/pallas_call | solution.py:153
  7.0 3.3 %collective-permute-start = (bf16[1,1168,256]{2,1,0:T(8,128)(2,1)S(1)}, bf16[1,1168,256]{2,1,0:T(8,128)(2,1)S(1)}, u32[]{:S(2)}, u32[]{:S(2)}) collective-permute-start(bf16[1,1168,256]{2,1,0:T(8,128)(2,1)S(1)} %get-tuple-element.41), channel_id=1, source_target_pairs={{0,1},{1,0},{2,3},{3,2},{4,5},{5,4},{6,7},{7,6},{8,9},{9,8},{10,11... | collective-permute-start | bytes 1794056 | tf_op jit(solution)/shard_map/ppermute | solution.py:571
  10.4 1.6 %collective-permute-done.in_ref = bf16[1,1168,256]{2,1,0:T(8,128)(2,1)S(1)} collective-permute-done((bf16[1,1168,256]{2,1,0:T(8,128)(2,1)S(1)}, bf16[1,1168,256]{2,1,0:T(8,128)(2,1)S(1)}, u32[]{:S(2)}, u32[]{:S(2)}) %collective-permute-start) | collective-permute-done | bytes 598048 | tf_op jit(solution)/shard_map/ppermute | solution.py:571
  12.0 0.4 collective-permute-start.1
  12.4 0.8 forward_own.2
  13.2 0.0 copy-start.3
  13.2 1.3 %collective-permute-start.2 = (bf16[1168,256]{1,0:T(8,128)(2,1)S(1)}, bf16[1168,256]{1,0:T(8,128)(2,1)S(1)}, u32[]{:S(2)}, u32[]{:S(2)}) collective-permute-start(bf16[1168,256]{1,0:T(8,128)(2,1)S(1)} %forward_own.2), channel_id=1, source_target_pairs={{0,4},{1,5},{2,6},{3,7},{4,0},{5,1},{6,2},{7,3},{8,12},{9,13},{10,... | collective-permute-start | bytes 1794056 | tf_op jit(solution)/shard_map/ppermute | solution.py:565
  14.5 1.2 %collective-permute-done.1.in_ref = bf16[3,1168,256]{2,1,0:T(8,128)(2,1)S(1)} collective-permute-done((bf16[3,1168,256]{2,1,0:T(8,128)(2,1)S(1)}, bf16[3,1168,256]{2,1,0:T(8,128)(2,1)S(1)}, u32[]{:S(2)}, u32[]{:S(2)}) %collective-permute-start.1) | collective-permute-done | bytes 1794080 | tf_op jit(solution)/shard_map/ppermute | solution.py:571
  15.7 3.7 %forward_own.3 = (bf16[1168,256]{1,0:T(8,128)(2,1)}, bf16[1168,256]{1,0:T(8,128)(2,1)S(1)}, bf16[1168,256]{1,0:T(8,128)(2,1)}) custom-call(bf16[1152,1024]{1,0:T(8,128)(2,1)S(1)} %get-tuple-element.42.scaled_ref, f32[16,128]{1,0:T(8,128)S(1)} %get-tuple-element.38.lanes_ref, bf16[1024,1024]{1,0:T(8,128)(2,1)S(1)} %get-tuple-element.39.wk_ref, ...), custom_call_target="tpu_custom_call" | custom-call | flops 1048576 | bytes 65536 | tf_op jit(solution)/shard_map/forward_own/pallas_call | solution.py:191
  19.4 0.1 collective-permute-start.3
  19.5 2.7 %collective-permute-start.4 = (bf16[1168,256]{1,0:T(8,128)(2,1)S(1)}, bf16[1168,256]{1,0:T(8,128)(2,1)S(1)}, u32[]{:S(2)}, u32[]{:S(2)}) collective-permute-start(bf16[1168,256]{1,0:T(8,128)(2,1)S(1)} %get-tuple-element.47), channel_id=1, source_target_pairs={{0,6},{1,7},{2,0},{3,1},{4,2},{5,3},{6,4},{7,5},{8,14},{9,15},{10,... | collective-permute-start | bytes 1794056 | tf_op jit(solution)/shard_map/ppermute | solution.py:565
  22.2 0.0 copy-done.3
  22.2 2.4 %gather_targets.1 = bf16[768,256]{1,0:T(8,128)(2,1)} custom-call(s32[1,512]{1,0:T(1,128)S(1)} %bitcast.8, bf16[768,128]{1,0:T(8,128)(2,1)} %kt_from.1, bf16[768,128]{1,0:T(8,128)(2,1)} %vt_from.1), custom_call_target="tpu_custom_call" | custom-call | flops 1048576 | bytes 65536 | tf_op jit(solution)/shard_map/gather_targets/pallas_call | solution.py:424
  24.6 9.8 %all-to-all-start = ((bf16[32,24,256]{2,1,0:T(8,128)(2,1)}), bf16[32,24,256]{2,1,0:T(8,128)(2,1)S(1)}, u32[]{:S(2)}, u32[]{:S(2)}) async-start(bf16[32,24,256]{2,1,0:T(8,128)(2,1)} %bitcast.17), calls=%async_computation | async-start | bytes 786432 | tf_op jit(solution)/shard_map/all_to_all | solution.py:583
  34.4 0.0 collective-permute-done.2.b
  34.4 8.7 %collective-permute-done.3.c = bf16[1168,256]{1,0:T(8,128)(2,1)S(1)} collective-permute-done((bf16[1168,256]{1,0:T(8,128)(2,1)}, bf16[1168,256]{1,0:T(8,128)(2,1)S(1)}, u32[]{:S(2)}, u32[]{:S(2)}) %collective-permute-start.3) | collective-permute-done | bytes 598048 | tf_op jit(solution)/shard_map/ppermute | solution.py:565
  43.1 0.0 collective-permute-done.4.d
  43.1 3.5 %text_combine.1 = (bf16[768,256]{1,0:T(8,128)(2,1)}, bf16[784,256]{1,0:T(8,128)(2,1)}, f32[16,128]{1,0:T(8,128)S(1)}) custom-call(bf16[1168,256]{1,0:T(8,128)(2,1)} %get-tuple-element.50.a, bf16[1168,256]{1,0:T(8,128)(2,1)S(1)} %collective-permute-done.2.b, bf16[1168,256]{1,0:T(8,128)(2,1)S(1)} %collective-permute-done.3.c, ...), custom_call_target="tpu_custom_call" | custom-call | flops 1048576 | bytes 65536 | tf_op jit(solution)/shard_map/text_combine/pallas_call | solution.py:265
  46.6 0.1 collective-permute-start.5
  46.7 2.1 %collective-permute-start.6 = (bf16[784,256]{1,0:T(8,128)(2,1)}, bf16[784,256]{1,0:T(8,128)(2,1)S(1)}, u32[]{:S(2)}, u32[]{:S(2)}) collective-permute-start(bf16[784,256]{1,0:T(8,128)(2,1)} %get-tuple-element.48.rest_0_), channel_id=1, source_target_pairs={{0,4},{1,5},{2,6},{3,7},{4,0},{5,1},{6,2},{7,3},{8,12},{9,13},{10,... | collective-permute-start | bytes 1204232 | tf_op jit(solution)/shard_map/ppermute | solution.py:565
  48.8 1.1 %collective-permute-start.7 = (bf16[784,256]{1,0:T(8,128)(2,1)}, bf16[784,256]{1,0:T(8,128)(2,1)S(1)}, u32[]{:S(2)}, u32[]{:S(2)}) collective-permute-start(bf16[784,256]{1,0:T(8,128)(2,1)} %get-tuple-element.48.rest_0_), channel_id=1, source_target_pairs={{0,6},{1,7},{2,0},{3,1},{4,2},{5,3},{6,4},{7,5},{8,14},{9,15},{10,... | collective-permute-start | bytes 1204232 | tf_op jit(solution)/shard_map/ppermute | solution.py:565
  49.9 1.3 %collective-permute-start.8 = (bf16[784,256]{1,0:T(8,128)(2,1)}, bf16[784,256]{1,0:T(8,128)(2,1)}, u32[]{:S(2)}, u32[]{:S(2)}) collective-permute-start(bf16[784,256]{1,0:T(8,128)(2,1)} %get-tuple-element.48.rest_0_), channel_id=1, source_target_pairs={{0,1},{1,0},{2,3},{3,2},{4,5},{5,4},{6,7},{7,6},{8,9},{9,8},{10,11... | collective-permute-start | bytes 1204232 | tf_op jit(solution)/shard_map/ppermute | solution.py:571
  51.3 2.2 %image_keys.1 = (bf16[768,256]{1,0:T(8,128)(2,1)}, bf16[384,256]{1,0:T(8,128)(2,1)}) custom-call(bf16[1168,256]{1,0:T(8,128)(2,1)} %get-tuple-element.50.a, bf16[1168,256]{1,0:T(8,128)(2,1)S(1)} %collective-permute-done.2.b, bf16[1168,256]{1,0:T(8,128)(2,1)S(1)} %collective-permute-done.3.c, bf16[1168,256]{1,0:T(8,128)(2,1)S(1)} %collective-permute-done.4.d, ...), custom_call_target="tpu_custom_call" | custom-call | flops 1048576 | bytes 65536 | tf_op jit(solution)/shard_map/image_keys/pallas_call | solution.py:353
  53.5 0.0 all-to-all-done
  53.5 2.0 %image_residual.1.rest_0_ = bf16[400,256]{1,0:T(8,128)(2,1)} custom-call(bf16[384,256]{1,0:T(8,128)(2,1)} %get-tuple-element.52.both_from, bf16[768,256]{1,0:T(8,128)(2,1)S(1)} %bitcast.7, s32[1,512]{1,0:T(1,128)S(1)} %bitcast.10), custom_call_target="tpu_custom_call" | custom-call | flops 1048576 | bytes 65536 | tf_op jit(solution)/shard_map/image_residual/pallas_call | solution.py:388
  55.5 11.1 %all-to-all-start.1 = ((bf16[32,24,256]{2,1,0:T(8,128)(2,1)}), bf16[32,24,256]{2,1,0:T(8,128)(2,1)S(1)}, u32[]{:S(2)}, u32[]{:S(2)}) async-start(bf16[32,24,256]{2,1,0:T(8,128)(2,1)} %bitcast.18), calls=%async_computation.1 | async-start | bytes 786432 | tf_op jit(solution)/shard_map/all_to_all | solution.py:583
  66.6 0.0 copy-start
  66.6 0.0 copy-start.1
  66.6 0.0 copy-start.5
  66.6 0.5 collective-permute-start.13
  67.1 0.0 collective-permute-done.5.rest_1_
  67.1 1.3 %collective-permute-start.9 = (bf16[784,256]{1,0:T(8,128)(2,1)S(1)}, bf16[784,256]{1,0:T(8,128)(2,1)S(1)}, u32[]{:S(2)}, u32[]{:S(2)}) collective-permute-start(bf16[784,256]{1,0:T(8,128)(2,1)S(1)} %collective-permute-done.5.rest_1_), channel_id=1, source_target_pairs={{0,1},{1,0},{2,3},{3,2},{4,5},{5,4},{6,7},{7,6},{8,9},{9,8},{10,11... | collective-permute-start | bytes 1204232 | tf_op jit(solution)/shard_map/ppermute | solution.py:571
  68.4 0.0 collective-permute-done.6.rest_2_
  68.4 0.0 collective-permute-start.10
  68.4 0.0 collective-permute-done.7.rest_3_
  68.4 0.7 collective-permute-start.11
  69.1 5.7 %collective-permute-done.13.rest_2_ = bf16[400,256]{1,0:T(8,128)(2,1)S(1)} collective-permute-done((bf16[400,256]{1,0:T(8,128)(2,1)}, bf16[400,256]{1,0:T(8,128)(2,1)S(1)}, u32[]{:S(2)}, u32[]{:S(2)}) %collective-permute-start.13) | collective-permute-done | bytes 204832 | tf_op jit(solution)/shard_map/ppermute | solution.py:565
  74.8 0.4 collective-permute-start.12
  75.2 0.0 collective-permute-done.8.rest_4_
  75.2 2.3 %collective-permute-start.14 = (bf16[400,256]{1,0:T(8,128)(2,1)}, bf16[400,256]{1,0:T(8,128)(2,1)S(1)}, u32[]{:S(2)}, u32[]{:S(2)}) collective-permute-start(bf16[400,256]{1,0:T(8,128)(2,1)} %image_residual.1.rest_0_), channel_id=1, source_target_pairs={{0,6},{1,7},{2,0},{3,1},{4,2},{5,3},{6,4},{7,5},{8,14},{9,15},{10,... | collective-permute-start | bytes 614408 | tf_op jit(solution)/shard_map/ppermute | solution.py:565
  77.5 2.9 %hold.1 = (bf16[1024,1024]{1,0:T(8,128)(2,1)S(1)}, bf16[1024,1024]{1,0:T(8,128)(2,1)S(1)}, bf16[768,1024]{1,0:T(8,128)(2,1)S(1)}, bf16[384,1024]{1,0:T(8,128)(2,1)S(1)}) custom-call(bf16[1024,1024]{1,0:T(8,128)(2,1)} %refs_0_.1, bf16[1024,1024]{1,0:T(8,128)(2,1)} %refs_1_.1, bf16[768,1024]{1,0:T(8,128)(2,1)} %refs_2_, bf16[384,1024]{1,0:T(8,128)(2,1)} %refs_3_), custom_call_target="tpu_custom_call" | custom-call | flops 1048576 | bytes 65536 | tf_op jit(solution)/shard_map/hold/pallas_call | solution.py:500
  80.4 0.0 collective-permute-done.9.rest_5_
  80.4 0.0 copy-done
  80.4 1.7 %collective-permute-start.15 = (bf16[400,256]{1,0:T(8,128)(2,1)S(1)}, bf16[400,256]{1,0:T(8,128)(2,1)S(1)}, u32[]{:S(2)}, u32[]{:S(2)}) collective-permute-start(bf16[400,256]{1,0:T(8,128)(2,1)S(1)} %copy-done), channel_id=1, source_target_pairs={{0,1},{1,0},{2,3},{3,2},{4,5},{5,4},{6,7},{7,6},{8,9},{9,8},{10,11... | collective-permute-start | bytes 614408 | tf_op jit(solution)/shard_map/ppermute | solution.py:571
  82.2 0.0 collective-permute-done.10.rest_6_
  82.2 0.1 collective-permute-start.17
  82.3 0.0 collective-permute-done.11.rest_7_
  82.3 0.0 copy-done.1
  82.3 0.0 copy-done.5
  82.3 6.6 %backward.2 = bf16[768,1024]{1,0:T(8,128)(2,1)} custom-call(bf16[768,1024]{1,0:T(8,128)(2,1)S(1)} %get-tuple-element.58.x_ref, f32[1,1024]{1,0:T(1,128)S(1)} %bitcast.15, s32[1,512]{1,0:T(1,128)S(1)} %bitcast.11, f32[16,128]{1,0:T(8,128)S(1)} %get-tuple-element.51.squares_ref, bf16[1024,1024]{1,0:T(8,128)(2,1)S(1)} %get-tuple-element.56.wk_ref, ...), custom_call_target="tpu_custom_call" | custom-call | flops 1048576 | bytes 65536 | tf_op jit(solution)/shard_map/backward/pallas_call | solution.py:547
  88.9 0.0 collective-permute-done.12.rest_1_
  88.9 0.0 collective-permute-done.14.rest_3_
  88.9 0.5 collective-permute-start.16
  89.4 0.1 collective-permute-start.18
  89.5 0.0 collective-permute-done.15.rest_4_
  89.5 0.0 collective-permute-done.17.rest_6_
  89.5 1.0 %collective-permute-done.16.rest_5_ = bf16[400,256]{1,0:T(8,128)(2,1)S(1)} collective-permute-done((bf16[400,256]{1,0:T(8,128)(2,1)S(1)}, bf16[400,256]{1,0:T(8,128)(2,1)S(1)}, u32[]{:S(2)}, u32[]{:S(2)}) %collective-permute-start.16) | collective-permute-done | bytes 204832 | tf_op jit(solution)/shard_map/ppermute | solution.py:571
  90.5 0.4 collective-permute-done.18.rest_7_
  90.8 3.1 %backward.3 = bf16[384,1024]{1,0:T(8,128)(2,1)} custom-call(bf16[384,1024]{1,0:T(8,128)(2,1)S(1)} %get-tuple-element.55.x_ref, f32[1,1024]{1,0:T(1,128)S(1)} %bitcast.16, s32[1,512]{1,0:T(1,128)S(1)} %bitcast.12, f32[16,128]{1,0:T(8,128)S(1)} %get-tuple-element.51.squares_ref, bf16[1024,1024]{1,0:T(8,128)(2,1)S(1)} %get-tuple-element.56.wk_ref, ...), custom_call_target="tpu_custom_call" | custom-call | flops 1048576 | bytes 65536 | tf_op jit(solution)/shard_map/backward/pallas_call | solution.py:547
  94.0 0.0 all-to-all-done.1
  94.0 0.0 copy-done.2
  94.0 1.8 %merge.1 = (bf16[768,128]{1,0:T(8,128)(2,1)}, bf16[768,128]{1,0:T(8,128)(2,1)}) custom-call(s32[1,512]{1,0:T(1,128)S(1)} %bitcast.13, bf16[768,256]{1,0:T(8,128)(2,1)S(1)} %bitcast.6, bf16[768,256]{1,0:T(8,128)(2,1)S(1)} %copy-done.2), custom_call_target="tpu_custom_call" | custom-call | flops 1048576 | bytes 65536 | tf_op jit(solution)/shard_map/merge/pallas_call | solution.py:471
  (1 shorter events, 0.0 us)
Async XLA Ops:
  0.6 0.7 copy-start.4
  7.0 5.0 %collective-permute-start = (bf16[1,1168,256]{2,1,0:T(8,128)(2,1)S(1)}, bf16[1,1168,256]{2,1,0:T(8,128)(2,1)S(1)}, u32[]{:S(2)}, u32[]{:S(2)}) collective-permute-start(bf16[1,1168,256]{2,1,0:T(8,128)(2,1)S(1)} %get-tuple-element.41), channel_id=1, source_target_pairs={{0,1},{1,0},{2,3},{3,2},{4,5},{5,4},{6,7},{7,6},{8,9},{9,8},{10,11... | collective-permute-start | bytes 1794056 | tf_op jit(solution)/shard_map/ppermute | solution.py:571
  12.0 3.7 %collective-permute-start.1 = (bf16[3,1168,256]{2,1,0:T(8,128)(2,1)S(1)}, bf16[3,1168,256]{2,1,0:T(8,128)(2,1)S(1)}, u32[]{:S(2)}, u32[]{:S(2)}) collective-permute-start(bf16[3,1168,256]{2,1,0:T(8,128)(2,1)S(1)} %get-tuple-element.44), channel_id=1, source_target_pairs={{0,1},{1,0},{2,3},{3,2},{4,5},{5,4},{6,7},{7,6},{8,9},{9,8},{10,11... | collective-permute-start | bytes 5382152 | tf_op jit(solution)/shard_map/ppermute | solution.py:571
  13.2 9.0 %copy-start.3 = (s32[512]{0:T(512)S(1)}, s32[512]{0:T(512)}, u32[]{:S(2)}) copy-start(s32[512]{0:T(512)} %param.10) | copy-start | bytes 6148
  13.2 21.2 %collective-permute-start.2 = (bf16[1168,256]{1,0:T(8,128)(2,1)S(1)}, bf16[1168,256]{1,0:T(8,128)(2,1)S(1)}, u32[]{:S(2)}, u32[]{:S(2)}) collective-permute-start(bf16[1168,256]{1,0:T(8,128)(2,1)S(1)} %forward_own.2), channel_id=1, source_target_pairs={{0,4},{1,5},{2,6},{3,7},{4,0},{5,1},{6,2},{7,3},{8,12},{9,13},{10,... | collective-permute-start | bytes 1794056 | tf_op jit(solution)/shard_map/ppermute | solution.py:565
  19.4 23.6 %collective-permute-start.3 = (bf16[1168,256]{1,0:T(8,128)(2,1)}, bf16[1168,256]{1,0:T(8,128)(2,1)S(1)}, u32[]{:S(2)}, u32[]{:S(2)}) collective-permute-start(bf16[1168,256]{1,0:T(8,128)(2,1)} %get-tuple-element.46), channel_id=1, source_target_pairs={{0,2},{1,3},{2,4},{3,5},{4,6},{5,7},{6,0},{7,1},{8,10},{9,11},{10,... | collective-permute-start | bytes 1794056 | tf_op jit(solution)/shard_map/ppermute | solution.py:565
  19.5 23.5 %collective-permute-start.4 = (bf16[1168,256]{1,0:T(8,128)(2,1)S(1)}, bf16[1168,256]{1,0:T(8,128)(2,1)S(1)}, u32[]{:S(2)}, u32[]{:S(2)}) collective-permute-start(bf16[1168,256]{1,0:T(8,128)(2,1)S(1)} %get-tuple-element.47), channel_id=1, source_target_pairs={{0,6},{1,7},{2,0},{3,1},{4,2},{5,3},{6,4},{7,5},{8,14},{9,15},{10,... | collective-permute-start | bytes 1794056 | tf_op jit(solution)/shard_map/ppermute | solution.py:565
  24.6 28.9 %all-to-all-start = ((bf16[32,24,256]{2,1,0:T(8,128)(2,1)}), bf16[32,24,256]{2,1,0:T(8,128)(2,1)S(1)}, u32[]{:S(2)}, u32[]{:S(2)}) async-start(bf16[32,24,256]{2,1,0:T(8,128)(2,1)} %bitcast.17), calls=%async_computation | async-start | bytes 786432 | tf_op jit(solution)/shard_map/all_to_all | solution.py:583
  46.6 20.5 %collective-permute-start.5 = (bf16[784,256]{1,0:T(8,128)(2,1)}, bf16[784,256]{1,0:T(8,128)(2,1)S(1)}, u32[]{:S(2)}, u32[]{:S(2)}) collective-permute-start(bf16[784,256]{1,0:T(8,128)(2,1)} %get-tuple-element.48.rest_0_), channel_id=1, source_target_pairs={{0,2},{1,3},{2,4},{3,5},{4,6},{5,7},{6,0},{7,1},{8,10},{9,11},{10,... | collective-permute-start | bytes 1204232 | tf_op jit(solution)/shard_map/ppermute | solution.py:565
  46.7 21.7 %collective-permute-start.6 = (bf16[784,256]{1,0:T(8,128)(2,1)}, bf16[784,256]{1,0:T(8,128)(2,1)S(1)}, u32[]{:S(2)}, u32[]{:S(2)}) collective-permute-start(bf16[784,256]{1,0:T(8,128)(2,1)} %get-tuple-element.48.rest_0_), channel_id=1, source_target_pairs={{0,4},{1,5},{2,6},{3,7},{4,0},{5,1},{6,2},{7,3},{8,12},{9,13},{10,... | collective-permute-start | bytes 1204232 | tf_op jit(solution)/shard_map/ppermute | solution.py:565
  48.8 19.6 %collective-permute-start.7 = (bf16[784,256]{1,0:T(8,128)(2,1)}, bf16[784,256]{1,0:T(8,128)(2,1)S(1)}, u32[]{:S(2)}, u32[]{:S(2)}) collective-permute-start(bf16[784,256]{1,0:T(8,128)(2,1)} %get-tuple-element.48.rest_0_), channel_id=1, source_target_pairs={{0,6},{1,7},{2,0},{3,1},{4,2},{5,3},{6,4},{7,5},{8,14},{9,15},{10,... | collective-permute-start | bytes 1204232 | tf_op jit(solution)/shard_map/ppermute | solution.py:565
  49.9 25.2 %collective-permute-start.8 = (bf16[784,256]{1,0:T(8,128)(2,1)}, bf16[784,256]{1,0:T(8,128)(2,1)}, u32[]{:S(2)}, u32[]{:S(2)}) collective-permute-start(bf16[784,256]{1,0:T(8,128)(2,1)} %get-tuple-element.48.rest_0_), channel_id=1, source_target_pairs={{0,1},{1,0},{2,3},{3,2},{4,5},{5,4},{6,7},{7,6},{8,9},{9,8},{10,11... | collective-permute-start | bytes 1204232 | tf_op jit(solution)/shard_map/ppermute | solution.py:571
  55.5 38.5 %all-to-all-start.1 = ((bf16[32,24,256]{2,1,0:T(8,128)(2,1)}), bf16[32,24,256]{2,1,0:T(8,128)(2,1)S(1)}, u32[]{:S(2)}, u32[]{:S(2)}) async-start(bf16[32,24,256]{2,1,0:T(8,128)(2,1)} %bitcast.18), calls=%async_computation.1 | async-start | bytes 786432 | tf_op jit(solution)/shard_map/all_to_all | solution.py:583
  66.6 13.8 %copy-start = (bf16[400,256]{1,0:T(8,128)(2,1)S(1)}, bf16[400,256]{1,0:T(8,128)(2,1)}, u32[]{:S(2)}) copy-start(bf16[400,256]{1,0:T(8,128)(2,1)} %image_residual.1.rest_0_) | copy-start | bytes 614404
  66.6 15.7 %copy-start.1 = (bf16[784,256]{1,0:T(8,128)(2,1)S(1)}, bf16[784,256]{1,0:T(8,128)(2,1)}, u32[]{:S(2)}) copy-start(bf16[784,256]{1,0:T(8,128)(2,1)} %get-tuple-element.48.rest_0_) | copy-start | bytes 1204228
  66.6 15.7 %copy-start.5 = (f32[1024]{0:T(1024)S(1)}, f32[1024]{0:T(1024)}, u32[]{:S(2)}) copy-start(f32[1024]{0:T(1024)} %param.11) | copy-start | bytes 12292
  66.6 8.2 %collective-permute-start.13 = (bf16[400,256]{1,0:T(8,128)(2,1)}, bf16[400,256]{1,0:T(8,128)(2,1)S(1)}, u32[]{:S(2)}, u32[]{:S(2)}) collective-permute-start(bf16[400,256]{1,0:T(8,128)(2,1)} %image_residual.1.rest_0_), channel_id=1, source_target_pairs={{0,4},{1,5},{2,6},{3,7},{4,0},{5,1},{6,2},{7,3},{8,12},{9,13},{10,... | collective-permute-start | bytes 614408 | tf_op jit(solution)/shard_map/ppermute | solution.py:565
  67.1 13.3 %collective-permute-start.9 = (bf16[784,256]{1,0:T(8,128)(2,1)S(1)}, bf16[784,256]{1,0:T(8,128)(2,1)S(1)}, u32[]{:S(2)}, u32[]{:S(2)}) collective-permute-start(bf16[784,256]{1,0:T(8,128)(2,1)S(1)} %collective-permute-done.5.rest_1_), channel_id=1, source_target_pairs={{0,1},{1,0},{2,3},{3,2},{4,5},{5,4},{6,7},{7,6},{8,9},{9,8},{10,11... | collective-permute-start | bytes 1204232 | tf_op jit(solution)/shard_map/ppermute | solution.py:571
  68.4 13.7 %collective-permute-start.10 = (bf16[784,256]{1,0:T(8,128)(2,1)S(1)}, bf16[784,256]{1,0:T(8,128)(2,1)S(1)}, u32[]{:S(2)}, u32[]{:S(2)}) collective-permute-start(bf16[784,256]{1,0:T(8,128)(2,1)S(1)} %collective-permute-done.6.rest_2_), channel_id=1, source_target_pairs={{0,1},{1,0},{2,3},{3,2},{4,5},{5,4},{6,7},{7,6},{8,9},{9,8},{10,11... | collective-permute-start | bytes 1204232 | tf_op jit(solution)/shard_map/ppermute | solution.py:571
  68.4 13.8 %collective-permute-start.11 = (bf16[784,256]{1,0:T(8,128)(2,1)S(1)}, bf16[784,256]{1,0:T(8,128)(2,1)S(1)}, u32[]{:S(2)}, u32[]{:S(2)}) collective-permute-start(bf16[784,256]{1,0:T(8,128)(2,1)S(1)} %collective-permute-done.7.rest_3_), channel_id=1, source_target_pairs={{0,1},{1,0},{2,3},{3,2},{4,5},{5,4},{6,7},{7,6},{8,9},{9,8},{10,11... | collective-permute-start | bytes 1204232 | tf_op jit(solution)/shard_map/ppermute | solution.py:571
  74.8 14.1 %collective-permute-start.12 = (bf16[400,256]{1,0:T(8,128)(2,1)}, bf16[400,256]{1,0:T(8,128)(2,1)S(1)}, u32[]{:S(2)}, u32[]{:S(2)}) collective-permute-start(bf16[400,256]{1,0:T(8,128)(2,1)} %image_residual.1.rest_0_), channel_id=1, source_target_pairs={{0,2},{1,3},{2,4},{3,5},{4,6},{5,7},{6,0},{7,1},{8,10},{9,11},{10,... | collective-permute-start | bytes 614408 | tf_op jit(solution)/shard_map/ppermute | solution.py:565
  75.2 13.7 %collective-permute-start.14 = (bf16[400,256]{1,0:T(8,128)(2,1)}, bf16[400,256]{1,0:T(8,128)(2,1)S(1)}, u32[]{:S(2)}, u32[]{:S(2)}) collective-permute-start(bf16[400,256]{1,0:T(8,128)(2,1)} %image_residual.1.rest_0_), channel_id=1, source_target_pairs={{0,6},{1,7},{2,0},{3,1},{4,2},{5,3},{6,4},{7,5},{8,14},{9,15},{10,... | collective-permute-start | bytes 614408 | tf_op jit(solution)/shard_map/ppermute | solution.py:565
  80.4 9.1 %collective-permute-start.15 = (bf16[400,256]{1,0:T(8,128)(2,1)S(1)}, bf16[400,256]{1,0:T(8,128)(2,1)S(1)}, u32[]{:S(2)}, u32[]{:S(2)}) collective-permute-start(bf16[400,256]{1,0:T(8,128)(2,1)S(1)} %copy-done), channel_id=1, source_target_pairs={{0,1},{1,0},{2,3},{3,2},{4,5},{5,4},{6,7},{7,6},{8,9},{9,8},{10,11... | collective-permute-start | bytes 614408 | tf_op jit(solution)/shard_map/ppermute | solution.py:571
  82.2 7.3 %collective-permute-start.17 = (bf16[400,256]{1,0:T(8,128)(2,1)S(1)}, bf16[400,256]{1,0:T(8,128)(2,1)S(1)}, u32[]{:S(2)}, u32[]{:S(2)}) collective-permute-start(bf16[400,256]{1,0:T(8,128)(2,1)S(1)} %collective-permute-done.13.rest_2_), channel_id=1, source_target_pairs={{0,1},{1,0},{2,3},{3,2},{4,5},{5,4},{6,7},{7,6},{8,9},{9,8},{10,11... | collective-permute-start | bytes 614408 | tf_op jit(solution)/shard_map/ppermute | solution.py:571
  88.9 1.6 %collective-permute-start.16 = (bf16[400,256]{1,0:T(8,128)(2,1)S(1)}, bf16[400,256]{1,0:T(8,128)(2,1)S(1)}, u32[]{:S(2)}, u32[]{:S(2)}) collective-permute-start(bf16[400,256]{1,0:T(8,128)(2,1)S(1)} %collective-permute-done.12.rest_1_), channel_id=1, source_target_pairs={{0,1},{1,0},{2,3},{3,2},{4,5},{5,4},{6,7},{7,6},{8,9},{9,8},{10,11... | collective-permute-start | bytes 614408 | tf_op jit(solution)/shard_map/ppermute | solution.py:571
  89.4 1.5 %collective-permute-start.18 = (bf16[400,256]{1,0:T(8,128)(2,1)S(1)}, bf16[400,256]{1,0:T(8,128)(2,1)S(1)}, u32[]{:S(2)}, u32[]{:S(2)}) collective-permute-start(bf16[400,256]{1,0:T(8,128)(2,1)S(1)} %collective-permute-done.14.rest_3_), channel_id=1, source_target_pairs={{0,1},{1,0},{2,3},{3,2},{4,5},{5,4},{6,7},{7,6},{8,9},{9,8},{10,11... | collective-permute-start | bytes 614408 | tf_op jit(solution)/shard_map/ppermute | solution.py:571
  90.8 3.2 %copy-start.2 = (bf16[768,256]{1,0:T(8,128)(2,1)S(1)}, bf16[768,256]{1,0:T(8,128)(2,1)}, u32[]{:S(2)}) copy-start(bf16[768,256]{1,0:T(8,128)(2,1)} %get-tuple-element.67.both_from) | copy-start | bytes 1179652

commit v6 on v5

--- a/solution.py
+++ b/solution.py
@@ -626,7 +626,7 @@
         *weights, after(text_embed, resid1, resid2, resid3), after(image_embed, image_resid)
     )
     own = [resid, resid1, resid3, resid2]
-    other = [across(r) for r in own]
+    other = [across(resid)] + [across(after(r, held[0])) for r in own[1:]]
     resids = [x[n] for x in (own, other) for n in (0, 1, 3, 2)]
     text_grad = backward(text_held, gain, squares, 0, held, starts, resids, True)
     own = [image_resid, image_resid1, image_resid3, image_resid2]

time: 96.4 us -> 93.3 us (0.968)
  waiting for transfers between devices: 18.6 us -> 15.5 us
    ppermute x9, waiting for transfers between devices: 14.4 us -> 11.3 us  [around(): lax.ppermute(x, 'tp', [(2 * y + c, 2 * ((y + shift) % RINGS) + c) for y i...]
  transfers between devices with their start and end apart: 21 -> 21, of which waited for: 6 -> 7; matrix products, arithmetic and copies ran while one was open for 0% -> 0% of each run, Pallas kernels for 28% -> 29%
where the time goes in v6:
time: 93.3 us; the launch traced here: 92.9 us
  starting transfers between devices  40.8 us (44%)
  Pallas kernels  34.8 us (37%)
  waiting for transfers between devices  15.5 us (17%)
  between operations  1.01 us (1%)
    all_to_all x2, starting transfers between devices, route(): return lax.all_to_all(x, 'rows', split_axis=0, concat_axis=0, tiled=True)  20.9 us
    ppermute x9, waiting for transfers between devices, around(): lax.ppermute(x, 'tp', [(2 * y + c, 2 * ((y + shift) % RINGS) + c) for y i...  11.3 us
    ppermute x9, starting transfers between devices, around(): lax.ppermute(x, 'tp', [(2 * y + c, 2 * ((y + shift) % RINGS) + c) for y i...  10.5 us
    pallas_call x2, Pallas kernels, backward(): pl.pallas_call(functools.partial(backward_kernel, first, masked), in_spec...  9.72 us
    ppermute x10, starting transfers between devices, across(): return lax.ppermute(x, 'tp', [(i, i ^ 1) for i in range(2 * RINGS)])  9.48 us
    pallas_call x1, Pallas kernels, forward_other(): pl.pallas_call(functools.partial(forward_other_kernel, splits), in_specs=...  5.7 us
    pallas_call x2, Pallas kernels, forward_own(): pl.pallas_call(functools.partial(forward_own_kernel, split, close), in_sp...  4.56 us
    ppermute x10, waiting for transfers between devices, across(): return lax.ppermute(x, 'tp', [(i, i ^ 1) for i in range(2 * RINGS)])  4.23 us
  transfers between devices with their start and end apart: 21, of which 7 were waited for; matrix products, arithmetic and copies ran while one was open for 0% of the time, Pallas kernels for 29%

profile of v6, /device:TPU:1, one launch (start us, length us, event | category | flops | bytes accessed | tf_op | source)
XLA Modules:
  0.0 92.9 jit_solution(5818726817616250763)
XLA Ops:
  0.6 0.0 copy-start.4
  0.6 0.7 copy-done.4
  1.3 5.7 %forward_other.1 = (bf16[1,1168,256]{2,1,0:T(8,128)(2,1)S(1)}, bf16[3,1168,256]{2,1,0:T(8,128)(2,1)S(1)}, bf16[1152,1024]{1,0:T(8,128)(2,1)S(1)}, f32[16,128]{1,...) custom-call(bf16[768,1024]{1,0:T(8,128)(2,1)} %refs_2_, bf16[384,1024]{1,0:T(8,128)(2,1)} %refs_3_, ...), custom_call_target="tpu_custom_call" | custom-call | flops 1048576 | bytes 65536 | tf_op jit(solution)/shard_map/forward_other/pallas_call | solution.py:153
  7.0 3.3 %collective-permute-start = (bf16[1,1168,256]{2,1,0:T(8,128)(2,1)S(1)}, bf16[1,1168,256]{2,1,0:T(8,128)(2,1)S(1)}, u32[]{:S(2)}, u32[]{:S(2)}) collective-permute-start(bf16[1,1168,256]{2,1,0:T(8,128)(2,1)S(1)} %get-tuple-element.44), channel_id=1, source_target_pairs={{0,1},{1,0},{2,3},{3,2},{4,5},{5,4},{6,7},{7,6},{8,9},{9,8},{10,11... | collective-permute-start | bytes 1794056 | tf_op jit(solution)/shard_map/ppermute | solution.py:571
  10.4 1.6 %collective-permute-done.in_ref = bf16[1,1168,256]{2,1,0:T(8,128)(2,1)S(1)} collective-permute-done((bf16[1,1168,256]{2,1,0:T(8,128)(2,1)S(1)}, bf16[1,1168,256]{2,1,0:T(8,128)(2,1)S(1)}, u32[]{:S(2)}, u32[]{:S(2)}) %collective-permute-start) | collective-permute-done | bytes 598048 | tf_op jit(solution)/shard_map/ppermute | solution.py:571
  12.0 0.4 collective-permute-start.1
  12.4 0.8 forward_own.2
  13.2 0.0 copy-start.3
  13.2 1.3 %collective-permute-start.2 = (bf16[1168,256]{1,0:T(8,128)(2,1)S(1)}, bf16[1168,256]{1,0:T(8,128)(2,1)S(1)}, u32[]{:S(2)}, u32[]{:S(2)}) collective-permute-start(bf16[1168,256]{1,0:T(8,128)(2,1)S(1)} %forward_own.2), channel_id=1, source_target_pairs={{0,4},{1,5},{2,6},{3,7},{4,0},{5,1},{6,2},{7,3},{8,12},{9,13},{10,... | collective-permute-start | bytes 1794056 | tf_op jit(solution)/shard_map/ppermute | solution.py:565
  14.5 1.2 %collective-permute-done.1.in_ref = bf16[3,1168,256]{2,1,0:T(8,128)(2,1)S(1)} collective-permute-done((bf16[3,1168,256]{2,1,0:T(8,128)(2,1)S(1)}, bf16[3,1168,256]{2,1,0:T(8,128)(2,1)S(1)}, u32[]{:S(2)}, u32[]{:S(2)}) %collective-permute-start.1) | collective-permute-done | bytes 1794080 | tf_op jit(solution)/shard_map/ppermute | solution.py:571
  15.7 3.7 %forward_own.3 = (bf16[1168,256]{1,0:T(8,128)(2,1)}, bf16[1168,256]{1,0:T(8,128)(2,1)S(1)}, bf16[1168,256]{1,0:T(8,128)(2,1)}) custom-call(bf16[1152,1024]{1,0:T(8,128)(2,1)S(1)} %get-tuple-element.45.scaled_ref, f32[16,128]{1,0:T(8,128)S(1)} %get-tuple-element.41.lanes_ref, bf16[1024,1024]{1,0:T(8,128)(2,1)S(1)} %get-tuple-element.42.wk_ref, ...), custom_call_target="tpu_custom_call" | custom-call | flops 1048576 | bytes 65536 | tf_op jit(solution)/shard_map/forward_own/pallas_call | solution.py:191
  19.4 0.1 collective-permute-start.3
  19.5 2.7 %collective-permute-start.4 = (bf16[1168,256]{1,0:T(8,128)(2,1)S(1)}, bf16[1168,256]{1,0:T(8,128)(2,1)S(1)}, u32[]{:S(2)}, u32[]{:S(2)}) collective-permute-start(bf16[1168,256]{1,0:T(8,128)(2,1)S(1)} %get-tuple-element.50), channel_id=1, source_target_pairs={{0,6},{1,7},{2,0},{3,1},{4,2},{5,3},{6,4},{7,5},{8,14},{9,15},{10,... | collective-permute-start | bytes 1794056 | tf_op jit(solution)/shard_map/ppermute | solution.py:565
  22.2 0.0 copy-done.3
  22.2 2.4 %gather_targets.1 = bf16[768,256]{1,0:T(8,128)(2,1)} custom-call(s32[1,512]{1,0:T(1,128)S(1)} %bitcast.8, bf16[768,128]{1,0:T(8,128)(2,1)} %kt_from.1, bf16[768,128]{1,0:T(8,128)(2,1)} %vt_from.1), custom_call_target="tpu_custom_call" | custom-call | flops 1048576 | bytes 65536 | tf_op jit(solution)/shard_map/gather_targets/pallas_call | solution.py:424
  24.6 9.8 %all-to-all-start = ((bf16[32,24,256]{2,1,0:T(8,128)(2,1)}), bf16[32,24,256]{2,1,0:T(8,128)(2,1)S(1)}, u32[]{:S(2)}, u32[]{:S(2)}) async-start(bf16[32,24,256]{2,1,0:T(8,128)(2,1)} %bitcast.17), calls=%async_computation | async-start | bytes 786432 | tf_op jit(solution)/shard_map/all_to_all | solution.py:583
  34.4 0.0 collective-permute-done.2.b
  34.4 8.7 %collective-permute-done.3.c = bf16[1168,256]{1,0:T(8,128)(2,1)S(1)} collective-permute-done((bf16[1168,256]{1,0:T(8,128)(2,1)}, bf16[1168,256]{1,0:T(8,128)(2,1)S(1)}, u32[]{:S(2)}, u32[]{:S(2)}) %collective-permute-start.3) | collective-permute-done | bytes 598048 | tf_op jit(solution)/shard_map/ppermute | solution.py:565
  43.1 0.0 collective-permute-done.4.d
  43.1 3.5 %text_combine.1 = (bf16[768,256]{1,0:T(8,128)(2,1)}, bf16[784,256]{1,0:T(8,128)(2,1)}, f32[16,128]{1,0:T(8,128)S(1)}) custom-call(bf16[1168,256]{1,0:T(8,128)(2,1)} %get-tuple-element.53.a, bf16[1168,256]{1,0:T(8,128)(2,1)S(1)} %collective-permute-done.2.b, bf16[1168,256]{1,0:T(8,128)(2,1)S(1)} %collective-permute-done.3.c, ...), custom_call_target="tpu_custom_call" | custom-call | flops 1048576 | bytes 65536 | tf_op jit(solution)/shard_map/text_combine/pallas_call | solution.py:265
  46.6 0.1 collective-permute-start.5
  46.7 2.1 %collective-permute-start.6 = (bf16[784,256]{1,0:T(8,128)(2,1)}, bf16[784,256]{1,0:T(8,128)(2,1)S(1)}, u32[]{:S(2)}, u32[]{:S(2)}) collective-permute-start(bf16[784,256]{1,0:T(8,128)(2,1)} %get-tuple-element.51.rest_0_), channel_id=1, source_target_pairs={{0,4},{1,5},{2,6},{3,7},{4,0},{5,1},{6,2},{7,3},{8,12},{9,13},{10,... | collective-permute-start | bytes 1204232 | tf_op jit(solution)/shard_map/ppermute | solution.py:565
  48.8 1.1 %collective-permute-start.7 = (bf16[784,256]{1,0:T(8,128)(2,1)}, bf16[784,256]{1,0:T(8,128)(2,1)S(1)}, u32[]{:S(2)}, u32[]{:S(2)}) collective-permute-start(bf16[784,256]{1,0:T(8,128)(2,1)} %get-tuple-element.51.rest_0_), channel_id=1, source_target_pairs={{0,6},{1,7},{2,0},{3,1},{4,2},{5,3},{6,4},{7,5},{8,14},{9,15},{10,... | collective-permute-start | bytes 1204232 | tf_op jit(solution)/shard_map/ppermute | solution.py:565
  49.9 1.3 %collective-permute-start.8 = (bf16[784,256]{1,0:T(8,128)(2,1)}, bf16[784,256]{1,0:T(8,128)(2,1)}, u32[]{:S(2)}, u32[]{:S(2)}) collective-permute-start(bf16[784,256]{1,0:T(8,128)(2,1)} %get-tuple-element.51.rest_0_), channel_id=1, source_target_pairs={{0,1},{1,0},{2,3},{3,2},{4,5},{5,4},{6,7},{7,6},{8,9},{9,8},{10,11... | collective-permute-start | bytes 1204232 | tf_op jit(solution)/shard_map/ppermute | solution.py:571
  51.3 2.2 %image_keys.1 = (bf16[768,256]{1,0:T(8,128)(2,1)}, bf16[384,256]{1,0:T(8,128)(2,1)}) custom-call(bf16[1168,256]{1,0:T(8,128)(2,1)} %get-tuple-element.53.a, bf16[1168,256]{1,0:T(8,128)(2,1)S(1)} %collective-permute-done.2.b, bf16[1168,256]{1,0:T(8,128)(2,1)S(1)} %collective-permute-done.3.c, bf16[1168,256]{1,0:T(8,128)(2,1)S(1)} %collective-permute-done.4.d, ...), custom_call_target="tpu_custom_call" | custom-call | flops 1048576 | bytes 65536 | tf_op jit(solution)/shard_map/image_keys/pallas_call | solution.py:353
  53.4 0.0 all-to-all-done
  53.4 2.0 %image_residual.1.rest_0_ = bf16[400,256]{1,0:T(8,128)(2,1)} custom-call(bf16[384,256]{1,0:T(8,128)(2,1)} %get-tuple-element.55.both_from, bf16[768,256]{1,0:T(8,128)(2,1)S(1)} %bitcast.7, s32[1,512]{1,0:T(1,128)S(1)} %bitcast.10), custom_call_target="tpu_custom_call" | custom-call | flops 1048576 | bytes 65536 | tf_op jit(solution)/shard_map/image_residual/pallas_call | solution.py:388
  55.5 11.1 %all-to-all-start.1 = ((bf16[32,24,256]{2,1,0:T(8,128)(2,1)}), bf16[32,24,256]{2,1,0:T(8,128)(2,1)S(1)}, u32[]{:S(2)}, u32[]{:S(2)}) async-start(bf16[32,24,256]{2,1,0:T(8,128)(2,1)} %bitcast.18), calls=%async_computation.1 | async-start | bytes 786432 | tf_op jit(solution)/shard_map/all_to_all | solution.py:583
  66.6 0.0 copy-start
  66.6 0.0 copy-start.1
  66.6 0.0 copy-start.5
  66.6 0.5 collective-permute-start.13
  67.1 0.0 collective-permute-done.5.rest_1_
  67.1 0.0 collective-permute-done.6.rest_2_
  67.1 0.5 collective-permute-done.7.rest_3_
  67.6 2.9 %hold.1 = (bf16[1024,1024]{1,0:T(8,128)(2,1)S(1)}, bf16[1024,1024]{1,0:T(8,128)(2,1)S(1)}, bf16[768,1024]{1,0:T(8,128)(2,1)S(1)}, bf16[384,1024]{1,0:T(8,128)(2,1)S(1)}) custom-call(bf16[1024,1024]{1,0:T(8,128)(2,1)} %refs_0_.1, bf16[1024,1024]{1,0:T(8,128)(2,1)} %refs_1_.1, bf16[768,1024]{1,0:T(8,128)(2,1)} %refs_2_, bf16[384,1024]{1,0:T(8,128)(2,1)} %refs_3_), custom_call_target="tpu_custom_call" | custom-call | flops 1048576 | bytes 65536 | tf_op jit(solution)/shard_map/hold/pallas_call | solution.py:500
  70.5 1.6 %collective-permute-start.9 = (bf16[784,256]{1,0:T(8,128)(2,1)S(1)}, bf16[784,256]{1,0:T(8,128)(2,1)S(1)}, u32[]{:S(2)}, u32[]{:S(2)}) collective-permute-start(bf16[784,256]{1,0:T(8,128)(2,1)S(1)} %collective-permute-done.5.rest_1_), channel_id=1, source_target_pairs={{0,1},{1,0},{2,3},{3,2},{4,5},{5,4},{6,7},{7,6},{8,9},{9,8},{10,11... | collective-permute-start | bytes 1204232 | tf_op jit(solution)/shard_map/ppermute | solution.py:571
  72.1 0.1 collective-permute-start.10
  72.2 0.4 collective-permute-start.11
  72.6 2.1 %collective-permute-done.13.rest_2_ = bf16[400,256]{1,0:T(8,128)(2,1)S(1)} collective-permute-done((bf16[400,256]{1,0:T(8,128)(2,1)}, bf16[400,256]{1,0:T(8,128)(2,1)S(1)}, u32[]{:S(2)}, u32[]{:S(2)}) %collective-permute-start.13) | collective-permute-done | bytes 204832 | tf_op jit(solution)/shard_map/ppermute | solution.py:565
  74.8 0.0 copy-done
  74.8 0.4 collective-permute-start.12
  75.2 0.0 collective-permute-done.8.rest_4_
  75.2 2.3 %collective-permute-start.14 = (bf16[400,256]{1,0:T(8,128)(2,1)S(1)}, bf16[400,256]{1,0:T(8,128)(2,1)S(1)}, u32[]{:S(2)}, u32[]{:S(2)}) collective-permute-start(bf16[400,256]{1,0:T(8,128)(2,1)S(1)} %copy-done), channel_id=1, source_target_pairs={{0,6},{1,7},{2,0},{3,1},{4,2},{5,3},{6,4},{7,5},{8,14},{9,15},{10,... | collective-permute-start | bytes 614408 | tf_op jit(solution)/shard_map/ppermute | solution.py:565
  77.5 0.0 collective-permute-done.9.rest_5_
  77.5 1.7 %collective-permute-start.15 = (bf16[400,256]{1,0:T(8,128)(2,1)S(1)}, bf16[400,256]{1,0:T(8,128)(2,1)S(1)}, u32[]{:S(2)}, u32[]{:S(2)}) collective-permute-start(bf16[400,256]{1,0:T(8,128)(2,1)S(1)} %copy-done), channel_id=1, source_target_pairs={{0,1},{1,0},{2,3},{3,2},{4,5},{5,4},{6,7},{7,6},{8,9},{9,8},{10,11... | collective-permute-start | bytes 614408 | tf_op jit(solution)/shard_map/ppermute | solution.py:571
  79.1 0.0 collective-permute-done.10.rest_6_
  79.1 0.1 collective-permute-start.17
  79.2 0.0 collective-permute-done.11.rest_7_
  79.2 0.0 copy-done.1
  79.2 0.0 copy-done.5
  79.2 6.6 %backward.2 = bf16[768,1024]{1,0:T(8,128)(2,1)} custom-call(bf16[768,1024]{1,0:T(8,128)(2,1)S(1)} %get-tuple-element.61.x_ref, f32[1,1024]{1,0:T(1,128)S(1)} %bitcast.15, s32[1,512]{1,0:T(1,128)S(1)} %bitcast.11, f32[16,128]{1,0:T(8,128)S(1)} %get-tuple-element.54.squares_ref, bf16[1024,1024]{1,0:T(8,128)(2,1)S(1)} %get-tuple-element.59.wk_ref, ...), custom_call_target="tpu_custom_call" | custom-call | flops 1048576 | bytes 65536 | tf_op jit(solution)/shard_map/backward/pallas_call | solution.py:547
  85.8 0.0 collective-permute-done.12.rest_1_
  85.9 0.0 collective-permute-done.14.rest_3_
  85.9 0.5 collective-permute-start.16
  86.3 0.1 collective-permute-start.18
  86.5 0.0 collective-permute-done.15.rest_4_
  86.5 0.0 collective-permute-done.17.rest_6_
  86.5 1.0 %collective-permute-done.16.rest_5_ = bf16[400,256]{1,0:T(8,128)(2,1)S(1)} collective-permute-done((bf16[400,256]{1,0:T(8,128)(2,1)S(1)}, bf16[400,256]{1,0:T(8,128)(2,1)S(1)}, u32[]{:S(2)}, u32[]{:S(2)}) %collective-permute-start.16) | collective-permute-done | bytes 204832 | tf_op jit(solution)/shard_map/ppermute | solution.py:571
  87.4 0.4 collective-permute-done.18.rest_7_
  87.8 3.1 %backward.3 = bf16[384,1024]{1,0:T(8,128)(2,1)} custom-call(bf16[384,1024]{1,0:T(8,128)(2,1)S(1)} %get-tuple-element.58.x_ref, f32[1,1024]{1,0:T(1,128)S(1)} %bitcast.16, s32[1,512]{1,0:T(1,128)S(1)} %bitcast.12, f32[16,128]{1,0:T(8,128)S(1)} %get-tuple-element.54.squares_ref, bf16[1024,1024]{1,0:T(8,128)(2,1)S(1)} %get-tuple-element.59.wk_ref, ...), custom_call_target="tpu_custom_call" | custom-call | flops 1048576 | bytes 65536 | tf_op jit(solution)/shard_map/backward/pallas_call | solution.py:547
  90.9 0.0 all-to-all-done.1
  90.9 0.0 copy-done.2
  91.0 1.8 %merge.1 = (bf16[768,128]{1,0:T(8,128)(2,1)}, bf16[768,128]{1,0:T(8,128)(2,1)}) custom-call(s32[1,512]{1,0:T(1,128)S(1)} %bitcast.13, bf16[768,256]{1,0:T(8,128)(2,1)S(1)} %bitcast.6, bf16[768,256]{1,0:T(8,128)(2,1)S(1)} %copy-done.2), custom_call_target="tpu_custom_call" | custom-call | flops 1048576 | bytes 65536 | tf_op jit(solution)/shard_map/merge/pallas_call | solution.py:471
  (1 shorter events, 0.0 us)
Async XLA Ops:
  0.6 0.7 copy-start.4
  7.0 5.0 %collective-permute-start = (bf16[1,1168,256]{2,1,0:T(8,128)(2,1)S(1)}, bf16[1,1168,256]{2,1,0:T(8,128)(2,1)S(1)}, u32[]{:S(2)}, u32[]{:S(2)}) collective-permute-start(bf16[1,1168,256]{2,1,0:T(8,128)(2,1)S(1)} %get-tuple-element.44), channel_id=1, source_target_pairs={{0,1},{1,0},{2,3},{3,2},{4,5},{5,4},{6,7},{7,6},{8,9},{9,8},{10,11... | collective-permute-start | bytes 1794056 | tf_op jit(solution)/shard_map/ppermute | solution.py:571
  12.0 3.7 %collective-permute-start.1 = (bf16[3,1168,256]{2,1,0:T(8,128)(2,1)S(1)}, bf16[3,1168,256]{2,1,0:T(8,128)(2,1)S(1)}, u32[]{:S(2)}, u32[]{:S(2)}) collective-permute-start(bf16[3,1168,256]{2,1,0:T(8,128)(2,1)S(1)} %get-tuple-element.47), channel_id=1, source_target_pairs={{0,1},{1,0},{2,3},{3,2},{4,5},{5,4},{6,7},{7,6},{8,9},{9,8},{10,11... | collective-permute-start | bytes 5382152 | tf_op jit(solution)/shard_map/ppermute | solution.py:571
  13.2 9.0 %copy-start.3 = (s32[512]{0:T(512)S(1)}, s32[512]{0:T(512)}, u32[]{:S(2)}) copy-start(s32[512]{0:T(512)} %param.10) | copy-start | bytes 6148
  13.2 21.2 %collective-permute-start.2 = (bf16[1168,256]{1,0:T(8,128)(2,1)S(1)}, bf16[1168,256]{1,0:T(8,128)(2,1)S(1)}, u32[]{:S(2)}, u32[]{:S(2)}) collective-permute-start(bf16[1168,256]{1,0:T(8,128)(2,1)S(1)} %forward_own.2), channel_id=1, source_target_pairs={{0,4},{1,5},{2,6},{3,7},{4,0},{5,1},{6,2},{7,3},{8,12},{9,13},{10,... | collective-permute-start | bytes 1794056 | tf_op jit(solution)/shard_map/ppermute | solution.py:565
  19.4 23.6 %collective-permute-start.3 = (bf16[1168,256]{1,0:T(8,128)(2,1)}, bf16[1168,256]{1,0:T(8,128)(2,1)S(1)}, u32[]{:S(2)}, u32[]{:S(2)}) collective-permute-start(bf16[1168,256]{1,0:T(8,128)(2,1)} %get-tuple-element.49), channel_id=1, source_target_pairs={{0,2},{1,3},{2,4},{3,5},{4,6},{5,7},{6,0},{7,1},{8,10},{9,11},{10,... | collective-permute-start | bytes 1794056 | tf_op jit(solution)/shard_map/ppermute | solution.py:565
  19.5 23.5 %collective-permute-start.4 = (bf16[1168,256]{1,0:T(8,128)(2,1)S(1)}, bf16[1168,256]{1,0:T(8,128)(2,1)S(1)}, u32[]{:S(2)}, u32[]{:S(2)}) collective-permute-start(bf16[1168,256]{1,0:T(8,128)(2,1)S(1)} %get-tuple-element.50), channel_id=1, source_target_pairs={{0,6},{1,7},{2,0},{3,1},{4,2},{5,3},{6,4},{7,5},{8,14},{9,15},{10,... | collective-permute-start | bytes 1794056 | tf_op jit(solution)/shard_map/ppermute | solution.py:565
  24.6 28.8 %all-to-all-start = ((bf16[32,24,256]{2,1,0:T(8,128)(2,1)}), bf16[32,24,256]{2,1,0:T(8,128)(2,1)S(1)}, u32[]{:S(2)}, u32[]{:S(2)}) async-start(bf16[32,24,256]{2,1,0:T(8,128)(2,1)} %bitcast.17), calls=%async_computation | async-start | bytes 786432 | tf_op jit(solution)/shard_map/all_to_all | solution.py:583
  46.6 20.5 %collective-permute-start.5 = (bf16[784,256]{1,0:T(8,128)(2,1)}, bf16[784,256]{1,0:T(8,128)(2,1)S(1)}, u32[]{:S(2)}, u32[]{:S(2)}) collective-permute-start(bf16[784,256]{1,0:T(8,128)(2,1)} %get-tuple-element.51.rest_0_), channel_id=1, source_target_pairs={{0,2},{1,3},{2,4},{3,5},{4,6},{5,7},{6,0},{7,1},{8,10},{9,11},{10,... | collective-permute-start | bytes 1204232 | tf_op jit(solution)/shard_map/ppermute | solution.py:565
  46.7 20.4 %collective-permute-start.6 = (bf16[784,256]{1,0:T(8,128)(2,1)}, bf16[784,256]{1,0:T(8,128)(2,1)S(1)}, u32[]{:S(2)}, u32[]{:S(2)}) collective-permute-start(bf16[784,256]{1,0:T(8,128)(2,1)} %get-tuple-element.51.rest_0_), channel_id=1, source_target_pairs={{0,4},{1,5},{2,6},{3,7},{4,0},{5,1},{6,2},{7,3},{8,12},{9,13},{10,... | collective-permute-start | bytes 1204232 | tf_op jit(solution)/shard_map/ppermute | solution.py:565
  48.8 18.8 %collective-permute-start.7 = (bf16[784,256]{1,0:T(8,128)(2,1)}, bf16[784,256]{1,0:T(8,128)(2,1)S(1)}, u32[]{:S(2)}, u32[]{:S(2)}) collective-permute-start(bf16[784,256]{1,0:T(8,128)(2,1)} %get-tuple-element.51.rest_0_), channel_id=1, source_target_pairs={{0,6},{1,7},{2,0},{3,1},{4,2},{5,3},{6,4},{7,5},{8,14},{9,15},{10,... | collective-permute-start | bytes 1204232 | tf_op jit(solution)/shard_map/ppermute | solution.py:565
  49.9 25.2 %collective-permute-start.8 = (bf16[784,256]{1,0:T(8,128)(2,1)}, bf16[784,256]{1,0:T(8,128)(2,1)}, u32[]{:S(2)}, u32[]{:S(2)}) collective-permute-start(bf16[784,256]{1,0:T(8,128)(2,1)} %get-tuple-element.51.rest_0_), channel_id=1, source_target_pairs={{0,1},{1,0},{2,3},{3,2},{4,5},{5,4},{6,7},{7,6},{8,9},{9,8},{10,11... | collective-permute-start | bytes 1204232 | tf_op jit(solution)/shard_map/ppermute | solution.py:571
  55.5 35.4 %all-to-all-start.1 = ((bf16[32,24,256]{2,1,0:T(8,128)(2,1)}), bf16[32,24,256]{2,1,0:T(8,128)(2,1)S(1)}, u32[]{:S(2)}, u32[]{:S(2)}) async-start(bf16[32,24,256]{2,1,0:T(8,128)(2,1)} %bitcast.18), calls=%async_computation.1 | async-start | bytes 786432 | tf_op jit(solution)/shard_map/all_to_all | solution.py:583
  66.6 8.2 %copy-start = (bf16[400,256]{1,0:T(8,128)(2,1)S(1)}, bf16[400,256]{1,0:T(8,128)(2,1)}, u32[]{:S(2)}) copy-start(bf16[400,256]{1,0:T(8,128)(2,1)} %image_residual.1.rest_0_) | copy-start | bytes 614404
  66.6 12.7 %copy-start.1 = (bf16[784,256]{1,0:T(8,128)(2,1)S(1)}, bf16[784,256]{1,0:T(8,128)(2,1)}, u32[]{:S(2)}) copy-start(bf16[784,256]{1,0:T(8,128)(2,1)} %get-tuple-element.51.rest_0_) | copy-start | bytes 1204228
  66.6 12.7 %copy-start.5 = (f32[1024]{0:T(1024)S(1)}, f32[1024]{0:T(1024)}, u32[]{:S(2)}) copy-start(f32[1024]{0:T(1024)} %param.11) | copy-start | bytes 12292
  66.6 8.2 %collective-permute-start.13 = (bf16[400,256]{1,0:T(8,128)(2,1)}, bf16[400,256]{1,0:T(8,128)(2,1)S(1)}, u32[]{:S(2)}, u32[]{:S(2)}) collective-permute-start(bf16[400,256]{1,0:T(8,128)(2,1)} %image_residual.1.rest_0_), channel_id=1, source_target_pairs={{0,4},{1,5},{2,6},{3,7},{4,0},{5,1},{6,2},{7,3},{8,12},{9,13},{10,... | collective-permute-start | bytes 614408 | tf_op jit(solution)/shard_map/ppermute | solution.py:565
  70.5 6.9 %collective-permute-start.9 = (bf16[784,256]{1,0:T(8,128)(2,1)S(1)}, bf16[784,256]{1,0:T(8,128)(2,1)S(1)}, u32[]{:S(2)}, u32[]{:S(2)}) collective-permute-start(bf16[784,256]{1,0:T(8,128)(2,1)S(1)} %collective-permute-done.5.rest_1_), channel_id=1, source_target_pairs={{0,1},{1,0},{2,3},{3,2},{4,5},{5,4},{6,7},{7,6},{8,9},{9,8},{10,11... | collective-permute-start | bytes 1204232 | tf_op jit(solution)/shard_map/ppermute | solution.py:571
  72.1 7.0 %collective-permute-start.10 = (bf16[784,256]{1,0:T(8,128)(2,1)S(1)}, bf16[784,256]{1,0:T(8,128)(2,1)S(1)}, u32[]{:S(2)}, u32[]{:S(2)}) collective-permute-start(bf16[784,256]{1,0:T(8,128)(2,1)S(1)} %collective-permute-done.6.rest_2_), channel_id=1, source_target_pairs={{0,1},{1,0},{2,3},{3,2},{4,5},{5,4},{6,7},{7,6},{8,9},{9,8},{10,11... | collective-permute-start | bytes 1204232 | tf_op jit(solution)/shard_map/ppermute | solution.py:571
  72.2 7.0 %collective-permute-start.11 = (bf16[784,256]{1,0:T(8,128)(2,1)S(1)}, bf16[784,256]{1,0:T(8,128)(2,1)S(1)}, u32[]{:S(2)}, u32[]{:S(2)}) collective-permute-start(bf16[784,256]{1,0:T(8,128)(2,1)S(1)} %collective-permute-done.7.rest_3_), channel_id=1, source_target_pairs={{0,1},{1,0},{2,3},{3,2},{4,5},{5,4},{6,7},{7,6},{8,9},{9,8},{10,11... | collective-permute-start | bytes 1204232 | tf_op jit(solution)/shard_map/ppermute | solution.py:571
  74.8 11.1 %collective-permute-start.12 = (bf16[400,256]{1,0:T(8,128)(2,1)S(1)}, bf16[400,256]{1,0:T(8,128)(2,1)S(1)}, u32[]{:S(2)}, u32[]{:S(2)}) collective-permute-start(bf16[400,256]{1,0:T(8,128)(2,1)S(1)} %copy-done), channel_id=1, source_target_pairs={{0,2},{1,3},{2,4},{3,5},{4,6},{5,7},{6,0},{7,1},{8,10},{9,11},{10,... | collective-permute-start | bytes 614408 | tf_op jit(solution)/shard_map/ppermute | solution.py:565
  75.2 10.7 %collective-permute-start.14 = (bf16[400,256]{1,0:T(8,128)(2,1)S(1)}, bf16[400,256]{1,0:T(8,128)(2,1)S(1)}, u32[]{:S(2)}, u32[]{:S(2)}) collective-permute-start(bf16[400,256]{1,0:T(8,128)(2,1)S(1)} %copy-done), channel_id=1, source_target_pairs={{0,6},{1,7},{2,0},{3,1},{4,2},{5,3},{6,4},{7,5},{8,14},{9,15},{10,... | collective-permute-start | bytes 614408 | tf_op jit(solution)/shard_map/ppermute | solution.py:565
  77.5 9.0 %collective-permute-start.15 = (bf16[400,256]{1,0:T(8,128)(2,1)S(1)}, bf16[400,256]{1,0:T(8,128)(2,1)S(1)}, u32[]{:S(2)}, u32[]{:S(2)}) collective-permute-start(bf16[400,256]{1,0:T(8,128)(2,1)S(1)} %copy-done), channel_id=1, source_target_pairs={{0,1},{1,0},{2,3},{3,2},{4,5},{5,4},{6,7},{7,6},{8,9},{9,8},{10,11... | collective-permute-start | bytes 614408 | tf_op jit(solution)/shard_map/ppermute | solution.py:571
  79.1 7.3 %collective-permute-start.17 = (bf16[400,256]{1,0:T(8,128)(2,1)S(1)}, bf16[400,256]{1,0:T(8,128)(2,1)S(1)}, u32[]{:S(2)}, u32[]{:S(2)}) collective-permute-start(bf16[400,256]{1,0:T(8,128)(2,1)S(1)} %collective-permute-done.13.rest_2_), channel_id=1, source_target_pairs={{0,1},{1,0},{2,3},{3,2},{4,5},{5,4},{6,7},{7,6},{8,9},{9,8},{10,11... | collective-permute-start | bytes 614408 | tf_op jit(solution)/shard_map/ppermute | solution.py:571
  85.9 1.6 %collective-permute-start.16 = (bf16[400,256]{1,0:T(8,128)(2,1)S(1)}, bf16[400,256]{1,0:T(8,128)(2,1)S(1)}, u32[]{:S(2)}, u32[]{:S(2)}) collective-permute-start(bf16[400,256]{1,0:T(8,128)(2,1)S(1)} %collective-permute-done.12.rest_1_), channel_id=1, source_target_pairs={{0,1},{1,0},{2,3},{3,2},{4,5},{5,4},{6,7},{7,6},{8,9},{9,8},{10,11... | collective-permute-start | bytes 614408 | tf_op jit(solution)/shard_map/ppermute | solution.py:571
  86.3 1.5 %collective-permute-start.18 = (bf16[400,256]{1,0:T(8,128)(2,1)S(1)}, bf16[400,256]{1,0:T(8,128)(2,1)S(1)}, u32[]{:S(2)}, u32[]{:S(2)}) collective-permute-start(bf16[400,256]{1,0:T(8,128)(2,1)S(1)} %collective-permute-done.14.rest_3_), channel_id=1, source_target_pairs={{0,1},{1,0},{2,3},{3,2},{4,5},{5,4},{6,7},{7,6},{8,9},{9,8},{10,11... | collective-permute-start | bytes 614408 | tf_op jit(solution)/shard_map/ppermute | solution.py:571
  87.8 3.1 %copy-start.2 = (bf16[768,256]{1,0:T(8,128)(2,1)S(1)}, bf16[768,256]{1,0:T(8,128)(2,1)}, u32[]{:S(2)}) copy-start(bf16[768,256]{1,0:T(8,128)(2,1)} %get-tuple-element.73.both_from) | copy-start | bytes 1179652

commit v7 on v6

--- a/solution.py
+++ b/solution.py
@@ -490,9 +490,9 @@
     count = (len(refs) - 1) // 2
     copies = []
     for n, (source, target) in enumerate(zip(refs[0:count], refs[count : 2 * count])):
-        half = source.shape[0] // 2
-        spans = [pl.ds(0, half), pl.ds(half, half)]
-        copies += fetch([(source.at[p], target.at[p]) for p in spans], refs[-1], 2 * n)
+        step = source.shape[0] // 4
+        spans = [pl.ds(m * step, step) for m in range(4)]
+        copies += fetch([(source.at[p], target.at[p]) for p in spans], refs[-1], 4 * n)
     finish(copies)
 
 
@@ -502,7 +502,7 @@
         in_specs=[ANYWHERE] * len(arrays),
         out_specs=[IN_VMEM] * len(arrays),
         out_shape=[pltpu.VMEM(x.shape, x.dtype) for x in arrays],
-        scratch_shapes=[pltpu.SemaphoreType.DMA((2 * len(arrays),))],
+        scratch_shapes=[pltpu.SemaphoreType.DMA((4 * len(arrays),))],
         compiler_params=PARAMS,
         cost_estimate=SMALL,
         name="hold",
@@ -600,7 +600,7 @@
     targets = (key_target, value_target)
 
     images = image_embed.shape[0]
-    early, late = (2,), (1, 3, 0)
+    early, late = (2,), (0, 1, 3)
     sent_early, sent_late, scaled, lanes, *held = forward_other(
         text_embed, image_embed, gain, weights, (early, late)
     )

time: 93.3 us -> 93.3 us (level)
  no operation moved by 1% of the time
where the time goes in v7:
time: 93.3 us; the launch traced here: 92.9 us
  starting transfers between devices  40.9 us (44%)
  Pallas kernels  34.8 us (37%)
  waiting for transfers between devices  15.5 us (17%)
  between operations  1.01 us (1%)
    all_to_all x2, starting transfers between devices, route(): return lax.all_to_all(x, 'rows', split_axis=0, concat_axis=0, tiled=True)  20.9 us
    ppermute x9, waiting for transfers between devices, around(): lax.ppermute(x, 'tp', [(2 * y + c, 2 * ((y + shift) % RINGS) + c) for y i...  11.3 us
    ppermute x9, starting transfers between devices, around(): lax.ppermute(x, 'tp', [(2 * y + c, 2 * ((y + shift) % RINGS) + c) for y i...  10.5 us
    pallas_call x2, Pallas kernels, backward(): pl.pallas_call(functools.partial(backward_kernel, first, masked), in_spec...  9.71 us
    ppermute x10, starting transfers between devices, across(): return lax.ppermute(x, 'tp', [(i, i ^ 1) for i in range(2 * RINGS)])  9.5 us
    pallas_call x1, Pallas kernels, forward_other(): pl.pallas_call(functools.partial(forward_other_kernel, splits), in_specs=...  5.68 us
    pallas_call x2, Pallas kernels, forward_own(): pl.pallas_call(functools.partial(forward_own_kernel, split, close), in_sp...  4.52 us
    ppermute x10, waiting for transfers between devices, across(): return lax.ppermute(x, 'tp', [(i, i ^ 1) for i in range(2 * RINGS)])  4.24 us
  transfers between devices with their start and end apart: 21, of which 7 were waited for; matrix products, arithmetic and copies ran while one was open for 0% of the time, Pallas kernels for 29%

profile of v7, /device:TPU:1, one launch (start us, length us, event | category | flops | bytes accessed | tf_op | source)
XLA Modules:
  0.0 92.9 jit_solution(13589408830953265265)
XLA Ops:
  0.6 0.0 copy-start.4
  0.6 0.7 copy-done.4
  1.3 5.7 %forward_other.1 = (bf16[1,1168,256]{2,1,0:T(8,128)(2,1)S(1)}, bf16[3,1168,256]{2,1,0:T(8,128)(2,1)S(1)}, bf16[1152,1024]{1,0:T(8,128)(2,1)S(1)}, f32[16,128]{1,...) custom-call(bf16[768,1024]{1,0:T(8,128)(2,1)} %refs_2_, bf16[384,1024]{1,0:T(8,128)(2,1)} %refs_3_, ...), custom_call_target="tpu_custom_call" | custom-call | flops 1048576 | bytes 65536 | tf_op jit(solution)/shard_map/forward_other/pallas_call | solution.py:153
  7.0 3.3 %collective-permute-start = (bf16[1,1168,256]{2,1,0:T(8,128)(2,1)S(1)}, bf16[1,1168,256]{2,1,0:T(8,128)(2,1)S(1)}, u32[]{:S(2)}, u32[]{:S(2)}) collective-permute-start(bf16[1,1168,256]{2,1,0:T(8,128)(2,1)S(1)} %get-tuple-element.44), channel_id=1, source_target_pairs={{0,1},{1,0},{2,3},{3,2},{4,5},{5,4},{6,7},{7,6},{8,9},{9,8},{10,11... | collective-permute-start | bytes 1794056 | tf_op jit(solution)/shard_map/ppermute | solution.py:571
  10.3 1.6 %collective-permute-done.in_ref = bf16[1,1168,256]{2,1,0:T(8,128)(2,1)S(1)} collective-permute-done((bf16[1,1168,256]{2,1,0:T(8,128)(2,1)S(1)}, bf16[1,1168,256]{2,1,0:T(8,128)(2,1)S(1)}, u32[]{:S(2)}, u32[]{:S(2)}) %collective-permute-start) | collective-permute-done | bytes 598048 | tf_op jit(solution)/shard_map/ppermute | solution.py:571
  12.0 0.4 collective-permute-start.1
  12.4 0.8 forward_own.2
  13.2 0.0 copy-start.3
  13.2 1.3 %collective-permute-start.2 = (bf16[1168,256]{1,0:T(8,128)(2,1)S(1)}, bf16[1168,256]{1,0:T(8,128)(2,1)S(1)}, u32[]{:S(2)}, u32[]{:S(2)}) collective-permute-start(bf16[1168,256]{1,0:T(8,128)(2,1)S(1)} %forward_own.2), channel_id=1, source_target_pairs={{0,4},{1,5},{2,6},{3,7},{4,0},{5,1},{6,2},{7,3},{8,12},{9,13},{10,... | collective-permute-start | bytes 1794056 | tf_op jit(solution)/shard_map/ppermute | solution.py:565
  14.5 1.2 %collective-permute-done.1.in_ref = bf16[3,1168,256]{2,1,0:T(8,128)(2,1)S(1)} collective-permute-done((bf16[3,1168,256]{2,1,0:T(8,128)(2,1)S(1)}, bf16[3,1168,256]{2,1,0:T(8,128)(2,1)S(1)}, u32[]{:S(2)}, u32[]{:S(2)}) %collective-permute-start.1) | collective-permute-done | bytes 1794080 | tf_op jit(solution)/shard_map/ppermute | solution.py:571
  15.7 3.7 %forward_own.3 = (bf16[1168,256]{1,0:T(8,128)(2,1)}, bf16[1168,256]{1,0:T(8,128)(2,1)}, bf16[1168,256]{1,0:T(8,128)(2,1)S(1)}) custom-call(bf16[1152,1024]{1,0:T(8,128)(2,1)S(1)} %get-tuple-element.45.scaled_ref, f32[16,128]{1,0:T(8,128)S(1)} %get-tuple-element.41.lanes_ref, bf16[1024,1024]{1,0:T(8,128)(2,1)S(1)} %get-tuple-element.42.wk_ref, ...), custom_call_target="tpu_custom_call" | custom-call | flops 1048576 | bytes 65536 | tf_op jit(solution)/shard_map/forward_own/pallas_call | solution.py:191
  19.4 0.1 collective-permute-start.3
  19.5 2.7 %collective-permute-start.4 = (bf16[1168,256]{1,0:T(8,128)(2,1)S(1)}, bf16[1168,256]{1,0:T(8,128)(2,1)S(1)}, u32[]{:S(2)}, u32[]{:S(2)}) collective-permute-start(bf16[1168,256]{1,0:T(8,128)(2,1)S(1)} %get-tuple-element.50), channel_id=1, source_target_pairs={{0,6},{1,7},{2,0},{3,1},{4,2},{5,3},{6,4},{7,5},{8,14},{9,15},{10,... | collective-permute-start | bytes 1794056 | tf_op jit(solution)/shard_map/ppermute | solution.py:565
  22.1 0.0 copy-done.3
  22.1 2.4 %gather_targets.1 = bf16[768,256]{1,0:T(8,128)(2,1)} custom-call(s32[1,512]{1,0:T(1,128)S(1)} %bitcast.8, bf16[768,128]{1,0:T(8,128)(2,1)} %kt_from.1, bf16[768,128]{1,0:T(8,128)(2,1)} %vt_from.1), custom_call_target="tpu_custom_call" | custom-call | flops 1048576 | bytes 65536 | tf_op jit(solution)/shard_map/gather_targets/pallas_call | solution.py:424
  24.5 9.8 %all-to-all-start = ((bf16[32,24,256]{2,1,0:T(8,128)(2,1)}), bf16[32,24,256]{2,1,0:T(8,128)(2,1)S(1)}, u32[]{:S(2)}, u32[]{:S(2)}) async-start(bf16[32,24,256]{2,1,0:T(8,128)(2,1)} %bitcast.17), calls=%async_computation | async-start | bytes 786432 | tf_op jit(solution)/shard_map/all_to_all | solution.py:583
  34.4 0.0 collective-permute-done.2.b
  34.4 8.7 %collective-permute-done.3.c = bf16[1168,256]{1,0:T(8,128)(2,1)S(1)} collective-permute-done((bf16[1168,256]{1,0:T(8,128)(2,1)}, bf16[1168,256]{1,0:T(8,128)(2,1)S(1)}, u32[]{:S(2)}, u32[]{:S(2)}) %collective-permute-start.3) | collective-permute-done | bytes 598048 | tf_op jit(solution)/shard_map/ppermute | solution.py:565
  43.1 0.0 collective-permute-done.4.d
  43.1 3.5 %text_combine.1 = (bf16[768,256]{1,0:T(8,128)(2,1)}, bf16[784,256]{1,0:T(8,128)(2,1)}, f32[16,128]{1,0:T(8,128)S(1)}) custom-call(bf16[1168,256]{1,0:T(8,128)(2,1)} %get-tuple-element.53.a, bf16[1168,256]{1,0:T(8,128)(2,1)S(1)} %collective-permute-done.2.b, bf16[1168,256]{1,0:T(8,128)(2,1)S(1)} %collective-permute-done.3.c, ...), custom_call_target="tpu_custom_call" | custom-call | flops 1048576 | bytes 65536 | tf_op jit(solution)/shard_map/text_combine/pallas_call | solution.py:265
  46.6 0.1 collective-permute-start.5
  46.7 2.1 %collective-permute-start.6 = (bf16[784,256]{1,0:T(8,128)(2,1)}, bf16[784,256]{1,0:T(8,128)(2,1)S(1)}, u32[]{:S(2)}, u32[]{:S(2)}) collective-permute-start(bf16[784,256]{1,0:T(8,128)(2,1)} %get-tuple-element.51.rest_0_), channel_id=1, source_target_pairs={{0,4},{1,5},{2,6},{3,7},{4,0},{5,1},{6,2},{7,3},{8,12},{9,13},{10,... | collective-permute-start | bytes 1204232 | tf_op jit(solution)/shard_map/ppermute | solution.py:565
  48.8 1.1 %collective-permute-start.7 = (bf16[784,256]{1,0:T(8,128)(2,1)}, bf16[784,256]{1,0:T(8,128)(2,1)S(1)}, u32[]{:S(2)}, u32[]{:S(2)}) collective-permute-start(bf16[784,256]{1,0:T(8,128)(2,1)} %get-tuple-element.51.rest_0_), channel_id=1, source_target_pairs={{0,6},{1,7},{2,0},{3,1},{4,2},{5,3},{6,4},{7,5},{8,14},{9,15},{10,... | collective-permute-start | bytes 1204232 | tf_op jit(solution)/shard_map/ppermute | solution.py:565
  49.9 1.3 %collective-permute-start.8 = (bf16[784,256]{1,0:T(8,128)(2,1)}, bf16[784,256]{1,0:T(8,128)(2,1)}, u32[]{:S(2)}, u32[]{:S(2)}) collective-permute-start(bf16[784,256]{1,0:T(8,128)(2,1)} %get-tuple-element.51.rest_0_), channel_id=1, source_target_pairs={{0,1},{1,0},{2,3},{3,2},{4,5},{5,4},{6,7},{7,6},{8,9},{9,8},{10,11... | collective-permute-start | bytes 1204232 | tf_op jit(solution)/shard_map/ppermute | solution.py:571
  51.3 2.2 %image_keys.1 = (bf16[768,256]{1,0:T(8,128)(2,1)}, bf16[384,256]{1,0:T(8,128)(2,1)}) custom-call(bf16[1168,256]{1,0:T(8,128)(2,1)} %get-tuple-element.53.a, bf16[1168,256]{1,0:T(8,128)(2,1)S(1)} %collective-permute-done.2.b, bf16[1168,256]{1,0:T(8,128)(2,1)S(1)} %collective-permute-done.3.c, bf16[1168,256]{1,0:T(8,128)(2,1)S(1)} %collective-permute-done.4.d, ...), custom_call_target="tpu_custom_call" | custom-call | flops 1048576 | bytes 65536 | tf_op jit(solution)/shard_map/image_keys/pallas_call | solution.py:353
  53.4 0.0 all-to-all-done
  53.4 2.0 %image_residual.1.rest_0_ = bf16[400,256]{1,0:T(8,128)(2,1)} custom-call(bf16[384,256]{1,0:T(8,128)(2,1)} %get-tuple-element.55.both_from, bf16[768,256]{1,0:T(8,128)(2,1)S(1)} %bitcast.7, s32[1,512]{1,0:T(1,128)S(1)} %bitcast.10), custom_call_target="tpu_custom_call" | custom-call | flops 1048576 | bytes 65536 | tf_op jit(solution)/shard_map/image_residual/pallas_call | solution.py:388
  55.5 11.1 %all-to-all-start.1 = ((bf16[32,24,256]{2,1,0:T(8,128)(2,1)}), bf16[32,24,256]{2,1,0:T(8,128)(2,1)S(1)}, u32[]{:S(2)}, u32[]{:S(2)}) async-start(bf16[32,24,256]{2,1,0:T(8,128)(2,1)} %bitcast.18), calls=%async_computation.1 | async-start | bytes 786432 | tf_op jit(solution)/shard_map/all_to_all | solution.py:583
  66.5 0.0 copy-start
  66.6 0.0 copy-start.1
  66.6 0.0 copy-start.5
  66.6 0.5 collective-permute-start.13
  67.1 0.0 collective-permute-done.5.rest_1_
  67.1 0.0 collective-permute-done.6.rest_2_
  67.1 0.5 collective-permute-done.7.rest_3_
  67.6 3.0 %hold.1 = (bf16[1024,1024]{1,0:T(8,128)(2,1)S(1)}, bf16[1024,1024]{1,0:T(8,128)(2,1)S(1)}, bf16[768,1024]{1,0:T(8,128)(2,1)S(1)}, bf16[384,1024]{1,0:T(8,128)(2,1)S(1)}) custom-call(bf16[1024,1024]{1,0:T(8,128)(2,1)} %refs_0_.1, bf16[1024,1024]{1,0:T(8,128)(2,1)} %refs_1_.1, bf16[768,1024]{1,0:T(8,128)(2,1)} %refs_2_, bf16[384,1024]{1,0:T(8,128)(2,1)} %refs_3_), custom_call_target="tpu_custom_call" | custom-call | flops 1048576 | bytes 65536 | tf_op jit(solution)/shard_map/hold/pallas_call | solution.py:500
  70.6 1.6 %collective-permute-start.9 = (bf16[784,256]{1,0:T(8,128)(2,1)S(1)}, bf16[784,256]{1,0:T(8,128)(2,1)S(1)}, u32[]{:S(2)}, u32[]{:S(2)}) collective-permute-start(bf16[784,256]{1,0:T(8,128)(2,1)S(1)} %collective-permute-done.5.rest_1_), channel_id=1, source_target_pairs={{0,1},{1,0},{2,3},{3,2},{4,5},{5,4},{6,7},{7,6},{8,9},{9,8},{10,11... | collective-permute-start | bytes 1204232 | tf_op jit(solution)/shard_map/ppermute | solution.py:571
  72.2 0.1 collective-permute-start.10
  72.3 0.4 collective-permute-start.11
  72.7 2.1 %collective-permute-done.13.rest_2_ = bf16[400,256]{1,0:T(8,128)(2,1)S(1)} collective-permute-done((bf16[400,256]{1,0:T(8,128)(2,1)}, bf16[400,256]{1,0:T(8,128)(2,1)S(1)}, u32[]{:S(2)}, u32[]{:S(2)}) %collective-permute-start.13) | collective-permute-done | bytes 204832 | tf_op jit(solution)/shard_map/ppermute | solution.py:565
  74.8 0.0 copy-done
  74.8 0.4 collective-permute-start.12
  75.2 0.0 collective-permute-done.8.rest_4_
  75.2 2.3 %collective-permute-start.14 = (bf16[400,256]{1,0:T(8,128)(2,1)S(1)}, bf16[400,256]{1,0:T(8,128)(2,1)S(1)}, u32[]{:S(2)}, u32[]{:S(2)}) collective-permute-start(bf16[400,256]{1,0:T(8,128)(2,1)S(1)} %copy-done), channel_id=1, source_target_pairs={{0,6},{1,7},{2,0},{3,1},{4,2},{5,3},{6,4},{7,5},{8,14},{9,15},{10,... | collective-permute-start | bytes 614408 | tf_op jit(solution)/shard_map/ppermute | solution.py:565
  77.5 0.0 collective-permute-done.9.rest_5_
  77.5 1.7 %collective-permute-start.15 = (bf16[400,256]{1,0:T(8,128)(2,1)S(1)}, bf16[400,256]{1,0:T(8,128)(2,1)S(1)}, u32[]{:S(2)}, u32[]{:S(2)}) collective-permute-start(bf16[400,256]{1,0:T(8,128)(2,1)S(1)} %copy-done), channel_id=1, source_target_pairs={{0,1},{1,0},{2,3},{3,2},{4,5},{5,4},{6,7},{7,6},{8,9},{9,8},{10,11... | collective-permute-start | bytes 614408 | tf_op jit(solution)/shard_map/ppermute | solution.py:571
  79.1 0.0 collective-permute-done.10.rest_6_
  79.1 0.1 collective-permute-start.17
  79.2 0.0 collective-permute-done.11.rest_7_
  79.2 0.0 copy-done.1
  79.2 0.0 copy-done.5
  79.2 6.6 %backward.2 = bf16[768,1024]{1,0:T(8,128)(2,1)} custom-call(bf16[768,1024]{1,0:T(8,128)(2,1)S(1)} %get-tuple-element.61.x_ref, f32[1,1024]{1,0:T(1,128)S(1)} %bitcast.15, s32[1,512]{1,0:T(1,128)S(1)} %bitcast.11, f32[16,128]{1,0:T(8,128)S(1)} %get-tuple-element.54.squares_ref, bf16[1024,1024]{1,0:T(8,128)(2,1)S(1)} %get-tuple-element.59.wk_ref, ...), custom_call_target="tpu_custom_call" | custom-call | flops 1048576 | bytes 65536 | tf_op jit(solution)/shard_map/backward/pallas_call | solution.py:547
  85.8 0.0 collective-permute-done.12.rest_1_
  85.8 0.0 collective-permute-done.14.rest_3_
  85.8 0.5 collective-permute-start.16
  86.4 0.1 collective-permute-start.18
  86.5 0.0 collective-permute-done.15.rest_4_
  86.5 0.0 collective-permute-done.17.rest_6_
  86.5 1.0 %collective-permute-done.16.rest_5_ = bf16[400,256]{1,0:T(8,128)(2,1)S(1)} collective-permute-done((bf16[400,256]{1,0:T(8,128)(2,1)S(1)}, bf16[400,256]{1,0:T(8,128)(2,1)S(1)}, u32[]{:S(2)}, u32[]{:S(2)}) %collective-permute-start.16) | collective-permute-done | bytes 204832 | tf_op jit(solution)/shard_map/ppermute | solution.py:571
  87.4 0.4 collective-permute-done.18.rest_7_
  87.8 3.1 %backward.3 = bf16[384,1024]{1,0:T(8,128)(2,1)} custom-call(bf16[384,1024]{1,0:T(8,128)(2,1)S(1)} %get-tuple-element.58.x_ref, f32[1,1024]{1,0:T(1,128)S(1)} %bitcast.16, s32[1,512]{1,0:T(1,128)S(1)} %bitcast.12, f32[16,128]{1,0:T(8,128)S(1)} %get-tuple-element.54.squares_ref, bf16[1024,1024]{1,0:T(8,128)(2,1)S(1)} %get-tuple-element.59.wk_ref, ...), custom_call_target="tpu_custom_call" | custom-call | flops 1048576 | bytes 65536 | tf_op jit(solution)/shard_map/backward/pallas_call | solution.py:547
  90.9 0.0 all-to-all-done.1
  91.0 0.0 copy-done.2
  91.0 1.8 %merge.1 = (bf16[768,128]{1,0:T(8,128)(2,1)}, bf16[768,128]{1,0:T(8,128)(2,1)}) custom-call(s32[1,512]{1,0:T(1,128)S(1)} %bitcast.13, bf16[768,256]{1,0:T(8,128)(2,1)S(1)} %bitcast.6, bf16[768,256]{1,0:T(8,128)(2,1)S(1)} %copy-done.2), custom_call_target="tpu_custom_call" | custom-call | flops 1048576 | bytes 65536 | tf_op jit(solution)/shard_map/merge/pallas_call | solution.py:471
  (1 shorter events, 0.0 us)
Async XLA Ops:
  0.6 0.7 copy-start.4
  7.0 5.0 %collective-permute-start = (bf16[1,1168,256]{2,1,0:T(8,128)(2,1)S(1)}, bf16[1,1168,256]{2,1,0:T(8,128)(2,1)S(1)}, u32[]{:S(2)}, u32[]{:S(2)}) collective-permute-start(bf16[1,1168,256]{2,1,0:T(8,128)(2,1)S(1)} %get-tuple-element.44), channel_id=1, source_target_pairs={{0,1},{1,0},{2,3},{3,2},{4,5},{5,4},{6,7},{7,6},{8,9},{9,8},{10,11... | collective-permute-start | bytes 1794056 | tf_op jit(solution)/shard_map/ppermute | solution.py:571
  12.0 3.7 %collective-permute-start.1 = (bf16[3,1168,256]{2,1,0:T(8,128)(2,1)S(1)}, bf16[3,1168,256]{2,1,0:T(8,128)(2,1)S(1)}, u32[]{:S(2)}, u32[]{:S(2)}) collective-permute-start(bf16[3,1168,256]{2,1,0:T(8,128)(2,1)S(1)} %get-tuple-element.47), channel_id=1, source_target_pairs={{0,1},{1,0},{2,3},{3,2},{4,5},{5,4},{6,7},{7,6},{8,9},{9,8},{10,11... | collective-permute-start | bytes 5382152 | tf_op jit(solution)/shard_map/ppermute | solution.py:571
  13.2 8.9 %copy-start.3 = (s32[512]{0:T(512)S(1)}, s32[512]{0:T(512)}, u32[]{:S(2)}) copy-start(s32[512]{0:T(512)} %param.10) | copy-start | bytes 6148
  13.2 21.1 %collective-permute-start.2 = (bf16[1168,256]{1,0:T(8,128)(2,1)S(1)}, bf16[1168,256]{1,0:T(8,128)(2,1)S(1)}, u32[]{:S(2)}, u32[]{:S(2)}) collective-permute-start(bf16[1168,256]{1,0:T(8,128)(2,1)S(1)} %forward_own.2), channel_id=1, source_target_pairs={{0,4},{1,5},{2,6},{3,7},{4,0},{5,1},{6,2},{7,3},{8,12},{9,13},{10,... | collective-permute-start | bytes 1794056 | tf_op jit(solution)/shard_map/ppermute | solution.py:565
  19.4 23.7 %collective-permute-start.3 = (bf16[1168,256]{1,0:T(8,128)(2,1)}, bf16[1168,256]{1,0:T(8,128)(2,1)S(1)}, u32[]{:S(2)}, u32[]{:S(2)}) collective-permute-start(bf16[1168,256]{1,0:T(8,128)(2,1)} %get-tuple-element.49), channel_id=1, source_target_pairs={{0,2},{1,3},{2,4},{3,5},{4,6},{5,7},{6,0},{7,1},{8,10},{9,11},{10,... | collective-permute-start | bytes 1794056 | tf_op jit(solution)/shard_map/ppermute | solution.py:565
  19.5 23.6 %collective-permute-start.4 = (bf16[1168,256]{1,0:T(8,128)(2,1)S(1)}, bf16[1168,256]{1,0:T(8,128)(2,1)S(1)}, u32[]{:S(2)}, u32[]{:S(2)}) collective-permute-start(bf16[1168,256]{1,0:T(8,128)(2,1)S(1)} %get-tuple-element.50), channel_id=1, source_target_pairs={{0,6},{1,7},{2,0},{3,1},{4,2},{5,3},{6,4},{7,5},{8,14},{9,15},{10,... | collective-permute-start | bytes 1794056 | tf_op jit(solution)/shard_map/ppermute | solution.py:565
  24.5 28.9 %all-to-all-start = ((bf16[32,24,256]{2,1,0:T(8,128)(2,1)}), bf16[32,24,256]{2,1,0:T(8,128)(2,1)S(1)}, u32[]{:S(2)}, u32[]{:S(2)}) async-start(bf16[32,24,256]{2,1,0:T(8,128)(2,1)} %bitcast.17), calls=%async_computation | async-start | bytes 786432 | tf_op jit(solution)/shard_map/all_to_all | solution.py:583
  46.6 20.5 %collective-permute-start.5 = (bf16[784,256]{1,0:T(8,128)(2,1)}, bf16[784,256]{1,0:T(8,128)(2,1)S(1)}, u32[]{:S(2)}, u32[]{:S(2)}) collective-permute-start(bf16[784,256]{1,0:T(8,128)(2,1)} %get-tuple-element.51.rest_0_), channel_id=1, source_target_pairs={{0,2},{1,3},{2,4},{3,5},{4,6},{5,7},{6,0},{7,1},{8,10},{9,11},{10,... | collective-permute-start | bytes 1204232 | tf_op jit(solution)/shard_map/ppermute | solution.py:565
  46.7 20.4 %collective-permute-start.6 = (bf16[784,256]{1,0:T(8,128)(2,1)}, bf16[784,256]{1,0:T(8,128)(2,1)S(1)}, u32[]{:S(2)}, u32[]{:S(2)}) collective-permute-start(bf16[784,256]{1,0:T(8,128)(2,1)} %get-tuple-element.51.rest_0_), channel_id=1, source_target_pairs={{0,4},{1,5},{2,6},{3,7},{4,0},{5,1},{6,2},{7,3},{8,12},{9,13},{10,... | collective-permute-start | bytes 1204232 | tf_op jit(solution)/shard_map/ppermute | solution.py:565
  48.8 18.8 %collective-permute-start.7 = (bf16[784,256]{1,0:T(8,128)(2,1)}, bf16[784,256]{1,0:T(8,128)(2,1)S(1)}, u32[]{:S(2)}, u32[]{:S(2)}) collective-permute-start(bf16[784,256]{1,0:T(8,128)(2,1)} %get-tuple-element.51.rest_0_), channel_id=1, source_target_pairs={{0,6},{1,7},{2,0},{3,1},{4,2},{5,3},{6,4},{7,5},{8,14},{9,15},{10,... | collective-permute-start | bytes 1204232 | tf_op jit(solution)/shard_map/ppermute | solution.py:565
  49.9 25.2 %collective-permute-start.8 = (bf16[784,256]{1,0:T(8,128)(2,1)}, bf16[784,256]{1,0:T(8,128)(2,1)}, u32[]{:S(2)}, u32[]{:S(2)}) collective-permute-start(bf16[784,256]{1,0:T(8,128)(2,1)} %get-tuple-element.51.rest_0_), channel_id=1, source_target_pairs={{0,1},{1,0},{2,3},{3,2},{4,5},{5,4},{6,7},{7,6},{8,9},{9,8},{10,11... | collective-permute-start | bytes 1204232 | tf_op jit(solution)/shard_map/ppermute | solution.py:571
  55.5 35.5 %all-to-all-start.1 = ((bf16[32,24,256]{2,1,0:T(8,128)(2,1)}), bf16[32,24,256]{2,1,0:T(8,128)(2,1)S(1)}, u32[]{:S(2)}, u32[]{:S(2)}) async-start(bf16[32,24,256]{2,1,0:T(8,128)(2,1)} %bitcast.18), calls=%async_computation.1 | async-start | bytes 786432 | tf_op jit(solution)/shard_map/all_to_all | solution.py:583
  66.5 8.2 %copy-start = (bf16[400,256]{1,0:T(8,128)(2,1)S(1)}, bf16[400,256]{1,0:T(8,128)(2,1)}, u32[]{:S(2)}) copy-start(bf16[400,256]{1,0:T(8,128)(2,1)} %image_residual.1.rest_0_) | copy-start | bytes 614404
  66.6 12.7 %copy-start.1 = (bf16[784,256]{1,0:T(8,128)(2,1)S(1)}, bf16[784,256]{1,0:T(8,128)(2,1)}, u32[]{:S(2)}) copy-start(bf16[784,256]{1,0:T(8,128)(2,1)} %get-tuple-element.51.rest_0_) | copy-start | bytes 1204228
  66.6 12.7 %copy-start.5 = (f32[1024]{0:T(1024)S(1)}, f32[1024]{0:T(1024)}, u32[]{:S(2)}) copy-start(f32[1024]{0:T(1024)} %param.11) | copy-start | bytes 12292
  66.6 8.2 %collective-permute-start.13 = (bf16[400,256]{1,0:T(8,128)(2,1)}, bf16[400,256]{1,0:T(8,128)(2,1)S(1)}, u32[]{:S(2)}, u32[]{:S(2)}) collective-permute-start(bf16[400,256]{1,0:T(8,128)(2,1)} %image_residual.1.rest_0_), channel_id=1, source_target_pairs={{0,4},{1,5},{2,6},{3,7},{4,0},{5,1},{6,2},{7,3},{8,12},{9,13},{10,... | collective-permute-start | bytes 614408 | tf_op jit(solution)/shard_map/ppermute | solution.py:565
  70.6 6.9 %collective-permute-start.9 = (bf16[784,256]{1,0:T(8,128)(2,1)S(1)}, bf16[784,256]{1,0:T(8,128)(2,1)S(1)}, u32[]{:S(2)}, u32[]{:S(2)}) collective-permute-start(bf16[784,256]{1,0:T(8,128)(2,1)S(1)} %collective-permute-done.5.rest_1_), channel_id=1, source_target_pairs={{0,1},{1,0},{2,3},{3,2},{4,5},{5,4},{6,7},{7,6},{8,9},{9,8},{10,11... | collective-permute-start | bytes 1204232 | tf_op jit(solution)/shard_map/ppermute | solution.py:571
  72.2 6.9 %collective-permute-start.10 = (bf16[784,256]{1,0:T(8,128)(2,1)S(1)}, bf16[784,256]{1,0:T(8,128)(2,1)S(1)}, u32[]{:S(2)}, u32[]{:S(2)}) collective-permute-start(bf16[784,256]{1,0:T(8,128)(2,1)S(1)} %collective-permute-done.6.rest_2_), channel_id=1, source_target_pairs={{0,1},{1,0},{2,3},{3,2},{4,5},{5,4},{6,7},{7,6},{8,9},{9,8},{10,11... | collective-permute-start | bytes 1204232 | tf_op jit(solution)/shard_map/ppermute | solution.py:571
  72.3 6.9 %collective-permute-start.11 = (bf16[784,256]{1,0:T(8,128)(2,1)S(1)}, bf16[784,256]{1,0:T(8,128)(2,1)S(1)}, u32[]{:S(2)}, u32[]{:S(2)}) collective-permute-start(bf16[784,256]{1,0:T(8,128)(2,1)S(1)} %collective-permute-done.7.rest_3_), channel_id=1, source_target_pairs={{0,1},{1,0},{2,3},{3,2},{4,5},{5,4},{6,7},{7,6},{8,9},{9,8},{10,11... | collective-permute-start | bytes 1204232 | tf_op jit(solution)/shard_map/ppermute | solution.py:571
  74.8 11.1 %collective-permute-start.12 = (bf16[400,256]{1,0:T(8,128)(2,1)S(1)}, bf16[400,256]{1,0:T(8,128)(2,1)S(1)}, u32[]{:S(2)}, u32[]{:S(2)}) collective-permute-start(bf16[400,256]{1,0:T(8,128)(2,1)S(1)} %copy-done), channel_id=1, source_target_pairs={{0,2},{1,3},{2,4},{3,5},{4,6},{5,7},{6,0},{7,1},{8,10},{9,11},{10,... | collective-permute-start | bytes 614408 | tf_op jit(solution)/shard_map/ppermute | solution.py:565
  75.2 10.7 %collective-permute-start.14 = (bf16[400,256]{1,0:T(8,128)(2,1)S(1)}, bf16[400,256]{1,0:T(8,128)(2,1)S(1)}, u32[]{:S(2)}, u32[]{:S(2)}) collective-permute-start(bf16[400,256]{1,0:T(8,128)(2,1)S(1)} %copy-done), channel_id=1, source_target_pairs={{0,6},{1,7},{2,0},{3,1},{4,2},{5,3},{6,4},{7,5},{8,14},{9,15},{10,... | collective-permute-start | bytes 614408 | tf_op jit(solution)/shard_map/ppermute | solution.py:565
  77.5 9.0 %collective-permute-start.15 = (bf16[400,256]{1,0:T(8,128)(2,1)S(1)}, bf16[400,256]{1,0:T(8,128)(2,1)S(1)}, u32[]{:S(2)}, u32[]{:S(2)}) collective-permute-start(bf16[400,256]{1,0:T(8,128)(2,1)S(1)} %copy-done), channel_id=1, source_target_pairs={{0,1},{1,0},{2,3},{3,2},{4,5},{5,4},{6,7},{7,6},{8,9},{9,8},{10,11... | collective-permute-start | bytes 614408 | tf_op jit(solution)/shard_map/ppermute | solution.py:571
  79.1 7.3 %collective-permute-start.17 = (bf16[400,256]{1,0:T(8,128)(2,1)S(1)}, bf16[400,256]{1,0:T(8,128)(2,1)S(1)}, u32[]{:S(2)}, u32[]{:S(2)}) collective-permute-start(bf16[400,256]{1,0:T(8,128)(2,1)S(1)} %collective-permute-done.13.rest_2_), channel_id=1, source_target_pairs={{0,1},{1,0},{2,3},{3,2},{4,5},{5,4},{6,7},{7,6},{8,9},{9,8},{10,11... | collective-permute-start | bytes 614408 | tf_op jit(solution)/shard_map/ppermute | solution.py:571
  85.8 1.6 %collective-permute-start.16 = (bf16[400,256]{1,0:T(8,128)(2,1)S(1)}, bf16[400,256]{1,0:T(8,128)(2,1)S(1)}, u32[]{:S(2)}, u32[]{:S(2)}) collective-permute-start(bf16[400,256]{1,0:T(8,128)(2,1)S(1)} %collective-permute-done.12.rest_1_), channel_id=1, source_target_pairs={{0,1},{1,0},{2,3},{3,2},{4,5},{5,4},{6,7},{7,6},{8,9},{9,8},{10,11... | collective-permute-start | bytes 614408 | tf_op jit(solution)/shard_map/ppermute | solution.py:571
  86.4 1.5 %collective-permute-start.18 = (bf16[400,256]{1,0:T(8,128)(2,1)S(1)}, bf16[400,256]{1,0:T(8,128)(2,1)S(1)}, u32[]{:S(2)}, u32[]{:S(2)}) collective-permute-start(bf16[400,256]{1,0:T(8,128)(2,1)S(1)} %collective-permute-done.14.rest_3_), channel_id=1, source_target_pairs={{0,1},{1,0},{2,3},{3,2},{4,5},{5,4},{6,7},{7,6},{8,9},{9,8},{10,11... | collective-permute-start | bytes 614408 | tf_op jit(solution)/shard_map/ppermute | solution.py:571
  87.8 3.1 %copy-start.2 = (bf16[768,256]{1,0:T(8,128)(2,1)S(1)}, bf16[768,256]{1,0:T(8,128)(2,1)}, u32[]{:S(2)}) copy-start(bf16[768,256]{1,0:T(8,128)(2,1)} %get-tuple-element.73.both_from) | copy-start | bytes 1179652
